TPU v7x, 32 devices: a whole 2x2x4 slice. The times are simulated.
32 devices in a mesh: seq: 8 (over z, y), head: 4 (over x, core).
Axes of the slice: x: 2, y: 2, z: 4, core: 2. Of those that a mesh axis runs over, the one named last changes fastest.
Arguments:
- tokens_in: bfloat16 [2048, 1536], P('seq'), may hold values from -6 to 6
- cotangent: bfloat16 [2048, 1536], P('seq'), may hold values from -6 to 6
- document_ids: int32 [2048], replicated, may hold values from 0 to 2, as said below
- expert_routes: int32 [2048, 2], P('seq'), may hold values from 0 to 3, all different within a row; in each aligned block of 256 rows (0 to 255, 256 to 511, ...) at most 160 rows name the same one
- norm_mixer: bfloat16 [1536], replicated, may hold values from 0.5 to 1.5
- mixer_inner: bfloat16 [1536, 3072], P(None, 'head'), may hold values from -0.15625 to 0.15625
- mixer_gate: bfloat16 [1536, 3072], P(None, 'head'), may hold values from -0.15625 to 0.15625
- conv_taps: bfloat16 [4, 3072], P(None, 'head'), may hold values from -5 to 5
- conv_bias: bfloat16 [3072], P('head'), may hold values from -3 to 3
- state_proj: bfloat16 [3072, 128], P('head'), may hold values from -0.109375 to 0.109375
- step_proj: bfloat16 [96, 3072], P(None, 'head'), may hold values from -0.625 to 0.625
- step_bias: bfloat16 [3072], P('head'), may hold values from -10 to -3
- decay_log: bfloat16 [3072, 16], P('head'), may hold values from -1 to 1
- skip_gain: bfloat16 [3072], P('head'), may hold values from 0.5 to 1.5
- mixer_out: bfloat16 [3072, 1536], P('head'), may hold values from -0.3125 to 0.3125
- norm_ffn: bfloat16 [1536], replicated, may hold values from 0.5 to 1.5
- ffn_gate: bfloat16 [1536, 4096], P(None, 'head'), may hold values from -0.15625 to 0.15625
- ffn_up: bfloat16 [1536, 4096], P(None, 'head'), may hold values from -0.15625 to 0.15625
- ffn_down: bfloat16 [4096, 1536], P('head'), may hold values from -0.125 to 0.125
- norm_attn: bfloat16 [1536], replicated, may hold values from 0.5 to 1.5
- attn_query: bfloat16 [1536, 1536], P(None, 'head'), may hold values from -0.15625 to 0.15625
- attn_key: bfloat16 [1536, 512], P(None, 'head'), may hold values from -0.15625 to 0.15625
- attn_value: bfloat16 [1536, 512], P(None, 'head'), may hold values from -0.15625 to 0.15625
- attn_output: bfloat16 [1536, 1536], P('head'), may hold values from -1.25 to 1.25
- norm_moe: bfloat16 [1536], replicated, may hold values from 0.5 to 1.5
- router: bfloat16 [1536, 4], replicated, may hold values from -0.15625 to 0.15625
- expert_gate: bfloat16 [4, 1536, 1024], P(None, None, 'head'), may hold values from -0.15625 to 0.15625
- expert_up: bfloat16 [4, 1536, 1024], P(None, None, 'head'), may hold values from -0.15625 to 0.15625
- expert_down: bfloat16 [4, 1024, 1536], P(None, 'head'), may hold values from -0.25 to 0.25
Outputs:
- mixed_out: bfloat16 [2048, 1536], P('seq')
- grad_tokens: float32 [2048, 1536], P('seq')
- grad_norm_mixer: float32 [1536], P('seq')
- grad_mixer_inner: float32 [1536, 3072], P('seq', 'head')
- grad_mixer_gate: float32 [1536, 3072], P('seq', 'head')
- grad_conv_taps: float32 [4, 3072], P(None, ('head', 'seq'))
- grad_conv_bias: float32 [3072], P(('head', 'seq'))
- grad_state_proj: float32 [3072, 128], P(('head', 'seq'))
- grad_step_proj: float32 [96, 3072], P(None, ('head', 'seq'))
- grad_step_bias: float32 [3072], P(('head', 'seq'))
- grad_decay_log: float32 [3072, 16], P(('head', 'seq'))
- grad_skip_gain: float32 [3072], P(('head', 'seq'))
- grad_mixer_out: float32 [3072, 1536], P('head', 'seq')
- grad_norm_ffn: float32 [1536], P('seq')
- grad_ffn_gate: float32 [1536, 4096], P('seq', 'head')
- grad_ffn_up: float32 [1536, 4096], P('seq', 'head')
- grad_ffn_down: float32 [4096, 1536], P('head', 'seq')
- grad_norm_attn: float32 [1536], P('seq')
- grad_attn_query: float32 [1536, 1536], P('seq', 'head')
- grad_attn_key: float32 [1536, 512], P('seq', 'head')
- grad_attn_value: float32 [1536, 512], P('seq', 'head')
- grad_attn_output: float32 [1536, 1536], P('head', 'seq')
- grad_norm_moe: float32 [1536], P('seq')
- grad_router: float32 [1536, 4], P('seq')
- grad_expert_gate: float32 [4, 1536, 1024], P(None, 'seq', 'head')
- grad_expert_up: float32 [4, 1536, 1024], P(None, 'seq', 'head')
- grad_expert_down: float32 [4, 1024, 1536], P(None, 'head', 'seq')
Inputs may be any that keep to these rules, and one draw needn't show every extreme that they name: `document_ids`: document ids never fall along the tokens; document 1 starts within the first 256 tokens and ends within the last 256 tokens. `expert_routes`: A token's two experts differ; among the tokens of one index of seq no expert is named more than 160 times.
All inputs are finite; a program needn't handle non-finite values.
Results may differ from a plain program's by a relative error of at most 0.03.
Values may be sent and summed in bfloat16 or wider, within the bound.
A program may use at most 256 MiB of HBM per device.

v0:
```python
import math

import jax
import jax.numpy as jnp
from jax import lax
from jax.sharding import PartitionSpec as P

HEAD_DIM = 64
CAP = 160


highest = lax.Precision.HIGHEST
epsilon = 1e-05
masked_score = -1e30


def from_behind(block, axis, distance):
    devices = range(lax.axis_size(axis))
    route = [(i - distance, i) for i in devices if i - distance in devices]
    return lax.ppermute(block, axis, route)


def to_low(values):
    return values.astype(jnp.bfloat16)


def product(left, right):
    return jnp.dot(left, right, preferred_element_type=jnp.float32)


def exact_product(left, right):
    return jnp.dot(left, right, precision=highest, preferred_element_type=jnp.float32)


def rms_scale(values, gain):
    return values * lax.rsqrt(jnp.mean(values * values, axis=-1, keepdims=True) + epsilon) * gain


def rms_back(values, gain, upstream):
    unused, pullback = jax.vjp(rms_scale, values, gain)
    return pullback(upstream)


def silu_slope(values):
    logistic = jax.nn.sigmoid(values)
    return logistic * (1.0 + values * (1.0 - logistic))


def head_total(values):
    return lax.psum(values, "head")


def block_shape(row_total):
    length = math.gcd(row_total, 32)
    return (length, row_total // length)


def state_sweep(initial, step_dt, inputs, inject, readout, retain, decay_rate, collect):
    length, count = block_shape(step_dt.shape[0])

    def reshaped(values):
        return values.reshape((count, length) + values.shape[1:])

    def advance(carried, pieces):
        step_rows, input_rows, inject_rows, readout_rows, retain_rows = pieces
        decays = jnp.exp(-step_rows[:, :, None] * decay_rate[None]) * retain_rows[:, None, None]
        drives = (step_rows * input_rows)[:, :, None] * inject_rows[:, None, :]
        begin = carried
        outputs = []
        for offset in range(length):
            carried = carried * decays[offset] + drives[offset]
            if collect:
                outputs.append(jnp.sum(carried * readout_rows[offset][None, :], axis=1))
        if collect:
            return (carried, (jnp.stack(outputs), begin))
        return (carried, begin)

    return lax.scan(
        advance,
        initial,
        (
            reshaped(step_dt),
            reshaped(inputs),
            reshaped(inject),
            reshaped(readout),
            reshaped(retain),
        ),
    )


def adjoint_summary(step_dt, readout, upstream, retain, decay_rate):
    length, count = block_shape(step_dt.shape[0])

    def reshaped(values):
        return values.reshape((count, length) + values.shape[1:])

    def retreat(carried, pieces):
        step_rows, readout_rows, upstream_rows, retain_rows = pieces
        decays = jnp.exp(-step_rows[:, :, None] * decay_rate[None]) * retain_rows[:, None, None]
        for offset in reversed(range(length)):
            adjoint = readout_rows[offset][None, :] * upstream_rows[offset][:, None] + carried
            carried = decays[offset] * adjoint
        return (carried, None)

    initial = jnp.zeros(decay_rate.shape, jnp.float32)
    final, unused = lax.scan(
        retreat,
        initial,
        (reshaped(step_dt), reshaped(readout), reshaped(upstream), reshaped(retain)),
        reverse=True,
    )
    return final


def adjoint_sweep(incoming, starts, step_dt, inputs, inject, readout, upstream, retain, decay_rate):
    row_total = step_dt.shape[0]
    length, count = block_shape(row_total)

    def reshaped(values):
        return values.reshape((count, length) + values.shape[1:])

    def retreat(carried, pieces):
        adjoint_in, rate_grad = carried
        begin, step_rows, input_rows, inject_rows, readout_rows, upstream_rows, retain_rows = pieces
        decays = jnp.exp(-step_rows[:, :, None] * decay_rate[None]) * retain_rows[:, None, None]
        drives = (step_rows * input_rows)[:, :, None] * inject_rows[:, None, :]
        states = []
        running = begin
        for offset in range(length):
            running = running * decays[offset] + drives[offset]
            states.append(running)
        step_list = [None] * length
        input_list = [None] * length
        inject_list = [None] * length
        readout_list = [None] * length
        for offset in reversed(range(length)):
            previous = states[offset - 1] if offset > 0 else begin
            adjoint = readout_rows[offset][None, :] * upstream_rows[offset][:, None] + adjoint_in
            readout_list[offset] = jnp.sum(upstream_rows[offset][:, None] * states[offset], axis=0)
            through = adjoint * previous * decays[offset]
            rate_grad = rate_grad - through * step_rows[offset][:, None]
            injected = jnp.sum(adjoint * inject_rows[offset][None, :], axis=1)
            step_list[offset] = (
                -jnp.sum(through * decay_rate, axis=1) + input_rows[offset] * injected
            )
            input_list[offset] = step_rows[offset] * injected
            inject_list[offset] = jnp.sum(
                adjoint * (step_rows[offset] * input_rows[offset])[:, None], axis=0
            )
            adjoint_in = decays[offset] * adjoint
        return (
            (adjoint_in, rate_grad),
            (
                jnp.stack(step_list),
                jnp.stack(input_list),
                jnp.stack(inject_list),
                jnp.stack(readout_list),
            ),
        )

    initial = (incoming, jnp.zeros(decay_rate.shape, jnp.float32))
    carried, stacked = lax.scan(
        retreat,
        initial,
        (
            starts,
            reshaped(step_dt),
            reshaped(inputs),
            reshaped(inject),
            reshaped(readout),
            reshaped(upstream),
            reshaped(retain),
        ),
        reverse=True,
    )
    step_grad = stacked[0].reshape(row_total, -1)
    input_grad = stacked[1].reshape(row_total, -1)
    inject_grad = stacked[2].reshape(row_total, -1)
    readout_grad = stacked[3].reshape(row_total, -1)
    return (carried[1], step_grad, input_grad, inject_grad, readout_grad)


def body(
    tokens_in,
    cotangent,
    document_ids,
    expert_routes,
    norm_mixer,
    mixer_inner,
    mixer_gate,
    conv_taps,
    conv_bias,
    state_proj,
    step_proj,
    step_bias,
    decay_log,
    skip_gain,
    mixer_out,
    norm_ffn,
    ffn_gate,
    ffn_up,
    ffn_down,
    norm_attn,
    attn_query,
    attn_key,
    attn_value,
    attn_output,
    norm_moe,
    router,
    expert_gate,
    expert_up,
    expert_down,
):
    seq_count = lax.axis_size("seq")
    row_count = tokens_in.shape[0]
    total_rows = seq_count * row_count
    first_row = lax.axis_index("seq") * row_count
    last_row = first_row + row_count - 1
    local_docs = lax.dynamic_slice_in_dim(document_ids, first_row, row_count)
    reach = conv_taps.shape[0] - 1
    border = jnp.arange(reach, dtype=jnp.int32)
    docs_before = jnp.take(document_ids, jnp.maximum(first_row - reach + border, 0))
    docs_after = jnp.take(document_ids, jnp.minimum(first_row + row_count + border, total_rows - 1))
    docs_prior = jnp.concatenate([docs_before[reach - 1 :], local_docs[:-1]])
    retain = (local_docs == docs_prior).astype(jnp.float32)
    tokens = tokens_in.astype(jnp.float32)
    gain_mixer = norm_mixer.astype(jnp.float32)
    normed_one = to_low(rms_scale(tokens, gain_mixer))
    conv_in = to_low(product(normed_one, mixer_inner))
    gate_in = product(normed_one, mixer_gate)
    conv_edge = from_behind(conv_in[row_count - reach :], "seq", 1)
    extended = jnp.concatenate([conv_edge, conv_in]).astype(jnp.float32)
    docs_ext = jnp.concatenate([docs_before, local_docs])
    taps = conv_taps.astype(jnp.float32)
    conv_sum = conv_bias.astype(jnp.float32)[None, :]
    masks = []
    for offset in range(reach + 1):
        same_doc = (docs_ext[offset : offset + row_count] == local_docs).astype(jnp.float32)[
            :, None
        ]
        masks.append(same_doc)
        conv_sum = conv_sum + taps[offset] * extended[offset : offset + row_count] * same_doc
    activated = jax.nn.silu(conv_sum)
    act_low = to_low(activated)
    projected = head_total(product(act_low, state_proj))
    rank_size = step_proj.shape[0]
    state_size = decay_log.shape[1]
    step_low = to_low(projected[:, :rank_size])
    inject = projected[:, rank_size : rank_size + state_size]
    readout = projected[:, rank_size + state_size :]
    step_pre = product(step_low, step_proj) + step_bias.astype(jnp.float32)
    step_dt = jax.nn.softplus(step_pre)
    decay_rate = jnp.exp(decay_log.astype(jnp.float32))
    zero_state = jnp.zeros(decay_rate.shape, jnp.float32)
    whole_decay = jnp.exp(-decay_rate * jnp.sum(step_dt, axis=0)[:, None]) * jnp.prod(retain)
    local_last, unused = state_sweep(
        zero_state, step_dt, activated, inject, readout, retain, decay_rate, False
    )

    def hop_forward(position, incoming):
        return from_behind(
            (whole_decay * incoming + local_last).astype(jnp.bfloat16), "seq", 1
        ).astype(jnp.float32)

    state_in = lax.fori_loop(0, seq_count - 1, hop_forward, zero_state)
    state_out, collected = state_sweep(
        state_in, step_dt, activated, inject, readout, retain, decay_rate, True
    )
    scanned = collected[0].reshape(row_count, -1)
    starts = collected[1]
    skipping = skip_gain.astype(jnp.float32)
    mixed_state = scanned + skipping * activated
    gate_act = jax.nn.silu(gate_in)
    gated = to_low(mixed_state * gate_act)
    hidden_one = tokens + head_total(product(gated, mixer_out))
    gain_ffn = norm_ffn.astype(jnp.float32)
    normed_two = to_low(rms_scale(hidden_one, gain_ffn))
    gate_two = product(normed_two, ffn_gate)
    up_two = product(normed_two, ffn_up)
    ffn_act = to_low(jax.nn.silu(gate_two) * up_two)
    hidden_two = hidden_one + head_total(product(ffn_act, ffn_down))
    gain_attn = norm_attn.astype(jnp.float32)
    normed_three = to_low(rms_scale(hidden_two, gain_attn))
    queries = to_low(product(normed_three, attn_query))
    key_rows = to_low(product(normed_three, attn_key))
    value_rows = to_low(product(normed_three, attn_value))
    shared_heads = attn_key.shape[1] // HEAD_DIM
    group_size = attn_query.shape[1] // attn_key.shape[1]
    query_heads = queries.reshape(row_count, shared_heads, group_size, HEAD_DIM)
    query_pos = first_row + jnp.arange(row_count, dtype=jnp.int32)

    def visible(offset, block_rows):
        key_pos = offset + jnp.arange(block_rows, dtype=jnp.int32)
        key_docs = lax.dynamic_slice_in_dim(document_ids, offset, block_rows)
        return (key_pos[None, :] <= query_pos[:, None]) & (key_docs[None, :] == local_docs[:, None])

    def split_blocks(pieces, begin_row):
        key_piece, value_piece = pieces
        piece_rows = key_piece.shape[0]
        block_rows = math.gcd(piece_rows, 512)
        block_count = piece_rows // block_rows
        key_blocks = key_piece.reshape(block_count, block_rows, shared_heads, HEAD_DIM)
        value_blocks = value_piece.reshape(block_count, block_rows, shared_heads, HEAD_DIM)
        offsets = begin_row + block_rows * jnp.arange(block_count, dtype=jnp.int32)
        return (block_rows, (key_blocks, value_blocks, offsets))

    start_max = jnp.full((shared_heads, group_size, row_count), masked_score, jnp.float32)
    block_rows, blocked = split_blocks(
        (
            lax.all_gather(key_rows, "seq", axis=0, tiled=True),
            lax.all_gather(value_rows, "seq", axis=0, tiled=True),
        ),
        jnp.int32(0),
    )

    def visit_block(running, element):
        key_block, value_block, offset = element

        def compute(current):
            row_max, row_sum, weighted = current
            scores = (
                jnp.einsum(
                    "qgrd,kgd->grqk", query_heads, key_block, preferred_element_type=jnp.float32
                )
                * 0.125
            )
            allowed = visible(offset, block_rows)
            masked = jnp.where(allowed, scores, masked_score)
            new_max = jnp.maximum(row_max, jnp.max(masked, axis=-1))
            weights = jnp.where(allowed, jnp.exp(masked - new_max[..., None]), 0.0)
            factor = jnp.exp(row_max - new_max)
            row_sum = row_sum * factor + jnp.sum(weights, axis=-1)
            weighted = weighted * factor[..., None] + jnp.einsum(
                "grqk,kgd->grqd", to_low(weights), value_block, preferred_element_type=jnp.float32
            )
            return (new_max, row_sum, weighted)

        return (lax.cond(offset <= last_row, compute, lambda untouched: untouched, running), None)

    result, unused_out = lax.scan(
        visit_block,
        (
            start_max,
            jnp.zeros_like(start_max),
            jnp.zeros((shared_heads, group_size, row_count, HEAD_DIM), jnp.float32),
        ),
        blocked,
    )
    folded = result
    attended = folded[2] / folded[1][..., None]
    log_sum = folded[0] + jnp.log(folded[1])
    attended_low = to_low(attended.transpose(2, 0, 1, 3).reshape(row_count, -1))
    hidden_three = hidden_two + head_total(product(attended_low, attn_output))
    gain_moe = norm_moe.astype(jnp.float32)
    normed_four = to_low(rms_scale(hidden_three, gain_moe))
    router_wide = router.astype(jnp.float32)
    logits = exact_product(normed_four.astype(jnp.float32), router_wide)
    chosen = jnp.take_along_axis(logits, expert_routes, axis=1)
    gate_weights = jax.nn.softmax(chosen, axis=1)
    expert_count = router.shape[1]
    route_flat = expert_routes.reshape(-1)
    one_hot = (route_flat[:, None] == jnp.arange(expert_count, dtype=jnp.int32)).astype(jnp.int32)
    within = jnp.sum((jnp.cumsum(one_hot, axis=0) - one_hot) * one_hot, axis=1)
    slot_index = route_flat * CAP + within
    pair_count = route_flat.shape[0]
    slot_pairs = (
        jnp.zeros((expert_count * CAP,), jnp.int32)
        .at[slot_index]
        .set(jnp.arange(pair_count, dtype=jnp.int32))
    )
    filled = jnp.zeros((expert_count * CAP,), jnp.float32).at[slot_index].set(1.0)
    expert_in = (jnp.take(normed_four, slot_pairs // 2, axis=0) * to_low(filled)[:, None]).reshape(
        expert_count, CAP, -1
    )
    gate_four = jnp.einsum(
        "ecd,edf->ecf", expert_in, expert_gate, preferred_element_type=jnp.float32
    )
    up_four = jnp.einsum("ecd,edf->ecf", expert_in, expert_up, preferred_element_type=jnp.float32)
    expert_act = to_low(jax.nn.silu(gate_four) * up_four)
    expert_res = jnp.einsum(
        "ecf,efd->ecd", expert_act, expert_down, preferred_element_type=jnp.float32
    ).reshape(expert_count * CAP, -1)
    picked = jnp.take(expert_res, slot_index, axis=0).reshape(row_count, 2, -1)
    hidden_four = hidden_three + head_total(jnp.sum(gate_weights[:, :, None] * picked, axis=1))
    mixed_out = to_low(hidden_four)
    upstream = cotangent.astype(jnp.float32)
    pair_grads = (gate_weights[:, :, None] * upstream[:, None, :]).reshape(pair_count, -1)
    res_grad = to_low(jnp.take(pair_grads, slot_pairs, axis=0) * filled[:, None]).reshape(
        expert_count, CAP, -1
    )
    dots_part = jnp.sum(picked * upstream[:, None, :], axis=2)
    act_back = to_low(
        jnp.einsum("ecd,efd->ecf", res_grad, expert_down, preferred_element_type=jnp.float32)
    ).astype(jnp.float32)
    gating_grad = to_low(act_back * up_four * silu_slope(gate_four))
    upward_grad = to_low(act_back * jax.nn.silu(gate_four))
    grad_expert_down = jnp.einsum(
        "ecf,ecd->efd", expert_act, res_grad, preferred_element_type=jnp.float32
    )
    grad_expert_gate = jnp.einsum(
        "ecd,ecf->edf", expert_in, gating_grad, preferred_element_type=jnp.float32
    )
    grad_expert_up = jnp.einsum(
        "ecd,ecf->edf", expert_in, upward_grad, preferred_element_type=jnp.float32
    )
    slot_grads = (
        jnp.einsum("ecf,edf->ecd", gating_grad, expert_gate, preferred_element_type=jnp.float32)
        + jnp.einsum("ecf,edf->ecd", upward_grad, expert_up, preferred_element_type=jnp.float32)
    ).reshape(expert_count * CAP, -1)
    token_part = jnp.sum(jnp.take(slot_grads, slot_index, axis=0).reshape(row_count, 2, -1), axis=1)
    normed_grad, dots = (
        lax.psum(token_part.astype(jnp.bfloat16), "head").astype(jnp.float32),
        lax.psum(dots_part.astype(jnp.bfloat16), "head").astype(jnp.float32),
    )
    chosen_grad = gate_weights * (dots - jnp.sum(gate_weights * dots, axis=1, keepdims=True))
    logit_grad = jnp.sum(
        (expert_routes[:, :, None] == jnp.arange(expert_count, dtype=jnp.int32)).astype(jnp.float32)
        * chosen_grad[:, :, None],
        axis=1,
    )
    grad_router = exact_product(normed_four.astype(jnp.float32).T, logit_grad)
    normed_grad = normed_grad + exact_product(logit_grad, router_wide.T)
    hidden_grad, grad_norm_moe = rms_back(hidden_three, gain_moe, normed_grad)
    three_grad = upstream + hidden_grad
    branch_grad = to_low(three_grad)
    grad_attn_output = product(attended_low.T, branch_grad)
    attended_grad = to_low(product(branch_grad, attn_output.T))
    out_heads = attended_grad.reshape(row_count, shared_heads, group_size, HEAD_DIM).transpose(
        1, 2, 0, 3
    )
    delta = jnp.sum(out_heads.astype(jnp.float32) * attended, axis=-1)
    key_width = key_rows.shape[1]
    initial = (
        jnp.zeros((shared_heads, group_size, row_count, HEAD_DIM), jnp.float32),
        jnp.zeros((total_rows, key_width), jnp.float32),
        jnp.zeros((total_rows, key_width), jnp.float32),
    )
    attend_block_rows, blocked = split_blocks(
        (
            lax.all_gather(key_rows, "seq", axis=0, tiled=True),
            lax.all_gather(value_rows, "seq", axis=0, tiled=True),
        ),
        jnp.int32(0),
    )

    def visit_back(running, element):
        key_block, value_block, offset = element

        def compute(current):
            query_acc, key_acc, value_acc = current
            scores = (
                jnp.einsum(
                    "qgrd,kgd->grqk", query_heads, key_block, preferred_element_type=jnp.float32
                )
                * 0.125
            )
            allowed = visible(offset, attend_block_rows)
            probs = jnp.where(allowed, jnp.exp(scores - log_sum[..., None]), 0.0)
            value_part = jnp.einsum(
                "grqk,grqd->kgd", to_low(probs), out_heads, preferred_element_type=jnp.float32
            )
            prob_grad = jnp.einsum(
                "grqd,kgd->grqk", out_heads, value_block, preferred_element_type=jnp.float32
            )
            score_grad = to_low(probs * (prob_grad - delta[..., None]))
            query_acc = (
                query_acc
                + jnp.einsum(
                    "grqk,kgd->grqd", score_grad, key_block, preferred_element_type=jnp.float32
                )
                * 0.125
            )
            key_part = (
                jnp.einsum(
                    "grqk,qgrd->kgd", score_grad, query_heads, preferred_element_type=jnp.float32
                )
                * 0.125
            )
            key_acc = lax.dynamic_update_slice_in_dim(
                key_acc,
                lax.dynamic_slice_in_dim(key_acc, offset, attend_block_rows, 0)
                + key_part.reshape(attend_block_rows, -1),
                offset,
                0,
            )
            value_acc = lax.dynamic_update_slice_in_dim(
                value_acc,
                lax.dynamic_slice_in_dim(value_acc, offset, attend_block_rows, 0)
                + value_part.reshape(attend_block_rows, -1),
                offset,
                0,
            )
            return (query_acc, key_acc, value_acc)

        return (lax.cond(offset <= last_row, compute, lambda untouched: untouched, running), None)

    result, unused_out = lax.scan(visit_back, initial, blocked)
    query_acc, key_acc, value_acc = result
    key_sum, value_sum = (
        lax.psum_scatter(
            key_acc.astype(jnp.bfloat16), "seq", scatter_dimension=0, tiled=True
        ).astype(jnp.float32),
        lax.psum_scatter(
            value_acc.astype(jnp.bfloat16), "seq", scatter_dimension=0, tiled=True
        ).astype(jnp.float32),
    )
    query_grad = to_low(query_acc.transpose(2, 0, 1, 3).reshape(row_count, -1))
    key_grad = to_low(key_sum)
    value_grad = to_low(value_sum)
    grad_attn_query = product(normed_three.T, query_grad)
    grad_attn_key = product(normed_three.T, key_grad)
    grad_attn_value = product(normed_three.T, value_grad)
    normed_grad = head_total(
        product(query_grad, attn_query.T)
        + product(key_grad, attn_key.T)
        + product(value_grad, attn_value.T)
    )
    hidden_grad, grad_norm_attn = rms_back(hidden_two, gain_attn, normed_grad)
    two_grad = three_grad + hidden_grad
    branch_grad = to_low(two_grad)
    grad_ffn_down = product(ffn_act.T, branch_grad)
    ffn_back = to_low(product(branch_grad, ffn_down.T)).astype(jnp.float32)
    feed_gate_grad = to_low(ffn_back * up_two * silu_slope(gate_two))
    feed_up_grad = to_low(ffn_back * jax.nn.silu(gate_two))
    grad_ffn_gate = product(normed_two.T, feed_gate_grad)
    grad_ffn_up = product(normed_two.T, feed_up_grad)
    normed_grad = head_total(product(feed_gate_grad, ffn_gate.T) + product(feed_up_grad, ffn_up.T))
    hidden_grad, grad_norm_ffn = rms_back(hidden_one, gain_ffn, normed_grad)
    one_grad = two_grad + hidden_grad
    branch_grad = to_low(one_grad)
    grad_mixer_out = product(gated.T, branch_grad)
    gated_grad = to_low(product(branch_grad, mixer_out.T)).astype(jnp.float32)
    scan_grad = gated_grad * gate_act
    gate_in_grad = to_low(gated_grad * mixed_state * silu_slope(gate_in))
    grad_skip_gain = jnp.sum(scan_grad * activated, axis=0)
    local_back = adjoint_summary(step_dt, readout, scan_grad, retain, decay_rate)

    def hop_backward(position, incoming):
        return from_behind(
            (whole_decay * incoming + local_back).astype(jnp.bfloat16), "seq", -1
        ).astype(jnp.float32)

    state_after = lax.fori_loop(0, seq_count - 1, hop_backward, zero_state)
    rate_grad, step_grad, input_grad, inject_grad, readout_grad = adjoint_sweep(
        state_after, starts, step_dt, activated, inject, readout, scan_grad, retain, decay_rate
    )
    grad_decay_log = rate_grad * decay_rate
    pre_grad = step_grad * jax.nn.sigmoid(step_pre)
    grad_step_bias = jnp.sum(pre_grad, axis=0)
    pre_low = to_low(pre_grad)
    grad_step_proj = product(step_low.T, pre_low)
    proj_part = jnp.concatenate([product(pre_low, step_proj.T), inject_grad, readout_grad], axis=1)
    proj_low = to_low(head_total(proj_part))
    grad_state_proj = product(act_low.T, proj_low)
    act_total = input_grad + skipping * scan_grad + product(proj_low, state_proj.T)
    conv_grad = act_total * silu_slope(conv_sum)
    grad_conv_bias = jnp.sum(conv_grad, axis=0)
    after_edge = from_behind(conv_grad[:reach], "seq", -1)
    grad_ext = jnp.concatenate([conv_grad, after_edge])
    docs_next = jnp.concatenate([local_docs, docs_after])
    conv_in_grad = jnp.zeros_like(conv_grad)
    tap_rows = []
    for offset in range(reach + 1):
        tap_rows.append(
            jnp.sum(conv_grad * extended[offset : offset + row_count] * masks[offset], axis=0)
        )
        lead = reach - offset
        same_next = (docs_next[lead : lead + row_count] == local_docs).astype(jnp.float32)[:, None]
        conv_in_grad = conv_in_grad + taps[offset] * grad_ext[lead : lead + row_count] * same_next
    grad_conv_taps = jnp.stack(tap_rows)
    conv_low = to_low(conv_in_grad)
    grad_mixer_inner = product(normed_one.T, conv_low)
    grad_mixer_gate = product(normed_one.T, gate_in_grad)
    normed_grad = head_total(product(conv_low, mixer_inner.T) + product(gate_in_grad, mixer_gate.T))
    hidden_grad, grad_norm_mixer = rms_back(tokens, gain_mixer, normed_grad)
    grad_tokens = one_grad + hidden_grad
    summed = (
        lax.psum_scatter(
            grad_norm_mixer.astype(jnp.bfloat16), "seq", scatter_dimension=0, tiled=True
        ).astype(jnp.float32),
        lax.psum_scatter(
            grad_mixer_inner.astype(jnp.bfloat16), "seq", scatter_dimension=0, tiled=True
        ).astype(jnp.float32),
        lax.psum_scatter(
            grad_mixer_gate.astype(jnp.bfloat16), "seq", scatter_dimension=0, tiled=True
        ).astype(jnp.float32),
        lax.psum_scatter(
            grad_conv_taps.astype(jnp.bfloat16), "seq", scatter_dimension=1, tiled=True
        ).astype(jnp.float32),
        lax.psum_scatter(
            grad_conv_bias.astype(jnp.bfloat16), "seq", scatter_dimension=0, tiled=True
        ).astype(jnp.float32),
        lax.psum_scatter(
            grad_state_proj.astype(jnp.bfloat16), "seq", scatter_dimension=0, tiled=True
        ).astype(jnp.float32),
        lax.psum_scatter(
            grad_step_proj.astype(jnp.bfloat16), "seq", scatter_dimension=1, tiled=True
        ).astype(jnp.float32),
        lax.psum_scatter(
            grad_step_bias.astype(jnp.bfloat16), "seq", scatter_dimension=0, tiled=True
        ).astype(jnp.float32),
        lax.psum_scatter(
            grad_decay_log.astype(jnp.bfloat16), "seq", scatter_dimension=0, tiled=True
        ).astype(jnp.float32),
        lax.psum_scatter(
            grad_skip_gain.astype(jnp.bfloat16), "seq", scatter_dimension=0, tiled=True
        ).astype(jnp.float32),
        lax.psum_scatter(
            grad_mixer_out.astype(jnp.bfloat16), "seq", scatter_dimension=1, tiled=True
        ).astype(jnp.float32),
        lax.psum_scatter(
            grad_norm_ffn.astype(jnp.bfloat16), "seq", scatter_dimension=0, tiled=True
        ).astype(jnp.float32),
        lax.psum_scatter(
            grad_ffn_gate.astype(jnp.bfloat16), "seq", scatter_dimension=0, tiled=True
        ).astype(jnp.float32),
        lax.psum_scatter(
            grad_ffn_up.astype(jnp.bfloat16), "seq", scatter_dimension=0, tiled=True
        ).astype(jnp.float32),
        lax.psum_scatter(
            grad_ffn_down.astype(jnp.bfloat16), "seq", scatter_dimension=1, tiled=True
        ).astype(jnp.float32),
        lax.psum_scatter(
            grad_norm_attn.astype(jnp.bfloat16), "seq", scatter_dimension=0, tiled=True
        ).astype(jnp.float32),
        lax.psum_scatter(
            grad_attn_query.astype(jnp.bfloat16), "seq", scatter_dimension=0, tiled=True
        ).astype(jnp.float32),
        lax.psum_scatter(
            grad_attn_key.astype(jnp.bfloat16), "seq", scatter_dimension=0, tiled=True
        ).astype(jnp.float32),
        lax.psum_scatter(
            grad_attn_value.astype(jnp.bfloat16), "seq", scatter_dimension=0, tiled=True
        ).astype(jnp.float32),
        lax.psum_scatter(
            grad_attn_output.astype(jnp.bfloat16), "seq", scatter_dimension=1, tiled=True
        ).astype(jnp.float32),
        lax.psum_scatter(
            grad_norm_moe.astype(jnp.bfloat16), "seq", scatter_dimension=0, tiled=True
        ).astype(jnp.float32),
        lax.psum_scatter(
            grad_router.astype(jnp.bfloat16), "seq", scatter_dimension=0, tiled=True
        ).astype(jnp.float32),
        lax.psum_scatter(
            grad_expert_gate.astype(jnp.bfloat16), "seq", scatter_dimension=1, tiled=True
        ).astype(jnp.float32),
        lax.psum_scatter(
            grad_expert_up.astype(jnp.bfloat16), "seq", scatter_dimension=1, tiled=True
        ).astype(jnp.float32),
        lax.psum_scatter(
            grad_expert_down.astype(jnp.bfloat16), "seq", scatter_dimension=2, tiled=True
        ).astype(jnp.float32),
    )
    return (
        mixed_out,
        grad_tokens,
        summed[0],
        summed[1],
        summed[2],
        summed[3],
        summed[4],
        summed[5],
        summed[6],
        summed[7],
        summed[8],
        summed[9],
        summed[10],
        summed[11],
        summed[12],
        summed[13],
        summed[14],
        summed[15],
        summed[16],
        summed[17],
        summed[18],
        summed[19],
        summed[20],
        summed[21],
        summed[22],
        summed[23],
        summed[24],
    )


def solution(mesh):
    in_specs = (
        P("seq", None),
        P("seq", None),
        P(),
        P("seq", None),
        P(),
        P(None, "head"),
        P(None, "head"),
        P(None, "head"),
        P("head"),
        P("head", None),
        P(None, "head"),
        P("head"),
        P("head", None),
        P("head"),
        P("head", None),
        P(),
        P(None, "head"),
        P(None, "head"),
        P("head", None),
        P(),
        P(None, "head"),
        P(None, "head"),
        P(None, "head"),
        P("head", None),
        P(),
        P(),
        P(None, None, "head"),
        P(None, None, "head"),
        P(None, "head", None),
    )
    out_specs = (
        P("seq", None),
        P("seq", None),
        P("seq"),
        P("seq", "head"),
        P("seq", "head"),
        P(None, ("head", "seq")),
        P(("head", "seq")),
        P(("head", "seq"), None),
        P(None, ("head", "seq")),
        P(("head", "seq")),
        P(("head", "seq"), None),
        P(("head", "seq")),
        P("head", "seq"),
        P("seq"),
        P("seq", "head"),
        P("seq", "head"),
        P("head", "seq"),
        P("seq"),
        P("seq", "head"),
        P("seq", "head"),
        P("seq", "head"),
        P("head", "seq"),
        P("seq"),
        P("seq", None),
        P(None, "seq", "head"),
        P(None, "seq", "head"),
        P(None, "head", "seq"),
    )
    return jax.shard_map(body, mesh=mesh, in_specs=in_specs, out_specs=out_specs, check_vma=False)
```

profile of v0, /device:TPU:0, one launch (start us, length us, event | category | flops | bytes accessed | tf_op | source)
XLA Modules:
  0.0 2984.4 jit_solution(14475426134360450625)
XLA Ops:
  28.6 29.8 all-reduce.19.cloned.1.call-done
  62.6 51.5 %while.120 = (s32[]{:T(128)}, f32[768,16]{0,1:T(8,128)S(1)}, f32[8,32,768]{2,1,0:T(8,128)}, f32[768,16]{0,1:T(8,128)S(1)}, f32[8,32]{1,0:T(8,128)}, /*index=5*/f...) while((s32[]{:T(128)}, f32[768,16]{0,1:T(8,128)S(1)}, f32[8,32,768]{2,1,0:T(8,128)}, ...), condition=%wide.region_5.7_spmd.clone, body=%wide.region_4.6_spmd.clone.sunk | while | flops 2027523 | bytes 7035387 | solution.py:78
  114.1 43.2 %while.121 = (s32[]{:T(128)}, f32[768,16]{0,1:T(8,128)S(1)}, f32[768,16]{0,1:T(8,128)S(1)}, f32[768,16]{0,1:T(8,128)S(1)}, s32[]{:T(128)}, /*index=5*/s32[]{:T(128)}) while((s32[]{:T(128)}, f32[768,16]{0,1:T(8,128)S(1)}, f32[768,16]{0,1:T(8,128)S(1)}, f32[768,16]{0,1:T(8,128)S(1)}, s32[]{:T(128)}, /*index=5*/s32[]{:T(128)}) %tuple.923), condition=%wide.region_7.9_spmd.clone, body=%wide.region_6.8_spmd.clone.sunk | while | flops 61443 | bytes 344183 | solution.py:265
  158.2 189.6 %while.117 = (s32[]{:T(128)}, f32[768,16]{0,1:T(8,128)S(1)}, f32[8,32,768]{2,1,0:T(8,128)}, f32[8,768,16]{1,2,0:T(8,128)}, f32[8,32,768]{2,1,0:T(8,128)}, /*inde...) while((s32[]{:T(128)}, f32[768,16]{0,1:T(8,128)S(1)}, ...), condition=%wide.region_41.43_spmd, body=%wide.region_8.42_spmd.sunk | while | flops 3170337 | bytes 24343948 | solution.py:78
  357.8 42.5 %all-reduce.21.cloned.1.call-done = f32[256,1536]{1,0:T(8,128)} async-done(((f32[256,1536]{1,0:T(8,128)}), f32[256,1536]{1,0:T(8,128)}) %all-reduce.21.cloned.1.call-update) | async-done | bytes 1572880 | tf_op jit(solution)/shard_map/psum | solution.py:50
  414.1 39.1 %all-reduce.23.cloned.1.call-done = f32[256,1536]{1,0:T(8,128)} async-done(((f32[256,1536]{1,0:T(8,128)}), f32[256,1536]{1,0:T(8,128)}) %all-reduce.23.cloned.1.call-update) | async-done | bytes 1572880 | tf_op jit(solution)/shard_map/psum | solution.py:50
  457.1 33.4 %all_gather.8 = bf16[2048,128]{1,0:T(8,128)(2,1)} all-gather(bf16[256,128]{1,0:T(8,128)(2,1)S(1)} %convolution_convert_fusion.23), channel_id=1, replica_groups=mesh['seq'=8,'head'=4] {'seq'}, dimensions={0}, use_global_device_ids=true | all-gather | bytes 589824 | tf_op jit(solution)/shard_map/all_gather | solution.py:310
  501.0 33.3 %all_gather.9 = bf16[2048,128]{1,0:T(8,128)(2,1)} all-gather(bf16[256,128]{1,0:T(8,128)(2,1)S(1)} %convolution_convert_fusion.22), channel_id=1, replica_groups=mesh['seq'=8,'head'=4] {'seq'}, dimensions={0}, use_global_device_ids=true | all-gather | bytes 589824 | tf_op jit(solution)/shard_map/all_gather | solution.py:311
  577.4 53.1 %all-reduce.25.cloned.1.call-done = f32[256,1536]{1,0:T(8,128)} async-done(((f32[256,1536]{1,0:T(8,128)}), f32[256,1536]{1,0:T(8,128)}) %all-reduce.25.cloned.1.call-update) | async-done | bytes 1572880 | tf_op jit(solution)/shard_map/psum | solution.py:50
  718.4 34.7 %all-reduce.27.cloned.1.call-done = bf16[256,1536]{1,0:T(8,128)(2,1)} async-done(((bf16[256,1536]{1,0:T(8,128)(2,1)}), bf16[256,1536]{1,0:T(8,128)(2,1)}) %all-reduce.27.cloned.1.call-update) | async-done | bytes 786448 | tf_op jit(solution)/shard_map/psum | solution.py:412
  761.2 24.7 while.119
  790.9 109.9 %reduce-scatter.29.cloned.1.call-done = bf16[256,128]{0,1:T(8,128)(2,1)} async-done(((bf16[2048,128]{0,1:T(8,128)(2,1)}), bf16[256,128]{0,1:T(8,128)(2,1)}) %reduce-scatter.29.cloned.1.call-update) | async-done | bytes 65552 | tf_op jit(solution)/shard_map/reduce_scatter | solution.py:500
  902.3 64.0 %reduce-scatter.31.cloned.1.call-done = bf16[256,128]{0,1:T(8,128)(2,1)} async-done(((bf16[2048,128]{0,1:T(8,128)(2,1)}), bf16[256,128]{0,1:T(8,128)(2,1)}) %reduce-scatter.31.cloned.1.call-update) | async-done | bytes 65552 | tf_op jit(solution)/shard_map/reduce_scatter | solution.py:503
  969.3 41.6 %all-reduce.29.cloned.1.call-done = f32[256,1536]{1,0:T(8,128)} async-done(((f32[256,1536]{1,0:T(8,128)}), f32[256,1536]{1,0:T(8,128)}) %all-reduce.29.cloned.1.call-update) | async-done | bytes 1572880 | tf_op jit(solution)/shard_map/psum | solution.py:50
  1036.4 29.3 all-reduce.31.cloned.1.call-done
  1073.7 56.6 %while.122 = (s32[]{:T(128)}, f32[768,16]{0,1:T(8,128)S(1)}, f32[8,32,768]{2,1,0:T(8,128)}, f32[768,16]{0,1:T(8,128)S(1)}, f32[8,32]{1,0:T(8,128)}, /*index=5*/f...) while((s32[]{:T(128)}, f32[768,16]{0,1:T(8,128)S(1)}, ...), condition=%wide.region_82.85_spmd.clone, body=%wide.region_81.84_spmd.clone.sunk | while | flops 2002979 | bytes 3890559 | solution.py:106
  1130.3 54.5 %while.123 = (s32[]{:T(128)}, f32[768,16]{0,1:T(8,128)}, f32[768,16]{0,1:T(8,128)S(1)}, f32[768,16]{0,1:T(8,128)S(1)}, s32[]{:T(128)}, /*index=5*/s32[]{:T(128)}) while((s32[]{:T(128)}, f32[768,16]{0,1:T(8,128)}, f32[768,16]{0,1:T(8,128)S(1)}, f32[768,16]{0,1:T(8,128)S(1)}, s32[]{:T(128)}, /*index=5*/s32[]{:T(128)}) %tuple.1021), condition=%wide.region_84.87_spmd.clone, body=%wide.region_83.86_spmd.clone.sunk | while | flops 61443 | bytes 344183 | solution.py:543
  1188.1 759.4 %while.124 = (s32[]{:T(128)}, f32[768,16]{0,1:T(8,128)}, f32[768,16]{0,1:T(8,128)}, f32[8,32,768]{2,1,0:T(8,128)}, f32[8,32,768]{2,1,0:T(8,128)}, /*index=5*/f32...) while((s32[]{:T(128)}, f32[768,16]{0,1:T(8,128)}, ...), condition=%wide.region_214.217_spmd.clone, body=%wide.region_85.216_spmd.clone.sunk | while | flops 8760355 | bytes 49825768 | solution.py:162
  2039.8 53.7 %reduce-scatter.65.cloned.1.call-done = bf16[96,16]{1,0:T(8,128)(2,1)} async-done(((bf16[768,16]{1,0:T(8,128)(2,1)}), bf16[96,16]{1,0:T(8,128)(2,1)}) %reduce-scatter.65.cloned.1.call-update) | async-done | bytes 3088
  2094.9 62.7 %reduce-scatter.63.cloned.1.call-done = bf16[96,96]{1,0:T(8,128)(2,1)} async-done(((bf16[768,96]{1,0:T(8,128)(2,1)}), bf16[96,96]{1,0:T(8,128)(2,1)}) %reduce-scatter.63.cloned.1.call-update) | async-done | bytes 18448
  2159.1 62.7 %reduce-scatter.37.cloned.1.call-done = bf16[96,128]{1,0:T(8,128)(2,1)} async-done(((bf16[768,128]{1,0:T(8,128)(2,1)}), bf16[96,128]{1,0:T(8,128)(2,1)}) %reduce-scatter.37.cloned.1.call-update) | async-done | bytes 24592 | tf_op jit(solution)/shard_map/reduce_scatter | solution.py:593
  2223.1 69.4 %all-reduce.33.cloned.1.call-done = (f32[256,1536]{1,0:T(8,128)}, f32[256,1536]{1,0:T(8,128)}) async-done(((f32[256,1536]{1,0:T(8,128)}, f32[256,1536]{1,0:T(8,128)}), (f32[256,1536]{1,0:T(8,128)}, f32[256,1536]{1,0:T(8,128)})) %all-reduce.33.cloned.1.call-update) | async-done | bytes 3145744 | tf_op jit(solution)/shard_map/psum | solution.py:50
  2294.6 38.1 %all-reduce.8 = (bf16[1536]{0:T(1024)(128)(2,1)S(1)}, bf16[768]{0:T(1024)(128)(2,1)S(1)}, bf16[768]{0:T(1024)(128)(2,1)S(1)}, bf16[768]{0:T(1024)(128)(2,1)S(1)}...) all-reduce(bf16[1536]{0:T(1024)(128)(2,1)S(1)} %get-tuple-element.1, ...), channel_id=4, replica_groups=mesh['seq'=8,'head'=4] {'seq'}, use_global_device_ids=true, to_apply=%region_219.222.clone | all-reduce | flops 8448 | bytes 33792
  2341.3 30.1 %reduce-scatter.55.cloned.1.call-done = bf16[4,192,256]{2,1,0:T(8,128)(2,1)} async-done(((bf16[4,1536,256]{2,1,0:T(8,128)(2,1)}), bf16[4,192,256]{2,1,0:T(8,128)(2,1)}) %reduce-scatter.55.cloned.1.call-update) | async-done | bytes 393232 | tf_op jit(solution)/shard_map/reduce_scatter | solution.py:644
  2373.4 76.0 %reduce-scatter.57.cloned.1.call-done = bf16[4,192,256]{2,1,0:T(8,128)(2,1)} async-done(((bf16[4,1536,256]{2,1,0:T(8,128)(2,1)}), bf16[4,192,256]{2,1,0:T(8,128)(2,1)}) %reduce-scatter.57.cloned.1.call-update) | async-done | bytes 393232 | tf_op jit(solution)/shard_map/reduce_scatter | solution.py:647
  2451.3 75.7 %reduce-scatter.59.cloned.1.call-done = bf16[4,256,192]{1,2,0:T(8,128)(2,1)} async-done(((bf16[4,256,1536]{1,2,0:T(8,128)(2,1)}), bf16[4,256,192]{1,2,0:T(8,128)(2,1)}) %reduce-scatter.59.cloned.1.call-update) | async-done | bytes 393232 | tf_op jit(solution)/shard_map/reduce_scatter | solution.py:650
  2528.9 70.0 %reduce-scatter.35.cloned.1.call-done = bf16[192,768]{1,0:T(8,128)(2,1)} async-done(((bf16[1536,768]{1,0:T(8,128)(2,1)}), bf16[192,768]{1,0:T(8,128)(2,1)}) %reduce-scatter.35.cloned.1.call-update) | async-done | bytes 294928 | tf_op jit(solution)/shard_map/reduce_scatter | solution.py:584
  2600.8 70.1 %reduce-scatter.39.cloned.1.call-done = bf16[768,192]{0,1:T(8,128)(2,1)} async-done(((bf16[768,1536]{0,1:T(8,128)(2,1)}), bf16[768,192]{0,1:T(8,128)(2,1)}) %reduce-scatter.39.cloned.1.call-update) | async-done | bytes 294928 | tf_op jit(solution)/shard_map/reduce_scatter | solution.py:608
  2672.7 70.2 %reduce-scatter.33.cloned.1.call-done = bf16[192,768]{1,0:T(8,128)(2,1)} async-done(((bf16[1536,768]{1,0:T(8,128)(2,1)}), bf16[192,768]{1,0:T(8,128)(2,1)}) %reduce-scatter.33.cloned.1.call-update) | async-done | bytes 294928 | tf_op jit(solution)/shard_map/reduce_scatter | solution.py:581
  2744.9 75.4 %reduce-scatter.41.cloned.1.call-done = bf16[192,1024]{1,0:T(8,128)(2,1)} async-done(((bf16[1536,1024]{1,0:T(8,128)(2,1)}), bf16[192,1024]{1,0:T(8,128)(2,1)}) %reduce-scatter.41.cloned.1.call-update) | async-done | bytes 393232 | tf_op jit(solution)/shard_map/reduce_scatter | solution.py:614
  2822.3 75.2 %reduce-scatter.43.cloned.1.call-done = bf16[192,1024]{1,0:T(8,128)(2,1)} async-done(((bf16[1536,1024]{1,0:T(8,128)(2,1)}), bf16[192,1024]{1,0:T(8,128)(2,1)}) %reduce-scatter.43.cloned.1.call-update) | async-done | bytes 393232 | tf_op jit(solution)/shard_map/reduce_scatter | solution.py:617
  2899.4 75.7 %reduce-scatter.45.cloned.1.call-done = bf16[1024,192]{0,1:T(8,128)(2,1)} async-done(((bf16[1024,1536]{0,1:T(8,128)(2,1)}), bf16[1024,192]{0,1:T(8,128)(2,1)}) %reduce-scatter.45.cloned.1.call-update) | async-done | bytes 393232 | tf_op jit(solution)/shard_map/reduce_scatter | solution.py:620
  (5364 shorter events, 1559.7 us)
Async XLA Ops:
  7.2 51.2 %all-reduce.19.cloned.1.call-start = ((), (), s32[]{:S(2)}) async-start(), calls=%async_computation.20 | async-start | bytes 262144 | tf_op jit(solution)/shard_map/psum | solution.py:50
  13.7 8.3 collective-permute-start.2
  26.6 373.8 %all-reduce.21.cloned.1.call-start = ((), (), s32[]{:S(2)}) async-start(), calls=%async_computation.21 | async-start | bytes 3145728 | tf_op jit(solution)/shard_map/psum | solution.py:50
  143.9 6.8 collective-permute-start
  354.7 98.5 %all-reduce.23.cloned.1.call-start = ((), (), s32[]{:S(2)}) async-start(), calls=%async_computation.22 | async-start | bytes 3145728 | tf_op jit(solution)/shard_map/psum | solution.py:50
  410.1 220.4 %all-reduce.25.cloned.1.call-start = ((), (), s32[]{:S(2)}) async-start(), calls=%async_computation.23 | async-start | bytes 3145728 | tf_op jit(solution)/shard_map/psum | solution.py:50
  562.6 190.5 %all-reduce.27.cloned.1.call-start = ((), (), s32[]{:S(2)}) async-start(), calls=%async_computation.24 | async-start | bytes 1572864 | tf_op jit(solution)/shard_map/psum | solution.py:412
  717.6 183.2 %reduce-scatter.29.cloned.1.call-start = ((), (), s32[]{:S(2)}) async-start(), calls=%async_computation.25 | async-start | bytes 589824 | tf_op jit(solution)/shard_map/reduce_scatter | solution.py:500
  788.0 178.3 %reduce-scatter.31.cloned.1.call-start = ((), (), s32[]{:S(2)}) async-start(), calls=%async_computation.26 | async-start | bytes 589824 | tf_op jit(solution)/shard_map/reduce_scatter | solution.py:503
  790.2 220.7 %all-reduce.29.cloned.1.call-start = ((), (), s32[]{:S(2)}) async-start(), calls=%async_computation.27 | async-start | bytes 3145728 | tf_op jit(solution)/shard_map/psum | solution.py:50
  968.9 96.8 %all-reduce.31.cloned.1.call-start = ((), (), s32[]{:S(2)}) async-start(), calls=%async_computation.28 | async-start | bytes 3145728 | tf_op jit(solution)/shard_map/psum | solution.py:50
  1022.6 1007.8 %reduce-scatter.67.cloned.1.call-start = ((), (), s32[]{:S(2)}) async-start(), calls=%async_computation.46 | async-start | bytes 442368
  1025.2 1006.8 %reduce-scatter.49.cloned.1.call-start = ((), (), s32[]{:S(2)}) async-start(), calls=%async_computation.37 | async-start | bytes 442368 | tf_op jit(solution)/shard_map/reduce_scatter | solution.py:629
  1026.4 1007.0 %reduce-scatter.51.cloned.1.call-start = ((), (), s32[]{:S(2)}) async-start(), calls=%async_computation.38 | async-start | bytes 442368 | tf_op jit(solution)/shard_map/reduce_scatter | solution.py:632
  1027.7 1007.2 %reduce-scatter.47.cloned.1.call-start = ((), (), s32[]{:S(2)}) async-start(), calls=%async_computation.36 | async-start | bytes 1327104 | tf_op jit(solution)/shard_map/reduce_scatter | solution.py:626
  1029.4 1007.2 %reduce-scatter.53.cloned.1.call-start = ((), (), s32[]{:S(2)}) async-start(), calls=%async_computation.39 | async-start | bytes 1327104 | tf_op jit(solution)/shard_map/reduce_scatter | solution.py:635
  1036.3 1002.0 %reduce-scatter.61.cloned.1.call-start = ((), (), s32[]{:S(2)}) async-start(), calls=%async_computation.43 | async-start | bytes 221184
  1153.1 6.7 collective-permute-start.1
  1169.4 6.7 collective-permute-start.1
  1967.3 126.1 %reduce-scatter.65.cloned.1.call-start = ((), (), s32[]{:S(2)}) async-start(), calls=%async_computation.45 | async-start | bytes 221184
  1968.3 189.3 %reduce-scatter.63.cloned.1.call-start = ((), (), s32[]{:S(2)}) async-start(), calls=%async_computation.44 | async-start | bytes 221184
  1969.5 252.3 %reduce-scatter.37.cloned.1.call-start = ((), (), s32[]{:S(2)}) async-start(), calls=%async_computation.31 | async-start | bytes 221184 | tf_op jit(solution)/shard_map/reduce_scatter | solution.py:593
  1979.4 313.1 %all-reduce.33.cloned.1.call-start = ((), (), s32[]{:S(2)}) async-start(), calls=%async_computation.47 | async-start | bytes 6291456 | tf_op jit(solution)/shard_map/psum | solution.py:50
  1988.9 382.5 %reduce-scatter.55.cloned.1.call-start = ((), (), s32[]{:S(2)}) async-start(), calls=%async_computation.40 | async-start | bytes 3538944 | tf_op jit(solution)/shard_map/reduce_scatter | solution.py:644
  1993.7 455.6 %reduce-scatter.57.cloned.1.call-start = ((), (), s32[]{:S(2)}) async-start(), calls=%async_computation.41 | async-start | bytes 3538944 | tf_op jit(solution)/shard_map/reduce_scatter | solution.py:647
  1997.9 529.1 %reduce-scatter.59.cloned.1.call-start = ((), (), s32[]{:S(2)}) async-start(), calls=%async_computation.42 | async-start | bytes 3538944 | tf_op jit(solution)/shard_map/reduce_scatter | solution.py:650
  2004.1 594.9 %reduce-scatter.35.cloned.1.call-start = ((), (), s32[]{:S(2)}) async-start(), calls=%async_computation.30 | async-start | bytes 2654208 | tf_op jit(solution)/shard_map/reduce_scatter | solution.py:584
  2007.6 663.3 %reduce-scatter.39.cloned.1.call-start = ((), (), s32[]{:S(2)}) async-start(), calls=%async_computation.32 | async-start | bytes 2654208 | tf_op jit(solution)/shard_map/reduce_scatter | solution.py:608
  2011.4 731.6 %reduce-scatter.33.cloned.1.call-start = ((), (), s32[]{:S(2)}) async-start(), calls=%async_computation.29 | async-start | bytes 2654208 | tf_op jit(solution)/shard_map/reduce_scatter | solution.py:581
  2013.8 806.5 %reduce-scatter.41.cloned.1.call-start = ((), (), s32[]{:S(2)}) async-start(), calls=%async_computation.33 | async-start | bytes 3538944 | tf_op jit(solution)/shard_map/reduce_scatter | solution.py:614
  2017.8 879.7 %reduce-scatter.43.cloned.1.call-start = ((), (), s32[]{:S(2)}) async-start(), calls=%async_computation.34 | async-start | bytes 3538944 | tf_op jit(solution)/shard_map/reduce_scatter | solution.py:617
  2022.8 952.3 %reduce-scatter.45.cloned.1.call-start = ((), (), s32[]{:S(2)}) async-start(), calls=%async_computation.35 | async-start | bytes 3538944 | tf_op jit(solution)/shard_map/reduce_scatter | solution.py:620
  (1701 other events, 22888.2 us)
Sparse Core Ops, SparseCore 0:
  26.7 31.6 all-reduce.18
  354.9 45.4 all-reduce.20
  410.2 42.9 all-reduce.22
  562.7 67.7 all-reduce.24
  717.8 35.2 all-reduce.26
  788.1 112.6 reduce-scatter.28
  904.7 61.4 reduce-scatter.30
  969.0 41.8 all-reduce.28
  1022.8 42.8 all-reduce.30
  1069.1 61.4 reduce-scatter.66
  1134.2 60.3 reduce-scatter.48
  1198.1 60.4 reduce-scatter.50
  1262.4 62.9 reduce-scatter.46
  1329.1 63.0 reduce-scatter.52
  1967.5 61.8 reduce-scatter.60
  2033.4 60.0 reduce-scatter.64
  2097.5 60.0 reduce-scatter.62
  2161.6 60.0 reduce-scatter.36
  2224.8 67.6 all-reduce.32
  2296.4 75.0 reduce-scatter.54
  2375.5 73.8 reduce-scatter.56
  2453.3 73.5 reduce-scatter.58
  2530.9 68.0 reduce-scatter.34
  2602.7 68.1 reduce-scatter.38
  2674.8 68.1 reduce-scatter.32
  2746.8 73.4 reduce-scatter.40
  2824.2 73.2 reduce-scatter.42
  2901.5 73.5 reduce-scatter.44
where the time goes:
time: 3030 us; the launch traced here: 2980 us
  waiting for transfers between devices  1360 us (45%)
  other arithmetic  707 us (23%)
  local copies, waits for them, and re-layouts  580 us (19%)
  blocking collectives  123 us (4%)
  matrix products  112 us (4%)
  starting transfers between devices  49.7 us (2%)
  loops' own time  31.7 us (1%)
    psum x7, waiting for transfers between devices, head_total(): return lax.psum(values, 'head')  305 us
    reduce_sum x240, other arithmetic, retreat(): jnp.sum(adjoint * (step_rows[offset] * input_rows[offset])[:, None], axis=0)  213 us
    unnamed x32, waiting for transfers between devices  117 us
    reduce_scatter x1, waiting for transfers between devices, body(): lax.psum_scatter(key_acc.astype(jnp.bfloat16), 'seq', scatter_dimension=0...  110 us
    mul x256, other arithmetic, retreat(): step_rows[offset] * input_rows[offset]  76.7 us
    reduce_scatter x1, waiting for transfers between devices, body(): lax.psum_scatter(grad_expert_up.astype(jnp.bfloat16), 'seq', scatter_dime...  76 us
    reduce_scatter x1, waiting for transfers between devices, body(): lax.psum_scatter(grad_expert_down.astype(jnp.bfloat16), 'seq', scatter_di...  75.7 us
    reduce_scatter x1, waiting for transfers between devices, body(): lax.psum_scatter(grad_ffn_down.astype(jnp.bfloat16), 'seq', scatter_dimen...  75.7 us

commit v1 on v0

--- a/solution.py
+++ b/solution.py
@@ -359,8 +359,11 @@
     gate_weights = jax.nn.softmax(chosen, axis=1)
     expert_count = router.shape[1]
     route_flat = expert_routes.reshape(-1)
-    one_hot = (route_flat[:, None] == jnp.arange(expert_count, dtype=jnp.int32)).astype(jnp.int32)
-    within = jnp.sum((jnp.cumsum(one_hot, axis=0) - one_hot) * one_hot, axis=1)
+    pair_order = jnp.arange(route_flat.shape[0], dtype=jnp.int32)
+    earlier = (pair_order[None, :] < pair_order[:, None]) & (
+        route_flat[None, :] == route_flat[:, None]
+    )
+    within = jnp.sum(earlier.astype(jnp.int32), axis=1)
     slot_index = route_flat * CAP + within
     pair_count = route_flat.shape[0]
     slot_pairs = (

time: 3030 us -> 3030 us (level)
  no operation moved by 1% of the time
where the time goes in v1:
time: 3030 us; the launch traced here: 2980 us
  waiting for transfers between devices  1360 us (45%)
  other arithmetic  706 us (23%)
  local copies, waits for them, and re-layouts  580 us (19%)
  blocking collectives  123 us (4%)
  matrix products  112 us (4%)
  starting transfers between devices  49.7 us (2%)
  loops' own time  31.7 us (1%)
    psum x7, waiting for transfers between devices, head_total(): return lax.psum(values, 'head')  306 us
    reduce_sum x240, other arithmetic, retreat(): jnp.sum(adjoint * (step_rows[offset] * input_rows[offset])[:, None], axis=0)  213 us
    unnamed x32, waiting for transfers between devices  117 us
    reduce_scatter x1, waiting for transfers between devices, body(): lax.psum_scatter(key_acc.astype(jnp.bfloat16), 'seq', scatter_dimension=0...  110 us
    mul x256, other arithmetic, retreat(): step_rows[offset] * input_rows[offset]  76.7 us
    reduce_scatter x1, waiting for transfers between devices, body(): lax.psum_scatter(grad_expert_up.astype(jnp.bfloat16), 'seq', scatter_dime...  76 us
    reduce_scatter x1, waiting for transfers between devices, body(): lax.psum_scatter(grad_expert_down.astype(jnp.bfloat16), 'seq', scatter_di...  75.7 us
    reduce_scatter x1, waiting for transfers between devices, body(): lax.psum_scatter(grad_ffn_down.astype(jnp.bfloat16), 'seq', scatter_dimen...  75.7 us

profile of v1, /device:TPU:0, one launch (start us, length us, event | category | flops | bytes accessed | tf_op | source)
XLA Modules:
  0.0 2984.2 jit_solution(8727801062494345846)
XLA Ops:
  28.6 29.8 all-reduce.19.cloned.1.call-done
  62.6 51.5 %while.120 = (s32[]{:T(128)}, f32[768,16]{0,1:T(8,128)S(1)}, f32[8,32,768]{2,1,0:T(8,128)}, f32[768,16]{0,1:T(8,128)S(1)}, f32[8,32]{1,0:T(8,128)}, /*index=5*/f...) while((s32[]{:T(128)}, f32[768,16]{0,1:T(8,128)S(1)}, f32[8,32,768]{2,1,0:T(8,128)}, ...), condition=%wide.region_5.7_spmd.clone, body=%wide.region_4.6_spmd.clone.sunk | while | flops 2027523 | bytes 7035387 | solution.py:78
  114.1 43.2 %while.121 = (s32[]{:T(128)}, f32[768,16]{0,1:T(8,128)S(1)}, f32[768,16]{0,1:T(8,128)S(1)}, f32[768,16]{0,1:T(8,128)S(1)}, s32[]{:T(128)}, /*index=5*/s32[]{:T(128)}) while((s32[]{:T(128)}, f32[768,16]{0,1:T(8,128)S(1)}, f32[768,16]{0,1:T(8,128)S(1)}, f32[768,16]{0,1:T(8,128)S(1)}, s32[]{:T(128)}, /*index=5*/s32[]{:T(128)}) %tuple.923), condition=%wide.region_7.9_spmd.clone, body=%wide.region_6.8_spmd.clone.sunk | while | flops 61443 | bytes 344183 | solution.py:265
  158.2 189.6 %while.117 = (s32[]{:T(128)}, f32[768,16]{0,1:T(8,128)S(1)}, f32[8,32,768]{2,1,0:T(8,128)}, f32[8,768,16]{1,2,0:T(8,128)}, f32[8,32,768]{2,1,0:T(8,128)}, /*inde...) while((s32[]{:T(128)}, f32[768,16]{0,1:T(8,128)S(1)}, ...), condition=%wide.region_41.43_spmd, body=%wide.region_8.42_spmd.sunk | while | flops 3170337 | bytes 24343948 | solution.py:78
  355.4 44.9 %all-reduce.21.cloned.1.call-done = f32[256,1536]{1,0:T(8,128)} async-done(((f32[256,1536]{1,0:T(8,128)}), f32[256,1536]{1,0:T(8,128)}) %all-reduce.21.cloned.1.call-update) | async-done | bytes 1572880 | tf_op jit(solution)/shard_map/psum | solution.py:50
  415.7 37.6 %all-reduce.23.cloned.1.call-done = f32[256,1536]{1,0:T(8,128)} async-done(((f32[256,1536]{1,0:T(8,128)}), f32[256,1536]{1,0:T(8,128)}) %all-reduce.23.cloned.1.call-update) | async-done | bytes 1572880 | tf_op jit(solution)/shard_map/psum | solution.py:50
  457.2 33.4 %all_gather.8 = bf16[2048,128]{1,0:T(8,128)(2,1)} all-gather(bf16[256,128]{1,0:T(8,128)(2,1)S(1)} %convolution_convert_fusion.23), channel_id=1, replica_groups=mesh['seq'=8,'head'=4] {'seq'}, dimensions={0}, use_global_device_ids=true | all-gather | bytes 589824 | tf_op jit(solution)/shard_map/all_gather | solution.py:310
  501.1 33.2 %all_gather.9 = bf16[2048,128]{1,0:T(8,128)(2,1)} all-gather(bf16[256,128]{1,0:T(8,128)(2,1)S(1)} %convolution_convert_fusion.22), channel_id=1, replica_groups=mesh['seq'=8,'head'=4] {'seq'}, dimensions={0}, use_global_device_ids=true | all-gather | bytes 589824 | tf_op jit(solution)/shard_map/all_gather | solution.py:311
  577.5 53.1 %all-reduce.25.cloned.1.call-done = f32[256,1536]{1,0:T(8,128)} async-done(((f32[256,1536]{1,0:T(8,128)}), f32[256,1536]{1,0:T(8,128)}) %all-reduce.25.cloned.1.call-update) | async-done | bytes 1572880 | tf_op jit(solution)/shard_map/psum | solution.py:50
  718.4 34.7 %all-reduce.27.cloned.1.call-done = bf16[256,1536]{1,0:T(8,128)(2,1)} async-done(((bf16[256,1536]{1,0:T(8,128)(2,1)}), bf16[256,1536]{1,0:T(8,128)(2,1)}) %all-reduce.27.cloned.1.call-update) | async-done | bytes 786448 | tf_op jit(solution)/shard_map/psum | solution.py:415
  761.2 24.7 while.119
  791.0 109.9 %reduce-scatter.29.cloned.1.call-done = bf16[256,128]{0,1:T(8,128)(2,1)} async-done(((bf16[2048,128]{0,1:T(8,128)(2,1)}), bf16[256,128]{0,1:T(8,128)(2,1)}) %reduce-scatter.29.cloned.1.call-update) | async-done | bytes 65552 | tf_op jit(solution)/shard_map/reduce_scatter | solution.py:503
  902.3 63.9 %reduce-scatter.31.cloned.1.call-done = bf16[256,128]{0,1:T(8,128)(2,1)} async-done(((bf16[2048,128]{0,1:T(8,128)(2,1)}), bf16[256,128]{0,1:T(8,128)(2,1)}) %reduce-scatter.31.cloned.1.call-update) | async-done | bytes 65552 | tf_op jit(solution)/shard_map/reduce_scatter | solution.py:506
  969.3 41.5 %all-reduce.29.cloned.1.call-done = f32[256,1536]{1,0:T(8,128)} async-done(((f32[256,1536]{1,0:T(8,128)}), f32[256,1536]{1,0:T(8,128)}) %all-reduce.29.cloned.1.call-update) | async-done | bytes 1572880 | tf_op jit(solution)/shard_map/psum | solution.py:50
  1036.3 29.3 all-reduce.31.cloned.1.call-done
  1073.6 56.6 %while.122 = (s32[]{:T(128)}, f32[768,16]{0,1:T(8,128)S(1)}, f32[8,32,768]{2,1,0:T(8,128)}, f32[768,16]{0,1:T(8,128)S(1)}, f32[8,32]{1,0:T(8,128)}, /*index=5*/f...) while((s32[]{:T(128)}, f32[768,16]{0,1:T(8,128)S(1)}, ...), condition=%wide.region_80.83_spmd.clone, body=%wide.region_79.82_spmd.clone.sunk | while | flops 2002979 | bytes 3890559 | solution.py:106
  1130.3 54.5 %while.123 = (s32[]{:T(128)}, f32[768,16]{0,1:T(8,128)}, f32[768,16]{0,1:T(8,128)S(1)}, f32[768,16]{0,1:T(8,128)S(1)}, s32[]{:T(128)}, /*index=5*/s32[]{:T(128)}) while((s32[]{:T(128)}, f32[768,16]{0,1:T(8,128)}, f32[768,16]{0,1:T(8,128)S(1)}, f32[768,16]{0,1:T(8,128)S(1)}, s32[]{:T(128)}, /*index=5*/s32[]{:T(128)}) %tuple.1021), condition=%wide.region_82.85_spmd.clone, body=%wide.region_81.84_spmd.clone.sunk | while | flops 61443 | bytes 344183 | solution.py:546
  1188.0 759.4 %while.124 = (s32[]{:T(128)}, f32[768,16]{0,1:T(8,128)}, f32[768,16]{0,1:T(8,128)}, f32[8,32,768]{2,1,0:T(8,128)}, f32[8,32,768]{2,1,0:T(8,128)}, /*index=5*/f32...) while((s32[]{:T(128)}, f32[768,16]{0,1:T(8,128)}, ...), condition=%wide.region_212.215_spmd.clone, body=%wide.region_83.214_spmd.clone.sunk | while | flops 8760355 | bytes 49825768 | solution.py:162
  2039.9 53.5 %reduce-scatter.65.cloned.1.call-done = bf16[96,16]{1,0:T(8,128)(2,1)} async-done(((bf16[768,16]{1,0:T(8,128)(2,1)}), bf16[96,16]{1,0:T(8,128)(2,1)}) %reduce-scatter.65.cloned.1.call-update) | async-done | bytes 3088
  2094.8 62.7 %reduce-scatter.63.cloned.1.call-done = bf16[96,96]{1,0:T(8,128)(2,1)} async-done(((bf16[768,96]{1,0:T(8,128)(2,1)}), bf16[96,96]{1,0:T(8,128)(2,1)}) %reduce-scatter.63.cloned.1.call-update) | async-done | bytes 18448
  2159.0 62.7 %reduce-scatter.37.cloned.1.call-done = bf16[96,128]{1,0:T(8,128)(2,1)} async-done(((bf16[768,128]{1,0:T(8,128)(2,1)}), bf16[96,128]{1,0:T(8,128)(2,1)}) %reduce-scatter.37.cloned.1.call-update) | async-done | bytes 24592 | tf_op jit(solution)/shard_map/reduce_scatter | solution.py:596
  2223.0 69.4 %all-reduce.33.cloned.1.call-done = (f32[256,1536]{1,0:T(8,128)}, f32[256,1536]{1,0:T(8,128)}) async-done(((f32[256,1536]{1,0:T(8,128)}, f32[256,1536]{1,0:T(8,128)}), (f32[256,1536]{1,0:T(8,128)}, f32[256,1536]{1,0:T(8,128)})) %all-reduce.33.cloned.1.call-update) | async-done | bytes 3145744 | tf_op jit(solution)/shard_map/psum | solution.py:50
  2294.5 38.1 %all-reduce.8 = (bf16[1536]{0:T(1024)(128)(2,1)S(1)}, bf16[768]{0:T(1024)(128)(2,1)S(1)}, bf16[768]{0:T(1024)(128)(2,1)S(1)}, bf16[768]{0:T(1024)(128)(2,1)S(1)}...) all-reduce(bf16[1536]{0:T(1024)(128)(2,1)S(1)} %get-tuple-element.1, ...), channel_id=4, replica_groups=mesh['seq'=8,'head'=4] {'seq'}, use_global_device_ids=true, to_apply=%region_217.220.clone | all-reduce | flops 8448 | bytes 33792
  2341.2 30.1 %reduce-scatter.55.cloned.1.call-done = bf16[4,192,256]{2,1,0:T(8,128)(2,1)} async-done(((bf16[4,1536,256]{2,1,0:T(8,128)(2,1)}), bf16[4,192,256]{2,1,0:T(8,128)(2,1)}) %reduce-scatter.55.cloned.1.call-update) | async-done | bytes 393232 | tf_op jit(solution)/shard_map/reduce_scatter | solution.py:647
  2373.2 76.0 %reduce-scatter.57.cloned.1.call-done = bf16[4,192,256]{2,1,0:T(8,128)(2,1)} async-done(((bf16[4,1536,256]{2,1,0:T(8,128)(2,1)}), bf16[4,192,256]{2,1,0:T(8,128)(2,1)}) %reduce-scatter.57.cloned.1.call-update) | async-done | bytes 393232 | tf_op jit(solution)/shard_map/reduce_scatter | solution.py:650
  2451.1 75.7 %reduce-scatter.59.cloned.1.call-done = bf16[4,256,192]{1,2,0:T(8,128)(2,1)} async-done(((bf16[4,256,1536]{1,2,0:T(8,128)(2,1)}), bf16[4,256,192]{1,2,0:T(8,128)(2,1)}) %reduce-scatter.59.cloned.1.call-update) | async-done | bytes 393232 | tf_op jit(solution)/shard_map/reduce_scatter | solution.py:653
  2528.8 70.0 %reduce-scatter.35.cloned.1.call-done = bf16[192,768]{1,0:T(8,128)(2,1)} async-done(((bf16[1536,768]{1,0:T(8,128)(2,1)}), bf16[192,768]{1,0:T(8,128)(2,1)}) %reduce-scatter.35.cloned.1.call-update) | async-done | bytes 294928 | tf_op jit(solution)/shard_map/reduce_scatter | solution.py:587
  2600.6 70.1 %reduce-scatter.39.cloned.1.call-done = bf16[768,192]{0,1:T(8,128)(2,1)} async-done(((bf16[768,1536]{0,1:T(8,128)(2,1)}), bf16[768,192]{0,1:T(8,128)(2,1)}) %reduce-scatter.39.cloned.1.call-update) | async-done | bytes 294928 | tf_op jit(solution)/shard_map/reduce_scatter | solution.py:611
  2672.6 70.2 %reduce-scatter.33.cloned.1.call-done = bf16[192,768]{1,0:T(8,128)(2,1)} async-done(((bf16[1536,768]{1,0:T(8,128)(2,1)}), bf16[192,768]{1,0:T(8,128)(2,1)}) %reduce-scatter.33.cloned.1.call-update) | async-done | bytes 294928 | tf_op jit(solution)/shard_map/reduce_scatter | solution.py:584
  2744.8 75.4 %reduce-scatter.41.cloned.1.call-done = bf16[192,1024]{1,0:T(8,128)(2,1)} async-done(((bf16[1536,1024]{1,0:T(8,128)(2,1)}), bf16[192,1024]{1,0:T(8,128)(2,1)}) %reduce-scatter.41.cloned.1.call-update) | async-done | bytes 393232 | tf_op jit(solution)/shard_map/reduce_scatter | solution.py:617
  2822.2 75.2 %reduce-scatter.43.cloned.1.call-done = bf16[192,1024]{1,0:T(8,128)(2,1)} async-done(((bf16[1536,1024]{1,0:T(8,128)(2,1)}), bf16[192,1024]{1,0:T(8,128)(2,1)}) %reduce-scatter.43.cloned.1.call-update) | async-done | bytes 393232 | tf_op jit(solution)/shard_map/reduce_scatter | solution.py:620
  2899.3 75.7 %reduce-scatter.45.cloned.1.call-done = bf16[1024,192]{0,1:T(8,128)(2,1)} async-done(((bf16[1024,1536]{0,1:T(8,128)(2,1)}), bf16[1024,192]{0,1:T(8,128)(2,1)}) %reduce-scatter.45.cloned.1.call-update) | async-done | bytes 393232 | tf_op jit(solution)/shard_map/reduce_scatter | solution.py:623
  (5358 shorter events, 1559.1 us)
Async XLA Ops:
  7.2 51.2 %all-reduce.19.cloned.1.call-start = ((), (), s32[]{:S(2)}) async-start(), calls=%async_computation.20 | async-start | bytes 262144 | tf_op jit(solution)/shard_map/psum | solution.py:50
  13.7 8.3 collective-permute-start.2
  26.6 373.8 %all-reduce.21.cloned.1.call-start = ((), (), s32[]{:S(2)}) async-start(), calls=%async_computation.21 | async-start | bytes 3145728 | tf_op jit(solution)/shard_map/psum | solution.py:50
  143.9 6.8 collective-permute-start
  354.7 98.6 %all-reduce.23.cloned.1.call-start = ((), (), s32[]{:S(2)}) async-start(), calls=%async_computation.22 | async-start | bytes 3145728 | tf_op jit(solution)/shard_map/psum | solution.py:50
  410.2 220.3 %all-reduce.25.cloned.1.call-start = ((), (), s32[]{:S(2)}) async-start(), calls=%async_computation.23 | async-start | bytes 3145728 | tf_op jit(solution)/shard_map/psum | solution.py:50
  562.6 190.5 %all-reduce.27.cloned.1.call-start = ((), (), s32[]{:S(2)}) async-start(), calls=%async_computation.24 | async-start | bytes 1572864 | tf_op jit(solution)/shard_map/psum | solution.py:415
  717.7 183.2 %reduce-scatter.29.cloned.1.call-start = ((), (), s32[]{:S(2)}) async-start(), calls=%async_computation.25 | async-start | bytes 589824 | tf_op jit(solution)/shard_map/reduce_scatter | solution.py:503
  788.0 178.2 %reduce-scatter.31.cloned.1.call-start = ((), (), s32[]{:S(2)}) async-start(), calls=%async_computation.26 | async-start | bytes 589824 | tf_op jit(solution)/shard_map/reduce_scatter | solution.py:506
  790.3 220.6 %all-reduce.29.cloned.1.call-start = ((), (), s32[]{:S(2)}) async-start(), calls=%async_computation.27 | async-start | bytes 3145728 | tf_op jit(solution)/shard_map/psum | solution.py:50
  968.9 96.8 %all-reduce.31.cloned.1.call-start = ((), (), s32[]{:S(2)}) async-start(), calls=%async_computation.28 | async-start | bytes 3145728 | tf_op jit(solution)/shard_map/psum | solution.py:50
  1022.6 1008.0 %reduce-scatter.67.cloned.1.call-start = ((), (), s32[]{:S(2)}) async-start(), calls=%async_computation.46 | async-start | bytes 442368
  1025.1 1007.0 %reduce-scatter.49.cloned.1.call-start = ((), (), s32[]{:S(2)}) async-start(), calls=%async_computation.37 | async-start | bytes 442368 | tf_op jit(solution)/shard_map/reduce_scatter | solution.py:632
  1026.4 1007.2 %reduce-scatter.51.cloned.1.call-start = ((), (), s32[]{:S(2)}) async-start(), calls=%async_computation.38 | async-start | bytes 442368 | tf_op jit(solution)/shard_map/reduce_scatter | solution.py:635
  1027.6 1007.4 %reduce-scatter.47.cloned.1.call-start = ((), (), s32[]{:S(2)}) async-start(), calls=%async_computation.36 | async-start | bytes 1327104 | tf_op jit(solution)/shard_map/reduce_scatter | solution.py:629
  1029.4 1007.3 %reduce-scatter.53.cloned.1.call-start = ((), (), s32[]{:S(2)}) async-start(), calls=%async_computation.39 | async-start | bytes 1327104 | tf_op jit(solution)/shard_map/reduce_scatter | solution.py:638
  1036.3 1002.2 %reduce-scatter.61.cloned.1.call-start = ((), (), s32[]{:S(2)}) async-start(), calls=%async_computation.43 | async-start | bytes 221184
  1153.1 6.7 collective-permute-start.1
  1177.4 6.7 collective-permute-start.1
  1967.3 126.1 %reduce-scatter.65.cloned.1.call-start = ((), (), s32[]{:S(2)}) async-start(), calls=%async_computation.45 | async-start | bytes 221184
  1968.2 189.2 %reduce-scatter.63.cloned.1.call-start = ((), (), s32[]{:S(2)}) async-start(), calls=%async_computation.44 | async-start | bytes 221184
  1969.4 252.2 %reduce-scatter.37.cloned.1.call-start = ((), (), s32[]{:S(2)}) async-start(), calls=%async_computation.31 | async-start | bytes 221184 | tf_op jit(solution)/shard_map/reduce_scatter | solution.py:596
  1979.4 313.0 %all-reduce.33.cloned.1.call-start = ((), (), s32[]{:S(2)}) async-start(), calls=%async_computation.47 | async-start | bytes 6291456 | tf_op jit(solution)/shard_map/psum | solution.py:50
  1989.1 382.3 %reduce-scatter.55.cloned.1.call-start = ((), (), s32[]{:S(2)}) async-start(), calls=%async_computation.40 | async-start | bytes 3538944 | tf_op jit(solution)/shard_map/reduce_scatter | solution.py:647
  1993.8 455.4 %reduce-scatter.57.cloned.1.call-start = ((), (), s32[]{:S(2)}) async-start(), calls=%async_computation.41 | async-start | bytes 3538944 | tf_op jit(solution)/shard_map/reduce_scatter | solution.py:650
  1998.0 528.9 %reduce-scatter.59.cloned.1.call-start = ((), (), s32[]{:S(2)}) async-start(), calls=%async_computation.42 | async-start | bytes 3538944 | tf_op jit(solution)/shard_map/reduce_scatter | solution.py:653
  2004.2 594.6 %reduce-scatter.35.cloned.1.call-start = ((), (), s32[]{:S(2)}) async-start(), calls=%async_computation.30 | async-start | bytes 2654208 | tf_op jit(solution)/shard_map/reduce_scatter | solution.py:587
  2007.7 663.0 %reduce-scatter.39.cloned.1.call-start = ((), (), s32[]{:S(2)}) async-start(), calls=%async_computation.32 | async-start | bytes 2654208 | tf_op jit(solution)/shard_map/reduce_scatter | solution.py:611
  2011.5 731.3 %reduce-scatter.33.cloned.1.call-start = ((), (), s32[]{:S(2)}) async-start(), calls=%async_computation.29 | async-start | bytes 2654208 | tf_op jit(solution)/shard_map/reduce_scatter | solution.py:584
  2013.9 806.3 %reduce-scatter.41.cloned.1.call-start = ((), (), s32[]{:S(2)}) async-start(), calls=%async_computation.33 | async-start | bytes 3538944 | tf_op jit(solution)/shard_map/reduce_scatter | solution.py:617
  2017.9 879.5 %reduce-scatter.43.cloned.1.call-start = ((), (), s32[]{:S(2)}) async-start(), calls=%async_computation.34 | async-start | bytes 3538944 | tf_op jit(solution)/shard_map/reduce_scatter | solution.py:620
  2022.9 952.1 %reduce-scatter.45.cloned.1.call-start = ((), (), s32[]{:S(2)}) async-start(), calls=%async_computation.35 | async-start | bytes 3538944 | tf_op jit(solution)/shard_map/reduce_scatter | solution.py:623
  (1701 other events, 22775.1 us)
Sparse Core Ops, SparseCore 0:
  26.7 31.6 all-reduce.18
  354.9 45.4 all-reduce.20
  410.4 42.8 all-reduce.22
  562.8 67.7 all-reduce.24
  717.8 35.2 all-reduce.26
  788.1 112.7 reduce-scatter.28
  904.8 61.3 reduce-scatter.30
  969.0 41.8 all-reduce.28
  1022.7 42.8 all-reduce.30
  1069.1 61.4 reduce-scatter.66
  1134.2 60.4 reduce-scatter.48
  1198.2 60.5 reduce-scatter.50
  1262.5 63.1 reduce-scatter.46
  1329.3 63.1 reduce-scatter.52
  1967.4 61.8 reduce-scatter.60
  2033.3 60.0 reduce-scatter.64
  2097.4 60.0 reduce-scatter.62
  2161.5 60.0 reduce-scatter.36
  2224.7 67.6 all-reduce.32
  2296.2 75.0 reduce-scatter.54
  2375.3 73.8 reduce-scatter.56
  2453.2 73.5 reduce-scatter.58
  2530.8 68.0 reduce-scatter.34
  2602.6 68.1 reduce-scatter.38
  2674.7 68.1 reduce-scatter.32
  2746.7 73.4 reduce-scatter.40
  2824.0 73.2 reduce-scatter.42
  2901.3 73.5 reduce-scatter.44

commit v2 on v1

v2 whole, which is shorter than its diff:
```python
import itertools
import math

import jax
import jax.numpy as jnp
from jax import lax
from jax.experimental import pallas as pl
from jax.experimental.pallas import tpu as pltpu
from jax.sharding import PartitionSpec as P

HEAD_DIM = 64
CAP = 160
LANES = 128
LOG2E = 1.4426950408889634
LN2 = 0.6931471805599453
NEVER = 1e30
LIMIT = 56 * 1024 * 1024
MESH = pl.DeviceIdType.MESH
VMEM = pl.BlockSpec(memory_space=pltpu.VMEM)
ANY = pl.BlockSpec(memory_space=pl.ANY)


highest = lax.Precision.HIGHEST
epsilon = 1e-05
masked_score = -1e30


def from_behind(block, axis, distance):
    devices = range(lax.axis_size(axis))
    route = [(i - distance, i) for i in devices if i - distance in devices]
    return lax.ppermute(block, axis, route)


def to_low(values):
    return values.astype(jnp.bfloat16)


def product(left, right):
    return jnp.dot(left, right, preferred_element_type=jnp.float32)


def exact_product(left, right):
    return jnp.dot(left, right, precision=highest, preferred_element_type=jnp.float32)


def rms_scale(values, gain):
    return values * lax.rsqrt(jnp.mean(values * values, axis=-1, keepdims=True) + epsilon) * gain


def rms_back(values, gain, upstream):
    unused, pullback = jax.vjp(rms_scale, values, gain)
    return pullback(upstream)


def silu_slope(values):
    logistic = jax.nn.sigmoid(values)
    return logistic * (1.0 + values * (1.0 - logistic))


def meet(peers):
    barrier = pltpu.get_barrier_semaphore()
    for peer in peers:
        pl.semaphore_signal(barrier, inc=1, device_id=peer, device_id_type=MESH)
    pl.semaphore_wait(barrier, len(peers))


def send_to(source, target, send_sem, recv_sem, peer):
    return pltpu.make_async_remote_copy(
        src_ref=source,
        dst_ref=target,
        send_sem=send_sem,
        recv_sem=recv_sem,
        device_id=peer,
        device_id_type=MESH,
    )


def talking(number):
    return pltpu.CompilerParams(
        collective_id=number, has_side_effects=True, vmem_limit_bytes=LIMIT
    )


def head_sum(values, number, wire, pieces):
    rows, width = values.shape
    half = rows // 2
    step = half // pieces

    def kernel(x_ref, o_ref, near_out, near_in, far_out, far_in, send, recv):
        seq = lax.axis_index("seq")
        head = lax.axis_index("head")
        core = head % 2
        near = (seq, head + 1 - 2 * core)
        far = (seq, (head + 2) % 4)
        meet([near, far])

        def rows_of(side, piece):
            return pl.ds(pl.multiple_of(side * half + piece * step, 8), step)

        copies = []
        for piece in range(pieces):
            local = pl.ds(piece * step, step)
            near_out[local] = x_ref[rows_of(1 - core, piece)].astype(wire)
            copy = send_to(
                near_out.at[local], near_in.at[local], send.at[0, piece], recv.at[0, piece], near
            )
            copy.start()
            copies.append(copy)
        second = []
        for piece in range(pieces):
            local = pl.ds(piece * step, step)
            copies[piece].wait_recv()
            total = x_ref[rows_of(core, piece)] + near_in[local].astype(jnp.float32)
            far_out[local] = total.astype(wire)
            copy = send_to(
                far_out.at[local], far_in.at[local], send.at[1, piece], recv.at[1, piece], far
            )
            copy.start()
            second.append(copy)
        third = []
        for piece in range(pieces):
            local = pl.ds(piece * step, step)
            second[piece].wait_recv()
            whole = far_out[local].astype(jnp.float32) + far_in[local].astype(jnp.float32)
            o_ref[rows_of(core, piece)] = whole
            copy = send_to(
                o_ref.at[rows_of(core, piece)],
                o_ref.at[rows_of(core, piece)],
                send.at[2, piece],
                recv.at[2, piece],
                near,
            )
            copy.start()
            third.append(copy)
        for copy in third:
            copy.wait_recv()
        for copy in copies + second + third:
            copy.wait_send()

    return pl.pallas_call(
        kernel,
        out_shape=jax.ShapeDtypeStruct((rows, width), jnp.float32),
        in_specs=[VMEM],
        out_specs=VMEM,
        scratch_shapes=[pltpu.VMEM((half, width), wire)] * 4
        + [pltpu.SemaphoreType.DMA((3, pieces))] * 2,
        compiler_params=talking(number),
        name="head_sum",
    )(values)


def seq_gather(block, number):
    rows, width = block.shape
    seq_count = lax.axis_size("seq")
    pairs = seq_count // 2

    def kernel(x_ref, o_ref, send, recv, pass_send, pass_recv, own_sem):
        seq = lax.axis_index("seq")
        head = lax.axis_index("head")
        place = seq % 2
        pair = seq // 2
        partner = (seq + 1 - 2 * place, head)
        others = [(((pair + k) % pairs) * 2 + place, head) for k in range(1, pairs)]
        meet([partner] + others)
        own = pltpu.make_async_copy(x_ref, o_ref.at[seq], own_sem)
        own.start()
        first = [
            send_to(x_ref, o_ref.at[seq], send.at[k], recv.at[k], others[k])
            for k in range(pairs - 1)
        ]
        passed = [send_to(x_ref, o_ref.at[seq], pass_send.at[0], pass_recv.at[0], partner)]
        passed[0].start()
        for copy in first:
            copy.start()
        for k in range(1, pairs):
            first[k - 1].wait_recv()
            origin = ((pair - k + pairs) % pairs) * 2 + place
            copy = send_to(
                o_ref.at[origin], o_ref.at[origin], pass_send.at[k], pass_recv.at[k], partner
            )
            copy.start()
            passed.append(copy)
        for copy in passed:
            copy.wait_recv()
        for copy in first + passed:
            copy.wait_send()
        own.wait()

    out = pl.pallas_call(
        kernel,
        out_shape=jax.ShapeDtypeStruct((seq_count, rows, width), block.dtype),
        in_specs=[VMEM],
        out_specs=VMEM,
        scratch_shapes=[pltpu.SemaphoreType.DMA((pairs,))] * 4 + [pltpu.SemaphoreType.DMA],
        compiler_params=talking(number),
        name="seq_gather",
    )(block)
    return out.reshape(seq_count * rows, width)


def seq_scatter(arrays, number):
    seq_count = lax.axis_size("seq")
    pairs = seq_count // 2
    count = len(arrays)
    shapes = [(a.shape[0] // seq_count, a.shape[1]) for a in arrays]
    blocks = [
        a.reshape(pairs, 2, shape[0], shape[1]) for a, shape in zip(arrays, shapes, strict=True)
    ]

    def kernel(*refs):
        takes, gives = refs[:count], refs[count : 2 * count]
        own, near = refs[2 * count : 3 * count], refs[3 * count : 4 * count]
        far = refs[4 * count : 5 * count]
        own_sem, near_send, near_recv, far_send, far_recv = refs[5 * count :]
        seq = lax.axis_index("seq")
        head = lax.axis_index("head")
        place = seq % 2
        pair = seq // 2
        partner = (seq + 1 - 2 * place, head)
        owners = [(pair + k) % pairs for k in range(1, pairs)]
        others = [(owner * 2 + place, head) for owner in owners]
        meet([partner] + others)
        loads = [
            pltpu.make_async_copy(takes[i].at[:, place], own[i], own_sem.at[i])
            for i in range(count)
        ]
        halves = [
            send_to(takes[i].at[:, 1 - place], near[i], near_send.at[i], near_recv.at[i], partner)
            for i in range(count)
        ]

        def launch(i):
            if i < count:
                halves[i].start()
                loads[i].start()

        sums = []

        def finish(i):
            rows = shapes[i][0]
            for copy in sums[i]:
                copy.wait_recv()

            @pl.loop(0, rows // 16)
            def add(step):
                part = pl.ds(pl.multiple_of(step * 16, 16), 16)
                total = own[i][pair, part].astype(jnp.float32)
                for k in range(pairs - 1):
                    total = total + far[i][k, part].astype(jnp.float32)
                gives[i][part] = total

        launch(0)
        launch(1)
        for i in range(count):
            rows = shapes[i][0]
            halves[i].wait_recv()
            loads[i].wait()
            launch(i + 2)

            @pl.loop(0, pairs)
            def merge(block):
                @pl.loop(0, rows // 16)
                def add(step):
                    part = pl.ds(pl.multiple_of(step * 16, 16), 16)
                    total = own[i][block, part].astype(jnp.float32) + near[i][block, part].astype(
                        jnp.float32
                    )
                    own[i][block, part] = total.astype(jnp.bfloat16)

            sums.append(
                [
                    send_to(
                        own[i].at[owners[k]],
                        far[i].at[k],
                        far_send.at[i, k],
                        far_recv.at[i, k],
                        others[k],
                    )
                    for k in range(pairs - 1)
                ]
            )
            for copy in sums[i]:
                copy.start()
            if i > 0:
                finish(i - 1)
        finish(count - 1)
        for copy in halves:
            copy.wait_send()
        for group in sums:
            for copy in group:
                copy.wait_send()

    return pl.pallas_call(
        kernel,
        out_shape=[jax.ShapeDtypeStruct(shape, jnp.float32) for shape in shapes],
        in_specs=[ANY] * count,
        out_specs=[VMEM] * count,
        scratch_shapes=[pltpu.VMEM((pairs,) + shape, jnp.bfloat16) for shape in shapes] * 2
        + [pltpu.VMEM((pairs - 1,) + shape, jnp.bfloat16) for shape in shapes]
        + [pltpu.SemaphoreType.DMA((count,))] * 3
        + [pltpu.SemaphoreType.DMA((count, pairs - 1))] * 2,
        compiler_params=talking(number),
        name="seq_scatter",
    )(*blocks)


def widen(column_block, width):
    return jnp.concatenate([column_block] * (width // LANES), axis=-1)


def narrow(wide):
    width = wide.shape[-1]
    total = wide[:, :LANES]
    for place in range(1, width // LANES):
        total = total + wide[:, place * LANES : (place + 1) * LANES]
    return total


def spread(columns):
    return jnp.broadcast_to(columns[:, :, None], columns.shape + (LANES,))


def run_summary(steps, drives, coefficients, slopes, number, forward):
    rows, width = steps.shape
    entries = slopes.shape[0]
    seq_count = lax.axis_size("seq")
    group = math.gcd(rows, 8)

    def kernel(step_ref, drive_ref, coef_ref, slope_ref, o_ref, outgoing, incoming, send, recv):
        seq = lax.axis_index("seq")
        head = lax.axis_index("head")
        peers = [((seq + k) % seq_count, head) for k in range(1, seq_count)]
        meet(peers)
        slope = slope_ref[...]

        def advance(position, state):
            for offset in range(group):
                t = position * group + offset
                t = t if forward else rows - 1 - t
                decays = jnp.exp2(step_ref[pl.ds(t, 1), :] * slope)
                drive = drive_ref[pl.ds(t, 1), :] * widen(coef_ref[t], width)
                state = state * decays + drive if forward else (state + drive) * decays
            return state

        state = lax.fori_loop(0, rows // group, advance, jnp.zeros((entries, width), jnp.float32))
        whole = jnp.exp2(jnp.sum(step_ref[...], axis=0, keepdims=True) * slope)
        outgoing[:entries] = state.astype(jnp.bfloat16)
        outgoing[entries:] = whole.astype(jnp.bfloat16)
        copies = [
            send_to(outgoing, incoming.at[k], send.at[k], recv.at[k], peers[k])
            for k in range(seq_count - 1)
        ]
        for copy in copies:
            copy.start()
        for copy in copies:
            copy.wait_recv()
        carried = jnp.zeros((entries, width), jnp.float32)
        order = range(seq_count - 1, 0, -1) if forward else range(1, seq_count)
        for k in order:
            known = seq - k >= 0 if forward else seq - k < 0
            block = incoming[k - 1].astype(jnp.float32)
            carried = jnp.where(known, block[entries:] * carried + block[:entries], 0.0)
        o_ref[...] = carried
        for copy in copies:
            copy.wait_send()

    return pl.pallas_call(
        kernel,
        out_shape=jax.ShapeDtypeStruct((entries, width), jnp.float32),
        in_specs=[VMEM] * 4,
        out_specs=VMEM,
        scratch_shapes=[
            pltpu.VMEM((2 * entries, width), jnp.bfloat16),
            pltpu.VMEM((seq_count - 1, 2 * entries, width), jnp.bfloat16),
            pltpu.SemaphoreType.DMA((seq_count - 1,)),
            pltpu.SemaphoreType.DMA((seq_count - 1,)),
        ],
        compiler_params=talking(number),
        name="run_summary",
    )(steps, drives, coefficients, slopes)


def state_sweep(initial, steps, drives, inject, readout, slopes):
    rows, width = steps.shape
    entries = slopes.shape[0]
    length = math.gcd(rows, 32)
    group = math.gcd(length, 8)

    def kernel(
        init_ref, step_ref, drive_ref, inject_ref, read_ref, slope_ref, y_ref, before_ref, end_ref
    ):
        @pl.when(pl.program_id(0) == 0)
        def begin():
            end_ref[...] = init_ref[...]

        slope = slope_ref[...]

        def advance(position, state):
            for offset in range(group):
                t = position * group + offset
                before_ref[t] = state
                decays = jnp.exp2(step_ref[pl.ds(t, 1), :] * slope)
                drive = drive_ref[pl.ds(t, 1), :] * widen(inject_ref[t], width)
                state = state * decays + drive
                y_ref[pl.ds(t, 1), :] = jnp.sum(
                    state * widen(read_ref[t], width), axis=0, keepdims=True
                )
            return state

        end_ref[...] = lax.fori_loop(0, length // group, advance, end_ref[...])

    row_spec = pl.BlockSpec((length, width), lambda i: (i, 0))
    entry_spec = pl.BlockSpec((length, entries, LANES), lambda i: (i, 0, 0))
    fixed = pl.BlockSpec((entries, width), lambda i: (0, 0))
    return pl.pallas_call(
        kernel,
        grid=(rows // length,),
        out_shape=(
            jax.ShapeDtypeStruct((rows, width), jnp.float32),
            jax.ShapeDtypeStruct((rows, entries, width), jnp.float32),
            jax.ShapeDtypeStruct((entries, width), jnp.float32),
        ),
        in_specs=[fixed, row_spec, row_spec, entry_spec, entry_spec, fixed],
        out_specs=(
            row_spec,
            pl.BlockSpec((length, entries, width), lambda i: (i, 0, 0)),
            fixed,
        ),
        compiler_params=pltpu.CompilerParams(vmem_limit_bytes=LIMIT),
        name="state_sweep",
    )(initial, steps, drives, inject, readout, slopes)


def adjoint_sweep(incoming, last_state, befores, steps, drives, inject, readout, upstream, slopes):
    rows, width = steps.shape
    entries = slopes.shape[0]
    length = math.gcd(rows, 32)
    group = math.gcd(length, 8)
    blocks = rows // length

    def kernel(
        in_ref,
        last_ref,
        before_ref,
        step_ref,
        drive_ref,
        inject_ref,
        read_ref,
        up_ref,
        slope_ref,
        through_ref,
        injected_ref,
        inject_out,
        read_out,
        rate_ref,
        adjoint_ref,
        state_ref,
    ):
        @pl.when(pl.program_id(0) == 0)
        def begin():
            adjoint_ref[...] = in_ref[...]
            state_ref[...] = last_ref[...]
            rate_ref[...] = jnp.zeros_like(rate_ref)

        slope = slope_ref[...]

        def retreat(position, carried):
            adjoint_in, rate = carried
            for offset in range(group):
                t = length - 1 - (position * group + offset)
                upper = up_ref[pl.ds(t, 1), :]
                step = step_ref[pl.ds(t, 1), :]
                adjoint = widen(read_ref[t], width) * upper + adjoint_in
                state = state_ref[...] if offset == 0 else before_ref[t + 1]
                read_out[t] = narrow(upper * state)
                adjoint_in = jnp.exp2(step * slope) * adjoint
                before = before_ref[t]
                through = adjoint_in * before
                rate = rate + through * step
                through_ref[pl.ds(t, 1), :] = jnp.sum(through * slope, axis=0, keepdims=True)
                injected_ref[pl.ds(t, 1), :] = jnp.sum(
                    adjoint * widen(inject_ref[t], width), axis=0, keepdims=True
                )
                inject_out[t] = narrow(adjoint * drive_ref[pl.ds(t, 1), :])
            state_ref[...] = before_ref[length - (position + 1) * group]
            return (adjoint_in, rate)

        adjoint_end, rate_end = lax.fori_loop(
            0, length // group, retreat, (adjoint_ref[...], rate_ref[...])
        )
        adjoint_ref[...] = adjoint_end
        rate_ref[...] = rate_end

    row_spec = pl.BlockSpec((length, width), lambda i: (blocks - 1 - i, 0))
    entry_spec = pl.BlockSpec((length, entries, LANES), lambda i: (blocks - 1 - i, 0, 0))
    fixed = pl.BlockSpec((entries, width), lambda i: (0, 0))
    wide = jax.ShapeDtypeStruct((rows, width), jnp.float32)
    partial = jax.ShapeDtypeStruct((rows, entries, LANES), jnp.float32)
    return pl.pallas_call(
        kernel,
        grid=(blocks,),
        out_shape=(
            wide,
            wide,
            partial,
            partial,
            jax.ShapeDtypeStruct((entries, width), jnp.float32),
        ),
        in_specs=[
            fixed,
            fixed,
            pl.BlockSpec((length, entries, width), lambda i: (blocks - 1 - i, 0, 0)),
            row_spec,
            row_spec,
            entry_spec,
            entry_spec,
            row_spec,
            fixed,
        ],
        out_specs=(row_spec, row_spec, entry_spec, entry_spec, fixed),
        scratch_shapes=[pltpu.VMEM((entries, width), jnp.float32)] * 2,
        compiler_params=pltpu.CompilerParams(vmem_limit_bytes=LIMIT),
        name="adjoint_sweep",
    )(incoming, last_state, befores, steps, drives, inject, readout, upstream, slopes)


def body(
    tokens_in,
    cotangent,
    document_ids,
    expert_routes,
    norm_mixer,
    mixer_inner,
    mixer_gate,
    conv_taps,
    conv_bias,
    state_proj,
    step_proj,
    step_bias,
    decay_log,
    skip_gain,
    mixer_out,
    norm_ffn,
    ffn_gate,
    ffn_up,
    ffn_down,
    norm_attn,
    attn_query,
    attn_key,
    attn_value,
    attn_output,
    norm_moe,
    router,
    expert_gate,
    expert_up,
    expert_down,
):
    numbers = itertools.count()
    seq_count = lax.axis_size("seq")
    row_count = tokens_in.shape[0]
    total_rows = seq_count * row_count
    first_row = lax.axis_index("seq") * row_count
    last_row = first_row + row_count - 1

    def by_model_rows(pattern, left, right):
        blocks = to_low(jnp.einsum(pattern, left, right, preferred_element_type=jnp.float32))
        return blocks.transpose(1, 0, 2).reshape(blocks.shape[1], -1)

    def branch_sum(values):
        return head_sum(values, next(numbers), jnp.bfloat16, 4)

    local_docs = lax.dynamic_slice_in_dim(document_ids, first_row, row_count)
    reach = conv_taps.shape[0] - 1
    border = jnp.arange(reach, dtype=jnp.int32)
    docs_before = jnp.take(document_ids, jnp.maximum(first_row - reach + border, 0))
    docs_after = jnp.take(document_ids, jnp.minimum(first_row + row_count + border, total_rows - 1))
    docs_prior = jnp.concatenate([docs_before[reach - 1 :], local_docs[:-1]])
    retain = (local_docs == docs_prior).astype(jnp.float32)
    tokens = tokens_in.astype(jnp.float32)
    gain_mixer = norm_mixer.astype(jnp.float32)
    normed_one = to_low(rms_scale(tokens, gain_mixer))
    conv_in = to_low(product(normed_one, mixer_inner))
    gate_in = product(normed_one, mixer_gate)
    conv_edge = from_behind(conv_in[row_count - reach :], "seq", 1)
    extended = jnp.concatenate([conv_edge, conv_in]).astype(jnp.float32)
    docs_ext = jnp.concatenate([docs_before, local_docs])
    taps = conv_taps.astype(jnp.float32)
    conv_sum = conv_bias.astype(jnp.float32)[None, :]
    masks = []
    for offset in range(reach + 1):
        same_doc = (docs_ext[offset : offset + row_count] == local_docs).astype(jnp.float32)[
            :, None
        ]
        masks.append(same_doc)
        conv_sum = conv_sum + taps[offset] * extended[offset : offset + row_count] * same_doc
    activated = jax.nn.silu(conv_sum)
    act_low = to_low(activated)
    projected = head_sum(product(act_low, state_proj), next(numbers), jnp.float32, 1)
    rank_size = step_proj.shape[0]
    state_size = decay_log.shape[1]
    step_low = to_low(projected[:, :rank_size])
    inject = projected[:, rank_size : rank_size + state_size]
    readout = projected[:, rank_size + state_size :]
    step_pre = product(step_low, step_proj) + step_bias.astype(jnp.float32)
    step_dt = jax.nn.softplus(step_pre)
    decay_rate = jnp.exp(decay_log.astype(jnp.float32)).T
    slopes = -LOG2E * decay_rate
    steps = jnp.where(retain[:, None] > 0.0, step_dt, NEVER)
    drives = step_dt * activated
    inject_wide = spread(inject)
    readout_wide = spread(readout)
    state_in = run_summary(steps, drives, inject_wide, slopes, next(numbers), True)
    scanned, befores, state_out = state_sweep(
        state_in, steps, drives, inject_wide, readout_wide, slopes
    )
    skipping = skip_gain.astype(jnp.float32)
    mixed_state = scanned + skipping * activated
    gate_act = jax.nn.silu(gate_in)
    gated = to_low(mixed_state * gate_act)
    hidden_one = tokens + branch_sum(product(gated, mixer_out))
    gain_ffn = norm_ffn.astype(jnp.float32)
    normed_two = to_low(rms_scale(hidden_one, gain_ffn))
    gate_two = product(normed_two, ffn_gate)
    up_two = product(normed_two, ffn_up)
    ffn_act = to_low(jax.nn.silu(gate_two) * up_two)
    hidden_two = hidden_one + branch_sum(product(ffn_act, ffn_down))
    gain_attn = norm_attn.astype(jnp.float32)
    normed_three = to_low(rms_scale(hidden_two, gain_attn))
    queries = to_low(product(normed_three, attn_query))
    key_rows = to_low(product(normed_three, attn_key))
    value_rows = to_low(product(normed_three, attn_value))
    shared_heads = attn_key.shape[1] // HEAD_DIM
    group_size = attn_query.shape[1] // attn_key.shape[1]
    query_heads = queries.reshape(row_count, shared_heads, group_size, HEAD_DIM)
    query_pos = first_row + jnp.arange(row_count, dtype=jnp.int32)

    def visible(offset, block_rows):
        key_pos = offset + jnp.arange(block_rows, dtype=jnp.int32)
        key_docs = lax.dynamic_slice_in_dim(document_ids, offset, block_rows)
        return (key_pos[None, :] <= query_pos[:, None]) & (key_docs[None, :] == local_docs[:, None])

    def split_blocks(pieces, begin_row):
        key_piece, value_piece = pieces
        piece_rows = key_piece.shape[0]
        block_rows = math.gcd(piece_rows, 512)
        block_count = piece_rows // block_rows
        key_blocks = key_piece.reshape(block_count, block_rows, shared_heads, HEAD_DIM)
        value_blocks = value_piece.reshape(block_count, block_rows, shared_heads, HEAD_DIM)
        offsets = begin_row + block_rows * jnp.arange(block_count, dtype=jnp.int32)
        return (block_rows, (key_blocks, value_blocks, offsets))

    both_rows = seq_gather(jnp.concatenate([key_rows, value_rows], axis=1), next(numbers))
    key_width = key_rows.shape[1]
    gathered = (both_rows[:, :key_width], both_rows[:, key_width:])
    start_max = jnp.full((shared_heads, group_size, row_count), masked_score, jnp.float32)
    block_rows, blocked = split_blocks(
        gathered,
        jnp.int32(0),
    )

    def visit_block(running, element):
        key_block, value_block, offset = element

        def compute(current):
            row_max, row_sum, weighted = current
            scores = (
                jnp.einsum(
                    "qgrd,kgd->grqk", query_heads, key_block, preferred_element_type=jnp.float32
                )
                * 0.125
            )
            allowed = visible(offset, block_rows)
            masked = jnp.where(allowed, scores, masked_score)
            new_max = jnp.maximum(row_max, jnp.max(masked, axis=-1))
            weights = jnp.where(allowed, jnp.exp(masked - new_max[..., None]), 0.0)
            factor = jnp.exp(row_max - new_max)
            row_sum = row_sum * factor + jnp.sum(weights, axis=-1)
            weighted = weighted * factor[..., None] + jnp.einsum(
                "grqk,kgd->grqd", to_low(weights), value_block, preferred_element_type=jnp.float32
            )
            return (new_max, row_sum, weighted)

        return (lax.cond(offset <= last_row, compute, lambda untouched: untouched, running), None)

    result, unused_out = lax.scan(
        visit_block,
        (
            start_max,
            jnp.zeros_like(start_max),
            jnp.zeros((shared_heads, group_size, row_count, HEAD_DIM), jnp.float32),
        ),
        blocked,
    )
    folded = result
    attended = folded[2] / folded[1][..., None]
    log_sum = folded[0] + jnp.log(folded[1])
    attended_low = to_low(attended.transpose(2, 0, 1, 3).reshape(row_count, -1))
    hidden_three = hidden_two + branch_sum(product(attended_low, attn_output))
    gain_moe = norm_moe.astype(jnp.float32)
    normed_four = to_low(rms_scale(hidden_three, gain_moe))
    logits = product(normed_four, router)
    expert_count = router.shape[1]
    experts = jnp.arange(expert_count, dtype=jnp.int32)
    named = (expert_routes[:, :, None] == experts).astype(jnp.float32)
    gate_weights = jax.nn.softmax(jnp.sum(named * logits[:, None, :], axis=2), axis=1)
    route_flat = expert_routes.reshape(-1)
    pair_count = route_flat.shape[0]
    pair_order = jnp.arange(pair_count, dtype=jnp.int32)
    earlier = (pair_order[None, :] < pair_order[:, None]) & (
        route_flat[None, :] == route_flat[:, None]
    )
    within = jnp.sum(earlier.astype(jnp.int32), axis=1)
    slot_index = (route_flat * CAP + within).reshape(row_count, 2)
    slots = jnp.arange(expert_count * CAP, dtype=jnp.int32)
    first_hit = slot_index[:, 0][None, :] == slots[:, None]
    second_hit = slot_index[:, 1][None, :] == slots[:, None]
    placing = (first_hit | second_hit).astype(jnp.bfloat16)
    slot_gates = jnp.sum(
        jnp.where(first_hit, gate_weights[:, 0][None, :], 0.0)
        + jnp.where(second_hit, gate_weights[:, 1][None, :], 0.0),
        axis=1,
    )
    expert_in = to_low(product(placing, normed_four)).reshape(expert_count, CAP, -1)
    slot_upstream = product(placing, cotangent)
    res_grad = to_low(slot_gates[:, None] * slot_upstream).reshape(expert_count, CAP, -1)
    gate_four = jnp.einsum(
        "ecd,edf->ecf", expert_in, expert_gate, preferred_element_type=jnp.float32
    )
    up_four = jnp.einsum("ecd,edf->ecf", expert_in, expert_up, preferred_element_type=jnp.float32)
    expert_act = to_low(jax.nn.silu(gate_four) * up_four)
    expert_res = jnp.einsum(
        "ecf,efd->ecd", expert_act, expert_down, preferred_element_type=jnp.float32
    ).reshape(expert_count * CAP, -1)
    upstream = cotangent.astype(jnp.float32)
    slot_dots = jnp.sum(expert_res * slot_upstream, axis=1)
    dots_part = jnp.stack(
        [
            jnp.sum(jnp.where(first_hit, slot_dots[:, None], 0.0), axis=0),
            jnp.sum(jnp.where(second_hit, slot_dots[:, None], 0.0), axis=0),
        ],
        axis=1,
    )
    combined = product(placing.T, to_low(slot_gates[:, None] * expert_res))
    act_back = to_low(
        jnp.einsum("ecd,efd->ecf", res_grad, expert_down, preferred_element_type=jnp.float32)
    ).astype(jnp.float32)
    gating_grad = to_low(act_back * up_four * silu_slope(gate_four))
    upward_grad = to_low(act_back * jax.nn.silu(gate_four))
    grad_expert_down = by_model_rows("ecd,ecf->edf", res_grad, expert_act)
    grad_expert_gate = by_model_rows("ecd,ecf->edf", expert_in, gating_grad)
    grad_expert_up = by_model_rows("ecd,ecf->edf", expert_in, upward_grad)
    slot_grads = (
        jnp.einsum("ecf,edf->ecd", gating_grad, expert_gate, preferred_element_type=jnp.float32)
        + jnp.einsum("ecf,edf->ecd", upward_grad, expert_up, preferred_element_type=jnp.float32)
    ).reshape(expert_count * CAP, -1)
    token_part = product(placing.T, to_low(slot_grads))
    model_width = tokens.shape[1]
    expert_sums = branch_sum(
        jnp.concatenate(
            [combined, token_part, jnp.pad(dots_part, ((0, 0), (0, LANES - 2)))], axis=1
        )
    )
    mixed_out = to_low(hidden_three + expert_sums[:, :model_width])
    normed_grad = expert_sums[:, model_width : 2 * model_width]
    dots = expert_sums[:, 2 * model_width : 2 * model_width + 2]
    chosen_grad = gate_weights * (dots - jnp.sum(gate_weights * dots, axis=1, keepdims=True))
    logit_grad = jnp.sum(named * chosen_grad[:, :, None], axis=1)
    grad_router = exact_product(normed_four.astype(jnp.float32).T, logit_grad)
    normed_grad = normed_grad + exact_product(logit_grad, router.astype(jnp.float32).T)
    hidden_grad, grad_norm_moe = rms_back(hidden_three, gain_moe, normed_grad)
    three_grad = upstream + hidden_grad
    branch_grad = to_low(three_grad)
    grad_attn_output = to_low(product(branch_grad.T, attended_low))
    attended_grad = to_low(product(branch_grad, attn_output.T))
    out_heads = attended_grad.reshape(row_count, shared_heads, group_size, HEAD_DIM).transpose(
        1, 2, 0, 3
    )
    delta = jnp.sum(out_heads.astype(jnp.float32) * attended, axis=-1)
    initial = (
        jnp.zeros((shared_heads, group_size, row_count, HEAD_DIM), jnp.float32),
        jnp.zeros((total_rows, key_width), jnp.float32),
        jnp.zeros((total_rows, key_width), jnp.float32),
    )
    attend_block_rows, blocked = split_blocks(
        gathered,
        jnp.int32(0),
    )

    def visit_back(running, element):
        key_block, value_block, offset = element

        def compute(current):
            query_acc, key_acc, value_acc = current
            scores = (
                jnp.einsum(
                    "qgrd,kgd->grqk", query_heads, key_block, preferred_element_type=jnp.float32
                )
                * 0.125
            )
            allowed = visible(offset, attend_block_rows)
            probs = jnp.where(allowed, jnp.exp(scores - log_sum[..., None]), 0.0)
            value_part = jnp.einsum(
                "grqk,grqd->kgd", to_low(probs), out_heads, preferred_element_type=jnp.float32
            )
            prob_grad = jnp.einsum(
                "grqd,kgd->grqk", out_heads, value_block, preferred_element_type=jnp.float32
            )
            score_grad = to_low(probs * (prob_grad - delta[..., None]))
            query_acc = (
                query_acc
                + jnp.einsum(
                    "grqk,kgd->grqd", score_grad, key_block, preferred_element_type=jnp.float32
                )
                * 0.125
            )
            key_part = (
                jnp.einsum(
                    "grqk,qgrd->kgd", score_grad, query_heads, preferred_element_type=jnp.float32
                )
                * 0.125
            )
            key_acc = lax.dynamic_update_slice_in_dim(
                key_acc,
                lax.dynamic_slice_in_dim(key_acc, offset, attend_block_rows, 0)
                + key_part.reshape(attend_block_rows, -1),
                offset,
                0,
            )
            value_acc = lax.dynamic_update_slice_in_dim(
                value_acc,
                lax.dynamic_slice_in_dim(value_acc, offset, attend_block_rows, 0)
                + value_part.reshape(attend_block_rows, -1),
                offset,
                0,
            )
            return (query_acc, key_acc, value_acc)

        return (lax.cond(offset <= last_row, compute, lambda untouched: untouched, running), None)

    result, unused_out = lax.scan(visit_back, initial, blocked)
    query_acc, key_acc, value_acc = result
    (both_sums,) = seq_scatter(
        [to_low(jnp.concatenate([key_acc, value_acc], axis=1))], next(numbers)
    )
    key_sum, value_sum = both_sums[:, :key_width], both_sums[:, key_width:]
    query_grad = to_low(query_acc.transpose(2, 0, 1, 3).reshape(row_count, -1))
    key_grad = to_low(key_sum)
    value_grad = to_low(value_sum)
    grad_attn_in = to_low(
        product(normed_three.T, jnp.concatenate([query_grad, key_grad, value_grad], axis=1))
    )
    normed_grad = branch_sum(
        product(query_grad, attn_query.T)
        + product(key_grad, attn_key.T)
        + product(value_grad, attn_value.T)
    )
    hidden_grad, grad_norm_attn = rms_back(hidden_two, gain_attn, normed_grad)
    two_grad = three_grad + hidden_grad
    branch_grad = to_low(two_grad)
    grad_ffn_down = to_low(product(branch_grad.T, ffn_act))
    ffn_back = to_low(product(branch_grad, ffn_down.T)).astype(jnp.float32)
    feed_gate_grad = to_low(ffn_back * up_two * silu_slope(gate_two))
    feed_up_grad = to_low(ffn_back * jax.nn.silu(gate_two))
    grad_ffn_gate = to_low(product(normed_two.T, feed_gate_grad))
    grad_ffn_up = to_low(product(normed_two.T, feed_up_grad))
    normed_grad = branch_sum(product(feed_gate_grad, ffn_gate.T) + product(feed_up_grad, ffn_up.T))
    hidden_grad, grad_norm_ffn = rms_back(hidden_one, gain_ffn, normed_grad)
    one_grad = two_grad + hidden_grad
    branch_grad = to_low(one_grad)
    grad_mixer_out = to_low(product(branch_grad.T, gated))
    gated_grad = to_low(product(branch_grad, mixer_out.T)).astype(jnp.float32)
    scan_grad = gated_grad * gate_act
    gate_in_grad = to_low(gated_grad * mixed_state * silu_slope(gate_in))
    grad_skip_gain = jnp.sum(scan_grad * activated, axis=0)
    state_after = run_summary(steps, scan_grad, readout_wide, slopes, next(numbers), False)
    through_sum, injected, inject_part, readout_part, rate_sum = adjoint_sweep(
        state_after,
        state_out,
        befores,
        steps,
        drives,
        inject_wide,
        readout_wide,
        scan_grad,
        slopes,
    )
    step_grad = LN2 * through_sum + activated * injected
    input_grad = step_dt * injected
    inject_grad = jnp.sum(inject_part, axis=2)
    readout_grad = jnp.sum(readout_part, axis=2)
    grad_decay_log = -rate_sum * decay_rate
    pre_grad = step_grad * jax.nn.sigmoid(step_pre)
    grad_step_bias = jnp.sum(pre_grad, axis=0)
    pre_low = to_low(pre_grad)
    grad_step_proj = product(step_low.T, pre_low)
    proj_part = jnp.concatenate([product(pre_low, step_proj.T), inject_grad, readout_grad], axis=1)
    proj_low = to_low(head_sum(proj_part, next(numbers), jnp.float32, 1))
    grad_state_proj = product(act_low.T, proj_low)
    act_total = input_grad + skipping * scan_grad + product(proj_low, state_proj.T)
    conv_grad = act_total * silu_slope(conv_sum)
    grad_conv_bias = jnp.sum(conv_grad, axis=0)
    after_edge = from_behind(conv_grad[:reach], "seq", -1)
    grad_ext = jnp.concatenate([conv_grad, after_edge])
    docs_next = jnp.concatenate([local_docs, docs_after])
    conv_in_grad = jnp.zeros_like(conv_grad)
    tap_rows = []
    for offset in range(reach + 1):
        tap_rows.append(
            jnp.sum(conv_grad * extended[offset : offset + row_count] * masks[offset], axis=0)
        )
        lead = reach - offset
        same_next = (docs_next[lead : lead + row_count] == local_docs).astype(jnp.float32)[:, None]
        conv_in_grad = conv_in_grad + taps[offset] * grad_ext[lead : lead + row_count] * same_next
    grad_conv_taps = jnp.stack(tap_rows)
    conv_low = to_low(conv_in_grad)
    grad_mixer_inner = to_low(product(normed_one.T, conv_low))
    grad_mixer_gate = to_low(product(normed_one.T, gate_in_grad))
    normed_grad = branch_sum(product(conv_low, mixer_inner.T) + product(gate_in_grad, mixer_gate.T))
    hidden_grad, grad_norm_mixer = rms_back(tokens, gain_mixer, normed_grad)
    grad_tokens = one_grad + hidden_grad
    own_channels = grad_conv_bias.shape[0] // seq_count

    def cut(values, axis):
        values = jnp.moveaxis(values, axis, 0)
        return values.reshape(seq_count, -1)

    packed = jnp.concatenate(
        [
            cut(grad_norm_mixer, 0),
            cut(grad_norm_ffn, 0),
            cut(grad_norm_attn, 0),
            cut(grad_norm_moe, 0),
            cut(grad_router, 0),
            cut(grad_conv_taps, 1),
            cut(grad_conv_bias, 0),
            cut(grad_state_proj, 0),
            cut(grad_step_proj, 1),
            cut(grad_step_bias, 0),
            cut(grad_decay_log, 1),
            cut(grad_skip_gain, 0),
        ],
        axis=1,
    )
    spare = -packed.shape[1] % (16 * LANES)
    packed = to_low(jnp.pad(packed, ((0, 0), (0, spare)))).reshape(-1, LANES)
    (
        sum_expert_gate,
        sum_expert_up,
        sum_expert_down,
        sum_ffn_gate,
        sum_ffn_up,
        sum_ffn_down,
        sum_attn_in,
        sum_attn_output,
        sum_mixer_out,
        sum_mixer_inner,
        sum_mixer_gate,
        sum_packed,
    ) = seq_scatter(
        [
            grad_expert_gate,
            grad_expert_up,
            grad_expert_down,
            grad_ffn_gate,
            grad_ffn_up,
            grad_ffn_down,
            grad_attn_in,
            grad_attn_output,
            grad_mixer_out,
            grad_mixer_inner,
            grad_mixer_gate,
            packed,
        ],
        next(numbers),
    )
    sum_packed = sum_packed.reshape(-1)
    own_rows = model_width // seq_count
    taken = itertools.accumulate(
        [0]
        + [own_rows] * 4
        + [own_rows * expert_count]
        + [own_channels * (reach + 1), own_channels, own_channels * state_proj.shape[1]]
        + [own_channels * rank_size, own_channels, own_channels * state_size, own_channels]
    )
    bounds = list(taken)
    pieces = [sum_packed[low:high] for low, high in itertools.pairwise(bounds)]
    query_width = attn_query.shape[1]

    def by_expert(values):
        return values.reshape(values.shape[0], expert_count, -1)

    return (
        mixed_out,
        grad_tokens,
        pieces[0],
        sum_mixer_inner,
        sum_mixer_gate,
        pieces[5].reshape(own_channels, -1).T,
        pieces[6],
        pieces[7].reshape(own_channels, -1),
        pieces[8].reshape(own_channels, -1).T,
        pieces[9],
        pieces[10].reshape(own_channels, -1),
        pieces[11],
        sum_mixer_out.T,
        pieces[1],
        sum_ffn_gate,
        sum_ffn_up,
        sum_ffn_down.T,
        pieces[2],
        sum_attn_in[:, :query_width],
        sum_attn_in[:, query_width : query_width + key_width],
        sum_attn_in[:, query_width + key_width :],
        sum_attn_output.T,
        pieces[3],
        pieces[4].reshape(own_rows, -1),
        by_expert(sum_expert_gate).transpose(1, 0, 2),
        by_expert(sum_expert_up).transpose(1, 0, 2),
        by_expert(sum_expert_down).transpose(1, 2, 0),
    )


def solution(mesh):
    in_specs = (
        P("seq", None),
        P("seq", None),
        P(),
        P("seq", None),
        P(),
        P(None, "head"),
        P(None, "head"),
        P(None, "head"),
        P("head"),
        P("head", None),
        P(None, "head"),
        P("head"),
        P("head", None),
        P("head"),
        P("head", None),
        P(),
        P(None, "head"),
        P(None, "head"),
        P("head", None),
        P(),
        P(None, "head"),
        P(None, "head"),
        P(None, "head"),
        P("head", None),
        P(),
        P(),
        P(None, None, "head"),
        P(None, None, "head"),
        P(None, "head", None),
    )
    out_specs = (
        P("seq", None),
        P("seq", None),
        P("seq"),
        P("seq", "head"),
        P("seq", "head"),
        P(None, ("head", "seq")),
        P(("head", "seq")),
        P(("head", "seq"), None),
        P(None, ("head", "seq")),
        P(("head", "seq")),
        P(("head", "seq"), None),
        P(("head", "seq")),
        P("head", "seq"),
        P("seq"),
        P("seq", "head"),
        P("seq", "head"),
        P("head", "seq"),
        P("seq"),
        P("seq", "head"),
        P("seq", "head"),
        P("seq", "head"),
        P("head", "seq"),
        P("seq"),
        P("seq", None),
        P(None, "seq", "head"),
        P(None, "seq", "head"),
        P(None, "head", "seq"),
    )
    return jax.shard_map(body, mesh=mesh, in_specs=in_specs, out_specs=out_specs, check_vma=False)
```

time: 3030 us -> 994 us (0.33); the launches traced: 2980 us -> 986 us
  waiting for transfers between devices: 1360 us -> 0.01 us
  Pallas kernels: 0 us -> 691 us
  other arithmetic: 706 us -> 56.2 us
  local copies, waits for them, and re-layouts: 580 us -> 118 us
  blocking collectives: 123 us -> 0 us
  starting transfers between devices: 49.7 us -> 6.14 us
    reduce_scatter x16 -> x0, waiting for transfers between devices: 855 us -> none  [the longest x1 110 us: body(): lax.psum_scatter(key_acc.astype(jnp.bfloat16), 'seq', scatter_dimension=0...]
    pallas_call x0 -> x16, Pallas kernels: none -> 691 us  [the longest x2 463 us: seq_scatter(): pl.pallas_call(kernel, out_shape=[jax.ShapeDtypeStruct(shape, jnp.float32...]
    reduce_sum x373 -> x6, other arithmetic: 348 us -> 4.99 us  [the longest x1 2.21 us: body(): readout_grad = jnp.sum(readout_part, axis=2)]
    psum x8 -> x0, waiting for transfers between devices: 340 us -> none  [the longest x7 306 us: head_total(): return lax.psum(values, 'head')]
    mul x347 -> x1, other arithmetic: 170 us -> 0.64 us  [body(): slopes = -LOG2E * decay_rate]
    another operation x305 -> x13, local copies, waits for them, and re-layouts: 163 us -> 17.1 us  [the longest x3 11.6 us: seq_scatter(): a.reshape(pairs, 2, shape[0], shape[1])]
    mul x127 -> x1, local copies, waits for them, and re-layouts: 120 us -> 0.07 us  [body(): gate_weights * (dots - jnp.sum(gate_weights * dots, axis=1, keepdims=True))]
    unnamed x32 -> x0, waiting for transfers between devices: 117 us -> none
where the time goes in v2:
time: 994 us; the launch traced here: 986 us
  Pallas kernels  691 us (70%)
  local copies, waits for them, and re-layouts  118 us (12%)
  matrix products  102 us (10%)
  other arithmetic  56.2 us (6%)
    pallas_call x2, Pallas kernels, seq_scatter(): pl.pallas_call(kernel, out_shape=[jax.ShapeDtypeStruct(shape, jnp.float32...  463 us
    pallas_call x9, Pallas kernels, head_sum(): pl.pallas_call(kernel, out_shape=jax.ShapeDtypeStruct((rows, width), jnp....  142 us
    dot_general x39, matrix products, product(): return jnp.dot(left, right, preferred_element_type=jnp.float32)  72.6 us
    unnamed x350, local copies, waits for them, and re-layouts  36.7 us
    pallas_call x2, Pallas kernels, run_summary(): pl.pallas_call(kernel, out_shape=jax.ShapeDtypeStruct((entries, width), j...  35.3 us
    pallas_call x1, Pallas kernels, seq_gather(): pl.pallas_call(kernel, out_shape=jax.ShapeDtypeStruct((seq_count, rows, w...  23.5 us
  transfers between devices with their start and end apart: 2, of which 0 were waited for; matrix products, arithmetic and copies ran while one was open for 4% of the time, Pallas kernels for 0%

profile of v2, /device:TPU:0, one launch (start us, length us, event | category | flops | bytes accessed | tf_op | source)
XLA Modules:
  0.0 986.3 jit_solution(1788016704959731549)
XLA Ops:
  7.1 4.9 collective-permute-start
  22.0 8.0 head_sum.9
  36.2 17.2 %run_summary.2.init_ref = f32[16,768]{1,0:T(8,128)} custom-call(f32[256,768]{1,0:T(8,128)} %get-tuple-element.930.step_ref, f32[256,768]{1,0:T(8,128)} %get-tuple-element.929.drive_ref, f32[256,16,128]{2,1,0:T(8,128)} %broadcast_in_dim.109.coef_ref.inject_ref, f32[16,768]{1,0:T(8,128)} %bitcast_multiply_fusion.4.slope_ref), custom_call_target="tpu_custom_call" | custom-call | tf_op jit(solution)/shard_map/run_summary/pallas_call | solution.py:367
  55.3 11.1 %state_sweep.1 = (f32[256,768]{1,0:T(8,128)}, f32[256,16,768]{2,1,0:T(8,128)}, f32[16,768]{1,0:T(8,128)}) custom-call(f32[16,768]{1,0:T(8,128)} %run_summary.2.init_ref, f32[256,768]{1,0:T(8,128)} %get-tuple-element.930.step_ref, f32[256,768]{1,0:T(8,128)} %get-tuple-element.929.drive_ref, f32[256,16,128]{2,1,0:T(8,128)} %broadcast_in_dim.109.coef_ref.inject_ref, ...), custom_call_target="tpu_custom_call" | custom-call | tf_op jit(solution)/shard_map/state_sweep/pallas_call | solution.py:415
  66.5 3.8 multiply_convert_fusion.6
  72.9 16.3 %head_sum.10 = f32[256,1536]{1,0:T(8,128)} custom-call(f32[256,1536]{1,0:T(8,128)} %fusion.138.x_ref), custom_call_target="tpu_custom_call" | custom-call | tf_op jit(solution)/shard_map/head_sum/pallas_call | solution.py:140
  98.6 16.6 %head_sum.11 = f32[256,1536]{1,0:T(8,128)} custom-call(f32[256,1536]{1,0:T(8,128)} %fusion.140.x_ref), custom_call_target="tpu_custom_call" | custom-call | tf_op jit(solution)/shard_map/head_sum/pallas_call | solution.py:140
  119.6 23.5 %seq_gather.1 = bf16[8,256,256]{2,1,0:T(8,128)(2,1)} custom-call(bf16[256,256]{1,0:T(8,128)(2,1)} %pad_maximum_fusion.2.x_ref), custom_call_target="tpu_custom_call" | custom-call | tf_op jit(solution)/shard_map/seq_gather/pallas_call | solution.py:189
  148.5 3.5 copy.245
  155.2 3.5 copy.246
  161.8 16.2 %while.30 = (s32[]{:T(128)}, f32[2,3,256]{2,1,0:T(4,128)S(1)}, f32[2,3,256]{2,1,0:T(4,128)S(1)}, f32[2,3,256,64]{2,3,1,0:T(8,128)}, s32[4]{0:T(128)}, /*index=5*...) while((s32[]{:T(128)}, f32[2,3,256]{2,1,0:T(4,128)S(1)}, ...), condition=%wide.region_8.10_spmd.clone, body=%wide.region_3.9_spmd.clone.sunk | while | flops 212143872 | bytes 14467477 | solution.py:685
  163.7 8.1 conditional.6
  182.8 16.6 %head_sum.12 = f32[256,1536]{1,0:T(8,128)} custom-call(f32[256,1536]{1,0:T(8,128)} %fusion.141.x_ref), custom_call_target="tpu_custom_call" | custom-call | tf_op jit(solution)/shard_map/head_sum/pallas_call | solution.py:140
  223.7 27.3 %head_sum.13 = f32[256,3200]{1,0:T(8,128)} custom-call(f32[256,3200]{1,0:T(8,128)} %select_maximum_fusion.x_ref), custom_call_target="tpu_custom_call" | custom-call | tf_op jit(solution)/shard_map/head_sum/pallas_call | solution.py:140
  266.0 20.1 %while.31 = (s32[]{:T(128)}, f32[2,3,256,64]{2,3,1,0:T(8,128)S(1)}, f32[2048,128]{0,1:T(8,128)}, f32[2048,128]{0,1:T(8,128)}, s32[4]{0:T(128)S(1)}, /*index=5*/s...) while((s32[]{:T(128)}, f32[2,3,256,64]{2,3,1,0:T(8,128)S(1)}, ...), condition=%wide.region_25.27_spmd.clone, body=%wide.region_22.26_spmd.clone.sunk | while | flops 511968000 | bytes 19696536 | solution.py:840
  267.2 15.0 %conditional.7 = ((f32[2,3,256,64]{2,3,1,0:T(8,128)S(1)}, f32[2048,128]{0,1:T(8,128)}, f32[2048,128]{0,1:T(8,128)})) conditional(s32[]{:T(128)} %convert_element_type.502, (f32[2,3,256,64]{2,3,1,0:T(8,128)S(1)}, f32[2048,128]{0,1:T(8,128)}, f32[2048,128]{0,1:T(8,128)}) %tuple.148, (s32[]{:T(128)}, s32[]{:T(128)}, s32[2048]{0:T(1024)S(1)}, ...), branch_computations={%region_23.24_spmd, %region_24.25_spmd} | conditional | flops 511968000 | bytes 19695194 | solution.py:838
  290.4 99.1 %seq_scatter.2 = f32[256,256]{1,0:T(8,128)} custom-call(bf16[4,2,256,256]{3,2,1,0:T(8,128)(2,1)} %pad_maximum_fusion.refs_0_), custom_call_target="tpu_custom_call" | custom-call | tf_op jit(solution)/shard_map/seq_scatter/pallas_call | solution.py:293
  393.7 15.7 %head_sum.14 = f32[256,1536]{1,0:T(8,128)} custom-call(f32[256,1536]{1,0:T(8,128)} %convolution_add_fusion.3.x_ref), custom_call_target="tpu_custom_call" | custom-call | tf_op jit(solution)/shard_map/head_sum/pallas_call | solution.py:140
  421.2 16.6 %head_sum.15 = f32[256,1536]{1,0:T(8,128)} custom-call(f32[256,1536]{1,0:T(8,128)} %convolution_add_fusion.x_ref), custom_call_target="tpu_custom_call" | custom-call | tf_op jit(solution)/shard_map/head_sum/pallas_call | solution.py:140
  446.1 18.1 %run_summary.3.in_ref = f32[16,768]{1,0:T(8,128)} custom-call(f32[256,768]{1,0:T(8,128)} %get-tuple-element.930.step_ref, f32[256,768]{1,0:T(8,128)} %get-tuple-element.907.drive_ref.up_ref, f32[256,16,128]{2,1,0:T(8,128)} %broadcast_in_dim.110.read_ref.coef_ref, f32[16,768]{1,0:T(8,128)} %bitcast_multiply_fusion.4.slope_ref), custom_call_target="tpu_custom_call" | custom-call | tf_op jit(solution)/shard_map/run_summary/pallas_call | solution.py:367
  464.3 15.7 %adjoint_sweep.1 = (f32[256,768]{1,0:T(8,128)}, f32[256,768]{1,0:T(8,128)}, f32[256,16,128]{2,1,0:T(8,128)}, f32[256,16,128]{2,1,0:T(8,128)}, f32[16,768]{1,0:T(8,128)}) custom-call(f32[16,768]{1,0:T(8,128)} %run_summary.3.in_ref, f32[16,768]{1,0:T(8,128)} %get-tuple-element.413.last_ref, f32[256,16,768]{2,1,0:T(8,128)} %get-tuple-element.414.before_ref, ...), custom_call_target="tpu_custom_call" | custom-call | tf_op jit(solution)/shard_map/adjoint_sweep/pallas_call | solution.py:499
  489.5 8.1 head_sum.16
  497.6 4.3 multiply_reduce_fusion.13
  504.7 4.5 convolution_convert_fusion.1
  542.1 4.6 copy.262
  546.7 3.9 reshape_reshape.14.refs_2_
  550.6 4.6 copy.260
  555.2 3.9 reshape_reshape.12.refs_0_
  559.1 4.6 copy.261
  563.8 3.9 reshape_reshape.13.refs_1_
  577.2 16.5 %head_sum.17 = f32[256,1536]{1,0:T(8,128)} custom-call(f32[256,1536]{1,0:T(8,128)} %convolution_add_fusion.2.x_ref), custom_call_target="tpu_custom_call" | custom-call | tf_op jit(solution)/shard_map/head_sum/pallas_call | solution.py:140
  597.6 364.4 %seq_scatter.3 = (f32[192,1024]{1,0:T(8,128)}, f32[192,1024]{1,0:T(8,128)}, f32[192,1024]{1,0:T(8,128)}, f32[192,1024]{1,0:T(8,128)}, f32[192,1024]{1,0:T(8,128)...) custom-call(bf16[4,2,192,1024]{3,2,1,0:T(8,128)(2,1)} %reshape_resha, ...), custom_call_target="tpu_custom_call" | custom-call | tf_op jit(solution)/shard_map/seq_scatter/pallas_call | solution.py:293
  (585 shorter events, 232.5 us)
Async XLA Ops:
  0.7 208.9 %copy-start = (bf16[4,256,1536]{2,1,0:T(8,128)(2,1)S(1)}, bf16[4,256,1536]{2,1,0:T(8,128)(2,1)}, u32[]{:S(2)}) copy-start(bf16[4,256,1536]{2,1,0:T(8,128)(2,1)} %param.67) | copy-start | bytes 9437188
  2.7 63.7 %copy-start.135 = (f32[256]{0:T(256)}, f32[256]{0:T(256)S(1)}, u32[]{:S(2)}) copy-start(f32[256]{0:T(256)S(1)} %fusion.115) | copy-start | bytes 3076
  3.4 63.0 %copy-start.101 = (f32[1536]{0:T(1024)}, f32[1536]{0:T(1024)S(1)}, u32[]{:S(2)}) copy-start(f32[1536]{0:T(1024)S(1)} %convert_element_type.273) | copy-start | bytes 18436
  3.5 14.6 %copy-start.151 = (bf16[1536]{0:T(1024)(128)(2,1)S(1)}, bf16[1536]{0:T(1024)(128)(2,1)}, u32[]{:S(2)}) copy-start(bf16[1536]{0:T(1024)(128)(2,1)} %param.63) | copy-start | bytes 9220
  7.1 11.6 %collective-permute-start = (bf16[3,768]{1,0:T(4,128)(2,1)S(1)}, bf16[3,768]{1,0:T(4,128)(2,1)S(1)}, u32[]{:S(2)}, u32[]{:S(2)}) collective-permute-start(bf16[3,768]{1,0:T(4,128)(2,1)S(1)} %slice.223), channel_id=1, source_target_pairs={{0,4},{4,8},{8,12},{12,16},{16,20},{20,24},{24,28},{1,5},{5,9},{9,... | collective-permute-start | bytes 13832 | tf_op jit(solution)/shard_map/ppermute | solution.py:31
  18.0 48.4 %copy-start.152 = (f32[768]{0:T(1024)}, f32[768]{0:T(1024)S(1)}, u32[]{:S(2)}) copy-start(f32[768]{0:T(1024)S(1)} %convert_element_type.283) | copy-start | bytes 9220
  18.0 73.1 %copy-start.93 = (f32[1536]{0:T(1024)}, f32[1536]{0:T(1024)S(1)}, u32[]{:S(2)}) copy-start(f32[1536]{0:T(1024)S(1)} %convert_element_type.285) | copy-start | bytes 18436
  18.1 98.9 %copy-start.95 = (f32[1536]{0:T(1024)}, f32[1536]{0:T(1024)S(1)}, u32[]{:S(2)}) copy-start(f32[1536]{0:T(1024)S(1)} %convert_element_type.288) | copy-start | bytes 18436
  21.0 45.4 %copy-start.77 = (f32[256,768]{1,0:T(8,128)}, f32[256,768]{1,0:T(8,128)S(1)}, u32[]{:S(2)}) copy-start(f32[256,768]{1,0:T(8,128)S(1)} %multiply_add_fusion.2) | copy-start | bytes 2359300
  91.1 24.1 %copy-start.7 = (f32[256,1536]{1,0:T(8,128)}, f32[256,1536]{1,0:T(8,128)S(1)}, u32[]{:S(2)}) copy-start(f32[256,1536]{1,0:T(8,128)S(1)} %get-tuple-element.917) | copy-start | bytes 4718596
  118.2 24.9 %copy-start.28 = (bf16[256,1536]{1,0:T(8,128)(2,1)}, bf16[256,1536]{1,0:T(8,128)(2,1)S(1)}, u32[]{:S(2)}) copy-start(bf16[256,1536]{1,0:T(8,128)(2,1)S(1)} %multiply_convert_fusion.2) | copy-start | bytes 2359300
  182.8 16.6 %copy-start.10 = (f32[256,1536]{1,0:T(8,128)S(1)}, f32[256,1536]{1,0:T(8,128)}, u32[]{:S(2)}) copy-start(f32[256,1536]{1,0:T(8,128)} %copy-done.9) | copy-start | bytes 4718596
  223.7 29.5 %copy-start.15 = (f32[256,1536]{1,0:T(8,128)S(1)}, f32[256,1536]{1,0:T(8,128)}, u32[]{:S(2)}) copy-start(f32[256,1536]{1,0:T(8,128)} %copy-done.14) | copy-start | bytes 4718596
  289.3 101.3 %copy-start.70 = (bf16[1536,384]{1,0:T(8,128)(2,1)S(1)}, bf16[1536,384]{1,0:T(8,128)(2,1)}, u32[]{:S(2)}) copy-start(bf16[1536,384]{1,0:T(8,128)(2,1)} %param.59) | copy-start | bytes 3538948
  393.7 15.7 %copy-start.11 = (f32[256,1536]{1,0:T(8,128)S(1)}, f32[256,1536]{1,0:T(8,128)}, u32[]{:S(2)}) copy-start(f32[256,1536]{1,0:T(8,128)} %copy-done.9) | copy-start | bytes 4718596
  393.7 15.8 %copy-start.96 = (f32[1536]{0:T(1024)S(1)}, f32[1536]{0:T(1024)}, u32[]{:S(2)}) copy-start(f32[1536]{0:T(1024)} %copy-done.95) | copy-start | bytes 18436
  393.7 15.8 %copy-start.123 = (f32[256]{0:T(256)S(1)}, f32[256]{0:T(256)}, u32[]{:S(2)}) copy-start(f32[256]{0:T(256)} %copy-done.122) | copy-start | bytes 3076
  412.5 27.9 %copy-start.16 = (f32[256,1536]{1,0:T(8,128)}, f32[256,1536]{1,0:T(8,128)S(1)}, u32[]{:S(2)}) copy-start(f32[256,1536]{1,0:T(8,128)S(1)} %fusion.54) | copy-start | bytes 4718596
  421.2 16.6 %copy-start.8 = (f32[256,1536]{1,0:T(8,128)S(1)}, f32[256,1536]{1,0:T(8,128)}, u32[]{:S(2)}) copy-start(f32[256,1536]{1,0:T(8,128)} %copy-done.7) | copy-start | bytes 4718596
  421.2 16.6 %copy-start.94 = (f32[1536]{0:T(1024)S(1)}, f32[1536]{0:T(1024)}, u32[]{:S(2)}) copy-start(f32[1536]{0:T(1024)} %copy-done.93) | copy-start | bytes 18436
  421.2 16.6 %copy-start.121 = (f32[256]{0:T(256)S(1)}, f32[256]{0:T(256)}, u32[]{:S(2)}) copy-start(f32[256]{0:T(256)} %copy-done.120) | copy-start | bytes 3076
  464.2 15.8 %copy-start.4 = (f32[259,768]{1,0:T(8,128)S(1)}, f32[259,768]{1,0:T(8,128)}, u32[]{:S(2)}) copy-start(f32[259,768]{1,0:T(8,128)} %copy-done.3) | copy-start | bytes 2386948
  464.2 15.8 %copy-start.71 = (f32[256,768]{1,0:T(8,128)S(1)}, f32[256,768]{1,0:T(8,128)}, u32[]{:S(2)}) copy-start(f32[256,768]{1,0:T(8,128)} %get-tuple-element.958) | copy-start | bytes 2359300
  464.2 15.8 %copy-start.105 = (f32[768]{0:T(1024)S(1)}, f32[768]{0:T(1024)}, u32[]{:S(2)}) copy-start(f32[768]{0:T(1024)} %copy-done.104) | copy-start | bytes 9220
  464.2 15.8 %copy-start.107 = (f32[768]{0:T(1024)S(1)}, f32[768]{0:T(1024)}, u32[]{:S(2)}) copy-start(f32[768]{0:T(1024)} %copy-done.106) | copy-start | bytes 9220
  464.2 15.8 %copy-start.109 = (f32[768]{0:T(1024)S(1)}, f32[768]{0:T(1024)}, u32[]{:S(2)}) copy-start(f32[768]{0:T(1024)} %copy-done.108) | copy-start | bytes 9220
  464.3 15.8 %copy-start.111 = (f32[768]{0:T(1024)S(1)}, f32[768]{0:T(1024)}, u32[]{:S(2)}) copy-start(f32[768]{0:T(1024)} %copy-done.110) | copy-start | bytes 9220
  464.3 15.8 %copy-start.116 = (f32[768]{0:T(1024)S(1)}, f32[768]{0:T(1024)}, u32[]{:S(2)}) copy-start(f32[768]{0:T(1024)} %copy-done.115) | copy-start | bytes 9220
  464.3 15.8 %copy-start.130 = (f32[256]{0:T(256)S(1)}, f32[256]{0:T(256)}, u32[]{:S(2)}) copy-start(f32[256]{0:T(256)} %copy-done.129) | copy-start | bytes 3076
  464.3 15.8 %copy-start.132 = (f32[256]{0:T(256)S(1)}, f32[256]{0:T(256)}, u32[]{:S(2)}) copy-start(f32[256]{0:T(256)} %copy-done.131) | copy-start | bytes 3076
  464.3 15.8 %copy-start.134 = (f32[256]{0:T(256)S(1)}, f32[256]{0:T(256)}, u32[]{:S(2)}) copy-start(f32[256]{0:T(256)} %copy-done.133) | copy-start | bytes 3076
  529.3 38.3 %collective-permute-start.1 = (f32[3,768]{1,0:T(4,128)}, f32[3,768]{1,0:T(4,128)}, u32[]{:S(2)}, u32[]{:S(2)}) collective-permute-start(f32[3,768]{1,0:T(4,128)} %slice.240), channel_id=1, source_target_pairs={{4,0},{8,4},{12,8},{16,12},{20,16},{24,20},{28,24},{5,1},{9,5},{13... | collective-permute-start | bytes 27656 | tf_op jit(solution)/shard_map/ppermute | solution.py:31
  (139 other events, 507.4 us)

commit v3 on v2

--- a/solution.py
+++ b/solution.py
@@ -72,6 +72,14 @@
         recv_sem=recv_sem,
         device_id=peer,
         device_id_type=MESH,
+    )
+
+
+def lasting(microseconds):
+    return pl.CostEstimate(
+        flops=int(microseconds * 1e3),
+        bytes_accessed=int(microseconds * 1e3),
+        transcendentals=0,
     )
 
 
@@ -145,6 +153,7 @@
         scratch_shapes=[pltpu.VMEM((half, width), wire)] * 4
         + [pltpu.SemaphoreType.DMA((3, pieces))] * 2,
         compiler_params=talking(number),
+        cost_estimate=lasting(6 + values.size // 40000),
         name="head_sum",
     )(values)
 
@@ -193,6 +202,7 @@
         out_specs=VMEM,
         scratch_shapes=[pltpu.SemaphoreType.DMA((pairs,))] * 4 + [pltpu.SemaphoreType.DMA],
         compiler_params=talking(number),
+        cost_estimate=lasting(20),
         name="seq_gather",
     )(block)
     return out.reshape(seq_count * rows, width)
@@ -300,6 +310,7 @@
         + [pltpu.SemaphoreType.DMA((count,))] * 3
         + [pltpu.SemaphoreType.DMA((count, pairs - 1))] * 2,
         compiler_params=talking(number),
+        cost_estimate=lasting(15 + sum(a.size for a in arrays) // 50000),
         name="seq_scatter",
     )(*blocks)
 
@@ -376,6 +387,7 @@
             pltpu.SemaphoreType.DMA((seq_count - 1,)),
         ],
         compiler_params=talking(number),
+        cost_estimate=lasting(16),
         name="run_summary",
     )(steps, drives, coefficients, slopes)
 
@@ -427,6 +439,7 @@
             fixed,
         ),
         compiler_params=pltpu.CompilerParams(vmem_limit_bytes=LIMIT),
+        cost_estimate=lasting(11),
         name="state_sweep",
     )(initial, steps, drives, inject, readout, slopes)
 
@@ -520,8 +533,181 @@
         out_specs=(row_spec, row_spec, entry_spec, entry_spec, fixed),
         scratch_shapes=[pltpu.VMEM((entries, width), jnp.float32)] * 2,
         compiler_params=pltpu.CompilerParams(vmem_limit_bytes=LIMIT),
+        cost_estimate=lasting(15),
         name="adjoint_sweep",
     )(incoming, last_state, befores, steps, drives, inject, readout, upstream, slopes)
+
+
+def over_rows(left, right):
+    return lax.dot_general(left, right, (((0,), (0,)), ((), ())), preferred_element_type=jnp.float32)
+
+
+def over_columns(left, right):
+    return lax.dot_general(left, right, (((1,), (1,)), ((), ())), preferred_element_type=jnp.float32)
+
+
+def stand_up(rows, target, shared_heads):
+    count, width = rows.shape
+    heads = width // HEAD_DIM
+    group = heads // shared_heads
+    turned = rows.astype(jnp.float32).T.astype(target.dtype)
+    target[...] = jnp.zeros_like(target)
+    for head in range(heads):
+        shared = head // group
+        target[shared * HEAD_DIM : (shared + 1) * HEAD_DIM, head * count : (head + 1) * count] = (
+            turned[head * HEAD_DIM : (head + 1) * HEAD_DIM]
+        )
+
+
+def lie_down(upright, count, shared_heads):
+    heads = upright.shape[1] // count
+    group = heads // shared_heads
+    blocks = []
+    for head in range(heads):
+        shared = head // group
+        blocks.append(
+            upright[
+                shared * HEAD_DIM : (shared + 1) * HEAD_DIM, head * count : (head + 1) * count
+            ]
+        )
+    return jnp.concatenate(blocks, axis=0).T
+
+
+def hidden_bias(key_docs, query_docs, diagonal):
+    key_count, query_count = key_docs.shape[0], query_docs.shape[1]
+    shape = (key_count, query_count)
+    earlier = lax.broadcasted_iota(jnp.int32, shape, 0) <= lax.broadcasted_iota(
+        jnp.int32, shape, 1
+    )
+    bias = jnp.where(key_docs == query_docs, 0.0, masked_score)
+    return jnp.where(jnp.logical_or(earlier, jnp.logical_not(diagonal)), bias, masked_score)
+
+
+def attend(own, queries, both_rows, key_docs, query_docs):
+    rows, width = queries.shape
+    key_width = both_rows.shape[1] // 2
+    shared_heads = key_width // HEAD_DIM
+    heads = width // HEAD_DIM
+    scale = 0.125 * LOG2E
+
+    def kernel(own_ref, q_ref, kv_ref, kd_ref, qd_ref, low_ref, att_ref, lse_ref, qt_ref, max_ref, sum_ref):
+        stand_up(q_ref[...], qt_ref, shared_heads)
+        me = own_ref[0]
+
+        def block(step, first):
+            begin = pl.multiple_of((me - step) * rows, rows)
+            keys = kv_ref[pl.ds(begin, rows), :key_width]
+            values = kv_ref[pl.ds(begin, rows), key_width:]
+            bias = hidden_bias(kd_ref[pl.ds(begin, rows), :], qd_ref[...], step == 0)
+            for head in range(heads):
+                columns = slice(head * rows, (head + 1) * rows)
+                scores = product(keys, qt_ref[:, columns]) * scale + bias
+                top = jnp.max(scores, axis=0, keepdims=True)
+                if not first:
+                    old = max_ref[:, columns]
+                    top = jnp.maximum(top, old)
+                weights = jnp.exp2(scores - top)
+                total = jnp.sum(weights, axis=0, keepdims=True)
+                weighted = over_rows(values, to_low(weights))
+                if not first:
+                    factor = jnp.exp2(old - top)
+                    total = total + sum_ref[:, columns] * factor
+                    weighted = weighted + att_ref[:, columns] * factor
+                max_ref[:, columns] = top
+                sum_ref[:, columns] = total
+                att_ref[:, columns] = weighted
+
+        block(0, True)
+
+        @pl.loop(1, me + 1)
+        def earlier(step):
+            block(step, False)
+
+        att_ref[...] = att_ref[...] / sum_ref[...]
+        lse_ref[...] = max_ref[...] + jnp.log2(sum_ref[...])
+        low_ref[...] = to_low(lie_down(att_ref, rows, shared_heads))
+
+    return pl.pallas_call(
+        kernel,
+        out_shape=(
+            jax.ShapeDtypeStruct((rows, width), jnp.bfloat16),
+            jax.ShapeDtypeStruct((key_width, heads * rows), jnp.float32),
+            jax.ShapeDtypeStruct((1, heads * rows), jnp.float32),
+        ),
+        in_specs=[pl.BlockSpec(memory_space=pltpu.SMEM)] + [VMEM] * 4,
+        out_specs=(VMEM,) * 3,
+        scratch_shapes=[
+            pltpu.VMEM((key_width, heads * rows), jnp.bfloat16),
+            pltpu.VMEM((1, heads * rows), jnp.float32),
+            pltpu.VMEM((1, heads * rows), jnp.float32),
+        ],
+        compiler_params=pltpu.CompilerParams(vmem_limit_bytes=LIMIT),
+        cost_estimate=lasting(12),
+        name="attend",
+    )(own, queries, both_rows, key_docs, query_docs)
+
+
+def attend_back(own, queries, upstream, both_rows, key_docs, query_docs, attended, log_sum):
+    rows, width = queries.shape
+    total_rows = both_rows.shape[0]
+    key_width = both_rows.shape[1] // 2
+    shared_heads = key_width // HEAD_DIM
+    heads = width // HEAD_DIM
+    scale = 0.125 * LOG2E
+
+    def kernel(
+        own_ref, q_ref, up_ref, kv_ref, kd_ref, qd_ref, att_ref, lse_ref, qg_ref, kvg_ref, qt_ref, ut_ref, acc_ref
+    ):
+        stand_up(q_ref[...], qt_ref, shared_heads)
+        stand_up(up_ref[...], ut_ref, shared_heads)
+        me = own_ref[0]
+        delta = jnp.sum(ut_ref[...].astype(jnp.float32) * att_ref[...], axis=0, keepdims=True)
+        acc_ref[...] = jnp.zeros_like(acc_ref)
+
+        @pl.loop(me + 1, total_rows // rows)
+        def later(position):
+            begin = pl.multiple_of(position * rows, rows)
+            kvg_ref[pl.ds(begin, rows), :] = jnp.zeros((rows, 2 * key_width), jnp.bfloat16)
+
+        @pl.loop(0, me + 1)
+        def block(position):
+            begin = pl.multiple_of(position * rows, rows)
+            keys = kv_ref[pl.ds(begin, rows), :key_width]
+            values = kv_ref[pl.ds(begin, rows), key_width:]
+            bias = hidden_bias(kd_ref[pl.ds(begin, rows), :], qd_ref[...], position == me)
+            key_grad = jnp.zeros((rows, key_width), jnp.float32)
+            value_grad = jnp.zeros((rows, key_width), jnp.float32)
+            for head in range(heads):
+                columns = slice(head * rows, (head + 1) * rows)
+                query = qt_ref[:, columns]
+                upper = ut_ref[:, columns]
+                probs = jnp.exp2(product(keys, query) * scale + bias - lse_ref[:, columns])
+                value_grad = value_grad + over_columns(to_low(probs), upper)
+                score_grad = to_low(probs * (product(values, upper) - delta[:, columns]))
+                key_grad = key_grad + over_columns(score_grad, query)
+                acc_ref[:, columns] += over_rows(keys, score_grad)
+            kvg_ref[pl.ds(begin, rows), :key_width] = to_low(key_grad * 0.125)
+            kvg_ref[pl.ds(begin, rows), key_width:] = to_low(value_grad)
+
+        qg_ref[...] = to_low(lie_down(acc_ref, rows, shared_heads) * 0.125)
+
+    return pl.pallas_call(
+        kernel,
+        out_shape=(
+            jax.ShapeDtypeStruct((rows, width), jnp.bfloat16),
+            jax.ShapeDtypeStruct((total_rows, 2 * key_width), jnp.bfloat16),
+        ),
+        in_specs=[pl.BlockSpec(memory_space=pltpu.SMEM)] + [VMEM] * 7,
+        out_specs=(VMEM,) * 2,
+        scratch_shapes=[
+            pltpu.VMEM((key_width, heads * rows), jnp.bfloat16),
+            pltpu.VMEM((key_width, heads * rows), jnp.bfloat16),
+            pltpu.VMEM((key_width, heads * rows), jnp.float32),
+        ],
+        compiler_params=pltpu.CompilerParams(vmem_limit_bytes=LIMIT),
+        cost_estimate=lasting(20),
+        name="attend_back",
+    )(own, queries, upstream, both_rows, key_docs, query_docs, attended, log_sum)
 
 
 def body(
@@ -562,9 +748,70 @@
     first_row = lax.axis_index("seq") * row_count
     last_row = first_row + row_count - 1
 
-    def by_model_rows(pattern, left, right):
-        blocks = to_low(jnp.einsum(pattern, left, right, preferred_element_type=jnp.float32))
-        return blocks.transpose(1, 0, 2).reshape(blocks.shape[1], -1)
+    me = lax.axis_index("seq")
+    bit_count = seq_count.bit_length() - 1
+    across_first = [0] + list(range(1, bit_count))
+    along_first = [1, 0] + list(range(2, bit_count))
+
+    def by_owner(values, bits):
+        turned = values.transpose(0, 2, 1)
+        own_rows = turned.shape[1] // seq_count
+        order = [0]
+        for bit in reversed(bits):
+            order = order + [j + (1 << bit) for j in order]
+        blocks = []
+        for j in order:
+            owner = me
+            for bit in range(bit_count):
+                if j >> bit & 1:
+                    owner = owner + (1 << bit) * (1 - 2 * ((owner >> bit) & 1))
+            blocks.append(lax.dynamic_slice_in_dim(turned, owner * own_rows, own_rows, 1))
+        parts = []
+        while len(blocks) > 1:
+            half = len(blocks) // 2
+            parts.append(jnp.concatenate(blocks[half:], axis=1) if half > 1 else blocks[half])
+            blocks = blocks[:half]
+        return parts + blocks, bits
+
+    def begin_sum(rows, columns):
+        flow = {"rows": rows[0], "bits": rows[1], "columns": columns, "got": []}
+        settle(flow)
+        return flow
+
+    def settle(flow):
+        step = len(flow["got"])
+        part = flow["rows"][step]
+        total = jnp.einsum(
+            "bdt,btf->bdf", part, flow["columns"], preferred_element_type=jnp.float32
+        )
+        first = part.shape[1] if step < len(flow["bits"]) else 0
+        for got in flow["got"]:
+            total = total + got[:, first : first + part.shape[1]].astype(jnp.float32)
+        if step == len(flow["bits"]):
+            flow["total"] = total
+            return
+        bit = flow["bits"][step]
+        route = [(i, i ^ (1 << bit)) for i in range(seq_count)]
+        flow["got"].append(lax.ppermute(to_low(total), "seq", route))
+
+    def hold(values, *flows):
+        if flows:
+            tied = lax.optimization_barrier((values, *[flow["got"][-1] for flow in flows]))
+            values = tied[0]
+            for flow, got in zip(flows, tied[1:], strict=True):
+                flow["got"][-1] = got
+        return values
+
+    def after(values, *flows):
+        values = hold(values, *flows)
+        for flow in flows:
+            settle(flow)
+        return values
+
+    def finished(flow):
+        while "total" not in flow:
+            settle(flow)
+        return flow["total"]
 
     def branch_sum(values):
         return head_sum(values, next(numbers), jnp.bfloat16, 4)
@@ -629,72 +876,12 @@
     queries = to_low(product(normed_three, attn_query))
     key_rows = to_low(product(normed_three, attn_key))
     value_rows = to_low(product(normed_three, attn_value))
-    shared_heads = attn_key.shape[1] // HEAD_DIM
-    group_size = attn_query.shape[1] // attn_key.shape[1]
-    query_heads = queries.reshape(row_count, shared_heads, group_size, HEAD_DIM)
-    query_pos = first_row + jnp.arange(row_count, dtype=jnp.int32)
-
-    def visible(offset, block_rows):
-        key_pos = offset + jnp.arange(block_rows, dtype=jnp.int32)
-        key_docs = lax.dynamic_slice_in_dim(document_ids, offset, block_rows)
-        return (key_pos[None, :] <= query_pos[:, None]) & (key_docs[None, :] == local_docs[:, None])
-
-    def split_blocks(pieces, begin_row):
-        key_piece, value_piece = pieces
-        piece_rows = key_piece.shape[0]
-        block_rows = math.gcd(piece_rows, 512)
-        block_count = piece_rows // block_rows
-        key_blocks = key_piece.reshape(block_count, block_rows, shared_heads, HEAD_DIM)
-        value_blocks = value_piece.reshape(block_count, block_rows, shared_heads, HEAD_DIM)
-        offsets = begin_row + block_rows * jnp.arange(block_count, dtype=jnp.int32)
-        return (block_rows, (key_blocks, value_blocks, offsets))
-
     both_rows = seq_gather(jnp.concatenate([key_rows, value_rows], axis=1), next(numbers))
     key_width = key_rows.shape[1]
-    gathered = (both_rows[:, :key_width], both_rows[:, key_width:])
-    start_max = jnp.full((shared_heads, group_size, row_count), masked_score, jnp.float32)
-    block_rows, blocked = split_blocks(
-        gathered,
-        jnp.int32(0),
-    )
-
-    def visit_block(running, element):
-        key_block, value_block, offset = element
-
-        def compute(current):
-            row_max, row_sum, weighted = current
-            scores = (
-                jnp.einsum(
-                    "qgrd,kgd->grqk", query_heads, key_block, preferred_element_type=jnp.float32
-                )
-                * 0.125
-            )
-            allowed = visible(offset, block_rows)
-            masked = jnp.where(allowed, scores, masked_score)
-            new_max = jnp.maximum(row_max, jnp.max(masked, axis=-1))
-            weights = jnp.where(allowed, jnp.exp(masked - new_max[..., None]), 0.0)
-            factor = jnp.exp(row_max - new_max)
-            row_sum = row_sum * factor + jnp.sum(weights, axis=-1)
-            weighted = weighted * factor[..., None] + jnp.einsum(
-                "grqk,kgd->grqd", to_low(weights), value_block, preferred_element_type=jnp.float32
-            )
-            return (new_max, row_sum, weighted)
-
-        return (lax.cond(offset <= last_row, compute, lambda untouched: untouched, running), None)
-
-    result, unused_out = lax.scan(
-        visit_block,
-        (
-            start_max,
-            jnp.zeros_like(start_max),
-            jnp.zeros((shared_heads, group_size, row_count, HEAD_DIM), jnp.float32),
-        ),
-        blocked,
-    )
-    folded = result
-    attended = folded[2] / folded[1][..., None]
-    log_sum = folded[0] + jnp.log(folded[1])
-    attended_low = to_low(attended.transpose(2, 0, 1, 3).reshape(row_count, -1))
+    own_place = lax.axis_index("seq").reshape(1)
+    key_docs = document_ids[:, None]
+    query_docs = local_docs[None, :]
+    attended_low, attended, log_sum = attend(own_place, queries, both_rows, key_docs, query_docs)
     hidden_three = hidden_two + branch_sum(product(attended_low, attn_output))
     gain_moe = norm_moe.astype(jnp.float32)
     normed_four = to_low(rms_scale(hidden_three, gain_moe))
@@ -746,9 +933,9 @@
     ).astype(jnp.float32)
     gating_grad = to_low(act_back * up_four * silu_slope(gate_four))
     upward_grad = to_low(act_back * jax.nn.silu(gate_four))
-    grad_expert_down = by_model_rows("ecd,ecf->edf", res_grad, expert_act)
-    grad_expert_gate = by_model_rows("ecd,ecf->edf", expert_in, gating_grad)
-    grad_expert_up = by_model_rows("ecd,ecf->edf", expert_in, upward_grad)
+    flow_expert_down = begin_sum(by_owner(res_grad, along_first), expert_act)
+    expert_rows = by_owner(expert_in, across_first)
+    flow_expert_in = begin_sum(expert_rows, jnp.concatenate([gating_grad, upward_grad], axis=2))
     slot_grads = (
         jnp.einsum("ecf,edf->ecd", gating_grad, expert_gate, preferred_element_type=jnp.float32)
         + jnp.einsum("ecf,edf->ecd", upward_grad, expert_up, preferred_element_type=jnp.float32)
@@ -770,109 +957,65 @@
     hidden_grad, grad_norm_moe = rms_back(hidden_three, gain_moe, normed_grad)
     three_grad = upstream + hidden_grad
     branch_grad = to_low(three_grad)
-    grad_attn_output = to_low(product(branch_grad.T, attended_low))
+    flow_attn_output = begin_sum(by_owner(branch_grad[None], across_first), attended_low[None])
     attended_grad = to_low(product(branch_grad, attn_output.T))
-    out_heads = attended_grad.reshape(row_count, shared_heads, group_size, HEAD_DIM).transpose(
-        1, 2, 0, 3
-    )
-    delta = jnp.sum(out_heads.astype(jnp.float32) * attended, axis=-1)
-    initial = (
-        jnp.zeros((shared_heads, group_size, row_count, HEAD_DIM), jnp.float32),
-        jnp.zeros((total_rows, key_width), jnp.float32),
-        jnp.zeros((total_rows, key_width), jnp.float32),
-    )
-    attend_block_rows, blocked = split_blocks(
-        gathered,
-        jnp.int32(0),
-    )
-
-    def visit_back(running, element):
-        key_block, value_block, offset = element
-
-        def compute(current):
-            query_acc, key_acc, value_acc = current
-            scores = (
-                jnp.einsum(
-                    "qgrd,kgd->grqk", query_heads, key_block, preferred_element_type=jnp.float32
-                )
-                * 0.125
-            )
-            allowed = visible(offset, attend_block_rows)
-            probs = jnp.where(allowed, jnp.exp(scores - log_sum[..., None]), 0.0)
-            value_part = jnp.einsum(
-                "grqk,grqd->kgd", to_low(probs), out_heads, preferred_element_type=jnp.float32
-            )
-            prob_grad = jnp.einsum(
-                "grqd,kgd->grqk", out_heads, value_block, preferred_element_type=jnp.float32
-            )
-            score_grad = to_low(probs * (prob_grad - delta[..., None]))
-            query_acc = (
-                query_acc
-                + jnp.einsum(
-                    "grqk,kgd->grqd", score_grad, key_block, preferred_element_type=jnp.float32
-                )
-                * 0.125
-            )
-            key_part = (
-                jnp.einsum(
-                    "grqk,qgrd->kgd", score_grad, query_heads, preferred_element_type=jnp.float32
-                )
-                * 0.125
-            )
-            key_acc = lax.dynamic_update_slice_in_dim(
-                key_acc,
-                lax.dynamic_slice_in_dim(key_acc, offset, attend_block_rows, 0)
-                + key_part.reshape(attend_block_rows, -1),
-                offset,
-                0,
-            )
-            value_acc = lax.dynamic_update_slice_in_dim(
-                value_acc,
-                lax.dynamic_slice_in_dim(value_acc, offset, attend_block_rows, 0)
-                + value_part.reshape(attend_block_rows, -1),
-                offset,
-                0,
-            )
-            return (query_acc, key_acc, value_acc)
-
-        return (lax.cond(offset <= last_row, compute, lambda untouched: untouched, running), None)
-
-    result, unused_out = lax.scan(visit_back, initial, blocked)
-    query_acc, key_acc, value_acc = result
-    (both_sums,) = seq_scatter(
-        [to_low(jnp.concatenate([key_acc, value_acc], axis=1))], next(numbers)
-    )
+    attended_grad = after(attended_grad, flow_expert_down)
+    query_grad, both_grads = attend_back(
+        own_place, queries, attended_grad, both_rows, key_docs, query_docs, attended, log_sum
+    )
+    both_grads = after(
+        both_grads,
+        flow_expert_in,
+    )
+    (both_sums,) = seq_scatter([both_grads], next(numbers))
     key_sum, value_sum = both_sums[:, :key_width], both_sums[:, key_width:]
-    query_grad = to_low(query_acc.transpose(2, 0, 1, 3).reshape(row_count, -1))
     key_grad = to_low(key_sum)
     value_grad = to_low(value_sum)
-    grad_attn_in = to_low(
-        product(normed_three.T, jnp.concatenate([query_grad, key_grad, value_grad], axis=1))
-    )
-    normed_grad = branch_sum(
+    flow_attn_in = begin_sum(
+        by_owner(normed_three[None], across_first),
+        jnp.concatenate([query_grad, key_grad, value_grad], axis=1)[None],
+    )
+    normed_part = (
         product(query_grad, attn_query.T)
         + product(key_grad, attn_key.T)
         + product(value_grad, attn_value.T)
     )
+    normed_part = after(normed_part, flow_expert_down, flow_attn_output)
+    normed_grad = branch_sum(normed_part)
     hidden_grad, grad_norm_attn = rms_back(hidden_two, gain_attn, normed_grad)
     two_grad = three_grad + hidden_grad
     branch_grad = to_low(two_grad)
-    grad_ffn_down = to_low(product(branch_grad.T, ffn_act))
+    flow_ffn_down = begin_sum(by_owner(branch_grad[None], along_first), ffn_act[None])
     ffn_back = to_low(product(branch_grad, ffn_down.T)).astype(jnp.float32)
     feed_gate_grad = to_low(ffn_back * up_two * silu_slope(gate_two))
     feed_up_grad = to_low(ffn_back * jax.nn.silu(gate_two))
-    grad_ffn_gate = to_low(product(normed_two.T, feed_gate_grad))
-    grad_ffn_up = to_low(product(normed_two.T, feed_up_grad))
-    normed_grad = branch_sum(product(feed_gate_grad, ffn_gate.T) + product(feed_up_grad, ffn_up.T))
+    feed_rows = by_owner(normed_two[None], across_first)
+    flow_ffn_in = begin_sum(
+        feed_rows, jnp.concatenate([feed_gate_grad, feed_up_grad], axis=1)[None]
+    )
+    normed_part = product(feed_gate_grad, ffn_gate.T) + product(feed_up_grad, ffn_up.T)
+    normed_part = after(
+        normed_part, flow_expert_in, flow_expert_down, flow_attn_in, flow_attn_output
+    )
+    normed_grad = branch_sum(normed_part)
     hidden_grad, grad_norm_ffn = rms_back(hidden_one, gain_ffn, normed_grad)
     one_grad = two_grad + hidden_grad
     branch_grad = to_low(one_grad)
-    grad_mixer_out = to_low(product(branch_grad.T, gated))
+    mixer_out_rows = by_owner(branch_grad[None], across_first)
     gated_grad = to_low(product(branch_grad, mixer_out.T)).astype(jnp.float32)
     scan_grad = gated_grad * gate_act
     gate_in_grad = to_low(gated_grad * mixed_state * silu_slope(gate_in))
     grad_skip_gain = jnp.sum(scan_grad * activated, axis=0)
+    scan_grad = hold(
+        scan_grad, flow_expert_in, flow_attn_in, flow_attn_output, flow_ffn_down, flow_ffn_in
+    )
     state_after = run_summary(steps, scan_grad, readout_wide, slopes, next(numbers), False)
+    state_after, gated_late, gate_grad_late = lax.optimization_barrier(
+        (state_after, gated, gate_in_grad)
+    )
+    state_after = after(state_after, flow_attn_in, flow_ffn_down, flow_ffn_in)
+    flow_mixer_out = begin_sum(mixer_out_rows, gated_late[None])
+    flow_mixer_gate = begin_sum(by_owner(normed_one[None], across_first), gate_grad_late[None])
     through_sum, injected, inject_part, readout_part, rate_sum = adjoint_sweep(
         state_after,
         state_out,
@@ -894,6 +1037,7 @@
     pre_low = to_low(pre_grad)
     grad_step_proj = product(step_low.T, pre_low)
     proj_part = jnp.concatenate([product(pre_low, step_proj.T), inject_grad, readout_grad], axis=1)
+    proj_part = after(proj_part, flow_attn_in, flow_ffn_down)
     proj_low = to_low(head_sum(proj_part, next(numbers), jnp.float32, 1))
     grad_state_proj = product(act_low.T, proj_low)
     act_total = input_grad + skipping * scan_grad + product(proj_low, state_proj.T)
@@ -914,8 +1058,9 @@
     grad_conv_taps = jnp.stack(tap_rows)
     conv_low = to_low(conv_in_grad)
     grad_mixer_inner = to_low(product(normed_one.T, conv_low))
-    grad_mixer_gate = to_low(product(normed_one.T, gate_in_grad))
-    normed_grad = branch_sum(product(conv_low, mixer_inner.T) + product(gate_in_grad, mixer_gate.T))
+    normed_part = product(conv_low, mixer_inner.T) + product(gate_in_grad, mixer_gate.T)
+    normed_part = after(normed_part, flow_ffn_in, flow_mixer_out)
+    normed_grad = branch_sum(normed_part)
     hidden_grad, grad_norm_mixer = rms_back(tokens, gain_mixer, normed_grad)
     grad_tokens = one_grad + hidden_grad
     own_channels = grad_conv_bias.shape[0] // seq_count
@@ -943,36 +1088,17 @@
     )
     spare = -packed.shape[1] % (16 * LANES)
     packed = to_low(jnp.pad(packed, ((0, 0), (0, spare)))).reshape(-1, LANES)
-    (
-        sum_expert_gate,
-        sum_expert_up,
-        sum_expert_down,
-        sum_ffn_gate,
-        sum_ffn_up,
-        sum_ffn_down,
-        sum_attn_in,
-        sum_attn_output,
-        sum_mixer_out,
-        sum_mixer_inner,
-        sum_mixer_gate,
-        sum_packed,
-    ) = seq_scatter(
-        [
-            grad_expert_gate,
-            grad_expert_up,
-            grad_expert_down,
-            grad_ffn_gate,
-            grad_ffn_up,
-            grad_ffn_down,
-            grad_attn_in,
-            grad_attn_output,
-            grad_mixer_out,
-            grad_mixer_inner,
-            grad_mixer_gate,
-            packed,
-        ],
+    packed = after(packed, flow_mixer_gate, flow_mixer_out, flow_ffn_in)
+    inner_half = grad_mixer_inner.shape[1] // 2
+    first_inner, second_inner, sum_packed = seq_scatter(
+        [grad_mixer_inner[:, :inner_half], grad_mixer_inner[:, inner_half:], packed],
         next(numbers),
     )
+    sum_attn_in = finished(flow_attn_in)[0]
+    sum_ffn_in = finished(flow_ffn_in)[0]
+    sum_expert_in = finished(flow_expert_in)
+    expert_width = expert_gate.shape[2]
+    feed_width = ffn_gate.shape[1]
     sum_packed = sum_packed.reshape(-1)
     own_rows = model_width // seq_count
     taken = itertools.accumulate(
@@ -986,15 +1112,12 @@
     pieces = [sum_packed[low:high] for low, high in itertools.pairwise(bounds)]
     query_width = attn_query.shape[1]
 
-    def by_expert(values):
-        return values.reshape(values.shape[0], expert_count, -1)
-
     return (
         mixed_out,
         grad_tokens,
         pieces[0],
-        sum_mixer_inner,
-        sum_mixer_gate,
+        jnp.concatenate([first_inner, second_inner], axis=1),
+        finished(flow_mixer_gate)[0],
         pieces[5].reshape(own_channels, -1).T,
         pieces[6],
         pieces[7].reshape(own_channels, -1),
@@ -1002,21 +1125,21 @@
         pieces[9],
         pieces[10].reshape(own_channels, -1),
         pieces[11],
-        sum_mixer_out.T,
+        finished(flow_mixer_out)[0].T,
         pieces[1],
-        sum_ffn_gate,
-        sum_ffn_up,
-        sum_ffn_down.T,
+        sum_ffn_in[:, :feed_width],
+        sum_ffn_in[:, feed_width:],
+        finished(flow_ffn_down)[0].T,
         pieces[2],
         sum_attn_in[:, :query_width],
         sum_attn_in[:, query_width : query_width + key_width],
         sum_attn_in[:, query_width + key_width :],
-        sum_attn_output.T,
+        finished(flow_attn_output)[0].T,
         pieces[3],
         pieces[4].reshape(own_rows, -1),
-        by_expert(sum_expert_gate).transpose(1, 0, 2),
-        by_expert(sum_expert_up).transpose(1, 0, 2),
-        by_expert(sum_expert_down).transpose(1, 2, 0),
+        sum_expert_in[:, :, :expert_width],
+        sum_expert_in[:, :, expert_width:],
+        finished(flow_expert_down).transpose(0, 2, 1),
     )
 
 

time: 994 us -> 762 us (0.77)
  Pallas kernels: 691 us -> 347 us
  waiting for transfers between devices: 0.01 us -> 71.9 us
  local copies, waits for them, and re-layouts: 118 us -> 75.5 us
  starting transfers between devices: 6.14 us -> 47.1 us
  matrix products: 102 us -> 132 us
  other arithmetic: 56.2 us -> 78.3 us
    pallas_call x2, Pallas kernels: 463 us -> 112 us  [seq_scatter(): pl.pallas_call(kernel, out_shape=[jax.ShapeDtypeStruct(shape, jnp.float32...]
    ppermute x0 -> x24, waiting for transfers between devices: none -> 66.1 us  [settle(): flow['got'].append(lax.ppermute(to_low(total), 'seq', route))]
    dot_general x10 -> x32, matrix products: 19.8 us -> 73.5 us  [settle(): jnp.einsum('bdt,btf->bdf', part, flow['columns'], preferred_element_type=...]
    ppermute x0 -> x24, starting transfers between devices: none -> 40.1 us  [settle(): flow['got'].append(lax.ppermute(to_low(total), 'seq', route))]
    dot_general x39 -> x32, matrix products: 72.6 us -> 48.1 us  [product(): return jnp.dot(left, right, preferred_element_type=jnp.float32)]
    unnamed x350 -> x463, local copies, waits for them, and re-layouts: 36.7 us -> 18.1 us
    convert_element_type x5 -> x0, local copies, waits for them, and re-layouts: 14.9 us -> none  [to_low(): return values.astype(jnp.bfloat16)]
    another operation x12 -> x2, local copies, waits for them, and re-layouts: 16.3 us -> 1.83 us  [the longest x3 11.6 us: seq_scatter(): a.reshape(pairs, 2, shape[0], shape[1])]
  transfers between devices with their start and end apart: 2 -> 26, of which waited for: 0 -> 7; matrix products, arithmetic and copies ran while one was open for 4% -> 24% of each run, Pallas kernels for 0% -> 23%
where the time goes in v3:
time: 762 us; the launch traced here: 754 us
  Pallas kernels  347 us (46%)
  matrix products  132 us (17%)
  other arithmetic  78.3 us (10%)
  local copies, waits for them, and re-layouts  75.5 us (10%)
  waiting for transfers between devices  71.9 us (9%)
  starting transfers between devices  47.1 us (6%)
    pallas_call x9, Pallas kernels, head_sum(): pl.pallas_call(kernel, out_shape=jax.ShapeDtypeStruct((rows, width), jnp....  141 us
    pallas_call x2, Pallas kernels, seq_scatter(): pl.pallas_call(kernel, out_shape=[jax.ShapeDtypeStruct(shape, jnp.float32...  112 us
    dot_general x32, matrix products, settle(): jnp.einsum('bdt,btf->bdf', part, flow['columns'], preferred_element_type=...  73.5 us
    ppermute x24, waiting for transfers between devices, settle(): flow['got'].append(lax.ppermute(to_low(total), 'seq', route))  66.1 us
    dot_general x32, matrix products, product(): return jnp.dot(left, right, preferred_element_type=jnp.float32)  48.1 us
    ppermute x24, starting transfers between devices, settle(): flow['got'].append(lax.ppermute(to_low(total), 'seq', route))  40.1 us
    pallas_call x2, Pallas kernels, run_summary(): pl.pallas_call(kernel, out_shape=jax.ShapeDtypeStruct((entries, width), j...  32.8 us
    pallas_call x1, Pallas kernels, seq_gather(): pl.pallas_call(kernel, out_shape=jax.ShapeDtypeStruct((seq_count, rows, w...  24 us
  transfers between devices with their start and end apart: 26, of which 7 were waited for; matrix products, arithmetic and copies ran while one was open for 24% of the time, Pallas kernels for 23%

profile of v3, /device:TPU:0, one launch (start us, length us, event | category | flops | bytes accessed | tf_op | source)
XLA Modules:
  0.0 754.5 jit_solution(16714607605688723529)
XLA Ops:
  6.5 5.4 collective-permute-start
  32.3 8.1 %head_sum.9 = f32[256,128]{1,0:T(8,128)} custom-call(f32[256,128]{1,0:T(8,128)} %fusion.144.x_ref), custom_call_target="tpu_custom_call" | custom-call | flops 6000 | bytes 6000 | tf_op jit(solution)/shard_map/head_sum/pallas_call | solution.py:148
  46.6 16.9 %run_summary.2.init_ref = f32[16,768]{1,0:T(8,128)} custom-call(f32[256,768]{1,0:T(8,128)} %get-tuple-element.391.step_ref, f32[256,768]{1,0:T(8,128)} %get-tuple-element.390.drive_ref, f32[256,16,128]{2,1,0:T(8,128)} %broadcast_in_dim.69.coef_ref.inject_ref, f32[16,768]{1,0:T(8,128)} %bitcast_multiply_fusion.3.slope_ref), custom_call_target="tpu_custom_call" | custom-call | flops 16000 | bytes 16000 | tf_op jit(solution)/shard_map/run_summary/pallas_call | solution.py:378
  65.5 11.1 %state_sweep.1 = (f32[256,768]{1,0:T(8,128)}, f32[256,16,768]{2,1,0:T(8,128)}, f32[16,768]{1,0:T(8,128)}) custom-call(f32[16,768]{1,0:T(8,128)} %run_summary.2.init_ref, f32[256,768]{1,0:T(8,128)} %get-tuple-element.391.step_ref, f32[256,768]{1,0:T(8,128)} %get-tuple-element.390.drive_ref, f32[256,16,128]{2,1,0:T(8,128)} %broadcast_in_dim.69.coef_ref.inject_ref, ...), custom_call_target="tpu_custom_call" | custom-call | flops 11000 | bytes 11000 | tf_op jit(solution)/shard_map/state_sweep/pallas_call | solution.py:427
  76.6 3.7 multiply_convert_fusion.6
  83.6 15.8 %head_sum.10 = f32[256,1536]{1,0:T(8,128)} custom-call(f32[256,1536]{1,0:T(8,128)} %fusion.244.x_ref), custom_call_target="tpu_custom_call" | custom-call | flops 15000 | bytes 15000 | tf_op jit(solution)/shard_map/head_sum/pallas_call | solution.py:148
  108.8 16.5 %head_sum.11 = f32[256,1536]{1,0:T(8,128)} custom-call(f32[256,1536]{1,0:T(8,128)} %fusion.246.x_ref), custom_call_target="tpu_custom_call" | custom-call | flops 15000 | bytes 15000 | tf_op jit(solution)/shard_map/head_sum/pallas_call | solution.py:148
  129.9 24.0 %seq_gather.1 = bf16[8,256,256]{2,1,0:T(8,128)(2,1)} custom-call(bf16[256,256]{1,0:T(8,128)(2,1)} %pad_maximum_fusion.5.x_ref), custom_call_target="tpu_custom_call" | custom-call | flops 20000 | bytes 20000 | tf_op jit(solution)/shard_map/seq_gather/pallas_call | solution.py:198
  156.6 5.0 attend.1
  164.3 16.6 %head_sum.12 = f32[256,1536]{1,0:T(8,128)} custom-call(f32[256,1536]{1,0:T(8,128)} %fusion.247.x_ref), custom_call_target="tpu_custom_call" | custom-call | flops 15000 | bytes 15000 | tf_op jit(solution)/shard_map/head_sum/pallas_call | solution.py:148
  204.9 3.5 select_maximum_fusion.x_ref
  210.8 27.4 %head_sum.13 = f32[256,3200]{1,0:T(8,128)} custom-call(f32[256,3200]{1,0:T(8,128)} %select_maximum_fusion.x_ref), custom_call_target="tpu_custom_call" | custom-call | flops 26000 | bytes 26000 | tf_op jit(solution)/shard_map/head_sum/pallas_call | solution.py:148
  255.4 4.2 collective-permute-start.1
  280.5 14.1 %collective-permute-done.1 = bf16[4,768,256]{2,1,0:T(8,128)(2,1)} collective-permute-done((bf16[4,768,256]{2,1,0:T(8,128)(2,1)}, bf16[4,768,256]{2,1,0:T(8,128)(2,1)}, u32[]{:S(2)}, u32[]{:S(2)}) %collective-permute-start.1) | collective-permute-done | bytes 1572896 | tf_op jit(solution)/shard_map/ppermute | solution.py:795
  297.5 5.1 attend_back.1
  304.2 18.0 %collective-permute-done.2 = bf16[4,768,512]{2,1,0:T(8,128)(2,1)} collective-permute-done((bf16[4,768,512]{2,1,0:T(8,128)(2,1)}, bf16[4,768,512]{2,1,0:T(8,128)(2,1)}, u32[]{:S(2)}, u32[]{:S(2)}) %collective-permute-start.2) | collective-permute-done | bytes 3145760 | tf_op jit(solution)/shard_map/ppermute | solution.py:795
  322.1 62.7 %seq_scatter.2 = f32[256,256]{1,0:T(8,128)} custom-call(bf16[4,2,256,256]{3,2,1,0:T(8,128)(2,1)} %bitcast.547), custom_call_target="tpu_custom_call" | custom-call | flops 25000 | bytes 25000 | tf_op jit(solution)/shard_map/seq_scatter/pallas_call | solution.py:303
  401.7 3.5 add_convert_fusion.1
  407.3 16.0 %head_sum.14 = f32[256,1536]{1,0:T(8,128)} custom-call(f32[256,1536]{1,0:T(8,128)} %convolution_add_fusion.3.x_ref), custom_call_target="tpu_custom_call" | custom-call | flops 15000 | bytes 15000 | tf_op jit(solution)/shard_map/head_sum/pallas_call | solution.py:148
  426.0 3.9 fusion.233
  458.9 16.3 %head_sum.15 = f32[256,1536]{1,0:T(8,128)} custom-call(f32[256,1536]{1,0:T(8,128)} %convolution_add_fusion.x_ref), custom_call_target="tpu_custom_call" | custom-call | flops 15000 | bytes 15000 | tf_op jit(solution)/shard_map/head_sum/pallas_call | solution.py:148
  487.8 16.4 %collective-permute-done.12 = bf16[1,768,1024]{2,1,0:T(8,128)(2,1)} collective-permute-done((bf16[1,768,1024]{2,1,0:T(8,128)(2,1)}, bf16[1,768,1024]{2,1,0:T(8,128)(2,1)}, u32[]{:S(2)}, u32[]{:S(2)}) %collective-permute-start.12) | collective-permute-done | bytes 1572896 | tf_op jit(solution)/shard_map/ppermute | solution.py:795
  504.2 9.4 %collective-permute-done.10 = bf16[1,384,640]{2,1,0:T(8,128)(2,1)} collective-permute-done((bf16[1,384,640]{2,1,0:T(8,128)(2,1)}, bf16[1,384,640]{2,1,0:T(8,128)(2,1)}, u32[]{:S(2)}, u32[]{:S(2)}) %collective-permute-start.10) | collective-permute-done | bytes 491552 | tf_op jit(solution)/shard_map/ppermute | solution.py:795
  513.6 15.9 %run_summary.3.in_ref = f32[16,768]{1,0:T(8,128)} custom-call(f32[256,768]{1,0:T(8,128)} %get-tuple-element.391.step_ref, f32[256,768]{1,0:T(8,128)} %get-tuple-element.96.drive_ref.up_ref, f32[256,16,128]{2,1,0:T(8,128)} %broadcast_in_dim.70.read_ref.coef_ref, f32[16,768]{1,0:T(8,128)} %bitcast_multiply_fusion.3.slope_ref), custom_call_target="tpu_custom_call" | custom-call | flops 16000 | bytes 16000 | tf_op jit(solution)/shard_map/run_summary/pallas_call | solution.py:378
  529.6 15.4 %adjoint_sweep.1 = (f32[256,768]{1,0:T(8,128)}, f32[256,768]{1,0:T(8,128)}, f32[256,16,128]{2,1,0:T(8,128)}, f32[256,16,128]{2,1,0:T(8,128)}, f32[16,768]{1,0:T(8,128)}) custom-call(f32[16,768]{1,0:T(8,128)} %run_summary.3.in_ref, f32[16,768]{1,0:T(8,128)} %get-tuple-element.102.last_ref, f32[256,16,768]{2,1,0:T(8,128)} %get-tuple-element.103.before_ref, ...), custom_call_target="tpu_custom_call" | custom-call | flops 15000 | bytes 15000 | tf_op jit(solution)/shard_map/adjoint_sweep/pallas_call | solution.py:512
  570.1 3.4 fusion.2
  596.0 8.1 %head_sum.16 = f32[256,128]{1,0:T(8,128)} custom-call(f32[256,128]{1,0:T(8,128)} %pad_maximum_fusion.6.x_ref), custom_call_target="tpu_custom_call" | custom-call | flops 6000 | bytes 6000 | tf_op jit(solution)/shard_map/head_sum/pallas_call | solution.py:148
  614.8 5.8 collective-permute-done.16
  635.3 8.6 %collective-permute-start.21 = (bf16[1,192,2048]{2,1,0:T(8,128)(2,1)}, bf16[1,192,2048]{2,1,0:T(8,128)(2,1)}, u32[]{:S(2)}, u32[]{:S(2)}) collective-permute-start(bf16[1,192,2048]{2,1,0:T(8,128)(2,1)} %add_convert_fusion.2), channel_id=1, source_target_pairs={{0,16},{4,20},{8,24},{12,28},{16,0},{20,4},{24,8},{28,12},{1,17},{... | collective-permute-start | bytes 2359304 | tf_op jit(solution)/shard_map/ppermute | solution.py:795
  646.2 16.3 %head_sum.17 = f32[256,1536]{1,0:T(8,128)} custom-call(f32[256,1536]{1,0:T(8,128)} %convolution_add_fusion.2.x_ref), custom_call_target="tpu_custom_call" | custom-call | flops 15000 | bytes 15000 | tf_op jit(solution)/shard_map/head_sum/pallas_call | solution.py:148
  682.1 49.4 %seq_scatter.3 = (f32[192,384]{1,0:T(8,128)}, f32[192,384]{1,0:T(8,128)}, f32[208,128]{1,0:T(8,128)}) custom-call(bf16[4,2,192,384]{3,2,1,0:T(8,128)(2,1)} %bitcast.545, bf16[4,2,192,384]{3,2,1,0:T(8,128)(2,1)} %bitcast.544, bf16[4,2,208,128]{3,2,1,0:T(8,128)(2,1)} %bitcast.546), custom_call_target="tpu_custom_call" | custom-call | flops 42000 | bytes 42000 | tf_op jit(solution)/shard_map/seq_scatter/pallas_call | solution.py:303
  746.1 6.2 collective-permute-done.23
  (711 shorter events, 298.3 us)
Async XLA Ops:
  0.7 190.7 %copy-start = (bf16[4,256,1536]{2,1,0:T(8,128)(2,1)S(1)}, bf16[4,256,1536]{2,1,0:T(8,128)(2,1)}, u32[]{:S(2)}) copy-start(bf16[4,256,1536]{2,1,0:T(8,128)(2,1)} %param.59) | copy-start | bytes 9437188
  6.5 22.5 %collective-permute-start = (bf16[3,768]{1,0:T(4,128)(2,1)}, bf16[3,768]{1,0:T(4,128)(2,1)}, u32[]{:S(2)}, u32[]{:S(2)}) collective-permute-start(bf16[3,768]{1,0:T(4,128)(2,1)} %slice.399), channel_id=1, source_target_pairs={{0,4},{4,8},{8,12},{12,16},{16,20},{20,24},{24,28},{1,5},{5,9},{9,... | collective-permute-start | bytes 13832 | tf_op jit(solution)/shard_map/ppermute | solution.py:31
  27.7 48.8 %copy-start.213 = (f32[768]{0:T(1024)}, f32[768]{0:T(1024)S(1)}, u32[]{:S(2)}) copy-start(f32[768]{0:T(1024)S(1)} %convert_element_type.431) | copy-start | bytes 9220
  32.3 94.7 %copy-start.163 = (f32[1536]{0:T(1024)}, f32[1536]{0:T(1024)S(1)}, u32[]{:S(2)}) copy-start(f32[1536]{0:T(1024)S(1)} %convert_element_type.436) | copy-start | bytes 18436
  250.1 72.1 %collective-permute-start.2 = (bf16[4,768,512]{2,1,0:T(8,128)(2,1)}, bf16[4,768,512]{2,1,0:T(8,128)(2,1)}, u32[]{:S(2)}, u32[]{:S(2)}) collective-permute-start(bf16[4,768,512]{2,1,0:T(8,128)(2,1)} %convolution_convert_fusion.3), channel_id=1, source_target_pairs={{0,4},{4,0},{8,12},{12,8},{16,20},{20,16},{24,28},{28,24},{1,5},{5... | collective-permute-start | bytes 9437192 | tf_op jit(solution)/shard_map/ppermute | solution.py:795
  255.4 39.2 %collective-permute-start.1 = (bf16[4,768,256]{2,1,0:T(8,128)(2,1)}, bf16[4,768,256]{2,1,0:T(8,128)(2,1)}, u32[]{:S(2)}, u32[]{:S(2)}) collective-permute-start(bf16[4,768,256]{2,1,0:T(8,128)(2,1)} %convolution_convert_fusion.6), channel_id=1, source_target_pairs={{0,8},{4,12},{8,0},{12,4},{16,24},{20,28},{24,16},{28,20},{1,9},{5... | collective-permute-start | bytes 4718600 | tf_op jit(solution)/shard_map/ppermute | solution.py:795
  262.7 125.8 %collective-permute-start.4 = (bf16[1,768,384]{2,1,0:T(8,128)(2,1)}, bf16[1,768,384]{2,1,0:T(8,128)(2,1)}, u32[]{:S(2)}, u32[]{:S(2)}) collective-permute-start(bf16[1,768,384]{2,1,0:T(8,128)(2,1)} %fusion.23), channel_id=1, source_target_pairs={{0,4},{4,0},{8,12},{12,8},{16,20},{20,16},{24,28},{28,24},{1,5},{5... | collective-permute-start | bytes 1769480 | tf_op jit(solution)/shard_map/ppermute | solution.py:795
  297.3 91.3 %collective-permute-start.3 = (bf16[4,384,256]{2,1,0:T(8,128)(2,1)}, bf16[4,384,256]{2,1,0:T(8,128)(2,1)}, u32[]{:S(2)}, u32[]{:S(2)}) collective-permute-start(bf16[4,384,256]{2,1,0:T(8,128)(2,1)} %add_convert_fusion.4), channel_id=1, source_target_pairs={{0,4},{4,0},{8,12},{12,8},{16,20},{20,16},{24,28},{28,24},{1,5},{5... | collective-permute-start | bytes 2359304 | tf_op jit(solution)/shard_map/ppermute | solution.py:795
  304.2 81.7 %copy-start.77 = (bf16[1536,128]{1,0:T(8,128)(2,1)S(1)}, bf16[1536,128]{1,0:T(8,128)(2,1)}, u32[]{:S(2)}) copy-start(bf16[1536,128]{1,0:T(8,128)(2,1)} %param.52) | copy-start | bytes 1179652
  390.6 55.9 %collective-permute-start.8 = (bf16[1,384,384]{2,1,0:T(8,128)(2,1)}, bf16[1,384,384]{2,1,0:T(8,128)(2,1)}, u32[]{:S(2)}, u32[]{:S(2)}) collective-permute-start(bf16[1,384,384]{2,1,0:T(8,128)(2,1)} %add_convert_fusion.13), channel_id=1, source_target_pairs={{0,8},{4,12},{8,0},{12,4},{16,24},{20,28},{24,16},{28,20},{1,9},{5... | collective-permute-start | bytes 884744 | tf_op jit(solution)/shard_map/ppermute | solution.py:795
  395.6 51.1 %collective-permute-start.7 = (bf16[1,768,640]{2,1,0:T(8,128)(2,1)}, bf16[1,768,640]{2,1,0:T(8,128)(2,1)}, u32[]{:S(2)}, u32[]{:S(2)}) collective-permute-start(bf16[1,768,640]{2,1,0:T(8,128)(2,1)} %fusion.20), channel_id=1, source_target_pairs={{0,4},{4,0},{8,12},{12,8},{16,20},{20,16},{24,28},{28,24},{1,5},{5... | collective-permute-start | bytes 2949128 | tf_op jit(solution)/shard_map/ppermute | solution.py:795
  400.0 46.7 %collective-permute-start.6 = (bf16[4,192,256]{2,1,0:T(8,128)(2,1)}, bf16[4,192,256]{2,1,0:T(8,128)(2,1)}, u32[]{:S(2)}, u32[]{:S(2)}) collective-permute-start(bf16[4,192,256]{2,1,0:T(8,128)(2,1)} %add_convert_fusion.10), channel_id=1, source_target_pairs={{0,16},{4,20},{8,24},{12,28},{16,0},{20,4},{24,8},{28,12},{1,17},{... | collective-permute-start | bytes 1179656 | tf_op jit(solution)/shard_map/ppermute | solution.py:795
  405.3 41.4 %collective-permute-start.5 = (bf16[4,384,512]{2,1,0:T(8,128)(2,1)}, bf16[4,384,512]{2,1,0:T(8,128)(2,1)}, u32[]{:S(2)}, u32[]{:S(2)}) collective-permute-start(bf16[4,384,512]{2,1,0:T(8,128)(2,1)} %add_convert_fusion.1), channel_id=1, source_target_pairs={{0,8},{4,12},{8,0},{12,4},{16,24},{20,28},{24,16},{28,20},{1,9},{5... | collective-permute-start | bytes 4718600 | tf_op jit(solution)/shard_map/ppermute | solution.py:795
  439.2 74.4 %collective-permute-start.13 = (bf16[1,768,2048]{2,1,0:T(8,128)(2,1)}, bf16[1,768,2048]{2,1,0:T(8,128)(2,1)}, u32[]{:S(2)}, u32[]{:S(2)}) collective-permute-start(bf16[1,768,2048]{2,1,0:T(8,128)(2,1)} %fusion.3), channel_id=1, source_target_pairs={{0,4},{4,0},{8,12},{12,8},{16,20},{20,16},{24,28},{28,24},{1,5},{5... | collective-permute-start | bytes 9437192 | tf_op jit(solution)/shard_map/ppermute | solution.py:795
  446.5 57.7 %collective-permute-start.12 = (bf16[1,768,1024]{2,1,0:T(8,128)(2,1)}, bf16[1,768,1024]{2,1,0:T(8,128)(2,1)}, u32[]{:S(2)}, u32[]{:S(2)}) collective-permute-start(bf16[1,768,1024]{2,1,0:T(8,128)(2,1)} %fusion.17), channel_id=1, source_target_pairs={{0,8},{4,12},{8,0},{12,4},{16,24},{20,28},{24,16},{28,20},{1,9},{5... | collective-permute-start | bytes 4718600 | tf_op jit(solution)/shard_map/ppermute | solution.py:795
  448.8 55.4 %collective-permute-start.11 = (bf16[1,192,384]{2,1,0:T(8,128)(2,1)}, bf16[1,192,384]{2,1,0:T(8,128)(2,1)}, u32[]{:S(2)}, u32[]{:S(2)}) collective-permute-start(bf16[1,192,384]{2,1,0:T(8,128)(2,1)} %add_convert_fusion.15), channel_id=1, source_target_pairs={{0,16},{4,20},{8,24},{12,28},{16,0},{20,4},{24,8},{28,12},{1,17},{... | collective-permute-start | bytes 442376 | tf_op jit(solution)/shard_map/ppermute | solution.py:795
  452.8 60.7 %collective-permute-start.10 = (bf16[1,384,640]{2,1,0:T(8,128)(2,1)}, bf16[1,384,640]{2,1,0:T(8,128)(2,1)}, u32[]{:S(2)}, u32[]{:S(2)}) collective-permute-start(bf16[1,384,640]{2,1,0:T(8,128)(2,1)} %add_convert_fusion.8), channel_id=1, source_target_pairs={{0,8},{4,12},{8,0},{12,4},{16,24},{20,28},{24,16},{28,20},{1,9},{5... | collective-permute-start | bytes 1474568 | tf_op jit(solution)/shard_map/ppermute | solution.py:795
  458.4 55.2 %collective-permute-start.9 = (bf16[4,192,512]{2,1,0:T(8,128)(2,1)}, bf16[4,192,512]{2,1,0:T(8,128)(2,1)S(1)}, u32[]{:S(2)}, u32[]{:S(2)}) collective-permute-start(bf16[4,192,512]{2,1,0:T(8,128)(2,1)} %add_convert_fusion.3), channel_id=1, source_target_pairs={{0,16},{4,20},{8,24},{12,28},{16,0},{20,4},{24,8},{28,12},{1,17},{... | collective-permute-start | bytes 2359304 | tf_op jit(solution)/shard_map/ppermute | solution.py:795
  479.1 87.7 %copy-start.36 = (bf16[256,1536]{1,0:T(8,128)(2,1)}, bf16[256,1536]{1,0:T(8,128)(2,1)S(1)}, u32[]{:S(2)}) copy-start(bf16[256,1536]{1,0:T(8,128)(2,1)S(1)} %get-tuple-element.318) | copy-start | bytes 2359300
  552.3 40.8 %collective-permute-start.15 = (bf16[1,384,1024]{2,1,0:T(8,128)(2,1)}, bf16[1,384,1024]{2,1,0:T(8,128)(2,1)}, u32[]{:S(2)}, u32[]{:S(2)}) collective-permute-start(bf16[1,384,1024]{2,1,0:T(8,128)(2,1)} %fusion.16), channel_id=1, source_target_pairs={{0,4},{4,0},{8,12},{12,8},{16,20},{20,16},{24,28},{28,24},{1,5},{5... | collective-permute-start | bytes 2359304 | tf_op jit(solution)/shard_map/ppermute | solution.py:795
  557.0 36.1 %collective-permute-start.14 = (bf16[1,192,640]{2,1,0:T(8,128)(2,1)}, bf16[1,192,640]{2,1,0:T(8,128)(2,1)}, u32[]{:S(2)}, u32[]{:S(2)}) collective-permute-start(bf16[1,192,640]{2,1,0:T(8,128)(2,1)} %add_convert_fusion.14), channel_id=1, source_target_pairs={{0,16},{4,20},{8,24},{12,28},{16,0},{20,4},{24,8},{28,12},{1,17},{... | collective-permute-start | bytes 737288 | tf_op jit(solution)/shard_map/ppermute | solution.py:795
  569.8 62.6 %collective-permute-start.18 = (bf16[1,768,768]{2,1,0:T(8,128)(2,1)}, bf16[1,768,768]{2,1,0:T(8,128)(2,1)}, u32[]{:S(2)}, u32[]{:S(2)}) collective-permute-start(bf16[1,768,768]{2,1,0:T(8,128)(2,1)} %fusion.18), channel_id=1, source_target_pairs={{0,4},{4,0},{8,12},{12,8},{16,20},{20,16},{24,28},{28,24},{1,5},{5... | collective-permute-start | bytes 3538952 | tf_op jit(solution)/shard_map/ppermute | solution.py:795
  573.5 58.9 %collective-permute-start.17 = (bf16[1,384,2048]{2,1,0:T(8,128)(2,1)}, bf16[1,384,2048]{2,1,0:T(8,128)(2,1)}, u32[]{:S(2)}, u32[]{:S(2)}) collective-permute-start(bf16[1,384,2048]{2,1,0:T(8,128)(2,1)} %fusion.2), channel_id=1, source_target_pairs={{0,8},{4,12},{8,0},{12,4},{16,24},{20,28},{24,16},{28,20},{1,9},{5... | collective-permute-start | bytes 4718600 | tf_op jit(solution)/shard_map/ppermute | solution.py:795
  582.9 93.3 %collective-permute-start.19 = (bf16[1,768,768]{2,1,0:T(8,128)(2,1)}, bf16[1,768,768]{2,1,0:T(8,128)(2,1)}, u32[]{:S(2)}, u32[]{:S(2)}) collective-permute-start(bf16[1,768,768]{2,1,0:T(8,128)(2,1)} %fusion.19), channel_id=1, source_target_pairs={{0,4},{4,0},{8,12},{12,8},{16,20},{20,16},{24,28},{28,24},{1,5},{5... | collective-permute-start | bytes 3538952 | tf_op jit(solution)/shard_map/ppermute | solution.py:795
  609.2 21.0 %collective-permute-start.25 = (bf16[1,192,1024]{2,1,0:T(8,128)(2,1)S(1)}, bf16[1,192,1024]{2,1,0:T(8,128)(2,1)S(1)}, u32[]{:S(2)}, u32[]{:S(2)}) collective-permute-start(bf16[1,192,1024]{2,1,0:T(8,128)(2,1)S(1)} %add_convert_fusion.9), channel_id=1, source_target_pairs={{0,16},{4,20},{8,24},{12,28},{16,0},{20,4},{24,8},{28,12},{1,17},{... | collective-permute-start | bytes 1179656 | tf_op jit(solution)/shard_map/ppermute | solution.py:795
  610.8 9.9 %collective-permute-start.16 = (f32[3,768]{1,0:T(4,128)S(1)}, f32[3,768]{1,0:T(4,128)S(1)}, u32[]{:S(2)}, u32[]{:S(2)}) collective-permute-start(f32[3,768]{1,0:T(4,128)S(1)} %slice.414), channel_id=1, source_target_pairs={{4,0},{8,4},{12,8},{16,12},{20,16},{24,20},{28,24},{5,1},{9,5},{13... | collective-permute-start | bytes 27656 | tf_op jit(solution)/shard_map/ppermute | solution.py:31
  635.3 43.0 %collective-permute-start.21 = (bf16[1,192,2048]{2,1,0:T(8,128)(2,1)}, bf16[1,192,2048]{2,1,0:T(8,128)(2,1)}, u32[]{:S(2)}, u32[]{:S(2)}) collective-permute-start(bf16[1,192,2048]{2,1,0:T(8,128)(2,1)} %add_convert_fusion.2), channel_id=1, source_target_pairs={{0,16},{4,20},{8,24},{12,28},{16,0},{20,4},{24,8},{28,12},{1,17},{... | collective-permute-start | bytes 2359304 | tf_op jit(solution)/shard_map/ppermute | solution.py:795
  646.2 32.0 %collective-permute-start.20 = (bf16[1,384,768]{2,1,0:T(8,128)(2,1)}, bf16[1,384,768]{2,1,0:T(8,128)(2,1)}, u32[]{:S(2)}, u32[]{:S(2)}) collective-permute-start(bf16[1,384,768]{2,1,0:T(8,128)(2,1)} %add_convert_fusion.7), channel_id=1, source_target_pairs={{0,8},{4,12},{8,0},{12,4},{16,24},{20,28},{24,16},{28,20},{1,9},{5... | collective-permute-start | bytes 1769480 | tf_op jit(solution)/shard_map/ppermute | solution.py:795
  680.5 63.1 %collective-permute-start.24 = (bf16[1,192,768]{2,1,0:T(8,128)(2,1)}, bf16[1,192,768]{2,1,0:T(8,128)(2,1)}, u32[]{:S(2)}, u32[]{:S(2)}) collective-permute-start(bf16[1,192,768]{2,1,0:T(8,128)(2,1)} %add_convert_fusion.11), channel_id=1, source_target_pairs={{0,16},{4,20},{8,24},{12,28},{16,0},{20,4},{24,8},{28,12},{1,17},{... | collective-permute-start | bytes 884744 | tf_op jit(solution)/shard_map/ppermute | solution.py:795
  682.0 51.0 %copy-start.34 = (f32[1,192,2048]{2,1,0:T(8,128)S(1)}, f32[1,192,2048]{2,1,0:T(8,128)}, u32[]{:S(2)}) copy-start(f32[1,192,2048]{2,1,0:T(8,128)} %fusion.5) | copy-start | bytes 4718596
  682.0 55.2 %collective-permute-start.22 = (bf16[1,384,768]{2,1,0:T(8,128)(2,1)S(1)}, bf16[1,384,768]{2,1,0:T(8,128)(2,1)S(1)}, u32[]{:S(2)}, u32[]{:S(2)}) collective-permute-start(bf16[1,384,768]{2,1,0:T(8,128)(2,1)S(1)} %add_convert_fusion.6), channel_id=1, source_target_pairs={{0,8},{4,12},{8,0},{12,4},{16,24},{20,28},{24,16},{28,20},{1,9},{5... | collective-permute-start | bytes 1769480 | tf_op jit(solution)/shard_map/ppermute | solution.py:795
  738.8 13.5 %collective-permute-start.23 = (bf16[1,192,768]{2,1,0:T(8,128)(2,1)S(1)}, bf16[1,192,768]{2,1,0:T(8,128)(2,1)}, u32[]{:S(2)}, u32[]{:S(2)}) collective-permute-start(bf16[1,192,768]{2,1,0:T(8,128)(2,1)S(1)} %add_convert_fusion.12), channel_id=1, source_target_pairs={{0,16},{4,20},{8,24},{12,28},{16,0},{20,4},{24,8},{28,12},{1,17},{... | collective-permute-start | bytes 884744 | tf_op jit(solution)/shard_map/ppermute | solution.py:795
  (223 other events, 1443.1 us)

commit v4 on v3

--- a/solution.py
+++ b/solution.py
@@ -89,230 +89,319 @@
     )
 
 
-def head_sum(values, number, wire, pieces):
-    rows, width = values.shape
-    half = rows // 2
+def together(*jobs):
+    waiting = list(jobs)
+    while waiting:
+        for job in list(waiting):
+            if next(job, waiting) is waiting:
+                waiting.remove(job)
+
+
+def head_peers():
+    seq = lax.axis_index("seq")
+    head = lax.axis_index("head")
+    return [(seq, head + 1 - 2 * (head % 2)), (seq, (head + 2) % 4)]
+
+
+def head_scratch(rows, width, wire, pieces):
+    return [pltpu.VMEM((rows // 2, width), wire)] * 4 + [
+        pltpu.SemaphoreType.DMA((3, pieces)),
+        pltpu.SemaphoreType.DMA((3, pieces)),
+    ]
+
+
+def head_job(x_ref, o_ref, scratch, wire, pieces):
+    near_out, near_in, far_out, far_in, send, recv = scratch
+    half = x_ref.shape[0] // 2
     step = half // pieces
-
-    def kernel(x_ref, o_ref, near_out, near_in, far_out, far_in, send, recv):
-        seq = lax.axis_index("seq")
-        head = lax.axis_index("head")
-        core = head % 2
-        near = (seq, head + 1 - 2 * core)
-        far = (seq, (head + 2) % 4)
-        meet([near, far])
-
-        def rows_of(side, piece):
-            return pl.ds(pl.multiple_of(side * half + piece * step, 8), step)
-
-        copies = []
-        for piece in range(pieces):
-            local = pl.ds(piece * step, step)
-            near_out[local] = x_ref[rows_of(1 - core, piece)].astype(wire)
-            copy = send_to(
+    near, far = head_peers()
+    core = lax.axis_index("head") % 2
+
+    def rows_of(side, piece):
+        return pl.ds(pl.multiple_of(side * half + piece * step, 8), step)
+
+    first, second, third = [], [], []
+    for piece in range(pieces):
+        local = pl.ds(piece * step, step)
+        near_out[local] = x_ref[rows_of(1 - core, piece)].astype(wire)
+        first.append(
+            send_to(
                 near_out.at[local], near_in.at[local], send.at[0, piece], recv.at[0, piece], near
             )
-            copy.start()
-            copies.append(copy)
-        second = []
-        for piece in range(pieces):
-            local = pl.ds(piece * step, step)
-            copies[piece].wait_recv()
-            total = x_ref[rows_of(core, piece)] + near_in[local].astype(jnp.float32)
-            far_out[local] = total.astype(wire)
-            copy = send_to(
-                far_out.at[local], far_in.at[local], send.at[1, piece], recv.at[1, piece], far
-            )
-            copy.start()
-            second.append(copy)
-        third = []
-        for piece in range(pieces):
-            local = pl.ds(piece * step, step)
-            second[piece].wait_recv()
-            whole = far_out[local].astype(jnp.float32) + far_in[local].astype(jnp.float32)
-            o_ref[rows_of(core, piece)] = whole
-            copy = send_to(
+        )
+        first[-1].start()
+    yield
+    for piece in range(pieces):
+        local = pl.ds(piece * step, step)
+        first[piece].wait_recv()
+        total = x_ref[rows_of(core, piece)] + near_in[local].astype(jnp.float32)
+        far_out[local] = total.astype(wire)
+        second.append(
+            send_to(far_out.at[local], far_in.at[local], send.at[1, piece], recv.at[1, piece], far)
+        )
+        second[-1].start()
+    yield
+    for piece in range(pieces):
+        local = pl.ds(piece * step, step)
+        second[piece].wait_recv()
+        whole = far_out[local].astype(jnp.float32) + far_in[local].astype(jnp.float32)
+        o_ref[rows_of(core, piece)] = whole
+        third.append(
+            send_to(
                 o_ref.at[rows_of(core, piece)],
                 o_ref.at[rows_of(core, piece)],
                 send.at[2, piece],
                 recv.at[2, piece],
                 near,
             )
-            copy.start()
-            third.append(copy)
-        for copy in third:
-            copy.wait_recv()
-        for copy in copies + second + third:
-            copy.wait_send()
+        )
+        third[-1].start()
+    yield
+    for copy in third:
+        copy.wait_recv()
+    for copy in first + second + third:
+        copy.wait_send()
+
+
+def head_sum(values, number, wire, pieces):
+    rows, width = values.shape
+
+    def kernel(x_ref, o_ref, *scratch):
+        meet(head_peers())
+        together(head_job(x_ref, o_ref, scratch, wire, pieces))
 
     return pl.pallas_call(
         kernel,
         out_shape=jax.ShapeDtypeStruct((rows, width), jnp.float32),
         in_specs=[VMEM],
         out_specs=VMEM,
-        scratch_shapes=[pltpu.VMEM((half, width), wire)] * 4
-        + [pltpu.SemaphoreType.DMA((3, pieces))] * 2,
+        scratch_shapes=head_scratch(rows, width, wire, pieces),
         compiler_params=talking(number),
         cost_estimate=lasting(6 + values.size // 40000),
         name="head_sum",
     )(values)
 
 
-def seq_gather(block, number):
-    rows, width = block.shape
+def pair_peers():
+    seq = lax.axis_index("seq")
+    head = lax.axis_index("head")
+    pairs = lax.axis_size("seq") // 2
+    place = seq % 2
+    pair = seq // 2
+    others = [(((pair + k) % pairs) * 2 + place, head) for k in range(1, pairs)]
+    return [(seq + 1 - 2 * place, head)] + others
+
+
+def scatter_shapes(arrays):
     seq_count = lax.axis_size("seq")
-    pairs = seq_count // 2
-
-    def kernel(x_ref, o_ref, send, recv, pass_send, pass_recv, own_sem):
+    return [(a.shape[0] // seq_count, a.shape[1]) for a in arrays]
+
+
+def scatter_blocks(arrays):
+    pairs = lax.axis_size("seq") // 2
+    return [
+        a.reshape(pairs, 2, shape[0], shape[1])
+        for a, shape in zip(arrays, scatter_shapes(arrays), strict=True)
+    ]
+
+
+def scatter_scratch(shapes):
+    pairs = lax.axis_size("seq") // 2
+    count = len(shapes)
+    return (
+        [pltpu.VMEM((pairs,) + shape, jnp.bfloat16) for shape in shapes] * 2
+        + [pltpu.VMEM((pairs - 1,) + shape, jnp.bfloat16) for shape in shapes]
+        + [pltpu.SemaphoreType.DMA((count,))] * 3
+        + [pltpu.SemaphoreType.DMA((count, pairs - 1))] * 2
+    )
+
+
+def scatter_job(takes, gives, scratch, shapes):
+    count = len(takes)
+    pairs = lax.axis_size("seq") // 2
+    own, near, far = scratch[:count], scratch[count : 2 * count], scratch[2 * count : 3 * count]
+    own_sem, near_send, near_recv, far_send, far_recv = scratch[3 * count :]
+    seq = lax.axis_index("seq")
+    place = seq % 2
+    pair = seq // 2
+    partner, *others = pair_peers()
+    owners = [(pair + k) % pairs for k in range(1, pairs)]
+    loads = [
+        pltpu.make_async_copy(takes[i].at[:, place], own[i], own_sem.at[i]) for i in range(count)
+    ]
+    halves = [
+        send_to(takes[i].at[:, 1 - place], near[i], near_send.at[i], near_recv.at[i], partner)
+        for i in range(count)
+    ]
+
+    def launch(i):
+        if i < count:
+            halves[i].start()
+            loads[i].start()
+
+    sums = []
+
+    def finish(i):
+        for copy in sums[i]:
+            copy.wait_recv()
+
+        @pl.loop(0, shapes[i][0] // 16)
+        def add(step):
+            part = pl.ds(pl.multiple_of(step * 16, 16), 16)
+            total = own[i][pair, part].astype(jnp.float32)
+            for k in range(pairs - 1):
+                total = total + far[i][k, part].astype(jnp.float32)
+            gives[i][part] = total
+
+    launch(0)
+    launch(1)
+    for i in range(count):
+        yield
+        halves[i].wait_recv()
+        loads[i].wait()
+        launch(i + 2)
+
+        @pl.loop(0, pairs)
+        def merge(block):
+            @pl.loop(0, shapes[i][0] // 16)
+            def add(step):
+                part = pl.ds(pl.multiple_of(step * 16, 16), 16)
+                total = own[i][block, part].astype(jnp.float32) + near[i][block, part].astype(
+                    jnp.float32
+                )
+                own[i][block, part] = total.astype(jnp.bfloat16)
+
+        sums.append(
+            [
+                send_to(
+                    own[i].at[owners[k]],
+                    far[i].at[k],
+                    far_send.at[i, k],
+                    far_recv.at[i, k],
+                    others[k],
+                )
+                for k in range(pairs - 1)
+            ]
+        )
+        for copy in sums[i]:
+            copy.start()
+        if i > 0:
+            finish(i - 1)
+    yield
+    finish(count - 1)
+    for copy in halves:
+        copy.wait_send()
+    for group in sums:
+        for copy in group:
+            copy.wait_send()
+
+
+def scatter_and_head_sum(arrays, values, number):
+    count = len(arrays)
+    shapes = scatter_shapes(arrays)
+    rows, width = values.shape
+    spaces = scatter_scratch(shapes)
+
+    def kernel(*refs):
+        takes, x_ref = refs[:count], refs[count]
+        gives, o_ref = refs[count + 1 : 2 * count + 1], refs[2 * count + 1]
+        scratch = refs[2 * count + 2 :]
+        meet(pair_peers() + head_peers())
+        together(
+            scatter_job(takes, gives, scratch[: len(spaces)], shapes),
+            head_job(x_ref, o_ref, scratch[len(spaces) :], jnp.bfloat16, 4),
+        )
+
+    return pl.pallas_call(
+        kernel,
+        out_shape=[jax.ShapeDtypeStruct(shape, jnp.float32) for shape in shapes]
+        + [jax.ShapeDtypeStruct((rows, width), jnp.float32)],
+        in_specs=[ANY] * count + [VMEM],
+        out_specs=[VMEM] * (count + 1),
+        scratch_shapes=spaces + head_scratch(rows, width, jnp.bfloat16, 4),
+        compiler_params=talking(number),
+        cost_estimate=lasting(20),
+        name="scatter_and_head_sum",
+    )(*scatter_blocks(arrays), values)
+
+
+def last_sums(arrays, values, tokens, gain, upstream, number):
+    count = len(arrays)
+    shapes = scatter_shapes(arrays)
+    rows, width = values.shape
+    seq_count = lax.axis_size("seq")
+    spaces = scatter_scratch(shapes)
+    step = 16
+
+    def kernel(*refs):
+        takes = refs[:count]
+        x_ref, token_ref, gain_ref, up_ref = refs[count : count + 4]
+        gives = refs[count + 4 : 2 * count + 4]
+        grad_ref, gain_out = refs[2 * count + 4 : 2 * count + 6]
+        scratch = refs[2 * count + 6 :]
+        total_ref, part_out, part_in, part_send, part_recv = scratch[-5:]
         seq = lax.axis_index("seq")
         head = lax.axis_index("head")
-        place = seq % 2
-        pair = seq // 2
-        partner = (seq + 1 - 2 * place, head)
-        others = [(((pair + k) % pairs) * 2 + place, head) for k in range(1, pairs)]
-        meet([partner] + others)
-        own = pltpu.make_async_copy(x_ref, o_ref.at[seq], own_sem)
-        own.start()
-        first = [
-            send_to(x_ref, o_ref.at[seq], send.at[k], recv.at[k], others[k])
-            for k in range(pairs - 1)
-        ]
-        passed = [send_to(x_ref, o_ref.at[seq], pass_send.at[0], pass_recv.at[0], partner)]
-        passed[0].start()
-        for copy in first:
-            copy.start()
-        for k in range(1, pairs):
-            first[k - 1].wait_recv()
-            origin = ((pair - k + pairs) % pairs) * 2 + place
-            copy = send_to(
-                o_ref.at[origin], o_ref.at[origin], pass_send.at[k], pass_recv.at[k], partner
-            )
-            copy.start()
-            passed.append(copy)
-        for copy in passed:
-            copy.wait_recv()
-        for copy in first + passed:
-            copy.wait_send()
-        own.wait()
-
-    out = pl.pallas_call(
+        peers = [((seq + k) % seq_count, head) for k in range(1, seq_count)]
+        meet(peers + head_peers())
+
+        def norm_job():
+            yield from head_job(x_ref, total_ref, scratch[len(spaces) : -5], jnp.bfloat16, 4)
+
+            def back(position, gained):
+                part = pl.ds(pl.multiple_of(position * step, step), step)
+                token = token_ref[part].astype(jnp.float32)
+                scale = lax.rsqrt(jnp.mean(token * token, axis=1, keepdims=True) + epsilon)
+                unit = token * scale
+                given = total_ref[part]
+                scaled = given * gain_ref[...]
+                pull = jnp.mean(scaled * unit, axis=1, keepdims=True)
+                grad_ref[part] = up_ref[part] + scale * (scaled - unit * pull)
+                product_rows = given * unit
+                return gained + product_rows[:8] + product_rows[8:]
+
+            gained = lax.fori_loop(0, rows // step, back, jnp.zeros((8, width), jnp.float32))
+            part_out[...] = jnp.sum(gained, axis=0, keepdims=True)
+            copies = [
+                send_to(part_out, part_in.at[k], part_send.at[k], part_recv.at[k], peers[k])
+                for k in range(seq_count - 1)
+            ]
+            for copy in copies:
+                copy.start()
+            yield
+            for copy in copies:
+                copy.wait_recv()
+            whole = part_out[...]
+            for k in range(seq_count - 1):
+                whole = whole + part_in[k]
+            gain_out[...] = whole
+            for copy in copies:
+                copy.wait_send()
+
+        together(norm_job(), scatter_job(takes, gives, scratch[: len(spaces)], shapes))
+
+    return pl.pallas_call(
         kernel,
-        out_shape=jax.ShapeDtypeStruct((seq_count, rows, width), block.dtype),
-        in_specs=[VMEM],
-        out_specs=VMEM,
-        scratch_shapes=[pltpu.SemaphoreType.DMA((pairs,))] * 4 + [pltpu.SemaphoreType.DMA],
+        out_shape=[jax.ShapeDtypeStruct(shape, jnp.float32) for shape in shapes]
+        + [
+            jax.ShapeDtypeStruct((rows, width), jnp.float32),
+            jax.ShapeDtypeStruct((1, width), jnp.float32),
+        ],
+        in_specs=[ANY] * count + [VMEM] * 4,
+        out_specs=[VMEM] * (count + 2),
+        scratch_shapes=spaces
+        + head_scratch(rows, width, jnp.bfloat16, 4)
+        + [
+            pltpu.VMEM((rows, width), jnp.float32),
+            pltpu.VMEM((1, width), jnp.float32),
+            pltpu.VMEM((seq_count - 1, 1, width), jnp.float32),
+            pltpu.SemaphoreType.DMA((seq_count - 1,)),
+            pltpu.SemaphoreType.DMA((seq_count - 1,)),
+        ],
         compiler_params=talking(number),
         cost_estimate=lasting(20),
-        name="seq_gather",
-    )(block)
-    return out.reshape(seq_count * rows, width)
-
-
-def seq_scatter(arrays, number):
-    seq_count = lax.axis_size("seq")
-    pairs = seq_count // 2
-    count = len(arrays)
-    shapes = [(a.shape[0] // seq_count, a.shape[1]) for a in arrays]
-    blocks = [
-        a.reshape(pairs, 2, shape[0], shape[1]) for a, shape in zip(arrays, shapes, strict=True)
-    ]
-
-    def kernel(*refs):
-        takes, gives = refs[:count], refs[count : 2 * count]
-        own, near = refs[2 * count : 3 * count], refs[3 * count : 4 * count]
-        far = refs[4 * count : 5 * count]
-        own_sem, near_send, near_recv, far_send, far_recv = refs[5 * count :]
-        seq = lax.axis_index("seq")
-        head = lax.axis_index("head")
-        place = seq % 2
-        pair = seq // 2
-        partner = (seq + 1 - 2 * place, head)
-        owners = [(pair + k) % pairs for k in range(1, pairs)]
-        others = [(owner * 2 + place, head) for owner in owners]
-        meet([partner] + others)
-        loads = [
-            pltpu.make_async_copy(takes[i].at[:, place], own[i], own_sem.at[i])
-            for i in range(count)
-        ]
-        halves = [
-            send_to(takes[i].at[:, 1 - place], near[i], near_send.at[i], near_recv.at[i], partner)
-            for i in range(count)
-        ]
-
-        def launch(i):
-            if i < count:
-                halves[i].start()
-                loads[i].start()
-
-        sums = []
-
-        def finish(i):
-            rows = shapes[i][0]
-            for copy in sums[i]:
-                copy.wait_recv()
-
-            @pl.loop(0, rows // 16)
-            def add(step):
-                part = pl.ds(pl.multiple_of(step * 16, 16), 16)
-                total = own[i][pair, part].astype(jnp.float32)
-                for k in range(pairs - 1):
-                    total = total + far[i][k, part].astype(jnp.float32)
-                gives[i][part] = total
-
-        launch(0)
-        launch(1)
-        for i in range(count):
-            rows = shapes[i][0]
-            halves[i].wait_recv()
-            loads[i].wait()
-            launch(i + 2)
-
-            @pl.loop(0, pairs)
-            def merge(block):
-                @pl.loop(0, rows // 16)
-                def add(step):
-                    part = pl.ds(pl.multiple_of(step * 16, 16), 16)
-                    total = own[i][block, part].astype(jnp.float32) + near[i][block, part].astype(
-                        jnp.float32
-                    )
-                    own[i][block, part] = total.astype(jnp.bfloat16)
-
-            sums.append(
-                [
-                    send_to(
-                        own[i].at[owners[k]],
-                        far[i].at[k],
-                        far_send.at[i, k],
-                        far_recv.at[i, k],
-                        others[k],
-                    )
-                    for k in range(pairs - 1)
-                ]
-            )
-            for copy in sums[i]:
-                copy.start()
-            if i > 0:
-                finish(i - 1)
-        finish(count - 1)
-        for copy in halves:
-            copy.wait_send()
-        for group in sums:
-            for copy in group:
-                copy.wait_send()
-
-    return pl.pallas_call(
-        kernel,
-        out_shape=[jax.ShapeDtypeStruct(shape, jnp.float32) for shape in shapes],
-        in_specs=[ANY] * count,
-        out_specs=[VMEM] * count,
-        scratch_shapes=[pltpu.VMEM((pairs,) + shape, jnp.bfloat16) for shape in shapes] * 2
-        + [pltpu.VMEM((pairs - 1,) + shape, jnp.bfloat16) for shape in shapes]
-        + [pltpu.SemaphoreType.DMA((count,))] * 3
-        + [pltpu.SemaphoreType.DMA((count, pairs - 1))] * 2,
-        compiler_params=talking(number),
-        cost_estimate=lasting(15 + sum(a.size for a in arrays) // 50000),
-        name="seq_scatter",
-    )(*blocks)
+        name="last_sums",
+    )(*scatter_blocks(arrays), values, tokens, gain, upstream)
 
 
 def widen(column_block, width):
@@ -337,12 +426,33 @@
     seq_count = lax.axis_size("seq")
     group = math.gcd(rows, 8)
 
-    def kernel(step_ref, drive_ref, coef_ref, slope_ref, o_ref, outgoing, incoming, send, recv):
+    def kernel(
+        step_ref,
+        drive_ref,
+        coef_ref,
+        slope_ref,
+        o_ref,
+        outgoing,
+        incoming,
+        span_out,
+        span_in,
+        send,
+        recv,
+    ):
         seq = lax.axis_index("seq")
         head = lax.axis_index("head")
         peers = [((seq + k) % seq_count, head) for k in range(1, seq_count)]
         meet(peers)
         slope = slope_ref[...]
+        span_out[...] = jnp.broadcast_to(
+            jnp.sum(step_ref[...], axis=0, keepdims=True), span_out.shape
+        )
+        spans = [
+            send_to(span_out, span_in.at[k], send.at[1, k], recv.at[1, k], peers[k])
+            for k in range(seq_count - 1)
+        ]
+        for copy in spans:
+            copy.start()
 
         def advance(position, state):
             for offset in range(group):
@@ -354,25 +464,25 @@
             return state
 
         state = lax.fori_loop(0, rows // group, advance, jnp.zeros((entries, width), jnp.float32))
-        whole = jnp.exp2(jnp.sum(step_ref[...], axis=0, keepdims=True) * slope)
-        outgoing[:entries] = state.astype(jnp.bfloat16)
-        outgoing[entries:] = whole.astype(jnp.bfloat16)
+        outgoing[...] = state.astype(jnp.bfloat16)
         copies = [
-            send_to(outgoing, incoming.at[k], send.at[k], recv.at[k], peers[k])
+            send_to(outgoing, incoming.at[k], send.at[0, k], recv.at[0, k], peers[k])
             for k in range(seq_count - 1)
         ]
         for copy in copies:
             copy.start()
+        for copy in spans:
+            copy.wait_recv()
         for copy in copies:
             copy.wait_recv()
         carried = jnp.zeros((entries, width), jnp.float32)
         order = range(seq_count - 1, 0, -1) if forward else range(1, seq_count)
         for k in order:
             known = seq - k >= 0 if forward else seq - k < 0
-            block = incoming[k - 1].astype(jnp.float32)
-            carried = jnp.where(known, block[entries:] * carried + block[:entries], 0.0)
+            whole = jnp.exp2(span_in[k - 1][:1] * slope)
+            carried = jnp.where(known, whole * carried + incoming[k - 1].astype(jnp.float32), 0.0)
         o_ref[...] = carried
-        for copy in copies:
+        for copy in copies + spans:
             copy.wait_send()
 
     return pl.pallas_call(
@@ -381,10 +491,12 @@
         in_specs=[VMEM] * 4,
         out_specs=VMEM,
         scratch_shapes=[
-            pltpu.VMEM((2 * entries, width), jnp.bfloat16),
-            pltpu.VMEM((seq_count - 1, 2 * entries, width), jnp.bfloat16),
-            pltpu.SemaphoreType.DMA((seq_count - 1,)),
-            pltpu.SemaphoreType.DMA((seq_count - 1,)),
+            pltpu.VMEM((entries, width), jnp.bfloat16),
+            pltpu.VMEM((seq_count - 1, entries, width), jnp.bfloat16),
+            pltpu.VMEM((8, width), jnp.float32),
+            pltpu.VMEM((seq_count - 1, 8, width), jnp.float32),
+            pltpu.SemaphoreType.DMA((2, seq_count - 1)),
+            pltpu.SemaphoreType.DMA((2, seq_count - 1)),
         ],
         compiler_params=talking(number),
         cost_estimate=lasting(16),
@@ -583,33 +695,65 @@
     return jnp.where(jnp.logical_or(earlier, jnp.logical_not(diagonal)), bias, masked_score)
 
 
-def attend(own, queries, both_rows, key_docs, query_docs):
+def attend(queries, both, key_docs, query_docs, number):
     rows, width = queries.shape
-    key_width = both_rows.shape[1] // 2
+    key_width = both.shape[1] // 2
     shared_heads = key_width // HEAD_DIM
     heads = width // HEAD_DIM
+    seq_count = lax.axis_size("seq")
+    pairs = seq_count // 2
     scale = 0.125 * LOG2E
 
-    def kernel(own_ref, q_ref, kv_ref, kd_ref, qd_ref, low_ref, att_ref, lse_ref, qt_ref, max_ref, sum_ref):
+    def kernel(
+        q_ref,
+        x_ref,
+        kd_ref,
+        qd_ref,
+        low_ref,
+        att_ref,
+        lse_ref,
+        kv_ref,
+        qt_ref,
+        max_ref,
+        sum_ref,
+        send,
+        recv,
+        pass_send,
+        pass_recv,
+    ):
+        me = lax.axis_index("seq")
+        place = me % 2
+        pair = me // 2
+        partner, *others = pair_peers()
+        meet([partner] + others)
+
+        first = [
+            send_to(x_ref, kv_ref.at[me], send.at[k], recv.at[k], others[k])
+            for k in range(pairs - 1)
+        ]
+        across = send_to(x_ref, kv_ref.at[me], pass_send.at[0], pass_recv.at[0], partner)
+        across.start()
+        for copy in first:
+            copy.start()
+        kv_ref[me] = x_ref[...]
         stand_up(q_ref[...], qt_ref, shared_heads)
-        me = own_ref[0]
-
-        def block(step, first):
-            begin = pl.multiple_of((me - step) * rows, rows)
-            keys = kv_ref[pl.ds(begin, rows), :key_width]
-            values = kv_ref[pl.ds(begin, rows), key_width:]
-            bias = hidden_bias(kd_ref[pl.ds(begin, rows), :], qd_ref[...], step == 0)
+
+        def block(owner, own):
+            keys = x_ref[:, :key_width] if own else kv_ref[owner, :, :key_width]
+            values = x_ref[:, key_width:] if own else kv_ref[owner, :, key_width:]
+            begin = pl.multiple_of(owner * rows, rows)
+            bias = hidden_bias(kd_ref[pl.ds(begin, rows), :], qd_ref[...], own)
             for head in range(heads):
                 columns = slice(head * rows, (head + 1) * rows)
                 scores = product(keys, qt_ref[:, columns]) * scale + bias
                 top = jnp.max(scores, axis=0, keepdims=True)
-                if not first:
+                if not own:
                     old = max_ref[:, columns]
                     top = jnp.maximum(top, old)
                 weights = jnp.exp2(scores - top)
                 total = jnp.sum(weights, axis=0, keepdims=True)
                 weighted = over_rows(values, to_low(weights))
-                if not first:
+                if not own:
                     factor = jnp.exp2(old - top)
                     total = total + sum_ref[:, columns] * factor
                     weighted = weighted + att_ref[:, columns] * factor
@@ -617,15 +761,45 @@
                 sum_ref[:, columns] = total
                 att_ref[:, columns] = weighted
 
-        block(0, True)
-
-        @pl.loop(1, me + 1)
-        def earlier(step):
-            block(step, False)
+        def earlier(owner):
+            @pl.when(owner < me)
+            def visit():
+                block(owner, False)
+
+        block(me, True)
+        for k in range(1, pairs):
+            first[k - 1].wait_recv()
+            origin = ((pair - k + pairs) % pairs) * 2 + place
+            passed = send_to(
+                kv_ref.at[origin], kv_ref.at[origin], pass_send.at[k], pass_recv.at[k], partner
+            )
+            passed.start()
+            if k == 1:
+                across.wait_recv()
+                earlier(me + 1 - 2 * place)
+            earlier(origin)
+
+        @pl.loop(1, pairs)
+        def arrived(k):
+            origin = ((pair - k + pairs) % pairs) * 2 + place
+            other = origin + 1 - 2 * place
+            send_to(
+                kv_ref.at[origin], kv_ref.at[origin], pass_send.at[k], pass_recv.at[k], partner
+            ).wait_recv()
+            earlier(other)
 
         att_ref[...] = att_ref[...] / sum_ref[...]
         lse_ref[...] = max_ref[...] + jnp.log2(sum_ref[...])
         low_ref[...] = to_low(lie_down(att_ref, rows, shared_heads))
+        for copy in first + [across]:
+            copy.wait_send()
+
+        @pl.loop(1, pairs)
+        def sent(k):
+            origin = ((pair - k + pairs) % pairs) * 2 + place
+            send_to(
+                kv_ref.at[origin], kv_ref.at[origin], pass_send.at[k], pass_recv.at[k], partner
+            ).wait_send()
 
     return pl.pallas_call(
         kernel,
@@ -633,18 +807,20 @@
             jax.ShapeDtypeStruct((rows, width), jnp.bfloat16),
             jax.ShapeDtypeStruct((key_width, heads * rows), jnp.float32),
             jax.ShapeDtypeStruct((1, heads * rows), jnp.float32),
+            jax.ShapeDtypeStruct((seq_count,) + both.shape, both.dtype),
         ),
-        in_specs=[pl.BlockSpec(memory_space=pltpu.SMEM)] + [VMEM] * 4,
-        out_specs=(VMEM,) * 3,
+        in_specs=[VMEM] * 4,
+        out_specs=(VMEM,) * 4,
         scratch_shapes=[
             pltpu.VMEM((key_width, heads * rows), jnp.bfloat16),
             pltpu.VMEM((1, heads * rows), jnp.float32),
             pltpu.VMEM((1, heads * rows), jnp.float32),
-        ],
-        compiler_params=pltpu.CompilerParams(vmem_limit_bytes=LIMIT),
+        ]
+        + [pltpu.SemaphoreType.DMA((pairs,))] * 4,
+        compiler_params=talking(number),
         cost_estimate=lasting(12),
         name="attend",
-    )(own, queries, both_rows, key_docs, query_docs)
+    )(queries, both, key_docs, query_docs)
 
 
 def attend_back(own, queries, upstream, both_rows, key_docs, query_docs, attended, log_sum):
@@ -656,7 +832,7 @@
     scale = 0.125 * LOG2E
 
     def kernel(
-        own_ref, q_ref, up_ref, kv_ref, kd_ref, qd_ref, att_ref, lse_ref, qg_ref, kvg_ref, qt_ref, ut_ref, acc_ref
+        own_ref, q_ref, up_ref, kv_ref, kd_ref, qd_ref, att_ref, lse_ref, qg_ref, kg_ref, vg_ref, qt_ref, ut_ref, acc_ref
     ):
         stand_up(q_ref[...], qt_ref, shared_heads)
         stand_up(up_ref[...], ut_ref, shared_heads)
@@ -667,7 +843,8 @@
         @pl.loop(me + 1, total_rows // rows)
         def later(position):
             begin = pl.multiple_of(position * rows, rows)
-            kvg_ref[pl.ds(begin, rows), :] = jnp.zeros((rows, 2 * key_width), jnp.bfloat16)
+            kg_ref[pl.ds(begin, rows), :] = jnp.zeros((rows, key_width), jnp.bfloat16)
+            vg_ref[pl.ds(begin, rows), :] = jnp.zeros((rows, key_width), jnp.bfloat16)
 
         @pl.loop(0, me + 1)
         def block(position):
@@ -686,8 +863,8 @@
                 score_grad = to_low(probs * (product(values, upper) - delta[:, columns]))
                 key_grad = key_grad + over_columns(score_grad, query)
                 acc_ref[:, columns] += over_rows(keys, score_grad)
-            kvg_ref[pl.ds(begin, rows), :key_width] = to_low(key_grad * 0.125)
-            kvg_ref[pl.ds(begin, rows), key_width:] = to_low(value_grad)
+            kg_ref[pl.ds(begin, rows), :] = to_low(key_grad * 0.125)
+            vg_ref[pl.ds(begin, rows), :] = to_low(value_grad)
 
         qg_ref[...] = to_low(lie_down(acc_ref, rows, shared_heads) * 0.125)
 
@@ -695,10 +872,11 @@
         kernel,
         out_shape=(
             jax.ShapeDtypeStruct((rows, width), jnp.bfloat16),
-            jax.ShapeDtypeStruct((total_rows, 2 * key_width), jnp.bfloat16),
+            jax.ShapeDtypeStruct((total_rows, key_width), jnp.bfloat16),
+            jax.ShapeDtypeStruct((total_rows, key_width), jnp.bfloat16),
         ),
         in_specs=[pl.BlockSpec(memory_space=pltpu.SMEM)] + [VMEM] * 7,
-        out_specs=(VMEM,) * 2,
+        out_specs=(VMEM,) * 3,
         scratch_shapes=[
             pltpu.VMEM((key_width, heads * rows), jnp.bfloat16),
             pltpu.VMEM((key_width, heads * rows), jnp.bfloat16),
@@ -773,20 +951,24 @@
             blocks = blocks[:half]
         return parts + blocks, bits
 
-    def begin_sum(rows, columns):
-        flow = {"rows": rows[0], "bits": rows[1], "columns": columns, "got": []}
+    def begin_sum(*parts):
+        flow = {"parts": parts, "bits": parts[0][0][1], "got": []}
         settle(flow)
         return flow
 
     def settle(flow):
         step = len(flow["got"])
-        part = flow["rows"][step]
-        total = jnp.einsum(
-            "bdt,btf->bdf", part, flow["columns"], preferred_element_type=jnp.float32
-        )
-        first = part.shape[1] if step < len(flow["bits"]) else 0
+        gradients = [
+            jnp.einsum(
+                "bdt,btf->bdf", rows[0][step], columns, preferred_element_type=jnp.float32
+            )
+            for rows, columns in flow["parts"]
+        ]
+        total = gradients[0] if len(gradients) == 1 else jnp.concatenate(gradients, axis=2)
+        count = total.shape[1]
+        first = count if step < len(flow["bits"]) else 0
         for got in flow["got"]:
-            total = total + got[:, first : first + part.shape[1]].astype(jnp.float32)
+            total = total + got[:, first : first + count].astype(jnp.float32)
         if step == len(flow["bits"]):
             flow["total"] = total
             return
@@ -876,12 +1058,18 @@
     queries = to_low(product(normed_three, attn_query))
     key_rows = to_low(product(normed_three, attn_key))
     value_rows = to_low(product(normed_three, attn_value))
-    both_rows = seq_gather(jnp.concatenate([key_rows, value_rows], axis=1), next(numbers))
     key_width = key_rows.shape[1]
     own_place = lax.axis_index("seq").reshape(1)
     key_docs = document_ids[:, None]
     query_docs = local_docs[None, :]
-    attended_low, attended, log_sum = attend(own_place, queries, both_rows, key_docs, query_docs)
+    attended_low, attended, log_sum, both_rows = attend(
+        queries,
+        jnp.concatenate([key_rows, value_rows], axis=1),
+        key_docs,
+        query_docs,
+        next(numbers),
+    )
+    both_rows = both_rows.reshape(total_rows, -1)
     hidden_three = hidden_two + branch_sum(product(attended_low, attn_output))
     gain_moe = norm_moe.astype(jnp.float32)
     normed_four = to_low(rms_scale(hidden_three, gain_moe))
@@ -933,9 +1121,11 @@
     ).astype(jnp.float32)
     gating_grad = to_low(act_back * up_four * silu_slope(gate_four))
     upward_grad = to_low(act_back * jax.nn.silu(gate_four))
-    flow_expert_down = begin_sum(by_owner(res_grad, along_first), expert_act)
+    flow_expert_down = begin_sum((by_owner(res_grad, along_first), expert_act))
     expert_rows = by_owner(expert_in, across_first)
-    flow_expert_in = begin_sum(expert_rows, jnp.concatenate([gating_grad, upward_grad], axis=2))
+    flow_expert_in = begin_sum(
+        (expert_rows, jnp.concatenate([gating_grad, upward_grad], axis=2))
+    )
     slot_grads = (
         jnp.einsum("ecf,edf->ecd", gating_grad, expert_gate, preferred_element_type=jnp.float32)
         + jnp.einsum("ecf,edf->ecd", upward_grad, expert_up, preferred_element_type=jnp.float32)
@@ -944,12 +1134,11 @@
     model_width = tokens.shape[1]
     expert_sums = branch_sum(
         jnp.concatenate(
-            [combined, token_part, jnp.pad(dots_part, ((0, 0), (0, LANES - 2)))], axis=1
+            [token_part, jnp.pad(dots_part, ((0, 0), (0, LANES - 2)))], axis=1
         )
     )
-    mixed_out = to_low(hidden_three + expert_sums[:, :model_width])
-    normed_grad = expert_sums[:, model_width : 2 * model_width]
-    dots = expert_sums[:, 2 * model_width : 2 * model_width + 2]
+    normed_grad = expert_sums[:, :model_width]
+    dots = expert_sums[:, model_width : model_width + 2]
     chosen_grad = gate_weights * (dots - jnp.sum(gate_weights * dots, axis=1, keepdims=True))
     logit_grad = jnp.sum(named * chosen_grad[:, :, None], axis=1)
     grad_router = exact_product(normed_four.astype(jnp.float32).T, logit_grad)
@@ -957,46 +1146,44 @@
     hidden_grad, grad_norm_moe = rms_back(hidden_three, gain_moe, normed_grad)
     three_grad = upstream + hidden_grad
     branch_grad = to_low(three_grad)
-    flow_attn_output = begin_sum(by_owner(branch_grad[None], across_first), attended_low[None])
+    attn_out_rows = by_owner(branch_grad[None], across_first)
     attended_grad = to_low(product(branch_grad, attn_output.T))
-    attended_grad = after(attended_grad, flow_expert_down)
-    query_grad, both_grads = attend_back(
+    query_grad, key_part, value_part = attend_back(
         own_place, queries, attended_grad, both_rows, key_docs, query_docs, attended, log_sum
     )
-    both_grads = after(
-        both_grads,
-        flow_expert_in,
-    )
-    (both_sums,) = seq_scatter([both_grads], next(numbers))
-    key_sum, value_sum = both_sums[:, :key_width], both_sums[:, key_width:]
+    key_part = hold(key_part, flow_expert_down, flow_expert_in)
+    key_sum, value_sum, combined_sum = scatter_and_head_sum(
+        [key_part, value_part], combined, next(numbers)
+    )
+    mixed_out = to_low(hidden_three + combined_sum)
+    key_sum, attended_late = lax.optimization_barrier((key_sum, attended_low))
+    key_sum = after(key_sum, flow_expert_down, flow_expert_in)
     key_grad = to_low(key_sum)
     value_grad = to_low(value_sum)
-    flow_attn_in = begin_sum(
-        by_owner(normed_three[None], across_first),
-        jnp.concatenate([query_grad, key_grad, value_grad], axis=1)[None],
+    flow_attn = begin_sum(
+        (
+            by_owner(normed_three[None], across_first),
+            jnp.concatenate([query_grad, key_grad, value_grad], axis=1)[None],
+        ),
+        (attn_out_rows, attended_late[None]),
     )
     normed_part = (
         product(query_grad, attn_query.T)
         + product(key_grad, attn_key.T)
         + product(value_grad, attn_value.T)
     )
-    normed_part = after(normed_part, flow_expert_down, flow_attn_output)
     normed_grad = branch_sum(normed_part)
     hidden_grad, grad_norm_attn = rms_back(hidden_two, gain_attn, normed_grad)
     two_grad = three_grad + hidden_grad
     branch_grad = to_low(two_grad)
-    flow_ffn_down = begin_sum(by_owner(branch_grad[None], along_first), ffn_act[None])
-    ffn_back = to_low(product(branch_grad, ffn_down.T)).astype(jnp.float32)
+    flow_ffn_down = begin_sum((by_owner(branch_grad[None], along_first), ffn_act[None]))
+    ffn_back = to_low(product(branch_grad, ffn_down.T))
+    ffn_back = after(ffn_back, flow_expert_down, flow_expert_in, flow_attn).astype(jnp.float32)
     feed_gate_grad = to_low(ffn_back * up_two * silu_slope(gate_two))
     feed_up_grad = to_low(ffn_back * jax.nn.silu(gate_two))
     feed_rows = by_owner(normed_two[None], across_first)
-    flow_ffn_in = begin_sum(
-        feed_rows, jnp.concatenate([feed_gate_grad, feed_up_grad], axis=1)[None]
-    )
+    flow_ffn_gate = begin_sum((feed_rows, feed_gate_grad[None]))
     normed_part = product(feed_gate_grad, ffn_gate.T) + product(feed_up_grad, ffn_up.T)
-    normed_part = after(
-        normed_part, flow_expert_in, flow_expert_down, flow_attn_in, flow_attn_output
-    )
     normed_grad = branch_sum(normed_part)
     hidden_grad, grad_norm_ffn = rms_back(hidden_one, gain_ffn, normed_grad)
     one_grad = two_grad + hidden_grad
@@ -1006,16 +1193,15 @@
     scan_grad = gated_grad * gate_act
     gate_in_grad = to_low(gated_grad * mixed_state * silu_slope(gate_in))
     grad_skip_gain = jnp.sum(scan_grad * activated, axis=0)
-    scan_grad = hold(
-        scan_grad, flow_expert_in, flow_attn_in, flow_attn_output, flow_ffn_down, flow_ffn_in
-    )
+    early_flows = (flow_expert_down, flow_expert_in, flow_attn, flow_ffn_down, flow_ffn_gate)
+    scan_grad = hold(scan_grad, *early_flows)
     state_after = run_summary(steps, scan_grad, readout_wide, slopes, next(numbers), False)
-    state_after, gated_late, gate_grad_late = lax.optimization_barrier(
-        (state_after, gated, gate_in_grad)
-    )
-    state_after = after(state_after, flow_attn_in, flow_ffn_down, flow_ffn_in)
-    flow_mixer_out = begin_sum(mixer_out_rows, gated_late[None])
-    flow_mixer_gate = begin_sum(by_owner(normed_one[None], across_first), gate_grad_late[None])
+    state_after, gate_grad_late, feed_up_late = lax.optimization_barrier(
+        (state_after, gate_in_grad, feed_up_grad)
+    )
+    state_after = after(state_after, flow_attn, flow_ffn_down, flow_ffn_gate)
+    flow_ffn_up = begin_sum((feed_rows, feed_up_late[None]))
+    flow_mixer_gate = begin_sum((by_owner(normed_one[None], along_first), gate_grad_late[None]))
     through_sum, injected, inject_part, readout_part, rate_sum = adjoint_sweep(
         state_after,
         state_out,
@@ -1037,13 +1223,18 @@
     pre_low = to_low(pre_grad)
     grad_step_proj = product(step_low.T, pre_low)
     proj_part = jnp.concatenate([product(pre_low, step_proj.T), inject_grad, readout_grad], axis=1)
-    proj_part = after(proj_part, flow_attn_in, flow_ffn_down)
+    proj_part, gated_late = lax.optimization_barrier((proj_part, gated))
+    proj_part = after(proj_part, flow_ffn_down, flow_ffn_gate, flow_attn)
+    flow_mixer_out = begin_sum((mixer_out_rows, gated_late[None]))
     proj_low = to_low(head_sum(proj_part, next(numbers), jnp.float32, 1))
+    proj_low = after(proj_low, flow_ffn_up, flow_mixer_gate)
     grad_state_proj = product(act_low.T, proj_low)
     act_total = input_grad + skipping * scan_grad + product(proj_low, state_proj.T)
     conv_grad = act_total * silu_slope(conv_sum)
+    conv_grad = after(conv_grad, flow_ffn_down, flow_ffn_gate)
     grad_conv_bias = jnp.sum(conv_grad, axis=0)
     after_edge = from_behind(conv_grad[:reach], "seq", -1)
+    after_edge = after(after_edge, flow_mixer_out, flow_mixer_gate, flow_ffn_up)
     grad_ext = jnp.concatenate([conv_grad, after_edge])
     docs_next = jnp.concatenate([local_docs, docs_after])
     conv_in_grad = jnp.zeros_like(conv_grad)
@@ -1057,12 +1248,9 @@
         conv_in_grad = conv_in_grad + taps[offset] * grad_ext[lead : lead + row_count] * same_next
     grad_conv_taps = jnp.stack(tap_rows)
     conv_low = to_low(conv_in_grad)
+    inner_half = conv_low.shape[1] // 2
     grad_mixer_inner = to_low(product(normed_one.T, conv_low))
     normed_part = product(conv_low, mixer_inner.T) + product(gate_in_grad, mixer_gate.T)
-    normed_part = after(normed_part, flow_ffn_in, flow_mixer_out)
-    normed_grad = branch_sum(normed_part)
-    hidden_grad, grad_norm_mixer = rms_back(tokens, gain_mixer, normed_grad)
-    grad_tokens = one_grad + hidden_grad
     own_channels = grad_conv_bias.shape[0] // seq_count
 
     def cut(values, axis):
@@ -1071,7 +1259,6 @@
 
     packed = jnp.concatenate(
         [
-            cut(grad_norm_mixer, 0),
             cut(grad_norm_ffn, 0),
             cut(grad_norm_attn, 0),
             cut(grad_norm_moe, 0),
@@ -1088,22 +1275,23 @@
     )
     spare = -packed.shape[1] % (16 * LANES)
     packed = to_low(jnp.pad(packed, ((0, 0), (0, spare)))).reshape(-1, LANES)
-    packed = after(packed, flow_mixer_gate, flow_mixer_out, flow_ffn_in)
-    inner_half = grad_mixer_inner.shape[1] // 2
-    first_inner, second_inner, sum_packed = seq_scatter(
+    packed = after(packed, flow_mixer_out)
+    first_inner, second_inner, sum_packed, grad_tokens, grad_norm_mixer = last_sums(
         [grad_mixer_inner[:, :inner_half], grad_mixer_inner[:, inner_half:], packed],
+        normed_part,
+        tokens_in,
+        gain_mixer[None, :],
+        one_grad,
         next(numbers),
     )
-    sum_attn_in = finished(flow_attn_in)[0]
-    sum_ffn_in = finished(flow_ffn_in)[0]
+    sum_attn = finished(flow_attn)[0]
     sum_expert_in = finished(flow_expert_in)
     expert_width = expert_gate.shape[2]
-    feed_width = ffn_gate.shape[1]
     sum_packed = sum_packed.reshape(-1)
     own_rows = model_width // seq_count
     taken = itertools.accumulate(
         [0]
-        + [own_rows] * 4
+        + [own_rows] * 3
         + [own_rows * expert_count]
         + [own_channels * (reach + 1), own_channels, own_channels * state_proj.shape[1]]
         + [own_channels * rank_size, own_channels, own_channels * state_size, own_channels]
@@ -1115,28 +1303,28 @@
     return (
         mixed_out,
         grad_tokens,
-        pieces[0],
+        lax.dynamic_slice_in_dim(grad_norm_mixer[0], me * own_rows, own_rows),
         jnp.concatenate([first_inner, second_inner], axis=1),
         finished(flow_mixer_gate)[0],
-        pieces[5].reshape(own_channels, -1).T,
-        pieces[6],
-        pieces[7].reshape(own_channels, -1),
-        pieces[8].reshape(own_channels, -1).T,
-        pieces[9],
-        pieces[10].reshape(own_channels, -1),
-        pieces[11],
+        pieces[4].reshape(own_channels, -1).T,
+        pieces[5],
+        pieces[6].reshape(own_channels, -1),
+        pieces[7].reshape(own_channels, -1).T,
+        pieces[8],
+        pieces[9].reshape(own_channels, -1),
+        pieces[10],
         finished(flow_mixer_out)[0].T,
+        pieces[0],
+        finished(flow_ffn_gate)[0],
+        finished(flow_ffn_up)[0],
+        finished(flow_ffn_down)[0].T,
         pieces[1],
-        sum_ffn_in[:, :feed_width],
-        sum_ffn_in[:, feed_width:],
-        finished(flow_ffn_down)[0].T,
+        sum_attn[:, :query_width],
+        sum_attn[:, query_width : query_width + key_width],
+        sum_attn[:, query_width + key_width : query_width + 2 * key_width],
+        sum_attn[:, query_width + 2 * key_width :].T,
         pieces[2],
-        sum_attn_in[:, :query_width],
-        sum_attn_in[:, query_width : query_width + key_width],
-        sum_attn_in[:, query_width + key_width :],
-        finished(flow_attn_output)[0].T,
-        pieces[3],
-        pieces[4].reshape(own_rows, -1),
+        pieces[3].reshape(own_rows, -1),
         sum_expert_in[:, :, :expert_width],
         sum_expert_in[:, :, expert_width:],
         finished(flow_expert_down).transpose(0, 2, 1),

time: 762 us -> 703 us (0.923)
  Pallas kernels: 347 us -> 285 us
  waiting for transfers between devices: 71.9 us -> 90.3 us
  starting transfers between devices: 47.1 us -> 31.4 us
    pallas_call x3 -> x2, Pallas kernels: 136 us -> 82.7 us  [the longest x1 53.2 us: last_sums(): pl.pallas_call(kernel, out_shape=[jax.ShapeDtypeStruct(shape, jnp.float32...]
    pallas_call x9 -> x8, Pallas kernels: 141 us -> 114 us  [head_sum(): pl.pallas_call(kernel, out_shape=jax.ShapeDtypeStruct((rows, width), jnp....]
    pallas_call x1, Pallas kernels: 5.03 us -> 24.6 us  [attend(): pl.pallas_call(kernel, out_shape=(jax.ShapeDtypeStruct((rows, width), jnp...]
    ppermute x24, starting transfers between devices: 40.1 us -> 24.4 us  [settle(): flow['got'].append(lax.ppermute(to_low(total), 'seq', route))]
    ppermute x24, waiting for transfers between devices: 66.1 us -> 80.5 us  [settle(): flow['got'].append(lax.ppermute(to_low(total), 'seq', route))]
    unnamed x463 -> x403, local copies, waits for them, and re-layouts: 18.1 us -> 24.8 us
    dot_general x32 -> x36, matrix products: 73.5 us -> 78.5 us  [settle(): jnp.einsum('bdt,btf->bdf', rows[0][step], columns, preferred_element_type...]
    convert_element_type x9 -> x14, other arithmetic: 11.9 us -> 16.4 us  [to_low(): return values.astype(jnp.bfloat16)]
  transfers between devices with their start and end apart: 26 -> 26, of which waited for: 7 -> 10; matrix products, arithmetic and copies ran while one was open for 24% -> 25% of each run, Pallas kernels for 23% -> 9%
where the time goes in v4:
time: 703 us; the launch traced here: 696 us
  Pallas kernels  285 us (41%)
  matrix products  132 us (19%)
  waiting for transfers between devices  90.3 us (13%)
  other arithmetic  77.7 us (11%)
  local copies, waits for them, and re-layouts  76.2 us (11%)
  starting transfers between devices  31.4 us (4%)
    pallas_call x8, Pallas kernels, head_sum(): pl.pallas_call(kernel, out_shape=jax.ShapeDtypeStruct((rows, width), jnp....  114 us
    ppermute x24, waiting for transfers between devices, settle(): flow['got'].append(lax.ppermute(to_low(total), 'seq', route))  80.5 us
    dot_general x36, matrix products, settle(): jnp.einsum('bdt,btf->bdf', rows[0][step], columns, preferred_element_type...  78.5 us
    pallas_call x1, Pallas kernels, last_sums(): pl.pallas_call(kernel, out_shape=[jax.ShapeDtypeStruct(shape, jnp.float32...  53.2 us
    dot_general x32, matrix products, product(): return jnp.dot(left, right, preferred_element_type=jnp.float32)  44.7 us
    pallas_call x2, Pallas kernels, run_summary(): pl.pallas_call(kernel, out_shape=jax.ShapeDtypeStruct((entries, width), j...  31.4 us
    pallas_call x1, Pallas kernels, scatter_and_head_sum(): pl.pallas_call(kernel, out_shape=[jax.ShapeDtypeStruct(shape, jnp.float32...  29.5 us
    unnamed x403, local copies, waits for them, and re-layouts  24.8 us
  transfers between devices with their start and end apart: 26, of which 10 were waited for; matrix products, arithmetic and copies ran while one was open for 25% of the time, Pallas kernels for 9%

profile of v4, /device:TPU:0, one launch (start us, length us, event | category | flops | bytes accessed | tf_op | source)
XLA Modules:
  0.0 695.6 jit_solution(14566647201532397150)
XLA Ops:
  6.0 5.5 collective-permute-start
  35.7 8.1 %head_sum.8 = f32[256,128]{1,0:T(8,128)} custom-call(f32[256,128]{1,0:T(8,128)} %fusion.125.x_ref), custom_call_target="tpu_custom_call" | custom-call | flops 6000 | bytes 6000 | tf_op jit(solution)/shard_map/head_sum/pallas_call | solution.py:173
  44.9 3.4 fusion.164
  50.3 15.7 %run_summary.2.init_ref = f32[16,768]{1,0:T(8,128)} custom-call(f32[256,768]{1,0:T(8,128)} %get-tuple-element.422.step_ref, f32[256,768]{1,0:T(8,128)} %get-tuple-element.421.drive_ref, f32[256,16,128]{2,1,0:T(8,128)} %broadcast_in_dim.69.coef_ref.inject_ref, f32[16,768]{1,0:T(8,128)} %bitcast_multiply_fusion.3.slope_ref), custom_call_target="tpu_custom_call" | custom-call | flops 16000 | bytes 16000 | tf_op jit(solution)/shard_map/run_summary/pallas_call | solution.py:488
  68.0 11.2 %state_sweep.1 = (f32[256,768]{1,0:T(8,128)}, f32[256,16,768]{2,1,0:T(8,128)}, f32[16,768]{1,0:T(8,128)}) custom-call(f32[16,768]{1,0:T(8,128)} %run_summary.2.init_ref, f32[256,768]{1,0:T(8,128)} %get-tuple-element.422.step_ref, f32[256,768]{1,0:T(8,128)} %get-tuple-element.421.drive_ref, f32[256,16,128]{2,1,0:T(8,128)} %broadcast_in_dim.69.coef_ref.inject_ref, ...), custom_call_target="tpu_custom_call" | custom-call | flops 11000 | bytes 11000 | tf_op jit(solution)/shard_map/state_sweep/pallas_call | solution.py:539
  84.1 15.7 %head_sum.9 = f32[256,1536]{1,0:T(8,128)} custom-call(f32[256,1536]{1,0:T(8,128)} %fusion.223.x_ref), custom_call_target="tpu_custom_call" | custom-call | flops 15000 | bytes 15000 | tf_op jit(solution)/shard_map/head_sum/pallas_call | solution.py:173
  109.5 16.7 %head_sum.10 = f32[256,1536]{1,0:T(8,128)} custom-call(f32[256,1536]{1,0:T(8,128)} %fusion.225.x_ref), custom_call_target="tpu_custom_call" | custom-call | flops 15000 | bytes 15000 | tf_op jit(solution)/shard_map/head_sum/pallas_call | solution.py:173
  132.7 24.6 %attend.1 = (bf16[256,384]{1,0:T(8,128)(2,1)}, f32[128,1536]{1,0:T(8,128)}, f32[1,1536]{1,0:T(1,128)}, bf16[8,256,256]{2,1,0:T(8,128)(2,1)}) custom-call(bf16[256,384]{1,0:T(8,128)(2,1)} %convolution_convert_fusion.17.q_ref, bf16[256,256]{1,0:T(8,128)(2,1)} %pad_maximum_fusion.4.x_ref, s32[2048,1]{1,0:T(8,128)} %copy.191.kd_ref, s32[1,256]{1,0:T(1,128)} %bitcast.585), custom_call_target="tpu_custom_call" | custom-call | flops 12000 | bytes 12000 | tf_op jit(solution)/shard_map/attend/pallas_call | solution.py:804
  160.0 15.8 %head_sum.11 = f32[256,1536]{1,0:T(8,128)} custom-call(f32[256,1536]{1,0:T(8,128)} %fusion.226.x_ref), custom_call_target="tpu_custom_call" | custom-call | flops 15000 | bytes 15000 | tf_op jit(solution)/shard_map/head_sum/pallas_call | solution.py:173
  196.8 3.2 convolution_convert_fusion.2
  210.2 17.4 %head_sum.12 = f32[256,1664]{1,0:T(8,128)} custom-call(f32[256,1664]{1,0:T(8,128)} %select_maximum_fusion.x_ref), custom_call_target="tpu_custom_call" | custom-call | flops 16000 | bytes 16000 | tf_op jit(solution)/shard_map/head_sum/pallas_call | solution.py:173
  235.8 5.1 attend_back.1
  248.1 3.1 fusion.97
  254.7 15.8 %collective-permute-done.2 = bf16[4,768,512]{2,1,0:T(8,128)(2,1)} collective-permute-done((bf16[4,768,512]{2,1,0:T(8,128)(2,1)}, bf16[4,768,512]{2,1,0:T(8,128)(2,1)}, u32[]{:S(2)}, u32[]{:S(2)}) %collective-permute-start.2) | collective-permute-done | bytes 3145760 | tf_op jit(solution)/shard_map/ppermute | solution.py:977
  270.5 29.5 %scatter_and_head_sum.1 = (f32[256,128]{1,0:T(8,128)}, f32[256,128]{1,0:T(8,128)}, f32[256,1536]{1,0:T(8,128)}) custom-call(bf16[4,2,256,128]{3,2,1,0:T(8,128)(2,1)} %bitcast.567, bf16[4,2,256,128]{3,2,1,0:T(8,128)(2,1)} %bitcast.568, f32[256,1536]{1,0:T(8,128)} %fusion.104.refs_2_), custom_call_target="tpu_custom_call" | custom-call | flops 20000 | bytes 20000 | tf_op jit(solution)/shard_map/scatter_and_head_sum/pallas_call | solution.py:315
  305.3 3.6 add_convert_fusion.1
  316.0 16.6 %head_sum.13 = f32[256,1536]{1,0:T(8,128)} custom-call(f32[256,1536]{1,0:T(8,128)} %convolution_add_fusion.3.x_ref), custom_call_target="tpu_custom_call" | custom-call | flops 15000 | bytes 15000 | tf_op jit(solution)/shard_map/head_sum/pallas_call | solution.py:173
  353.2 3.9 collective-permute-done.3
  366.7 3.5 add_convert_fusion.2
  377.8 16.6 %head_sum.14 = f32[256,1536]{1,0:T(8,128)} custom-call(f32[256,1536]{1,0:T(8,128)} %convolution_add_fusion.x_ref), custom_call_target="tpu_custom_call" | custom-call | flops 15000 | bytes 15000 | tf_op jit(solution)/shard_map/head_sum/pallas_call | solution.py:173
  403.5 6.3 collective-permute-done.9
  409.8 14.5 %collective-permute-done.6 = bf16[4,192,256]{2,1,0:T(8,128)(2,1)S(1)} collective-permute-done((bf16[4,192,256]{2,1,0:T(8,128)(2,1)}, bf16[4,192,256]{2,1,0:T(8,128)(2,1)S(1)}, u32[]{:S(2)}, u32[]{:S(2)}) %collective-permute-start.6) | collective-permute-done | bytes 393248 | tf_op jit(solution)/shard_map/ppermute | solution.py:977
  426.2 15.7 %run_summary.3.in_ref = f32[16,768]{1,0:T(8,128)} custom-call(f32[256,768]{1,0:T(8,128)} %get-tuple-element.422.step_ref, f32[256,768]{1,0:T(8,128)} %get-tuple-element.117.drive_ref.up_ref, f32[256,16,128]{2,1,0:T(8,128)} %broadcast_in_dim.70.read_ref.coef_ref, f32[16,768]{1,0:T(8,128)} %bitcast_multiply_fusion.3.slope_ref), custom_call_target="tpu_custom_call" | custom-call | flops 16000 | bytes 16000 | tf_op jit(solution)/shard_map/run_summary/pallas_call | solution.py:488
  446.1 15.4 %adjoint_sweep.1 = (f32[256,768]{1,0:T(8,128)}, f32[256,768]{1,0:T(8,128)}, f32[256,16,128]{2,1,0:T(8,128)}, f32[256,16,128]{2,1,0:T(8,128)}, f32[16,768]{1,0:T(8,128)}) custom-call(f32[16,768]{1,0:T(8,128)} %run_summary.3.in_ref, f32[16,768]{1,0:T(8,128)} %get-tuple-element.123.last_ref, f32[256,16,768]{2,1,0:T(8,128)} %get-tuple-element.124.before_ref, ...), custom_call_target="tpu_custom_call" | custom-call | flops 15000 | bytes 15000 | tf_op jit(solution)/shard_map/adjoint_sweep/pallas_call | solution.py:624
  522.6 7.6 %head_sum.15 = f32[256,128]{1,0:T(8,128)} custom-call(f32[256,128]{1,0:T(8,128)} %pad_maximum_fusion.5.x_ref), custom_call_target="tpu_custom_call" | custom-call | flops 6000 | bytes 6000 | tf_op jit(solution)/shard_map/head_sum/pallas_call | solution.py:173
  534.5 6.6 collective-permute-done.15
  543.7 5.7 collective-permute-done.16
  562.0 9.8 %collective-permute-done.18 = f32[3,768]{1,0:T(4,128)S(1)} collective-permute-done((f32[3,768]{1,0:T(4,128)S(1)}, f32[3,768]{1,0:T(4,128)S(1)}, u32[]{:S(2)}, u32[]{:S(2)}) %collective-permute-start.18) | collective-permute-done | bytes 9248 | tf_op jit(solution)/shard_map/ppermute | solution.py:31
  591.9 17.7 %collective-permute-done.23 = bf16[1,192,768]{2,1,0:T(8,128)(2,1)} collective-permute-done((bf16[1,192,768]{2,1,0:T(8,128)(2,1)}, bf16[1,192,768]{2,1,0:T(8,128)(2,1)}, u32[]{:S(2)}, u32[]{:S(2)}) %collective-permute-start.23) | collective-permute-done | bytes 294944 | tf_op jit(solution)/shard_map/ppermute | solution.py:977
  614.0 53.2 %last_sums.1 = (f32[192,384]{1,0:T(8,128)}, f32[192,384]{1,0:T(8,128)}, f32[208,128]{1,0:T(8,128)}, f32[256,1536]{1,0:T(8,128)}, f32[1,1536]{1,0:T(1,128)}) custom-call(bf16[4,2,192,384]{3,2,1,0:T(8,128)(2,1)} %bitcast.564, bf16[4,2,192,384]{3,2,1,0:T(8,128)(2,1)} %bitcast.563, bf16[4,2,208,128]{3,2,1,0:T(8,128)(2,1)} %bitcast.565, ...), custom_call_target="tpu_custom_call" | custom-call | flops 20000 | bytes 20000 | tf_op jit(solution)/shard_map/last_sums/pallas_call | solution.py:383
  667.2 5.5 slice.335
  682.8 8.1 %collective-permute-done.24 = bf16[1,192,768]{2,1,0:T(8,128)(2,1)S(1)} collective-permute-done((bf16[1,192,768]{2,1,0:T(8,128)(2,1)S(1)}, bf16[1,192,768]{2,1,0:T(8,128)(2,1)S(1)}, u32[]{:S(2)}, u32[]{:S(2)}) %collective-permute-start.24) | collective-permute-done | bytes 294944 | tf_op jit(solution)/shard_map/ppermute | solution.py:977
  (657 shorter events, 291.6 us)
Async XLA Ops:
  0.7 186.2 %copy-start = (bf16[4,256,1536]{2,1,0:T(8,128)(2,1)S(1)}, bf16[4,256,1536]{2,1,0:T(8,128)(2,1)}, u32[]{:S(2)}) copy-start(bf16[4,256,1536]{2,1,0:T(8,128)(2,1)} %param.59) | copy-start | bytes 9437188
  6.0 25.0 %collective-permute-start = (bf16[3,768]{1,0:T(4,128)(2,1)}, bf16[3,768]{1,0:T(4,128)(2,1)}, u32[]{:S(2)}, u32[]{:S(2)}) collective-permute-start(bf16[3,768]{1,0:T(4,128)(2,1)} %slice.376), channel_id=1, source_target_pairs={{0,4},{4,8},{8,12},{12,16},{16,20},{20,24},{24,28},{1,5},{5,9},{9,... | collective-permute-start | bytes 13832 | tf_op jit(solution)/shard_map/ppermute | solution.py:31
  177.6 55.1 %copy-start.165 = (f32[256]{0:T(256)}, f32[256]{0:T(256)S(1)}, u32[]{:S(2)}) copy-start(f32[256]{0:T(256)S(1)} %fusion.187) | copy-start | bytes 3076
  200.0 70.5 %collective-permute-start.2 = (bf16[4,768,512]{2,1,0:T(8,128)(2,1)}, bf16[4,768,512]{2,1,0:T(8,128)(2,1)}, u32[]{:S(2)}, u32[]{:S(2)}) collective-permute-start(bf16[4,768,512]{2,1,0:T(8,128)(2,1)} %convolution_convert_fusion.2), channel_id=1, source_target_pairs={{0,4},{4,0},{8,12},{12,8},{16,20},{20,16},{24,28},{28,24},{1,5},{5... | collective-permute-start | bytes 9437192 | tf_op jit(solution)/shard_map/ppermute | solution.py:977
  209.7 45.1 %collective-permute-start.1 = (bf16[4,768,256]{2,1,0:T(8,128)(2,1)}, bf16[4,768,256]{2,1,0:T(8,128)(2,1)}, u32[]{:S(2)}, u32[]{:S(2)}) collective-permute-start(bf16[4,768,256]{2,1,0:T(8,128)(2,1)} %convolution_convert_fusion.7), channel_id=1, source_target_pairs={{0,8},{4,12},{8,0},{12,4},{16,24},{20,28},{24,16},{28,20},{1,9},{5... | collective-permute-start | bytes 4718600 | tf_op jit(solution)/shard_map/ppermute | solution.py:977
  254.7 47.2 %copy-start.53 = (bf16[256,384]{1,0:T(8,128)(2,1)S(1)}, bf16[256,384]{1,0:T(8,128)(2,1)}, u32[]{:S(2)}) copy-start(bf16[256,384]{1,0:T(8,128)(2,1)} %get-tuple-element.112) | copy-start | bytes 589828
  254.7 47.2 %copy-start.145 = (bf16[1,192,256]{1,2,0:T(8,128)(2,1)S(1)}, bf16[1,192,256]{1,2,0:T(8,128)(2,1)}, u32[]{:S(2)}) copy-start(bf16[1,192,256]{1,2,0:T(8,128)(2,1)} %get-tuple-element.419) | copy-start | bytes 294916
  254.7 47.2 %copy-start.146 = (bf16[1,192,256]{1,2,0:T(8,128)(2,1)S(1)}, bf16[1,192,256]{1,2,0:T(8,128)(2,1)}, u32[]{:S(2)}) copy-start(bf16[1,192,256]{1,2,0:T(8,128)(2,1)} %get-tuple-element.420) | copy-start | bytes 294916
  304.3 52.8 %collective-permute-start.5 = (bf16[1,768,1024]{1,2,0:T(8,128)(2,1)}, bf16[1,768,1024]{1,2,0:T(8,128)(2,1)}, u32[]{:S(2)}, u32[]{:S(2)}) collective-permute-start(bf16[1,768,1024]{1,2,0:T(8,128)(2,1)} %pad_maximum_fusion), channel_id=1, source_target_pairs={{0,4},{4,0},{8,12},{12,8},{16,20},{20,16},{24,28},{28,24},{1,5},{5... | collective-permute-start | bytes 4718600 | tf_op jit(solution)/shard_map/ppermute | solution.py:977
  308.8 48.3 %collective-permute-start.4 = (bf16[4,384,512]{2,1,0:T(8,128)(2,1)}, bf16[4,384,512]{2,1,0:T(8,128)(2,1)}, u32[]{:S(2)}, u32[]{:S(2)}) collective-permute-start(bf16[4,384,512]{2,1,0:T(8,128)(2,1)} %add_convert_fusion.1), channel_id=1, source_target_pairs={{0,8},{4,12},{8,0},{12,4},{16,24},{20,28},{24,16},{28,20},{1,9},{5... | collective-permute-start | bytes 4718600 | tf_op jit(solution)/shard_map/ppermute | solution.py:977
  314.8 42.3 %collective-permute-start.3 = (bf16[4,384,256]{2,1,0:T(8,128)(2,1)}, bf16[4,384,256]{2,1,0:T(8,128)(2,1)}, u32[]{:S(2)}, u32[]{:S(2)}) collective-permute-start(bf16[4,384,256]{2,1,0:T(8,128)(2,1)} %add_convert_fusion.3), channel_id=1, source_target_pairs={{0,4},{4,0},{8,12},{12,8},{16,20},{20,16},{24,28},{28,24},{1,5},{5... | collective-permute-start | bytes 2359304 | tf_op jit(solution)/shard_map/ppermute | solution.py:977
  347.0 62.8 %collective-permute-start.9 = (bf16[1,768,1024]{2,1,0:T(8,128)(2,1)}, bf16[1,768,1024]{2,1,0:T(8,128)(2,1)}, u32[]{:S(2)}, u32[]{:S(2)}) collective-permute-start(bf16[1,768,1024]{2,1,0:T(8,128)(2,1)} %fusion.12), channel_id=1, source_target_pairs={{0,8},{4,12},{8,0},{12,4},{16,24},{20,28},{24,16},{28,20},{1,9},{5... | collective-permute-start | bytes 4718600 | tf_op jit(solution)/shard_map/ppermute | solution.py:977
  362.1 64.0 %collective-permute-start.10 = (bf16[1,768,1024]{2,1,0:T(8,128)(2,1)}, bf16[1,768,1024]{2,1,0:T(8,128)(2,1)}, u32[]{:S(2)}, u32[]{:S(2)}) collective-permute-start(bf16[1,768,1024]{2,1,0:T(8,128)(2,1)} %fusion.13), channel_id=1, source_target_pairs={{0,4},{4,0},{8,12},{12,8},{16,20},{20,16},{24,28},{28,24},{1,5},{5... | collective-permute-start | bytes 4718600 | tf_op jit(solution)/shard_map/ppermute | solution.py:977
  365.3 60.8 %collective-permute-start.8 = (bf16[1,384,1024]{1,2,0:T(8,128)(2,1)}, bf16[1,384,1024]{1,2,0:T(8,128)(2,1)}, u32[]{:S(2)}, u32[]{:S(2)}) collective-permute-start(bf16[1,384,1024]{1,2,0:T(8,128)(2,1)} %fusion.8), channel_id=1, source_target_pairs={{0,8},{4,12},{8,0},{12,4},{16,24},{20,28},{24,16},{28,20},{1,9},{5... | collective-permute-start | bytes 2359304 | tf_op jit(solution)/shard_map/ppermute | solution.py:977
  370.2 55.9 %collective-permute-start.7 = (bf16[4,192,512]{2,1,0:T(8,128)(2,1)}, bf16[4,192,512]{2,1,0:T(8,128)(2,1)}, u32[]{:S(2)}, u32[]{:S(2)}) collective-permute-start(bf16[4,192,512]{2,1,0:T(8,128)(2,1)} %add_convert_fusion.2), channel_id=1, source_target_pairs={{0,16},{4,20},{8,24},{12,28},{16,0},{20,4},{24,8},{28,12},{1,17},{... | collective-permute-start | bytes 2359304 | tf_op jit(solution)/shard_map/ppermute | solution.py:977
  377.1 47.2 %collective-permute-start.6 = (bf16[4,192,256]{2,1,0:T(8,128)(2,1)}, bf16[4,192,256]{2,1,0:T(8,128)(2,1)S(1)}, u32[]{:S(2)}, u32[]{:S(2)}) collective-permute-start(bf16[4,192,256]{2,1,0:T(8,128)(2,1)} %add_convert_fusion.10), channel_id=1, source_target_pairs={{0,16},{4,20},{8,24},{12,28},{16,0},{20,4},{24,8},{28,12},{1,17},{... | collective-permute-start | bytes 1179656 | tf_op jit(solution)/shard_map/ppermute | solution.py:977
  402.1 104.0 %copy-start.44 = (bf16[256,768]{1,0:T(8,128)(2,1)}, bf16[256,768]{1,0:T(8,128)(2,1)S(1)}, u32[]{:S(2)}) copy-start(bf16[256,768]{1,0:T(8,128)(2,1)S(1)} %get-tuple-element.135) | copy-start | bytes 1179652
  471.5 39.1 %collective-permute-start.13 = (bf16[1,192,1024]{1,2,0:T(8,128)(2,1)}, bf16[1,192,1024]{1,2,0:T(8,128)(2,1)}, u32[]{:S(2)}, u32[]{:S(2)}) collective-permute-start(bf16[1,192,1024]{1,2,0:T(8,128)(2,1)} %fusion.29), channel_id=1, source_target_pairs={{0,16},{4,20},{8,24},{12,28},{16,0},{20,4},{24,8},{28,12},{1,17},{... | collective-permute-start | bytes 1179656 | tf_op jit(solution)/shard_map/ppermute | solution.py:977
  475.1 36.8 %collective-permute-start.12 = (bf16[1,384,1024]{2,1,0:T(8,128)(2,1)}, bf16[1,384,1024]{2,1,0:T(8,128)(2,1)}, u32[]{:S(2)}, u32[]{:S(2)}) collective-permute-start(bf16[1,384,1024]{2,1,0:T(8,128)(2,1)} %fusion.10), channel_id=1, source_target_pairs={{0,8},{4,12},{8,0},{12,4},{16,24},{20,28},{24,16},{28,20},{1,9},{5... | collective-permute-start | bytes 2359304 | tf_op jit(solution)/shard_map/ppermute | solution.py:977
  482.1 29.8 %collective-permute-start.11 = (bf16[1,384,1024]{2,1,0:T(8,128)(2,1)}, bf16[1,384,1024]{2,1,0:T(8,128)(2,1)}, u32[]{:S(2)}, u32[]{:S(2)}) collective-permute-start(bf16[1,384,1024]{2,1,0:T(8,128)(2,1)} %fusion.11), channel_id=1, source_target_pairs={{0,4},{4,0},{8,12},{12,8},{16,20},{20,16},{24,28},{28,24},{1,5},{5... | collective-permute-start | bytes 2359304 | tf_op jit(solution)/shard_map/ppermute | solution.py:977
  488.4 52.7 %collective-permute-start.14 = (bf16[1,768,1024]{2,1,0:T(8,128)(2,1)}, bf16[1,768,1024]{2,1,0:T(8,128)(2,1)}, u32[]{:S(2)}, u32[]{:S(2)}) collective-permute-start(bf16[1,768,1024]{2,1,0:T(8,128)(2,1)} %fusion.14), channel_id=1, source_target_pairs={{0,4},{4,0},{8,12},{12,8},{16,20},{20,16},{24,28},{28,24},{1,5},{5... | collective-permute-start | bytes 4718600 | tf_op jit(solution)/shard_map/ppermute | solution.py:977
  492.2 49.0 %collective-permute-start.15 = (bf16[1,768,768]{2,1,0:T(8,128)(2,1)}, bf16[1,768,768]{2,1,0:T(8,128)(2,1)}, u32[]{:S(2)}, u32[]{:S(2)}) collective-permute-start(bf16[1,768,768]{2,1,0:T(8,128)(2,1)} %fusion.15), channel_id=1, source_target_pairs={{0,8},{4,12},{8,0},{12,4},{16,24},{20,28},{24,16},{28,20},{1,9},{5... | collective-permute-start | bytes 3538952 | tf_op jit(solution)/shard_map/ppermute | solution.py:977
  510.6 51.4 %collective-permute-start.19 = (bf16[1,768,768]{2,1,0:T(8,128)(2,1)}, bf16[1,768,768]{2,1,0:T(8,128)(2,1)}, u32[]{:S(2)}, u32[]{:S(2)}) collective-permute-start(bf16[1,768,768]{2,1,0:T(8,128)(2,1)} %fusion.16), channel_id=1, source_target_pairs={{0,4},{4,0},{8,12},{12,8},{16,20},{20,16},{24,28},{28,24},{1,5},{5... | collective-permute-start | bytes 3538952 | tf_op jit(solution)/shard_map/ppermute | solution.py:977
  514.2 29.5 %collective-permute-start.17 = (bf16[1,192,1024]{2,1,0:T(8,128)(2,1)}, bf16[1,192,1024]{2,1,0:T(8,128)(2,1)}, u32[]{:S(2)}, u32[]{:S(2)}) collective-permute-start(bf16[1,192,1024]{2,1,0:T(8,128)(2,1)} %add_convert_fusion.8), channel_id=1, source_target_pairs={{0,16},{4,20},{8,24},{12,28},{16,0},{20,4},{24,8},{28,12},{1,17},{... | collective-permute-start | bytes 1179656 | tf_op jit(solution)/shard_map/ppermute | solution.py:977
  518.5 30.9 %collective-permute-start.16 = (bf16[1,192,1024]{2,1,0:T(8,128)(2,1)}, bf16[1,192,1024]{2,1,0:T(8,128)(2,1)}, u32[]{:S(2)}, u32[]{:S(2)}) collective-permute-start(bf16[1,192,1024]{2,1,0:T(8,128)(2,1)} %add_convert_fusion.9), channel_id=1, source_target_pairs={{0,16},{4,20},{8,24},{12,28},{16,0},{20,4},{24,8},{28,12},{1,17},{... | collective-permute-start | bytes 1179656 | tf_op jit(solution)/shard_map/ppermute | solution.py:977
  551.9 20.0 %collective-permute-start.21 = (bf16[1,384,1024]{2,1,0:T(8,128)(2,1)}, bf16[1,384,1024]{2,1,0:T(8,128)(2,1)}, u32[]{:S(2)}, u32[]{:S(2)}) collective-permute-start(bf16[1,384,1024]{2,1,0:T(8,128)(2,1)} %fusion.9), channel_id=1, source_target_pairs={{0,8},{4,12},{8,0},{12,4},{16,24},{20,28},{24,16},{28,20},{1,9},{5... | collective-permute-start | bytes 2359304 | tf_op jit(solution)/shard_map/ppermute | solution.py:977
  554.3 17.6 %collective-permute-start.20 = (bf16[1,384,768]{2,1,0:T(8,128)(2,1)}, bf16[1,384,768]{2,1,0:T(8,128)(2,1)}, u32[]{:S(2)}, u32[]{:S(2)}) collective-permute-start(bf16[1,384,768]{2,1,0:T(8,128)(2,1)} %add_convert_fusion.6), channel_id=1, source_target_pairs={{0,4},{4,0},{8,12},{12,8},{16,20},{20,16},{24,28},{28,24},{1,5},{5... | collective-permute-start | bytes 1769480 | tf_op jit(solution)/shard_map/ppermute | solution.py:977
  554.9 17.0 %collective-permute-start.18 = (f32[3,768]{1,0:T(4,128)S(1)}, f32[3,768]{1,0:T(4,128)S(1)}, u32[]{:S(2)}, u32[]{:S(2)}) collective-permute-start(f32[3,768]{1,0:T(4,128)S(1)} %slice.319), channel_id=1, source_target_pairs={{4,0},{8,4},{12,8},{16,12},{20,16},{24,20},{28,24},{5,1},{9,5},{13... | collective-permute-start | bytes 27656 | tf_op jit(solution)/shard_map/ppermute | solution.py:31
  578.7 33.0 %collective-permute-start.25 = (bf16[1,192,1024]{2,1,0:T(8,128)(2,1)}, bf16[1,192,1024]{2,1,0:T(8,128)(2,1)}, u32[]{:S(2)}, u32[]{:S(2)}) collective-permute-start(bf16[1,192,1024]{2,1,0:T(8,128)(2,1)} %add_convert_fusion.7), channel_id=1, source_target_pairs={{0,16},{4,20},{8,24},{12,28},{16,0},{20,4},{24,8},{28,12},{1,17},{... | collective-permute-start | bytes 1179656 | tf_op jit(solution)/shard_map/ppermute | solution.py:977
  582.2 31.8 %collective-permute-start.22 = (bf16[1,384,768]{2,1,0:T(8,128)(2,1)}, bf16[1,384,768]{2,1,0:T(8,128)(2,1)}, u32[]{:S(2)}, u32[]{:S(2)}) collective-permute-start(bf16[1,384,768]{2,1,0:T(8,128)(2,1)} %add_convert_fusion.5), channel_id=1, source_target_pairs={{0,8},{4,12},{8,0},{12,4},{16,24},{20,28},{24,16},{28,20},{1,9},{5... | collective-permute-start | bytes 1769480 | tf_op jit(solution)/shard_map/ppermute | solution.py:977
  584.6 24.9 %collective-permute-start.23 = (bf16[1,192,768]{2,1,0:T(8,128)(2,1)}, bf16[1,192,768]{2,1,0:T(8,128)(2,1)}, u32[]{:S(2)}, u32[]{:S(2)}) collective-permute-start(bf16[1,192,768]{2,1,0:T(8,128)(2,1)} %add_convert_fusion.12), channel_id=1, source_target_pairs={{0,16},{4,20},{8,24},{12,28},{16,0},{20,4},{24,8},{28,12},{1,17},{... | collective-permute-start | bytes 884744 | tf_op jit(solution)/shard_map/ppermute | solution.py:977
  676.5 14.5 %collective-permute-start.24 = (bf16[1,192,768]{2,1,0:T(8,128)(2,1)S(1)}, bf16[1,192,768]{2,1,0:T(8,128)(2,1)S(1)}, u32[]{:S(2)}, u32[]{:S(2)}) collective-permute-start(bf16[1,192,768]{2,1,0:T(8,128)(2,1)S(1)} %add_convert_fusion.11), channel_id=1, source_target_pairs={{0,16},{4,20},{8,24},{12,28},{16,0},{20,4},{24,8},{28,12},{1,17},{... | collective-permute-start | bytes 884744 | tf_op jit(solution)/shard_map/ppermute | solution.py:977
  (191 other events, 1269.6 us)

commit v5 on v4

--- a/solution.py
+++ b/solution.py
@@ -14,7 +14,7 @@
 LOG2E = 1.4426950408889634
 LN2 = 0.6931471805599453
 NEVER = 1e30
-LIMIT = 56 * 1024 * 1024
+MEBI = 1024 * 1024
 MESH = pl.DeviceIdType.MESH
 VMEM = pl.BlockSpec(memory_space=pltpu.VMEM)
 ANY = pl.BlockSpec(memory_space=pl.ANY)
@@ -83,9 +83,9 @@
     )
 
 
-def talking(number):
+def talking(number, mebibytes):
     return pltpu.CompilerParams(
-        collective_id=number, has_side_effects=True, vmem_limit_bytes=LIMIT
+        collective_id=number, has_side_effects=True, vmem_limit_bytes=mebibytes * MEBI
     )
 
 
@@ -176,7 +176,7 @@
         in_specs=[VMEM],
         out_specs=VMEM,
         scratch_shapes=head_scratch(rows, width, wire, pieces),
-        compiler_params=talking(number),
+        compiler_params=talking(number, 10),
         cost_estimate=lasting(6 + values.size // 40000),
         name="head_sum",
     )(values)
@@ -319,7 +319,7 @@
         in_specs=[ANY] * count + [VMEM],
         out_specs=[VMEM] * (count + 1),
         scratch_shapes=spaces + head_scratch(rows, width, jnp.bfloat16, 4),
-        compiler_params=talking(number),
+        compiler_params=talking(number, 24),
         cost_estimate=lasting(20),
         name="scatter_and_head_sum",
     )(*scatter_blocks(arrays), values)
@@ -398,7 +398,7 @@
             pltpu.SemaphoreType.DMA((seq_count - 1,)),
             pltpu.SemaphoreType.DMA((seq_count - 1,)),
         ],
-        compiler_params=talking(number),
+        compiler_params=talking(number, 28),
         cost_estimate=lasting(20),
         name="last_sums",
     )(*scatter_blocks(arrays), values, tokens, gain, upstream)
@@ -498,7 +498,7 @@
             pltpu.SemaphoreType.DMA((2, seq_count - 1)),
             pltpu.SemaphoreType.DMA((2, seq_count - 1)),
         ],
-        compiler_params=talking(number),
+        compiler_params=talking(number, 10),
         cost_estimate=lasting(16),
         name="run_summary",
     )(steps, drives, coefficients, slopes)
@@ -541,7 +541,7 @@
         grid=(rows // length,),
         out_shape=(
             jax.ShapeDtypeStruct((rows, width), jnp.float32),
-            jax.ShapeDtypeStruct((rows, entries, width), jnp.float32),
+            pltpu.HBM((rows, entries, width), jnp.float32),
             jax.ShapeDtypeStruct((entries, width), jnp.float32),
         ),
         in_specs=[fixed, row_spec, row_spec, entry_spec, entry_spec, fixed],
@@ -550,7 +550,7 @@
             pl.BlockSpec((length, entries, width), lambda i: (i, 0, 0)),
             fixed,
         ),
-        compiler_params=pltpu.CompilerParams(vmem_limit_bytes=LIMIT),
+        compiler_params=pltpu.CompilerParams(vmem_limit_bytes=12 * MEBI),
         cost_estimate=lasting(11),
         name="state_sweep",
     )(initial, steps, drives, inject, readout, slopes)
@@ -644,10 +644,20 @@
         ],
         out_specs=(row_spec, row_spec, entry_spec, entry_spec, fixed),
         scratch_shapes=[pltpu.VMEM((entries, width), jnp.float32)] * 2,
-        compiler_params=pltpu.CompilerParams(vmem_limit_bytes=LIMIT),
+        compiler_params=pltpu.CompilerParams(vmem_limit_bytes=14 * MEBI),
         cost_estimate=lasting(15),
         name="adjoint_sweep",
-    )(incoming, last_state, befores, steps, drives, inject, readout, upstream, slopes)
+    )(
+        incoming,
+        last_state,
+        pltpu.with_memory_space_constraint(befores, pltpu.HBM),
+        steps,
+        drives,
+        inject,
+        readout,
+        upstream,
+        slopes,
+    )
 
 
 def over_rows(left, right):
@@ -817,7 +827,7 @@
             pltpu.VMEM((1, heads * rows), jnp.float32),
         ]
         + [pltpu.SemaphoreType.DMA((pairs,))] * 4,
-        compiler_params=talking(number),
+        compiler_params=talking(number, 24),
         cost_estimate=lasting(12),
         name="attend",
     )(queries, both, key_docs, query_docs)
@@ -882,7 +892,7 @@
             pltpu.VMEM((key_width, heads * rows), jnp.bfloat16),
             pltpu.VMEM((key_width, heads * rows), jnp.float32),
         ],
-        compiler_params=pltpu.CompilerParams(vmem_limit_bytes=LIMIT),
+        compiler_params=pltpu.CompilerParams(vmem_limit_bytes=28 * MEBI),
         cost_estimate=lasting(20),
         name="attend_back",
     )(own, queries, upstream, both_rows, key_docs, query_docs, attended, log_sum)
@@ -952,9 +962,25 @@
         return parts + blocks, bits
 
     def begin_sum(*parts):
+        flow = prepare_sum(*parts)
+        send(flow)
+        return flow
+
+    def prepare_sum(*parts):
         flow = {"parts": parts, "bits": parts[0][0][1], "got": []}
         settle(flow)
         return flow
+
+    def send(flow):
+        bit = flow["bits"][len(flow["got"])]
+        route = [(i, i ^ (1 << bit)) for i in range(seq_count)]
+        flow["got"].append(lax.ppermute(flow["out"], "seq", route))
+
+    def bind(values, *flows):
+        tied = lax.optimization_barrier((values, *[flow["out"] for flow in flows]))
+        for flow, out in zip(flows, tied[1:], strict=True):
+            flow["out"] = out
+        return tied[0]
 
     def settle(flow):
         step = len(flow["got"])
@@ -972,9 +998,7 @@
         if step == len(flow["bits"]):
             flow["total"] = total
             return
-        bit = flow["bits"][step]
-        route = [(i, i ^ (1 << bit)) for i in range(seq_count)]
-        flow["got"].append(lax.ppermute(to_low(total), "seq", route))
+        flow["out"] = to_low(total)
 
     def hold(values, *flows):
         if flows:
@@ -988,11 +1012,15 @@
         values = hold(values, *flows)
         for flow in flows:
             settle(flow)
+            if "total" not in flow:
+                send(flow)
         return values
 
     def finished(flow):
         while "total" not in flow:
             settle(flow)
+            if "total" not in flow:
+                send(flow)
         return flow["total"]
 
     def branch_sum(values):
@@ -1194,14 +1222,17 @@
     gate_in_grad = to_low(gated_grad * mixed_state * silu_slope(gate_in))
     grad_skip_gain = jnp.sum(scan_grad * activated, axis=0)
     early_flows = (flow_expert_down, flow_expert_in, flow_attn, flow_ffn_down, flow_ffn_gate)
+    flow_ffn_up = prepare_sum((feed_rows, feed_up_grad[None]))
+    flow_mixer_gate = prepare_sum((by_owner(normed_one[None], along_first), gate_in_grad[None]))
+    flow_mixer_out = prepare_sum((mixer_out_rows, gated[None]))
+    late_flows = (flow_ffn_up, flow_mixer_gate, flow_mixer_out)
+    scan_grad = bind(scan_grad, *late_flows)
     scan_grad = hold(scan_grad, *early_flows)
     state_after = run_summary(steps, scan_grad, readout_wide, slopes, next(numbers), False)
-    state_after, gate_grad_late, feed_up_late = lax.optimization_barrier(
-        (state_after, gate_in_grad, feed_up_grad)
-    )
-    state_after = after(state_after, flow_attn, flow_ffn_down, flow_ffn_gate)
-    flow_ffn_up = begin_sum((feed_rows, feed_up_late[None]))
-    flow_mixer_gate = begin_sum((by_owner(normed_one[None], along_first), gate_grad_late[None]))
+    state_after = bind(state_after, *late_flows)
+    state_after = after(state_after, flow_attn, flow_ffn_gate)
+    send(flow_ffn_up)
+    send(flow_mixer_gate)
     through_sum, injected, inject_part, readout_part, rate_sum = adjoint_sweep(
         state_after,
         state_out,
@@ -1221,20 +1252,20 @@
     pre_grad = step_grad * jax.nn.sigmoid(step_pre)
     grad_step_bias = jnp.sum(pre_grad, axis=0)
     pre_low = to_low(pre_grad)
-    grad_step_proj = product(step_low.T, pre_low)
+    pre_low = bind(pre_low, flow_mixer_out)
+    pre_low = after(pre_low, flow_ffn_up, flow_ffn_gate, flow_ffn_down, flow_attn)
+    send(flow_mixer_out)
+    grad_step_proj = product(pre_low.T, step_low)
     proj_part = jnp.concatenate([product(pre_low, step_proj.T), inject_grad, readout_grad], axis=1)
-    proj_part, gated_late = lax.optimization_barrier((proj_part, gated))
-    proj_part = after(proj_part, flow_ffn_down, flow_ffn_gate, flow_attn)
-    flow_mixer_out = begin_sum((mixer_out_rows, gated_late[None]))
     proj_low = to_low(head_sum(proj_part, next(numbers), jnp.float32, 1))
-    proj_low = after(proj_low, flow_ffn_up, flow_mixer_gate)
+    proj_low = after(proj_low, flow_mixer_gate, flow_ffn_down)
     grad_state_proj = product(act_low.T, proj_low)
     act_total = input_grad + skipping * scan_grad + product(proj_low, state_proj.T)
     conv_grad = act_total * silu_slope(conv_sum)
-    conv_grad = after(conv_grad, flow_ffn_down, flow_ffn_gate)
+    conv_grad = after(conv_grad, flow_ffn_up, flow_mixer_out, flow_ffn_gate)
     grad_conv_bias = jnp.sum(conv_grad, axis=0)
     after_edge = from_behind(conv_grad[:reach], "seq", -1)
-    after_edge = after(after_edge, flow_mixer_out, flow_mixer_gate, flow_ffn_up)
+    after_edge = after(after_edge, flow_mixer_gate, flow_ffn_down)
     grad_ext = jnp.concatenate([conv_grad, after_edge])
     docs_next = jnp.concatenate([local_docs, docs_after])
     conv_in_grad = jnp.zeros_like(conv_grad)
@@ -1253,31 +1284,36 @@
     normed_part = product(conv_low, mixer_inner.T) + product(gate_in_grad, mixer_gate.T)
     own_channels = grad_conv_bias.shape[0] // seq_count
 
-    def cut(values, axis):
-        values = jnp.moveaxis(values, axis, 0)
+    def cut(values):
         return values.reshape(seq_count, -1)
 
+    channel_rows = jnp.concatenate(
+        [grad_state_proj, jnp.pad(grad_step_proj, ((0, 0), (0, LANES - rank_size)))], axis=1
+    )
     packed = jnp.concatenate(
         [
-            cut(grad_norm_ffn, 0),
-            cut(grad_norm_attn, 0),
-            cut(grad_norm_moe, 0),
-            cut(grad_router, 0),
-            cut(grad_conv_taps, 1),
-            cut(grad_conv_bias, 0),
-            cut(grad_state_proj, 0),
-            cut(grad_step_proj, 1),
-            cut(grad_step_bias, 0),
-            cut(grad_decay_log, 1),
-            cut(grad_skip_gain, 0),
+            cut(grad_decay_log.T),
+            cut(grad_norm_ffn),
+            cut(grad_norm_attn),
+            cut(grad_norm_moe),
+            cut(grad_router),
+            cut(grad_conv_taps.T),
+            cut(grad_conv_bias),
+            cut(grad_step_bias),
+            cut(grad_skip_gain),
         ],
         axis=1,
     )
     spare = -packed.shape[1] % (16 * LANES)
     packed = to_low(jnp.pad(packed, ((0, 0), (0, spare)))).reshape(-1, LANES)
     packed = after(packed, flow_mixer_out)
-    first_inner, second_inner, sum_packed, grad_tokens, grad_norm_mixer = last_sums(
-        [grad_mixer_inner[:, :inner_half], grad_mixer_inner[:, inner_half:], packed],
+    first_inner, second_inner, sum_rows, sum_packed, grad_tokens, grad_norm_mixer = last_sums(
+        [
+            grad_mixer_inner[:, :inner_half],
+            grad_mixer_inner[:, inner_half:],
+            to_low(channel_rows),
+            packed,
+        ],
         normed_part,
         tokens_in,
         gain_mixer[None, :],
@@ -1290,11 +1326,10 @@
     sum_packed = sum_packed.reshape(-1)
     own_rows = model_width // seq_count
     taken = itertools.accumulate(
-        [0]
+        [0, own_channels * state_size]
         + [own_rows] * 3
-        + [own_rows * expert_count]
-        + [own_channels * (reach + 1), own_channels, own_channels * state_proj.shape[1]]
-        + [own_channels * rank_size, own_channels, own_channels * state_size, own_channels]
+        + [own_rows * expert_count, own_channels * (reach + 1)]
+        + [own_channels] * 3
     )
     bounds = list(taken)
     pieces = [sum_packed[low:high] for low, high in itertools.pairwise(bounds)]
@@ -1306,25 +1341,25 @@
         lax.dynamic_slice_in_dim(grad_norm_mixer[0], me * own_rows, own_rows),
         jnp.concatenate([first_inner, second_inner], axis=1),
         finished(flow_mixer_gate)[0],
-        pieces[4].reshape(own_channels, -1).T,
-        pieces[5],
-        pieces[6].reshape(own_channels, -1),
-        pieces[7].reshape(own_channels, -1).T,
+        pieces[5].reshape(own_channels, -1).T,
+        pieces[6],
+        sum_rows[:, :LANES],
+        sum_rows[:, LANES : LANES + rank_size].T,
+        pieces[7],
+        pieces[0].reshape(own_channels, -1),
         pieces[8],
-        pieces[9].reshape(own_channels, -1),
-        pieces[10],
         finished(flow_mixer_out)[0].T,
-        pieces[0],
+        pieces[1],
         finished(flow_ffn_gate)[0],
         finished(flow_ffn_up)[0],
         finished(flow_ffn_down)[0].T,
-        pieces[1],
+        pieces[2],
         sum_attn[:, :query_width],
         sum_attn[:, query_width : query_width + key_width],
         sum_attn[:, query_width + key_width : query_width + 2 * key_width],
         sum_attn[:, query_width + 2 * key_width :].T,
-        pieces[2],
-        pieces[3].reshape(own_rows, -1),
+        pieces[3],
+        pieces[4].reshape(own_rows, -1),
         sum_expert_in[:, :, :expert_width],
         sum_expert_in[:, :, expert_width:],
         finished(flow_expert_down).transpose(0, 2, 1),

time: 703 us -> 636 us (0.905)
  Pallas kernels: 285 us -> 246 us
  other arithmetic: 77.7 us -> 55.5 us
  matrix products: 132 us -> 116 us
    unnamed x403 -> x490, local copies, waits for them, and re-layouts: 24.8 us -> 49.4 us
    pallas_call x8, Pallas kernels: 114 us -> 96.4 us  [head_sum(): pl.pallas_call(kernel, out_shape=jax.ShapeDtypeStruct((rows, width), jnp....]
    dot_general x32, matrix products: 44.7 us -> 31.6 us  [product(): return jnp.dot(left, right, preferred_element_type=jnp.float32)]
    ppermute x2, waiting for transfers between devices: 9.85 us -> 0.01 us  [from_behind(): return lax.ppermute(block, axis, route)]
    ppermute x24, waiting for transfers between devices: 80.5 us -> 89.2 us  [send(): flow['got'].append(lax.ppermute(flow['out'], 'seq', route))]
    pallas_call x2, Pallas kernels: 31.4 us -> 23.3 us  [run_summary(): pl.pallas_call(kernel, out_shape=jax.ShapeDtypeStruct((entries, width), j...]
  transfers between devices with their start and end apart: 26 -> 26, of which waited for: 10 -> 9; matrix products, arithmetic and copies ran while one was open for 25% -> 25% of each run, Pallas kernels for 9% -> 19%
where the time goes in v5:
time: 636 us; the launch traced here: 630 us
  Pallas kernels  246 us (39%)
  matrix products  116 us (18%)
  waiting for transfers between devices  89.3 us (14%)
  local copies, waits for them, and re-layouts  82.5 us (13%)
  other arithmetic  55.5 us (9%)
  starting transfers between devices  36.5 us (6%)
    pallas_call x8, Pallas kernels, head_sum(): pl.pallas_call(kernel, out_shape=jax.ShapeDtypeStruct((rows, width), jnp....  96.4 us
    ppermute x24, waiting for transfers between devices, send(): flow['got'].append(lax.ppermute(flow['out'], 'seq', route))  89.2 us
    dot_general x36, matrix products, settle(): jnp.einsum('bdt,btf->bdf', rows[0][step], columns, preferred_element_type...  74.9 us
    pallas_call x1, Pallas kernels, last_sums(): pl.pallas_call(kernel, out_shape=[jax.ShapeDtypeStruct(shape, jnp.float32...  55.5 us
    unnamed x490, local copies, waits for them, and re-layouts  49.4 us
    dot_general x32, matrix products, product(): return jnp.dot(left, right, preferred_element_type=jnp.float32)  31.6 us
    ppermute x24, starting transfers between devices, send(): flow['got'].append(lax.ppermute(flow['out'], 'seq', route))  30 us
    pallas_call x1, Pallas kernels, scatter_and_head_sum(): pl.pallas_call(kernel, out_shape=[jax.ShapeDtypeStruct(shape, jnp.float32...  26.4 us
  transfers between devices with their start and end apart: 26, of which 9 were waited for; matrix products, arithmetic and copies ran while one was open for 25% of the time, Pallas kernels for 19%

profile of v5, /device:TPU:0, one launch (start us, length us, event | category | flops | bytes accessed | tf_op | source)
XLA Modules:
  0.0 629.6 jit_solution(10265984396981458903)
XLA Ops:
  6.0 4.9 collective-permute-start
  23.6 6.5 %head_sum.8 = f32[256,128]{1,0:T(8,128)S(1)} custom-call(f32[256,128]{1,0:T(8,128)S(1)} %fusion.121.x_ref), custom_call_target="tpu_custom_call" | custom-call | flops 6000 | bytes 6000 | tf_op jit(solution)/shard_map/head_sum/pallas_call | solution.py:173
  33.8 13.3 %run_summary.2.init_ref = f32[16,768]{1,0:T(8,128)S(1)} custom-call(f32[256,768]{1,0:T(8,128)S(1)} %get-tuple-element.434.step_ref, f32[256,768]{1,0:T(8,128)S(1)} %get-tuple-element.433.drive_ref, f32[256,16,128]{2,1,0:T(8,128)S(1)} %broadcast_in_dim.69.coef_ref.inject_ref, f32[16,768]{1,0:T(8,128)S(1)} %bitcast_multiply_fusion.3.slope_ref), custom_call_target="tpu_custom_call" | custom-call | flops 16000 | bytes 16000 | tf_op jit(solution)/shard_map/run_summary/pallas_call | solution.py:488
  47.8 8.1 %state_sweep.1 = (f32[256,768]{1,0:T(8,128)S(1)}, f32[256,16,768]{2,1,0:T(8,128)}, f32[16,768]{1,0:T(8,128)S(1)}) custom-call(f32[16,768]{1,0:T(8,128)S(1)} %run_summary.2.init_ref, f32[256,768]{1,0:T(8,128)S(1)} %get-tuple-element.434.step_ref, f32[256,768]{1,0:T(8,128)S(1)} %get-tuple-element.433.drive_ref, ...), custom_call_target="tpu_custom_call" | custom-call | flops 11000 | bytes 11000 | tf_op jit(solution)/shard_map/state_sweep/pallas_call | solution.py:539
  58.9 13.8 %head_sum.9 = f32[256,1536]{1,0:T(8,128)S(1)} custom-call(f32[256,1536]{1,0:T(8,128)S(1)} %fusion.221.x_ref), custom_call_target="tpu_custom_call" | custom-call | flops 15000 | bytes 15000 | tf_op jit(solution)/shard_map/head_sum/pallas_call | solution.py:173
  83.7 14.0 %head_sum.10 = f32[256,1536]{1,0:T(8,128)S(1)} custom-call(f32[256,1536]{1,0:T(8,128)S(1)} %copy-done.15), custom_call_target="tpu_custom_call" | custom-call | flops 15000 | bytes 15000 | tf_op jit(solution)/shard_map/head_sum/pallas_call | solution.py:173
  101.5 21.5 %attend.1 = (bf16[256,384]{1,0:T(8,128)(2,1)S(1)}, f32[128,1536]{1,0:T(8,128)S(1)}, f32[1,1536]{1,0:T(1,128)S(1)}, bf16[8,256,256]{2,1,0:T(8,128)(2,1)S(1)}) custom-call(bf16[256,384]{1,0:T(8,128)(2,1)S(1)} %convolution_convert_fusion.17.q_ref, bf16[256,256]{1,0:T(8,128)(2,1)S(1)} %pad_maximum_fusion.5.x_ref, s32[2048,1]{1,0:T(8,128)S(1)} %copy-done.10, ...), custom_call_target="tpu_custom_call" | custom-call | flops 12000 | bytes 12000 | tf_op jit(solution)/shard_map/attend/pallas_call | solution.py:814
  128.1 13.1 %head_sum.11 = f32[256,1536]{1,0:T(8,128)S(1)} custom-call(f32[256,1536]{1,0:T(8,128)S(1)} %copy-done.14), custom_call_target="tpu_custom_call" | custom-call | flops 15000 | bytes 15000 | tf_op jit(solution)/shard_map/head_sum/pallas_call | solution.py:173
  168.4 3.3 convolution_convert_fusion.2
  179.2 14.8 %head_sum.12 = f32[256,1664]{1,0:T(8,128)S(1)} custom-call(f32[256,1664]{1,0:T(8,128)S(1)} %select_maximum_fusion.x_ref), custom_call_target="tpu_custom_call" | custom-call | flops 16000 | bytes 16000 | tf_op jit(solution)/shard_map/head_sum/pallas_call | solution.py:173
  210.5 3.0 fusion.95
  215.9 26.3 %collective-permute-done.2 = bf16[4,768,512]{2,1,0:T(8,128)(2,1)} collective-permute-done((bf16[4,768,512]{2,1,0:T(8,128)(2,1)}, bf16[4,768,512]{2,1,0:T(8,128)(2,1)}, u32[]{:S(2)}, u32[]{:S(2)}) %collective-permute-start.2) | collective-permute-done | bytes 3145760 | tf_op jit(solution)/shard_map/ppermute | solution.py:977
  242.1 26.4 %scatter_and_head_sum.1 = (f32[256,128]{1,0:T(8,128)S(1)}, f32[256,128]{1,0:T(8,128)S(1)}, f32[256,1536]{1,0:T(8,128)S(1)}) custom-call(bf16[4,2,256,128]{3,2,1,0:T(8,128)(2,1)S(1)} %bitcast.556, bf16[4,2,256,128]{3,2,1,0:T(8,128)(2,1)S(1)} %bitcast.557, f32[256,1536]{1,0:T(8,128)S(1)} %fusion.102.refs_2_), custom_call_target="tpu_custom_call" | custom-call | flops 20000 | bytes 20000 | tf_op jit(solution)/shard_map/scatter_and_head_sum/pallas_call | solution.py:315
  271.7 3.6 add_convert_fusion.1
  282.1 13.9 %head_sum.13 = f32[256,1536]{1,0:T(8,128)S(1)} custom-call(f32[256,1536]{1,0:T(8,128)S(1)} %convolution_add_fusion.3.x_ref), custom_call_target="tpu_custom_call" | custom-call | flops 15000 | bytes 15000 | tf_op jit(solution)/shard_map/head_sum/pallas_call | solution.py:173
  319.2 4.8 collective-permute-done.3
  333.9 3.7 add_convert_fusion.2
  344.2 13.9 %head_sum.14 = f32[256,1536]{1,0:T(8,128)S(1)} custom-call(f32[256,1536]{1,0:T(8,128)S(1)} %convolution_add_fusion.x_ref), custom_call_target="tpu_custom_call" | custom-call | flops 15000 | bytes 15000 | tf_op jit(solution)/shard_map/head_sum/pallas_call | solution.py:173
  377.0 13.6 %collective-permute-done.6 = bf16[4,192,256]{2,1,0:T(8,128)(2,1)} collective-permute-done((bf16[4,192,256]{2,1,0:T(8,128)(2,1)}, bf16[4,192,256]{2,1,0:T(8,128)(2,1)}, u32[]{:S(2)}, u32[]{:S(2)}) %collective-permute-start.6) | collective-permute-done | bytes 393248 | tf_op jit(solution)/shard_map/ppermute | solution.py:977
  390.6 9.9 %run_summary.3.in_ref = f32[16,768]{1,0:T(8,128)S(1)} custom-call(f32[256,768]{1,0:T(8,128)S(1)} %copy-done.7, f32[256,768]{1,0:T(8,128)S(1)} %get-tuple-element.124.drive_ref.up_ref, f32[256,16,128]{2,1,0:T(8,128)S(1)} %copy-done.5, f32[16,768]{1,0:T(8,128)S(1)} %bitcast_multiply_fusion.3.slope_ref), custom_call_target="tpu_custom_call" | custom-call | flops 16000 | bytes 16000 | tf_op jit(solution)/shard_map/run_summary/pallas_call | solution.py:488
  409.6 12.8 %adjoint_sweep.1 = (f32[256,768]{1,0:T(8,128)S(1)}, f32[256,768]{1,0:T(8,128)S(1)}, f32[256,16,128]{2,1,0:T(8,128)S(1)}, f32[256,16,128]{2,1,0:T(8,128)S(1)}, f32[16,768]{1,0:T(8,128)S(1)}) custom-call(f32[16,768]{1,0:T(8,128)S(1)} %run_summary.3.in_ref, f32[16,768]{1,0:T(8,128)S(1)} %copy-done.27, f32[256,16,768]{2,1,0:T(8,128)} %get-tuple-element.133.before_ref, ...), custom_call_target="tpu_custom_call" | custom-call | flops 15000 | bytes 15000 | tf_op jit(solution)/shard_map/adjoint_sweep/pallas_call | solution.py:624
  426.7 2.9 reduce_sum.307
  429.6 2.9 reduce_sum.308
  453.8 6.5 %head_sum.15 = f32[256,128]{1,0:T(8,128)S(1)} custom-call(f32[256,128]{1,0:T(8,128)S(1)} %pad_maximum_fusion.6.x_ref), custom_call_target="tpu_custom_call" | custom-call | flops 6000 | bytes 6000 | tf_op jit(solution)/shard_map/head_sum/pallas_call | solution.py:173
  477.4 4.4 collective-permute-done.15
  487.4 4.1 collective-permute-done.18
  491.6 10.7 %collective-permute-done.16 = bf16[1,384,1024]{2,1,0:T(8,128)(2,1)} collective-permute-done((bf16[1,384,1024]{2,1,0:T(8,128)(2,1)}, bf16[1,384,1024]{2,1,0:T(8,128)(2,1)}, u32[]{:S(2)}, u32[]{:S(2)}) %collective-permute-start.16) | collective-permute-done | bytes 786464 | tf_op jit(solution)/shard_map/ppermute | solution.py:977
  513.6 3.0 collective-permute-start.21
  516.7 10.3 %collective-permute-done.25 = bf16[1,192,1024]{2,1,0:T(8,128)(2,1)S(1)} collective-permute-done((bf16[1,192,1024]{2,1,0:T(8,128)(2,1)S(1)}, bf16[1,192,1024]{2,1,0:T(8,128)(2,1)S(1)}, u32[]{:S(2)}, u32[]{:S(2)}) %collective-permute-start.25) | collective-permute-done | bytes 393248 | tf_op jit(solution)/shard_map/ppermute | solution.py:977
  529.3 12.8 %collective-permute-done.21 = bf16[1,192,1024]{2,1,0:T(8,128)(2,1)S(1)} collective-permute-done((bf16[1,192,1024]{2,1,0:T(8,128)(2,1)S(1)}, bf16[1,192,1024]{2,1,0:T(8,128)(2,1)S(1)}, u32[]{:S(2)}, u32[]{:S(2)}) %collective-permute-start.21) | collective-permute-done | bytes 393248 | tf_op jit(solution)/shard_map/ppermute | solution.py:977
  552.0 3.0 collective-permute-start.23
  556.9 55.5 %last_sums.1 = (f32[192,384]{1,0:T(8,128)S(1)}, f32[192,384]{1,0:T(8,128)S(1)}, f32[96,256]{1,0:T(8,128)S(1)}, f32[32,128]{1,0:T(8,128)S(1)}, f32[256,1536]{1,0:T(8,128)S(1)}, /*index=5*/f32[1,1536]{1,0:T(1,128)S(1)}) custom-call(bf16[4,2,192,384]{3,2,1,0:T(8,128)(2,1)S(1)} %bitcast.554, bf16[4,2,192,384]{3,2,1,0:T(8,128)(2,1)S(1)} %bitcast.553, ...), custom_call_target="tpu_custom_call" | custom-call | flops 20000 | bytes 20000 | tf_op jit(solution)/shard_map/last_sums/pallas_call | solution.py:383
  (741 shorter events, 264.7 us)
Async XLA Ops:
  0.7 157.8 %copy-start = (bf16[4,256,1536]{2,1,0:T(8,128)(2,1)S(1)}, bf16[4,256,1536]{2,1,0:T(8,128)(2,1)}, u32[]{:S(2)}) copy-start(bf16[4,256,1536]{2,1,0:T(8,128)(2,1)} %param.59) | copy-start | bytes 9437188
  6.0 13.2 %collective-permute-start = (bf16[3,768]{1,0:T(4,128)(2,1)S(1)}, bf16[3,768]{1,0:T(4,128)(2,1)S(1)}, u32[]{:S(2)}, u32[]{:S(2)}) collective-permute-start(bf16[3,768]{1,0:T(4,128)(2,1)S(1)} %slice.376), channel_id=1, source_target_pairs={{0,4},{4,8},{8,12},{12,16},{16,20},{20,24},{24,28},{1,5},{5,9},{9,... | collective-permute-start | bytes 13832 | tf_op jit(solution)/shard_map/ppermute | solution.py:31
  19.1 36.8 %copy-start.228 = (f32[768]{0:T(1024)}, f32[768]{0:T(1024)S(1)}, u32[]{:S(2)}) copy-start(f32[768]{0:T(1024)S(1)} %convert_element_type.442) | copy-start | bytes 9220
  19.1 53.9 %copy-start.161 = (f32[1536]{0:T(1024)}, f32[1536]{0:T(1024)S(1)}, u32[]{:S(2)}) copy-start(f32[1536]{0:T(1024)S(1)} %convert_element_type.444) | copy-start | bytes 18436
  19.1 78.9 %copy-start.169 = (f32[1536]{0:T(1024)}, f32[1536]{0:T(1024)S(1)}, u32[]{:S(2)}) copy-start(f32[1536]{0:T(1024)S(1)} %convert_element_type.447) | copy-start | bytes 18436
  171.6 70.5 %collective-permute-start.2 = (bf16[4,768,512]{2,1,0:T(8,128)(2,1)}, bf16[4,768,512]{2,1,0:T(8,128)(2,1)}, u32[]{:S(2)}, u32[]{:S(2)}) collective-permute-start(bf16[4,768,512]{2,1,0:T(8,128)(2,1)} %convolution_convert_fusion.2), channel_id=1, source_target_pairs={{0,4},{4,0},{8,12},{12,8},{16,20},{20,16},{24,28},{28,24},{1,5},{5... | collective-permute-start | bytes 9437192 | tf_op jit(solution)/shard_map/ppermute | solution.py:977
  178.5 37.3 %collective-permute-start.1 = (bf16[4,768,256]{2,1,0:T(8,128)(2,1)}, bf16[4,768,256]{2,1,0:T(8,128)(2,1)}, u32[]{:S(2)}, u32[]{:S(2)}) collective-permute-start(bf16[4,768,256]{2,1,0:T(8,128)(2,1)} %convolution_convert_fusion.7), channel_id=1, source_target_pairs={{0,8},{4,12},{8,0},{12,4},{16,24},{20,28},{24,16},{28,20},{1,9},{5... | collective-permute-start | bytes 4718600 | tf_op jit(solution)/shard_map/ppermute | solution.py:977
  271.0 53.0 %collective-permute-start.5 = (bf16[1,768,1024]{1,2,0:T(8,128)(2,1)}, bf16[1,768,1024]{1,2,0:T(8,128)(2,1)}, u32[]{:S(2)}, u32[]{:S(2)}) collective-permute-start(bf16[1,768,1024]{1,2,0:T(8,128)(2,1)} %pad_maximum_fusion), channel_id=1, source_target_pairs={{0,4},{4,0},{8,12},{12,8},{16,20},{20,16},{24,28},{28,24},{1,5},{5... | collective-permute-start | bytes 4718600 | tf_op jit(solution)/shard_map/ppermute | solution.py:977
  275.3 48.7 %collective-permute-start.4 = (bf16[4,384,512]{2,1,0:T(8,128)(2,1)}, bf16[4,384,512]{2,1,0:T(8,128)(2,1)}, u32[]{:S(2)}, u32[]{:S(2)}) collective-permute-start(bf16[4,384,512]{2,1,0:T(8,128)(2,1)} %add_convert_fusion.1), channel_id=1, source_target_pairs={{0,8},{4,12},{8,0},{12,4},{16,24},{20,28},{24,16},{28,20},{1,9},{5... | collective-permute-start | bytes 4718600 | tf_op jit(solution)/shard_map/ppermute | solution.py:977
  281.0 43.0 %collective-permute-start.3 = (bf16[4,384,256]{2,1,0:T(8,128)(2,1)}, bf16[4,384,256]{2,1,0:T(8,128)(2,1)}, u32[]{:S(2)}, u32[]{:S(2)}) collective-permute-start(bf16[4,384,256]{2,1,0:T(8,128)(2,1)} %add_convert_fusion.3), channel_id=1, source_target_pairs={{0,4},{4,0},{8,12},{12,8},{16,20},{20,16},{24,28},{28,24},{1,5},{5... | collective-permute-start | bytes 2359304 | tf_op jit(solution)/shard_map/ppermute | solution.py:977
  303.6 73.4 %collective-permute-start.9 = (bf16[1,768,1024]{2,1,0:T(8,128)(2,1)}, bf16[1,768,1024]{2,1,0:T(8,128)(2,1)}, u32[]{:S(2)}, u32[]{:S(2)}) collective-permute-start(bf16[1,768,1024]{2,1,0:T(8,128)(2,1)} %fusion.13), channel_id=1, source_target_pairs={{0,8},{4,12},{8,0},{12,4},{16,24},{20,28},{24,16},{28,20},{1,9},{5... | collective-permute-start | bytes 4718600 | tf_op jit(solution)/shard_map/ppermute | solution.py:977
  324.7 42.3 %copy-start.47 = (bf16[256,1024]{1,0:T(8,128)(2,1)}, bf16[256,1024]{1,0:T(8,128)(2,1)S(1)}, u32[]{:S(2)}) copy-start(bf16[256,1024]{1,0:T(8,128)(2,1)S(1)} %get-tuple-element.387) | copy-start | bytes 1572868
  329.3 61.3 %collective-permute-start.10 = (bf16[1,768,1024]{2,1,0:T(8,128)(2,1)}, bf16[1,768,1024]{2,1,0:T(8,128)(2,1)}, u32[]{:S(2)}, u32[]{:S(2)}) collective-permute-start(bf16[1,768,1024]{2,1,0:T(8,128)(2,1)} %fusion.14), channel_id=1, source_target_pairs={{0,4},{4,0},{8,12},{12,8},{16,20},{20,16},{24,28},{28,24},{1,5},{5... | collective-permute-start | bytes 4718600 | tf_op jit(solution)/shard_map/ppermute | solution.py:977
  332.3 58.3 %collective-permute-start.8 = (bf16[1,384,1024]{1,2,0:T(8,128)(2,1)}, bf16[1,384,1024]{1,2,0:T(8,128)(2,1)}, u32[]{:S(2)}, u32[]{:S(2)}) collective-permute-start(bf16[1,384,1024]{1,2,0:T(8,128)(2,1)} %fusion.8), channel_id=1, source_target_pairs={{0,8},{4,12},{8,0},{12,4},{16,24},{20,28},{24,16},{28,20},{1,9},{5... | collective-permute-start | bytes 2359304 | tf_op jit(solution)/shard_map/ppermute | solution.py:977
  337.6 53.0 %collective-permute-start.7 = (bf16[4,192,512]{2,1,0:T(8,128)(2,1)}, bf16[4,192,512]{2,1,0:T(8,128)(2,1)}, u32[]{:S(2)}, u32[]{:S(2)}) collective-permute-start(bf16[4,192,512]{2,1,0:T(8,128)(2,1)} %add_convert_fusion.2), channel_id=1, source_target_pairs={{0,16},{4,20},{8,24},{12,28},{16,0},{20,4},{24,8},{28,12},{1,17},{... | collective-permute-start | bytes 2359304 | tf_op jit(solution)/shard_map/ppermute | solution.py:977
  343.1 47.5 %collective-permute-start.6 = (bf16[4,192,256]{2,1,0:T(8,128)(2,1)}, bf16[4,192,256]{2,1,0:T(8,128)(2,1)}, u32[]{:S(2)}, u32[]{:S(2)}) collective-permute-start(bf16[4,192,256]{2,1,0:T(8,128)(2,1)} %add_convert_fusion.10), channel_id=1, source_target_pairs={{0,16},{4,20},{8,24},{12,28},{16,0},{20,4},{24,8},{28,12},{1,17},{... | collective-permute-start | bytes 1179656 | tf_op jit(solution)/shard_map/ppermute | solution.py:977
  403.4 40.5 %collective-permute-start.13 = (bf16[1,192,1024]{1,2,0:T(8,128)(2,1)}, bf16[1,192,1024]{1,2,0:T(8,128)(2,1)}, u32[]{:S(2)}, u32[]{:S(2)}) collective-permute-start(bf16[1,192,1024]{1,2,0:T(8,128)(2,1)} %fusion.27), channel_id=1, source_target_pairs={{0,16},{4,20},{8,24},{12,28},{16,0},{20,4},{24,8},{28,12},{1,17},{... | collective-permute-start | bytes 1179656 | tf_op jit(solution)/shard_map/ppermute | solution.py:977
  407.4 36.4 %collective-permute-start.12 = (bf16[1,384,1024]{2,1,0:T(8,128)(2,1)}, bf16[1,384,1024]{2,1,0:T(8,128)(2,1)}, u32[]{:S(2)}, u32[]{:S(2)}) collective-permute-start(bf16[1,384,1024]{2,1,0:T(8,128)(2,1)} %fusion.11), channel_id=1, source_target_pairs={{0,8},{4,12},{8,0},{12,4},{16,24},{20,28},{24,16},{28,20},{1,9},{5... | collective-permute-start | bytes 2359304 | tf_op jit(solution)/shard_map/ppermute | solution.py:977
  408.4 37.6 %collective-permute-start.11 = (bf16[1,768,1024]{2,1,0:T(8,128)(2,1)}, bf16[1,768,1024]{2,1,0:T(8,128)(2,1)}, u32[]{:S(2)}, u32[]{:S(2)}) collective-permute-start(bf16[1,768,1024]{2,1,0:T(8,128)(2,1)} %fusion.12), channel_id=1, source_target_pairs={{0,4},{4,0},{8,12},{12,8},{16,20},{20,16},{24,28},{28,24},{1,5},{5... | collective-permute-start | bytes 4718600 | tf_op jit(solution)/shard_map/ppermute | solution.py:977
  432.5 44.9 %collective-permute-start.14 = (bf16[1,768,768]{2,1,0:T(8,128)(2,1)}, bf16[1,768,768]{2,1,0:T(8,128)(2,1)}, u32[]{:S(2)}, u32[]{:S(2)}) collective-permute-start(bf16[1,768,768]{2,1,0:T(8,128)(2,1)} %fusion.15), channel_id=1, source_target_pairs={{0,8},{4,12},{8,0},{12,4},{16,24},{20,28},{24,16},{28,20},{1,9},{5... | collective-permute-start | bytes 3538952 | tf_op jit(solution)/shard_map/ppermute | solution.py:977
  433.3 54.1 %collective-permute-start.17 = (bf16[1,768,768]{2,1,0:T(8,128)(2,1)}, bf16[1,768,768]{2,1,0:T(8,128)(2,1)}, u32[]{:S(2)}, u32[]{:S(2)}) collective-permute-start(bf16[1,768,768]{2,1,0:T(8,128)(2,1)} %fusion.16), channel_id=1, source_target_pairs={{0,4},{4,0},{8,12},{12,8},{16,20},{20,16},{24,28},{28,24},{1,5},{5... | collective-permute-start | bytes 3538952 | tf_op jit(solution)/shard_map/ppermute | solution.py:977
  451.7 30.1 %collective-permute-start.15 = (bf16[1,384,1024]{2,1,0:T(8,128)(2,1)}, bf16[1,384,1024]{2,1,0:T(8,128)(2,1)}, u32[]{:S(2)}, u32[]{:S(2)}) collective-permute-start(bf16[1,384,1024]{2,1,0:T(8,128)(2,1)} %fusion.10), channel_id=1, source_target_pairs={{0,4},{4,0},{8,12},{12,8},{16,20},{20,16},{24,28},{28,24},{1,5},{5... | collective-permute-start | bytes 2359304 | tf_op jit(solution)/shard_map/ppermute | solution.py:977
  470.4 21.1 %collective-permute-start.18 = (bf16[1,192,1024]{2,1,0:T(8,128)(2,1)}, bf16[1,192,1024]{2,1,0:T(8,128)(2,1)}, u32[]{:S(2)}, u32[]{:S(2)}) collective-permute-start(bf16[1,192,1024]{2,1,0:T(8,128)(2,1)} %add_convert_fusion.9), channel_id=1, source_target_pairs={{0,16},{4,20},{8,24},{12,28},{16,0},{20,4},{24,8},{28,12},{1,17},{... | collective-permute-start | bytes 1179656 | tf_op jit(solution)/shard_map/ppermute | solution.py:977
  474.4 27.8 %collective-permute-start.16 = (bf16[1,384,1024]{2,1,0:T(8,128)(2,1)}, bf16[1,384,1024]{2,1,0:T(8,128)(2,1)}, u32[]{:S(2)}, u32[]{:S(2)}) collective-permute-start(bf16[1,384,1024]{2,1,0:T(8,128)(2,1)} %fusion.9), channel_id=1, source_target_pairs={{0,8},{4,12},{8,0},{12,4},{16,24},{20,28},{24,16},{28,20},{1,9},{5... | collective-permute-start | bytes 2359304 | tf_op jit(solution)/shard_map/ppermute | solution.py:977
  485.3 56.8 %collective-permute-start.20 = (bf16[1,384,768]{2,1,0:T(8,128)(2,1)S(1)}, bf16[1,384,768]{2,1,0:T(8,128)(2,1)S(1)}, u32[]{:S(2)}, u32[]{:S(2)}) collective-permute-start(bf16[1,384,768]{2,1,0:T(8,128)(2,1)S(1)} %add_convert_fusion.6), channel_id=1, source_target_pairs={{0,4},{4,0},{8,12},{12,8},{16,20},{20,16},{24,28},{28,24},{1,5},{5... | collective-permute-start | bytes 1769480 | tf_op jit(solution)/shard_map/ppermute | solution.py:977
  502.3 27.0 %collective-permute-start.19 = (f32[3,768]{1,0:T(4,128)S(1)}, f32[3,768]{1,0:T(4,128)S(1)}, u32[]{:S(2)}, u32[]{:S(2)}) collective-permute-start(f32[3,768]{1,0:T(4,128)S(1)} %slice.318), channel_id=1, source_target_pairs={{4,0},{8,4},{12,8},{16,12},{20,16},{24,20},{28,24},{5,1},{9,5},{13... | collective-permute-start | bytes 27656 | tf_op jit(solution)/shard_map/ppermute | solution.py:31
  505.5 21.5 %collective-permute-start.25 = (bf16[1,192,1024]{2,1,0:T(8,128)(2,1)S(1)}, bf16[1,192,1024]{2,1,0:T(8,128)(2,1)S(1)}, u32[]{:S(2)}, u32[]{:S(2)}) collective-permute-start(bf16[1,192,1024]{2,1,0:T(8,128)(2,1)S(1)} %add_convert_fusion.7), channel_id=1, source_target_pairs={{0,16},{4,20},{8,24},{12,28},{16,0},{20,4},{24,8},{28,12},{1,17},{... | collective-permute-start | bytes 1179656 | tf_op jit(solution)/shard_map/ppermute | solution.py:977
  509.9 38.1 %collective-permute-start.22 = (bf16[1,384,768]{2,1,0:T(8,128)(2,1)}, bf16[1,384,768]{2,1,0:T(8,128)(2,1)}, u32[]{:S(2)}, u32[]{:S(2)}) collective-permute-start(bf16[1,384,768]{2,1,0:T(8,128)(2,1)} %add_convert_fusion.5), channel_id=1, source_target_pairs={{0,8},{4,12},{8,0},{12,4},{16,24},{20,28},{24,16},{28,20},{1,9},{5... | collective-permute-start | bytes 1769480 | tf_op jit(solution)/shard_map/ppermute | solution.py:977
  513.6 28.5 %collective-permute-start.21 = (bf16[1,192,1024]{2,1,0:T(8,128)(2,1)S(1)}, bf16[1,192,1024]{2,1,0:T(8,128)(2,1)S(1)}, u32[]{:S(2)}, u32[]{:S(2)}) collective-permute-start(bf16[1,192,1024]{2,1,0:T(8,128)(2,1)S(1)} %add_convert_fusion.8), channel_id=1, source_target_pairs={{0,16},{4,20},{8,24},{12,28},{16,0},{20,4},{24,8},{28,12},{1,17},{... | collective-permute-start | bytes 1179656 | tf_op jit(solution)/shard_map/ppermute | solution.py:977
  550.5 72.2 %collective-permute-start.24 = (bf16[1,192,768]{2,1,0:T(8,128)(2,1)}, bf16[1,192,768]{2,1,0:T(8,128)(2,1)}, u32[]{:S(2)}, u32[]{:S(2)}) collective-permute-start(bf16[1,192,768]{2,1,0:T(8,128)(2,1)} %add_convert_fusion.11), channel_id=1, source_target_pairs={{0,16},{4,20},{8,24},{12,28},{16,0},{20,4},{24,8},{28,12},{1,17},{... | collective-permute-start | bytes 884744 | tf_op jit(solution)/shard_map/ppermute | solution.py:977
  552.0 73.0 %collective-permute-start.23 = (bf16[1,192,768]{2,1,0:T(8,128)(2,1)S(1)}, bf16[1,192,768]{2,1,0:T(8,128)(2,1)}, u32[]{:S(2)}, u32[]{:S(2)}) collective-permute-start(bf16[1,192,768]{2,1,0:T(8,128)(2,1)S(1)} %add_convert_fusion.12), channel_id=1, source_target_pairs={{0,16},{4,20},{8,24},{12,28},{16,0},{20,4},{24,8},{28,12},{1,17},{... | collective-permute-start | bytes 884744 | tf_op jit(solution)/shard_map/ppermute | solution.py:977
  556.9 57.9 %copy-start.151 = (bf16[1,192,1024]{2,1,0:T(8,128)(2,1)S(1)}, bf16[1,192,1024]{2,1,0:T(8,128)(2,1)}, u32[]{:S(2)}) copy-start(bf16[1,192,1024]{2,1,0:T(8,128)(2,1)} %copy-done.150) | copy-start | bytes 1179652
  (233 other events, 1407.4 us)

commit v6 on v5

--- a/solution.py
+++ b/solution.py
@@ -954,12 +954,16 @@
                 if j >> bit & 1:
                     owner = owner + (1 << bit) * (1 - 2 * ((owner >> bit) & 1))
             blocks.append(lax.dynamic_slice_in_dim(turned, owner * own_rows, own_rows, 1))
-        parts = []
-        while len(blocks) > 1:
-            half = len(blocks) // 2
-            parts.append(jnp.concatenate(blocks[half:], axis=1) if half > 1 else blocks[half])
-            blocks = blocks[:half]
-        return parts + blocks, bits
+        half = len(blocks) // 2
+        return (
+            jnp.concatenate(blocks[half:], axis=1),
+            jnp.concatenate(blocks[:half], axis=1),
+        ), bits
+
+    def over_tokens(rows, columns):
+        if rows.shape[0] == 1:
+            return product(rows[0], columns[0])[None]
+        return jnp.einsum("bdt,btf->bdf", rows, columns, preferred_element_type=jnp.float32)
 
     def begin_sum(*parts):
         flow = prepare_sum(*parts)
@@ -984,21 +988,21 @@
 
     def settle(flow):
         step = len(flow["got"])
-        gradients = [
-            jnp.einsum(
-                "bdt,btf->bdf", rows[0][step], columns, preferred_element_type=jnp.float32
-            )
-            for rows, columns in flow["parts"]
-        ]
-        total = gradients[0] if len(gradients) == 1 else jnp.concatenate(gradients, axis=2)
-        count = total.shape[1]
-        first = count if step < len(flow["bits"]) else 0
-        for got in flow["got"]:
-            total = total + got[:, first : first + count].astype(jnp.float32)
-        if step == len(flow["bits"]):
-            flow["total"] = total
-            return
-        flow["out"] = to_low(total)
+        if step < 2:
+            gradients = [over_tokens(rows[0][step], columns) for rows, columns in flow["parts"]]
+            total = gradients[0] if len(gradients) == 1 else jnp.concatenate(gradients, axis=2)
+            if step == 0:
+                flow["out"] = to_low(total)
+                return
+            flow["own"] = total + flow["got"][0].astype(jnp.float32)
+        count = flow["own"].shape[1] >> (step - 1)
+        half = count // 2
+        last = step == len(flow["bits"])
+        part = slice(0, count) if last else slice(half, count)
+        total = flow["own"][:, part]
+        for got in flow["got"][1:]:
+            total = total + got[:, part].astype(jnp.float32)
+        flow["total" if last else "out"] = total if last else to_low(total)
 
     def hold(values, *flows):
         if flows:
@@ -1179,7 +1183,7 @@
     query_grad, key_part, value_part = attend_back(
         own_place, queries, attended_grad, both_rows, key_docs, query_docs, attended, log_sum
     )
-    key_part = hold(key_part, flow_expert_down, flow_expert_in)
+    key_part = hold(key_part, flow_expert_down)
     key_sum, value_sum, combined_sum = scatter_and_head_sum(
         [key_part, value_part], combined, next(numbers)
     )
@@ -1265,7 +1269,7 @@
     conv_grad = after(conv_grad, flow_ffn_up, flow_mixer_out, flow_ffn_gate)
     grad_conv_bias = jnp.sum(conv_grad, axis=0)
     after_edge = from_behind(conv_grad[:reach], "seq", -1)
-    after_edge = after(after_edge, flow_mixer_gate, flow_ffn_down)
+    after_edge = after(after_edge, flow_ffn_down)
     grad_ext = jnp.concatenate([conv_grad, after_edge])
     docs_next = jnp.concatenate([local_docs, docs_after])
     conv_in_grad = jnp.zeros_like(conv_grad)
@@ -1306,7 +1310,7 @@
     )
     spare = -packed.shape[1] % (16 * LANES)
     packed = to_low(jnp.pad(packed, ((0, 0), (0, spare)))).reshape(-1, LANES)
-    packed = after(packed, flow_mixer_out)
+    packed = after(packed, flow_mixer_out, flow_mixer_gate)
     first_inner, second_inner, sum_rows, sum_packed, grad_tokens, grad_norm_mixer = last_sums(
         [
             grad_mixer_inner[:, :inner_half],

time: 636 us -> 613 us (0.964)
  matrix products: 116 us -> 77.9 us
  waiting for transfers between devices: 89.3 us -> 56.4 us
  other arithmetic: 55.5 us -> 81 us
  Pallas kernels: 246 us -> 267 us
    dot_general x36 -> x4, matrix products: 74.9 us -> 8.63 us  [over_tokens(): jnp.einsum('bdt,btf->bdf', rows, columns, preferred_element_type=jnp.floa...]
    ppermute x24, waiting for transfers between devices: 89.2 us -> 56.4 us  [send(): flow['got'].append(lax.ppermute(flow['out'], 'seq', route))]
    dot_general x32 -> x46, matrix products: 31.6 us -> 59 us  [product(): return jnp.dot(left, right, preferred_element_type=jnp.float32)]
    pallas_call x1, Pallas kernels: 26.4 us -> 46.5 us  [scatter_and_head_sum(): pl.pallas_call(kernel, out_shape=[jax.ShapeDtypeStruct(shape, jnp.float32...]
    convert_element_type x14 -> x20, other arithmetic: 14.1 us -> 31.7 us  [to_low(): return values.astype(jnp.bfloat16)]
    unnamed x490, local copies, waits for them, and re-layouts: 49.4 us -> 36.7 us
    add x1 -> x5, other arithmetic: 2.02 us -> 11.9 us  [the longest x4 8.44 us: settle(): flow['own'] = total + flow['got'][0].astype(jnp.float32)]
    slice x0 -> x8, local copies, waits for them, and re-layouts: none -> 8.61 us  [settle(): total = flow['own'][:, part]]
  transfers between devices with their start and end apart: 26 -> 26, of which waited for: 9 -> 6; matrix products, arithmetic and copies ran while one was open for 25% -> 25% of each run, Pallas kernels for 19% -> 27%
where the time goes in v6:
time: 613 us; the launch traced here: 606 us
  Pallas kernels  267 us (44%)
  local copies, waits for them, and re-layouts  82.8 us (14%)
  other arithmetic  81 us (13%)
  matrix products  77.9 us (13%)
  waiting for transfers between devices  56.4 us (9%)
  starting transfers between devices  37.2 us (6%)
    pallas_call x8, Pallas kernels, head_sum(): pl.pallas_call(kernel, out_shape=jax.ShapeDtypeStruct((rows, width), jnp....  95.4 us
    dot_general x46, matrix products, product(): return jnp.dot(left, right, preferred_element_type=jnp.float32)  59 us
    ppermute x24, waiting for transfers between devices, send(): flow['got'].append(lax.ppermute(flow['out'], 'seq', route))  56.4 us
    pallas_call x1, Pallas kernels, last_sums(): pl.pallas_call(kernel, out_shape=[jax.ShapeDtypeStruct(shape, jnp.float32...  55.2 us
    pallas_call x1, Pallas kernels, scatter_and_head_sum(): pl.pallas_call(kernel, out_shape=[jax.ShapeDtypeStruct(shape, jnp.float32...  46.5 us
    unnamed x490, local copies, waits for them, and re-layouts  36.7 us
    convert_element_type x20, other arithmetic, to_low(): return values.astype(jnp.bfloat16)  31.7 us
    ppermute x24, starting transfers between devices, send(): flow['got'].append(lax.ppermute(flow['out'], 'seq', route))  30.8 us
  transfers between devices with their start and end apart: 26, of which 6 were waited for; matrix products, arithmetic and copies ran while one was open for 25% of the time, Pallas kernels for 27%

profile of v6, /device:TPU:0, one launch (start us, length us, event | category | flops | bytes accessed | tf_op | source)
XLA Modules:
  0.0 606.0 jit_solution(6983640106618382165)
XLA Ops:
  6.0 4.9 collective-permute-start
  20.8 6.5 %head_sum.8 = f32[256,128]{1,0:T(8,128)S(1)} custom-call(f32[256,128]{1,0:T(8,128)S(1)} %fusion.157.x_ref), custom_call_target="tpu_custom_call" | custom-call | flops 6000 | bytes 6000 | tf_op jit(solution)/shard_map/head_sum/pallas_call | solution.py:173
  29.7 13.3 %run_summary.2.init_ref = f32[16,768]{1,0:T(8,128)S(1)} custom-call(f32[256,768]{1,0:T(8,128)S(1)} %get-tuple-element.448.step_ref, f32[256,768]{1,0:T(8,128)S(1)} %get-tuple-element.447.drive_ref, f32[256,16,128]{2,1,0:T(8,128)S(1)} %broadcast_in_dim.83.coef_ref.inject_ref, f32[16,768]{1,0:T(8,128)S(1)} %bitcast_multiply_fusion.3.slope_ref), custom_call_target="tpu_custom_call" | custom-call | flops 16000 | bytes 16000 | tf_op jit(solution)/shard_map/run_summary/pallas_call | solution.py:488
  43.7 8.1 %state_sweep.1 = (f32[256,768]{1,0:T(8,128)S(1)}, f32[256,16,768]{2,1,0:T(8,128)}, f32[16,768]{1,0:T(8,128)S(1)}) custom-call(f32[16,768]{1,0:T(8,128)S(1)} %run_summary.2.init_ref, f32[256,768]{1,0:T(8,128)S(1)} %get-tuple-element.448.step_ref, f32[256,768]{1,0:T(8,128)S(1)} %get-tuple-element.447.drive_ref, ...), custom_call_target="tpu_custom_call" | custom-call | flops 11000 | bytes 11000 | tf_op jit(solution)/shard_map/state_sweep/pallas_call | solution.py:539
  54.8 13.8 %head_sum.9 = f32[256,1536]{1,0:T(8,128)S(1)} custom-call(f32[256,1536]{1,0:T(8,128)S(1)} %fusion.203.x_ref), custom_call_target="tpu_custom_call" | custom-call | flops 15000 | bytes 15000 | tf_op jit(solution)/shard_map/head_sum/pallas_call | solution.py:173
  80.8 14.0 %head_sum.10 = f32[256,1536]{1,0:T(8,128)S(1)} custom-call(f32[256,1536]{1,0:T(8,128)S(1)} %copy-done.14), custom_call_target="tpu_custom_call" | custom-call | flops 15000 | bytes 15000 | tf_op jit(solution)/shard_map/head_sum/pallas_call | solution.py:173
  98.6 21.5 %attend.1 = (bf16[256,384]{1,0:T(8,128)(2,1)S(1)}, f32[128,1536]{1,0:T(8,128)S(1)}, f32[1,1536]{1,0:T(1,128)S(1)}, bf16[8,256,256]{2,1,0:T(8,128)(2,1)S(1)}) custom-call(bf16[256,384]{1,0:T(8,128)(2,1)S(1)} %convolution_convert_fusion.17.q_ref, bf16[256,256]{1,0:T(8,128)(2,1)S(1)} %pad_maximum_fusion.9.x_ref, s32[2048,1]{1,0:T(8,128)S(1)} %copy-done.10, ...), custom_call_target="tpu_custom_call" | custom-call | flops 12000 | bytes 12000 | tf_op jit(solution)/shard_map/attend/pallas_call | solution.py:814
  120.8 13.1 %head_sum.11 = f32[256,1536]{1,0:T(8,128)S(1)} custom-call(f32[256,1536]{1,0:T(8,128)S(1)} %fusion.206.x_ref), custom_call_target="tpu_custom_call" | custom-call | flops 15000 | bytes 15000 | tf_op jit(solution)/shard_map/head_sum/pallas_call | solution.py:173
  163.1 3.3 convolution_convert_fusion.2
  174.2 14.7 %head_sum.12 = f32[256,1664]{1,0:T(8,128)S(1)} custom-call(f32[256,1664]{1,0:T(8,128)S(1)} %select_maximum_fusion.x_ref), custom_call_target="tpu_custom_call" | custom-call | flops 16000 | bytes 16000 | tf_op jit(solution)/shard_map/head_sum/pallas_call | solution.py:173
  213.1 46.5 %scatter_and_head_sum.1 = (f32[256,128]{1,0:T(8,128)S(1)}, f32[256,128]{1,0:T(8,128)S(1)}, f32[256,1536]{1,0:T(8,128)S(1)}) custom-call(bf16[4,2,256,128]{3,2,1,0:T(8,128)(2,1)S(1)} %bitcast.448, bf16[4,2,256,128]{3,2,1,0:T(8,128)(2,1)S(1)} %bitcast.449, f32[256,1536]{1,0:T(8,128)S(1)} %fusion.149.refs_2_), custom_call_target="tpu_custom_call" | custom-call | flops 20000 | bytes 20000 | tf_op jit(solution)/shard_map/scatter_and_head_sum/pallas_call | solution.py:315
  264.6 3.0 convert_add_fusion
  277.2 13.9 %head_sum.13 = f32[256,1536]{1,0:T(8,128)S(1)} custom-call(f32[256,1536]{1,0:T(8,128)S(1)} %convolution_add_fusion.3.x_ref), custom_call_target="tpu_custom_call" | custom-call | flops 15000 | bytes 15000 | tf_op jit(solution)/shard_map/head_sum/pallas_call | solution.py:173
  292.6 3.7 fusion.193
  302.9 3.7 fusion.128
  307.6 7.1 %collective-permute-done.3 = bf16[4,384,256]{2,1,0:T(8,128)(2,1)} collective-permute-done((bf16[4,384,256]{2,1,0:T(8,128)(2,1)}, bf16[4,384,256]{2,1,0:T(8,128)(2,1)}, u32[]{:S(2)}, u32[]{:S(2)}) %collective-permute-start.3) | collective-permute-done | bytes 786464 | tf_op jit(solution)/shard_map/ppermute | solution.py:981
  325.3 3.1 fusion.9
  328.5 4.5 collective-permute-start.7
  336.2 13.5 %head_sum.14 = f32[256,1536]{1,0:T(8,128)S(1)} custom-call(f32[256,1536]{1,0:T(8,128)S(1)} %convolution_add_fusion.x_ref), custom_call_target="tpu_custom_call" | custom-call | flops 15000 | bytes 15000 | tf_op jit(solution)/shard_map/head_sum/pallas_call | solution.py:173
  364.3 19.5 %collective-permute-done.6 = bf16[4,192,256]{2,1,0:T(8,128)(2,1)} collective-permute-done((bf16[4,192,256]{2,1,0:T(8,128)(2,1)}, bf16[4,192,256]{2,1,0:T(8,128)(2,1)}, u32[]{:S(2)}, u32[]{:S(2)}) %collective-permute-start.6) | collective-permute-done | bytes 393248 | tf_op jit(solution)/shard_map/ppermute | solution.py:981
  384.9 11.6 %run_summary.3.in_ref = f32[16,768]{1,0:T(8,128)S(1)} custom-call(f32[256,768]{1,0:T(8,128)S(1)} %copy-done.7, f32[256,768]{1,0:T(8,128)S(1)} %copy-done.16, f32[256,16,128]{2,1,0:T(8,128)S(1)} %copy-done.5, f32[16,768]{1,0:T(8,128)S(1)} %bitcast_multiply_fusion.3.slope_ref), custom_call_target="tpu_custom_call" | custom-call | flops 16000 | bytes 16000 | tf_op jit(solution)/shard_map/run_summary/pallas_call | solution.py:488
  396.6 3.0 fusion.24
  407.7 12.8 %adjoint_sweep.1 = (f32[256,768]{1,0:T(8,128)S(1)}, f32[256,768]{1,0:T(8,128)S(1)}, f32[256,16,128]{2,1,0:T(8,128)S(1)}, f32[256,16,128]{2,1,0:T(8,128)S(1)}, f32[16,768]{1,0:T(8,128)S(1)}) custom-call(f32[16,768]{1,0:T(8,128)S(1)} %run_summary.3.in_ref, f32[16,768]{1,0:T(8,128)S(1)} %copy-done.33, f32[256,16,768]{2,1,0:T(8,128)} %get-tuple-element.131.before_ref, ...), custom_call_target="tpu_custom_call" | custom-call | flops 15000 | bytes 15000 | tf_op jit(solution)/shard_map/adjoint_sweep/pallas_call | solution.py:624
  423.6 3.0 reduce_sum.307
  429.3 3.4 fusion.8
  439.0 5.2 collective-permute-done.11
  458.5 6.0 head_sum.15
  470.0 12.4 %collective-permute-done.15 = bf16[1,384,1024]{2,1,0:T(8,128)(2,1)} collective-permute-done((bf16[1,384,1024]{2,1,0:T(8,128)(2,1)}, bf16[1,384,1024]{2,1,0:T(8,128)(2,1)}, u32[]{:S(2)}, u32[]{:S(2)}) %collective-permute-start.15) | collective-permute-done | bytes 786464 | tf_op jit(solution)/shard_map/ppermute | solution.py:981
  492.1 3.6 collective-permute-start.25
  505.4 8.2 %collective-permute-done.20 = bf16[1,192,1024]{2,1,0:T(8,128)(2,1)S(1)} collective-permute-done((bf16[1,192,1024]{2,1,0:T(8,128)(2,1)S(1)}, bf16[1,192,1024]{2,1,0:T(8,128)(2,1)S(1)}, u32[]{:S(2)}, u32[]{:S(2)}) %collective-permute-start.20) | collective-permute-done | bytes 393248 | tf_op jit(solution)/shard_map/ppermute | solution.py:981
  526.5 4.0 collective-permute-done.21
  537.2 55.2 %last_sums.1 = (f32[192,384]{1,0:T(8,128)S(1)}, f32[192,384]{1,0:T(8,128)S(1)}, f32[96,256]{1,0:T(8,128)S(1)}, f32[32,128]{1,0:T(8,128)S(1)}, f32[256,1536]{1,0:T(8,128)S(1)}, /*index=5*/f32[1,1536]{1,0:T(1,128)S(1)}) custom-call(bf16[4,2,192,384]{3,2,1,0:T(8,128)(2,1)S(1)} %bitcast.446, bf16[4,2,192,384]{3,2,1,0:T(8,128)(2,1)S(1)} %bitcast.445, ...), custom_call_target="tpu_custom_call" | custom-call | flops 20000 | bytes 20000 | tf_op jit(solution)/shard_map/last_sums/pallas_call | solution.py:383
  (741 shorter events, 241.9 us)
Async XLA Ops:
  0.7 151.9 %copy-start = (bf16[4,256,1536]{2,1,0:T(8,128)(2,1)S(1)}, bf16[4,256,1536]{2,1,0:T(8,128)(2,1)}, u32[]{:S(2)}) copy-start(bf16[4,256,1536]{2,1,0:T(8,128)(2,1)} %param.59) | copy-start | bytes 9437188
  6.0 12.9 %collective-permute-start = (bf16[3,768]{1,0:T(4,128)(2,1)S(1)}, bf16[3,768]{1,0:T(4,128)(2,1)S(1)}, u32[]{:S(2)}, u32[]{:S(2)}) collective-permute-start(bf16[3,768]{1,0:T(4,128)(2,1)S(1)} %slice.384), channel_id=1, source_target_pairs={{0,4},{4,8},{8,12},{12,16},{16,20},{20,24},{24,28},{1,5},{5,9},{9,... | collective-permute-start | bytes 13832 | tf_op jit(solution)/shard_map/ppermute | solution.py:31
  20.8 48.1 %copy-start.167 = (f32[1536]{0:T(1024)}, f32[1536]{0:T(1024)S(1)}, u32[]{:S(2)}) copy-start(f32[1536]{0:T(1024)S(1)} %convert_element_type.380) | copy-start | bytes 18436
  54.8 40.3 %copy-start.173 = (f32[1536]{0:T(1024)}, f32[1536]{0:T(1024)S(1)}, u32[]{:S(2)}) copy-start(f32[1536]{0:T(1024)S(1)} %convert_element_type.383) | copy-start | bytes 18436
  95.0 38.9 %copy-start.43 = (f32[256,1536]{1,0:T(8,128)}, f32[256,1536]{1,0:T(8,128)S(1)}, u32[]{:S(2)}) copy-start(f32[256,1536]{1,0:T(8,128)S(1)} %get-tuple-element.365) | copy-start | bytes 4718596
  166.5 95.1 %collective-permute-start.2 = (bf16[4,768,512]{2,1,0:T(8,128)(2,1)}, bf16[4,768,512]{2,1,0:T(8,128)(2,1)}, u32[]{:S(2)}, u32[]{:S(2)}) collective-permute-start(bf16[4,768,512]{2,1,0:T(8,128)(2,1)} %convolution_convert_fusion.2), channel_id=1, source_target_pairs={{0,4},{4,0},{8,12},{12,8},{16,20},{20,16},{24,28},{28,24},{1,5},{5... | collective-permute-start | bytes 9437192 | tf_op jit(solution)/shard_map/ppermute | solution.py:981
  173.6 39.5 %collective-permute-start.1 = (bf16[4,768,256]{2,1,0:T(8,128)(2,1)}, bf16[4,768,256]{2,1,0:T(8,128)(2,1)}, u32[]{:S(2)}, u32[]{:S(2)}) collective-permute-start(bf16[4,768,256]{2,1,0:T(8,128)(2,1)} %convolution_convert_fusion.7), channel_id=1, source_target_pairs={{0,8},{4,12},{8,0},{12,4},{16,24},{20,28},{24,16},{28,20},{1,9},{5... | collective-permute-start | bytes 4718600 | tf_op jit(solution)/shard_map/ppermute | solution.py:981
  207.2 193.3 %copy-start.121 = (bf16[1,192,256]{1,2,0:T(8,128)(2,1)}, bf16[1,192,256]{1,2,0:T(8,128)(2,1)S(1)}, u32[]{:S(2)}) copy-start(bf16[1,192,256]{1,2,0:T(8,128)(2,1)S(1)} %get-tuple-element.423) | copy-start | bytes 294916
  263.5 51.3 %collective-permute-start.5 = (bf16[1,768,1024]{1,2,0:T(8,128)(2,1)}, bf16[1,768,1024]{1,2,0:T(8,128)(2,1)}, u32[]{:S(2)}, u32[]{:S(2)}) collective-permute-start(bf16[1,768,1024]{1,2,0:T(8,128)(2,1)} %pad_maximum_fusion), channel_id=1, source_target_pairs={{0,4},{4,0},{8,12},{12,8},{16,20},{20,16},{24,28},{28,24},{1,5},{5... | collective-permute-start | bytes 4718600 | tf_op jit(solution)/shard_map/ppermute | solution.py:981
  269.1 45.6 %collective-permute-start.4 = (bf16[4,384,512]{2,1,0:T(8,128)(2,1)}, bf16[4,384,512]{2,1,0:T(8,128)(2,1)}, u32[]{:S(2)}, u32[]{:S(2)}) collective-permute-start(bf16[4,384,512]{2,1,0:T(8,128)(2,1)} %slice.576), channel_id=1, source_target_pairs={{0,8},{4,12},{8,0},{12,4},{16,24},{20,28},{24,16},{28,20},{1,9},{5... | collective-permute-start | bytes 4718600 | tf_op jit(solution)/shard_map/ppermute | solution.py:981
  276.2 38.5 %collective-permute-start.3 = (bf16[4,384,256]{2,1,0:T(8,128)(2,1)}, bf16[4,384,256]{2,1,0:T(8,128)(2,1)}, u32[]{:S(2)}, u32[]{:S(2)}) collective-permute-start(bf16[4,384,256]{2,1,0:T(8,128)(2,1)} %slice.581), channel_id=1, source_target_pairs={{0,4},{4,0},{8,12},{12,8},{16,20},{20,16},{24,28},{28,24},{1,5},{5... | collective-permute-start | bytes 2359304 | tf_op jit(solution)/shard_map/ppermute | solution.py:981
  299.5 64.7 %collective-permute-start.9 = (bf16[1,768,1024]{2,1,0:T(8,128)(2,1)}, bf16[1,768,1024]{2,1,0:T(8,128)(2,1)}, u32[]{:S(2)}, u32[]{:S(2)}) collective-permute-start(bf16[1,768,1024]{2,1,0:T(8,128)(2,1)} %fusion.11), channel_id=1, source_target_pairs={{0,8},{4,12},{8,0},{12,4},{16,24},{20,28},{24,16},{28,20},{1,9},{5... | collective-permute-start | bytes 4718600 | tf_op jit(solution)/shard_map/ppermute | solution.py:981
  315.5 45.4 %copy-start.64 = (bf16[256,1024]{1,0:T(8,128)(2,1)}, bf16[256,1024]{1,0:T(8,128)(2,1)S(1)}, u32[]{:S(2)}) copy-start(bf16[256,1024]{1,0:T(8,128)(2,1)S(1)} %get-tuple-element.389) | copy-start | bytes 1572868
  320.1 63.7 %collective-permute-start.10 = (bf16[1,768,1024]{2,1,0:T(8,128)(2,1)}, bf16[1,768,1024]{2,1,0:T(8,128)(2,1)}, u32[]{:S(2)}, u32[]{:S(2)}) collective-permute-start(bf16[1,768,1024]{2,1,0:T(8,128)(2,1)} %fusion.12), channel_id=1, source_target_pairs={{0,4},{4,0},{8,12},{12,8},{16,20},{20,16},{24,28},{28,24},{1,5},{5... | collective-permute-start | bytes 4718600 | tf_op jit(solution)/shard_map/ppermute | solution.py:981
  324.0 59.8 %collective-permute-start.8 = (bf16[1,384,1024]{1,2,0:T(8,128)(2,1)}, bf16[1,384,1024]{1,2,0:T(8,128)(2,1)}, u32[]{:S(2)}, u32[]{:S(2)}) collective-permute-start(bf16[1,384,1024]{1,2,0:T(8,128)(2,1)} %slice.580), channel_id=1, source_target_pairs={{0,8},{4,12},{8,0},{12,4},{16,24},{20,28},{24,16},{28,20},{1,9},{5... | collective-permute-start | bytes 2359304 | tf_op jit(solution)/shard_map/ppermute | solution.py:981
  328.5 55.3 %collective-permute-start.7 = (bf16[4,192,512]{2,1,0:T(8,128)(2,1)}, bf16[4,192,512]{2,1,0:T(8,128)(2,1)}, u32[]{:S(2)}, u32[]{:S(2)}) collective-permute-start(bf16[4,192,512]{2,1,0:T(8,128)(2,1)} %fusion.9), channel_id=1, source_target_pairs={{0,16},{4,20},{8,24},{12,28},{16,0},{20,4},{24,8},{28,12},{1,17},{... | collective-permute-start | bytes 2359304 | tf_op jit(solution)/shard_map/ppermute | solution.py:981
  336.1 47.6 %collective-permute-start.6 = (bf16[4,192,256]{2,1,0:T(8,128)(2,1)}, bf16[4,192,256]{2,1,0:T(8,128)(2,1)}, u32[]{:S(2)}, u32[]{:S(2)}) collective-permute-start(bf16[4,192,256]{2,1,0:T(8,128)(2,1)} %fusion.75), channel_id=1, source_target_pairs={{0,16},{4,20},{8,24},{12,28},{16,0},{20,4},{24,8},{28,12},{1,17},{... | collective-permute-start | bytes 1179656 | tf_op jit(solution)/shard_map/ppermute | solution.py:981
  399.6 39.4 %collective-permute-start.13 = (bf16[1,192,1024]{1,2,0:T(8,128)(2,1)}, bf16[1,192,1024]{1,2,0:T(8,128)(2,1)}, u32[]{:S(2)}, u32[]{:S(2)}) collective-permute-start(bf16[1,192,1024]{1,2,0:T(8,128)(2,1)} %fusion.24), channel_id=1, source_target_pairs={{0,16},{4,20},{8,24},{12,28},{16,0},{20,4},{24,8},{28,12},{1,17},{... | collective-permute-start | bytes 1179656 | tf_op jit(solution)/shard_map/ppermute | solution.py:981
  403.9 35.0 %collective-permute-start.12 = (bf16[1,384,1024]{2,1,0:T(8,128)(2,1)}, bf16[1,384,1024]{2,1,0:T(8,128)(2,1)}, u32[]{:S(2)}, u32[]{:S(2)}) collective-permute-start(bf16[1,384,1024]{2,1,0:T(8,128)(2,1)} %slice.579), channel_id=1, source_target_pairs={{0,8},{4,12},{8,0},{12,4},{16,24},{20,28},{24,16},{28,20},{1,9},{5... | collective-permute-start | bytes 2359304 | tf_op jit(solution)/shard_map/ppermute | solution.py:981
  406.5 37.6 %collective-permute-start.11 = (bf16[1,768,1024]{2,1,0:T(8,128)(2,1)}, bf16[1,768,1024]{2,1,0:T(8,128)(2,1)}, u32[]{:S(2)}, u32[]{:S(2)}) collective-permute-start(bf16[1,768,1024]{2,1,0:T(8,128)(2,1)} %fusion.10), channel_id=1, source_target_pairs={{0,4},{4,0},{8,12},{12,8},{16,20},{20,16},{24,28},{28,24},{1,5},{5... | collective-permute-start | bytes 4718600 | tf_op jit(solution)/shard_map/ppermute | solution.py:981
  427.9 42.1 %collective-permute-start.14 = (bf16[1,768,768]{2,1,0:T(8,128)(2,1)}, bf16[1,768,768]{2,1,0:T(8,128)(2,1)}, u32[]{:S(2)}, u32[]{:S(2)}) collective-permute-start(bf16[1,768,768]{2,1,0:T(8,128)(2,1)} %fusion.13), channel_id=1, source_target_pairs={{0,8},{4,12},{8,0},{12,4},{16,24},{20,28},{24,16},{28,20},{1,9},{5... | collective-permute-start | bytes 3538952 | tf_op jit(solution)/shard_map/ppermute | solution.py:981
  428.2 56.4 %collective-permute-start.17 = (bf16[1,768,768]{2,1,0:T(8,128)(2,1)}, bf16[1,768,768]{2,1,0:T(8,128)(2,1)}, u32[]{:S(2)}, u32[]{:S(2)}) collective-permute-start(bf16[1,768,768]{2,1,0:T(8,128)(2,1)} %fusion.14), channel_id=1, source_target_pairs={{0,4},{4,0},{8,12},{12,8},{16,20},{20,16},{24,28},{28,24},{1,5},{5... | collective-permute-start | bytes 3538952 | tf_op jit(solution)/shard_map/ppermute | solution.py:981
  447.2 35.2 %collective-permute-start.15 = (bf16[1,384,1024]{2,1,0:T(8,128)(2,1)}, bf16[1,384,1024]{2,1,0:T(8,128)(2,1)}, u32[]{:S(2)}, u32[]{:S(2)}) collective-permute-start(bf16[1,384,1024]{2,1,0:T(8,128)(2,1)} %slice.578), channel_id=1, source_target_pairs={{0,4},{4,0},{8,12},{12,8},{16,20},{20,16},{24,28},{28,24},{1,5},{5... | collective-permute-start | bytes 2359304 | tf_op jit(solution)/shard_map/ppermute | solution.py:981
  450.5 34.1 %collective-permute-start.18 = (bf16[1,192,1024]{2,1,0:T(8,128)(2,1)}, bf16[1,192,1024]{2,1,0:T(8,128)(2,1)}, u32[]{:S(2)}, u32[]{:S(2)}) collective-permute-start(bf16[1,192,1024]{2,1,0:T(8,128)(2,1)} %fusion.74), channel_id=1, source_target_pairs={{0,16},{4,20},{8,24},{12,28},{16,0},{20,4},{24,8},{28,12},{1,17},{... | collective-permute-start | bytes 1179656 | tf_op jit(solution)/shard_map/ppermute | solution.py:981
  454.4 30.2 %collective-permute-start.16 = (bf16[1,384,1024]{2,1,0:T(8,128)(2,1)}, bf16[1,384,1024]{2,1,0:T(8,128)(2,1)}, u32[]{:S(2)}, u32[]{:S(2)}) collective-permute-start(bf16[1,384,1024]{2,1,0:T(8,128)(2,1)} %slice.577), channel_id=1, source_target_pairs={{0,8},{4,12},{8,0},{12,4},{16,24},{20,28},{24,16},{28,20},{1,9},{5... | collective-permute-start | bytes 2359304 | tf_op jit(solution)/shard_map/ppermute | solution.py:981
  487.8 25.8 %collective-permute-start.20 = (bf16[1,192,1024]{2,1,0:T(8,128)(2,1)S(1)}, bf16[1,192,1024]{2,1,0:T(8,128)(2,1)S(1)}, u32[]{:S(2)}, u32[]{:S(2)}) collective-permute-start(bf16[1,192,1024]{2,1,0:T(8,128)(2,1)S(1)} %fusion.73), channel_id=1, source_target_pairs={{0,16},{4,20},{8,24},{12,28},{16,0},{20,4},{24,8},{28,12},{1,17},{... | collective-permute-start | bytes 1179656 | tf_op jit(solution)/shard_map/ppermute | solution.py:981
  489.5 15.8 %collective-permute-start.19 = (f32[3,768]{1,0:T(4,128)S(1)}, f32[3,768]{1,0:T(4,128)S(1)}, u32[]{:S(2)}, u32[]{:S(2)}) collective-permute-start(f32[3,768]{1,0:T(4,128)S(1)} %slice.326), channel_id=1, source_target_pairs={{4,0},{8,4},{12,8},{16,12},{20,16},{24,20},{28,24},{5,1},{9,5},{13... | collective-permute-start | bytes 27656 | tf_op jit(solution)/shard_map/ppermute | solution.py:31
  492.1 29.7 %collective-permute-start.25 = (bf16[1,192,1024]{2,1,0:T(8,128)(2,1)S(1)}, bf16[1,192,1024]{2,1,0:T(8,128)(2,1)S(1)}, u32[]{:S(2)}, u32[]{:S(2)}) collective-permute-start(bf16[1,192,1024]{2,1,0:T(8,128)(2,1)S(1)} %fusion.61), channel_id=1, source_target_pairs={{0,16},{4,20},{8,24},{12,28},{16,0},{20,4},{24,8},{28,12},{1,17},{... | collective-permute-start | bytes 1179656 | tf_op jit(solution)/shard_map/ppermute | solution.py:981
  498.8 27.7 %collective-permute-start.22 = (bf16[1,384,768]{2,1,0:T(8,128)(2,1)}, bf16[1,384,768]{2,1,0:T(8,128)(2,1)}, u32[]{:S(2)}, u32[]{:S(2)}) collective-permute-start(bf16[1,384,768]{2,1,0:T(8,128)(2,1)} %slice.582), channel_id=1, source_target_pairs={{0,4},{4,0},{8,12},{12,8},{16,20},{20,16},{24,28},{28,24},{1,5},{5... | collective-permute-start | bytes 1769480 | tf_op jit(solution)/shard_map/ppermute | solution.py:981
  502.1 28.3 %collective-permute-start.21 = (bf16[1,384,768]{2,1,0:T(8,128)(2,1)}, bf16[1,384,768]{2,1,0:T(8,128)(2,1)}, u32[]{:S(2)}, u32[]{:S(2)}) collective-permute-start(bf16[1,384,768]{2,1,0:T(8,128)(2,1)} %slice.583), channel_id=1, source_target_pairs={{0,8},{4,12},{8,0},{12,4},{16,24},{20,28},{24,16},{28,20},{1,9},{5... | collective-permute-start | bytes 1769480 | tf_op jit(solution)/shard_map/ppermute | solution.py:981
  532.4 67.9 %collective-permute-start.24 = (bf16[1,192,768]{2,1,0:T(8,128)(2,1)}, bf16[1,192,768]{2,1,0:T(8,128)(2,1)S(1)}, u32[]{:S(2)}, u32[]{:S(2)}) collective-permute-start(bf16[1,192,768]{2,1,0:T(8,128)(2,1)} %fusion.80), channel_id=1, source_target_pairs={{0,16},{4,20},{8,24},{12,28},{16,0},{20,4},{24,8},{28,12},{1,17},{... | collective-permute-start | bytes 884744 | tf_op jit(solution)/shard_map/ppermute | solution.py:981
  534.5 68.0 %collective-permute-start.23 = (bf16[1,192,768]{2,1,0:T(8,128)(2,1)}, bf16[1,192,768]{2,1,0:T(8,128)(2,1)S(1)}, u32[]{:S(2)}, u32[]{:S(2)}) collective-permute-start(bf16[1,192,768]{2,1,0:T(8,128)(2,1)} %fusion.83), channel_id=1, source_target_pairs={{0,16},{4,20},{8,24},{12,28},{16,0},{20,4},{24,8},{28,12},{1,17},{... | collective-permute-start | bytes 884744 | tf_op jit(solution)/shard_map/ppermute | solution.py:981
  (233 other events, 1368.5 us)

commit v7 on v6

--- a/solution.py
+++ b/solution.py
@@ -1109,7 +1109,8 @@
     expert_count = router.shape[1]
     experts = jnp.arange(expert_count, dtype=jnp.int32)
     named = (expert_routes[:, :, None] == experts).astype(jnp.float32)
-    gate_weights = jax.nn.softmax(jnp.sum(named * logits[:, None, :], axis=2), axis=1)
+    lead = jnp.sum((named[:, 0] - named[:, 1]) * logits, axis=1, keepdims=True)
+    gate_weights = jax.nn.sigmoid(jnp.concatenate([lead, -lead], axis=1))
     route_flat = expert_routes.reshape(-1)
     pair_count = route_flat.shape[0]
     pair_order = jnp.arange(pair_count, dtype=jnp.int32)

time: 613 us -> 609 us (level)
    unnamed x490 -> x488, local copies, waits for them, and re-layouts: 36.7 us -> 35.9 us
where the time goes in v7:
time: 609 us; the launch traced here: 603 us
  Pallas kernels  267 us (44%)
  local copies, waits for them, and re-layouts  82 us (13%)
  other arithmetic  78.4 us (13%)
  matrix products  78 us (13%)
  waiting for transfers between devices  56 us (9%)
  starting transfers between devices  37.3 us (6%)
    pallas_call x8, Pallas kernels, head_sum(): pl.pallas_call(kernel, out_shape=jax.ShapeDtypeStruct((rows, width), jnp....  95.4 us
    dot_general x46, matrix products, product(): return jnp.dot(left, right, preferred_element_type=jnp.float32)  59.2 us
    ppermute x24, waiting for transfers between devices, send(): flow['got'].append(lax.ppermute(flow['out'], 'seq', route))  56 us
    pallas_call x1, Pallas kernels, last_sums(): pl.pallas_call(kernel, out_shape=[jax.ShapeDtypeStruct(shape, jnp.float32...  55.3 us
    pallas_call x1, Pallas kernels, scatter_and_head_sum(): pl.pallas_call(kernel, out_shape=[jax.ShapeDtypeStruct(shape, jnp.float32...  46.8 us
    unnamed x488, local copies, waits for them, and re-layouts  35.9 us
    convert_element_type x20, other arithmetic, to_low(): return values.astype(jnp.bfloat16)  31.7 us
    ppermute x24, starting transfers between devices, send(): flow['got'].append(lax.ppermute(flow['out'], 'seq', route))  31 us
  transfers between devices with their start and end apart: 26, of which 6 were waited for; matrix products, arithmetic and copies ran while one was open for 25% of the time, Pallas kernels for 27%

profile of v7, /device:TPU:0, one launch (start us, length us, event | category | flops | bytes accessed | tf_op | source)
XLA Modules:
  0.0 602.9 jit_solution(10028586423219677700)
XLA Ops:
  5.2 4.9 collective-permute-start
  20.7 6.5 %head_sum.8 = f32[256,128]{1,0:T(8,128)S(1)} custom-call(f32[256,128]{1,0:T(8,128)S(1)} %fusion.158.x_ref), custom_call_target="tpu_custom_call" | custom-call | flops 6000 | bytes 6000 | tf_op jit(solution)/shard_map/head_sum/pallas_call | solution.py:173
  29.6 13.3 %run_summary.2.init_ref = f32[16,768]{1,0:T(8,128)S(1)} custom-call(f32[256,768]{1,0:T(8,128)S(1)} %get-tuple-element.446.step_ref, f32[256,768]{1,0:T(8,128)S(1)} %get-tuple-element.445.drive_ref, f32[256,16,128]{2,1,0:T(8,128)S(1)} %broadcast_in_dim.85.coef_ref.inject_ref, f32[16,768]{1,0:T(8,128)S(1)} %bitcast_multiply_fusion.3.slope_ref), custom_call_target="tpu_custom_call" | custom-call | flops 16000 | bytes 16000 | tf_op jit(solution)/shard_map/run_summary/pallas_call | solution.py:488
  43.6 8.1 %state_sweep.1 = (f32[256,768]{1,0:T(8,128)S(1)}, f32[256,16,768]{2,1,0:T(8,128)}, f32[16,768]{1,0:T(8,128)S(1)}) custom-call(f32[16,768]{1,0:T(8,128)S(1)} %run_summary.2.init_ref, f32[256,768]{1,0:T(8,128)S(1)} %get-tuple-element.446.step_ref, f32[256,768]{1,0:T(8,128)S(1)} %get-tuple-element.445.drive_ref, ...), custom_call_target="tpu_custom_call" | custom-call | flops 11000 | bytes 11000 | tf_op jit(solution)/shard_map/state_sweep/pallas_call | solution.py:539
  54.7 13.8 %head_sum.9 = f32[256,1536]{1,0:T(8,128)S(1)} custom-call(f32[256,1536]{1,0:T(8,128)S(1)} %fusion.205.x_ref), custom_call_target="tpu_custom_call" | custom-call | flops 15000 | bytes 15000 | tf_op jit(solution)/shard_map/head_sum/pallas_call | solution.py:173
  80.6 14.0 %head_sum.10 = f32[256,1536]{1,0:T(8,128)S(1)} custom-call(f32[256,1536]{1,0:T(8,128)S(1)} %copy-done.14), custom_call_target="tpu_custom_call" | custom-call | flops 15000 | bytes 15000 | tf_op jit(solution)/shard_map/head_sum/pallas_call | solution.py:173
  98.4 21.5 %attend.1 = (bf16[256,384]{1,0:T(8,128)(2,1)S(1)}, f32[128,1536]{1,0:T(8,128)S(1)}, f32[1,1536]{1,0:T(1,128)S(1)}, bf16[8,256,256]{2,1,0:T(8,128)(2,1)S(1)}) custom-call(bf16[256,384]{1,0:T(8,128)(2,1)S(1)} %convolution_convert_fusion.17.q_ref, bf16[256,256]{1,0:T(8,128)(2,1)S(1)} %pad_maximum_fusion.9.x_ref, s32[2048,1]{1,0:T(8,128)S(1)} %copy-done.10, ...), custom_call_target="tpu_custom_call" | custom-call | flops 12000 | bytes 12000 | tf_op jit(solution)/shard_map/attend/pallas_call | solution.py:814
  120.7 13.1 %head_sum.11 = f32[256,1536]{1,0:T(8,128)S(1)} custom-call(f32[256,1536]{1,0:T(8,128)S(1)} %fusion.208.x_ref), custom_call_target="tpu_custom_call" | custom-call | flops 15000 | bytes 15000 | tf_op jit(solution)/shard_map/head_sum/pallas_call | solution.py:173
  159.9 3.3 convolution_convert_fusion.2
  170.8 14.7 %head_sum.12 = f32[256,1664]{1,0:T(8,128)S(1)} custom-call(f32[256,1664]{1,0:T(8,128)S(1)} %select_maximum_fusion.x_ref), custom_call_target="tpu_custom_call" | custom-call | flops 16000 | bytes 16000 | tf_op jit(solution)/shard_map/head_sum/pallas_call | solution.py:173
  209.6 46.8 %scatter_and_head_sum.1 = (f32[256,128]{1,0:T(8,128)S(1)}, f32[256,128]{1,0:T(8,128)S(1)}, f32[256,1536]{1,0:T(8,128)S(1)}) custom-call(bf16[4,2,256,128]{3,2,1,0:T(8,128)(2,1)S(1)} %bitcast.453, bf16[4,2,256,128]{3,2,1,0:T(8,128)(2,1)S(1)} %bitcast.454, f32[256,1536]{1,0:T(8,128)S(1)} %fusion.150.refs_2_), custom_call_target="tpu_custom_call" | custom-call | flops 20000 | bytes 20000 | tf_op jit(solution)/shard_map/scatter_and_head_sum/pallas_call | solution.py:315
  261.5 3.0 convert_add_fusion
  274.2 13.9 %head_sum.13 = f32[256,1536]{1,0:T(8,128)S(1)} custom-call(f32[256,1536]{1,0:T(8,128)S(1)} %convolution_add_fusion.3.x_ref), custom_call_target="tpu_custom_call" | custom-call | flops 15000 | bytes 15000 | tf_op jit(solution)/shard_map/head_sum/pallas_call | solution.py:173
  289.6 3.7 fusion.196
  299.9 3.8 fusion.129
  304.7 7.0 %collective-permute-done.3 = bf16[4,384,256]{2,1,0:T(8,128)(2,1)} collective-permute-done((bf16[4,384,256]{2,1,0:T(8,128)(2,1)}, bf16[4,384,256]{2,1,0:T(8,128)(2,1)}, u32[]{:S(2)}, u32[]{:S(2)}) %collective-permute-start.3) | collective-permute-done | bytes 786464 | tf_op jit(solution)/shard_map/ppermute | solution.py:981
  322.5 3.1 fusion.9
  325.6 4.0 collective-permute-start.7
  332.9 13.5 %head_sum.14 = f32[256,1536]{1,0:T(8,128)S(1)} custom-call(f32[256,1536]{1,0:T(8,128)S(1)} %convolution_add_fusion.x_ref), custom_call_target="tpu_custom_call" | custom-call | flops 15000 | bytes 15000 | tf_op jit(solution)/shard_map/head_sum/pallas_call | solution.py:173
  360.9 19.5 %collective-permute-done.6 = bf16[4,192,256]{2,1,0:T(8,128)(2,1)} collective-permute-done((bf16[4,192,256]{2,1,0:T(8,128)(2,1)}, bf16[4,192,256]{2,1,0:T(8,128)(2,1)}, u32[]{:S(2)}, u32[]{:S(2)}) %collective-permute-start.6) | collective-permute-done | bytes 393248 | tf_op jit(solution)/shard_map/ppermute | solution.py:981
  381.6 11.7 %run_summary.3.in_ref = f32[16,768]{1,0:T(8,128)S(1)} custom-call(f32[256,768]{1,0:T(8,128)S(1)} %copy-done.7, f32[256,768]{1,0:T(8,128)S(1)} %copy-done.16, f32[256,16,128]{2,1,0:T(8,128)S(1)} %copy-done.5, f32[16,768]{1,0:T(8,128)S(1)} %bitcast_multiply_fusion.3.slope_ref), custom_call_target="tpu_custom_call" | custom-call | flops 16000 | bytes 16000 | tf_op jit(solution)/shard_map/run_summary/pallas_call | solution.py:488
  393.3 3.0 fusion.25
  404.5 12.8 %adjoint_sweep.1 = (f32[256,768]{1,0:T(8,128)S(1)}, f32[256,768]{1,0:T(8,128)S(1)}, f32[256,16,128]{2,1,0:T(8,128)S(1)}, f32[256,16,128]{2,1,0:T(8,128)S(1)}, f32[16,768]{1,0:T(8,128)S(1)}) custom-call(f32[16,768]{1,0:T(8,128)S(1)} %run_summary.3.in_ref, f32[16,768]{1,0:T(8,128)S(1)} %copy-done.33, f32[256,16,768]{2,1,0:T(8,128)} %get-tuple-element.131.before_ref, ...), custom_call_target="tpu_custom_call" | custom-call | flops 15000 | bytes 15000 | tf_op jit(solution)/shard_map/adjoint_sweep/pallas_call | solution.py:624
  420.4 3.0 reduce_sum.297
  426.1 3.4 fusion.8
  435.7 5.1 collective-permute-done.11
  455.3 6.0 %head_sum.15 = f32[256,128]{1,0:T(8,128)S(1)} custom-call(f32[256,128]{1,0:T(8,128)S(1)} %pad_maximum_fusion.10.x_ref), custom_call_target="tpu_custom_call" | custom-call | flops 6000 | bytes 6000 | tf_op jit(solution)/shard_map/head_sum/pallas_call | solution.py:173
  466.8 12.2 %collective-permute-done.15 = bf16[1,384,1024]{2,1,0:T(8,128)(2,1)} collective-permute-done((bf16[1,384,1024]{2,1,0:T(8,128)(2,1)}, bf16[1,384,1024]{2,1,0:T(8,128)(2,1)}, u32[]{:S(2)}, u32[]{:S(2)}) %collective-permute-start.15) | collective-permute-done | bytes 786464 | tf_op jit(solution)/shard_map/ppermute | solution.py:981
  488.8 3.7 collective-permute-start.25
  502.2 8.1 %collective-permute-done.20 = bf16[1,192,1024]{2,1,0:T(8,128)(2,1)S(1)} collective-permute-done((bf16[1,192,1024]{2,1,0:T(8,128)(2,1)S(1)}, bf16[1,192,1024]{2,1,0:T(8,128)(2,1)S(1)}, u32[]{:S(2)}, u32[]{:S(2)}) %collective-permute-start.20) | collective-permute-done | bytes 393248 | tf_op jit(solution)/shard_map/ppermute | solution.py:981
  523.2 4.1 collective-permute-done.21
  534.0 55.3 %last_sums.1 = (f32[192,384]{1,0:T(8,128)S(1)}, f32[192,384]{1,0:T(8,128)S(1)}, f32[96,256]{1,0:T(8,128)S(1)}, f32[32,128]{1,0:T(8,128)S(1)}, f32[256,1536]{1,0:T(8,128)S(1)}, /*index=5*/f32[1,1536]{1,0:T(1,128)S(1)}) custom-call(bf16[4,2,192,384]{3,2,1,0:T(8,128)(2,1)S(1)} %bitcast.451, bf16[4,2,192,384]{3,2,1,0:T(8,128)(2,1)S(1)} %bitcast.450, ...), custom_call_target="tpu_custom_call" | custom-call | flops 20000 | bytes 20000 | tf_op jit(solution)/shard_map/last_sums/pallas_call | solution.py:383
  (739 shorter events, 239.0 us)
Async XLA Ops:
  0.7 148.6 %copy-start = (bf16[4,256,1536]{2,1,0:T(8,128)(2,1)S(1)}, bf16[4,256,1536]{2,1,0:T(8,128)(2,1)}, u32[]{:S(2)}) copy-start(bf16[4,256,1536]{2,1,0:T(8,128)(2,1)} %param.59) | copy-start | bytes 9437188
  5.2 13.5 %collective-permute-start = (bf16[3,768]{1,0:T(4,128)(2,1)S(1)}, bf16[3,768]{1,0:T(4,128)(2,1)S(1)}, u32[]{:S(2)}, u32[]{:S(2)}) collective-permute-start(bf16[3,768]{1,0:T(4,128)(2,1)S(1)} %slice.392), channel_id=1, source_target_pairs={{0,4},{4,8},{8,12},{12,16},{16,20},{20,24},{24,28},{1,5},{5,9},{9,... | collective-permute-start | bytes 13832 | tf_op jit(solution)/shard_map/ppermute | solution.py:31
  20.7 48.1 %copy-start.167 = (f32[1536]{0:T(1024)}, f32[1536]{0:T(1024)S(1)}, u32[]{:S(2)}) copy-start(f32[1536]{0:T(1024)S(1)} %convert_element_type.382) | copy-start | bytes 18436
  54.7 40.2 %copy-start.173 = (f32[1536]{0:T(1024)}, f32[1536]{0:T(1024)S(1)}, u32[]{:S(2)}) copy-start(f32[1536]{0:T(1024)S(1)} %convert_element_type.385) | copy-start | bytes 18436
  94.9 38.9 %copy-start.43 = (f32[256,1536]{1,0:T(8,128)}, f32[256,1536]{1,0:T(8,128)S(1)}, u32[]{:S(2)}) copy-start(f32[256,1536]{1,0:T(8,128)S(1)} %get-tuple-element.363) | copy-start | bytes 4718596
  163.2 95.3 %collective-permute-start.2 = (bf16[4,768,512]{2,1,0:T(8,128)(2,1)}, bf16[4,768,512]{2,1,0:T(8,128)(2,1)}, u32[]{:S(2)}, u32[]{:S(2)}) collective-permute-start(bf16[4,768,512]{2,1,0:T(8,128)(2,1)} %convolution_convert_fusion.2), channel_id=1, source_target_pairs={{0,4},{4,0},{8,12},{12,8},{16,20},{20,16},{24,28},{28,24},{1,5},{5... | collective-permute-start | bytes 9437192 | tf_op jit(solution)/shard_map/ppermute | solution.py:981
  170.2 39.4 %collective-permute-start.1 = (bf16[4,768,256]{2,1,0:T(8,128)(2,1)}, bf16[4,768,256]{2,1,0:T(8,128)(2,1)}, u32[]{:S(2)}, u32[]{:S(2)}) collective-permute-start(bf16[4,768,256]{2,1,0:T(8,128)(2,1)} %convolution_convert_fusion.7), channel_id=1, source_target_pairs={{0,8},{4,12},{8,0},{12,4},{16,24},{20,28},{24,16},{28,20},{1,9},{5... | collective-permute-start | bytes 4718600 | tf_op jit(solution)/shard_map/ppermute | solution.py:981
  203.7 193.4 %copy-start.121 = (bf16[1,192,256]{1,2,0:T(8,128)(2,1)}, bf16[1,192,256]{1,2,0:T(8,128)(2,1)S(1)}, u32[]{:S(2)}) copy-start(bf16[1,192,256]{1,2,0:T(8,128)(2,1)S(1)} %get-tuple-element.421) | copy-start | bytes 294916
  260.3 51.4 %collective-permute-start.5 = (bf16[1,768,1024]{1,2,0:T(8,128)(2,1)}, bf16[1,768,1024]{1,2,0:T(8,128)(2,1)}, u32[]{:S(2)}, u32[]{:S(2)}) collective-permute-start(bf16[1,768,1024]{1,2,0:T(8,128)(2,1)} %pad_maximum_fusion), channel_id=1, source_target_pairs={{0,4},{4,0},{8,12},{12,8},{16,20},{20,16},{24,28},{28,24},{1,5},{5... | collective-permute-start | bytes 4718600 | tf_op jit(solution)/shard_map/ppermute | solution.py:981
  266.0 45.7 %collective-permute-start.4 = (bf16[4,384,512]{2,1,0:T(8,128)(2,1)}, bf16[4,384,512]{2,1,0:T(8,128)(2,1)}, u32[]{:S(2)}, u32[]{:S(2)}) collective-permute-start(bf16[4,384,512]{2,1,0:T(8,128)(2,1)} %slice.592), channel_id=1, source_target_pairs={{0,8},{4,12},{8,0},{12,4},{16,24},{20,28},{24,16},{28,20},{1,9},{5... | collective-permute-start | bytes 4718600 | tf_op jit(solution)/shard_map/ppermute | solution.py:981
  273.2 38.5 %collective-permute-start.3 = (bf16[4,384,256]{2,1,0:T(8,128)(2,1)}, bf16[4,384,256]{2,1,0:T(8,128)(2,1)}, u32[]{:S(2)}, u32[]{:S(2)}) collective-permute-start(bf16[4,384,256]{2,1,0:T(8,128)(2,1)} %slice.597), channel_id=1, source_target_pairs={{0,4},{4,0},{8,12},{12,8},{16,20},{20,16},{24,28},{28,24},{1,5},{5... | collective-permute-start | bytes 2359304 | tf_op jit(solution)/shard_map/ppermute | solution.py:981
  296.5 64.4 %collective-permute-start.9 = (bf16[1,768,1024]{2,1,0:T(8,128)(2,1)}, bf16[1,768,1024]{2,1,0:T(8,128)(2,1)}, u32[]{:S(2)}, u32[]{:S(2)}) collective-permute-start(bf16[1,768,1024]{2,1,0:T(8,128)(2,1)} %fusion.11), channel_id=1, source_target_pairs={{0,8},{4,12},{8,0},{12,4},{16,24},{20,28},{24,16},{28,20},{1,9},{5... | collective-permute-start | bytes 4718600 | tf_op jit(solution)/shard_map/ppermute | solution.py:981
  312.5 45.1 %copy-start.64 = (bf16[256,1024]{1,0:T(8,128)(2,1)}, bf16[256,1024]{1,0:T(8,128)(2,1)S(1)}, u32[]{:S(2)}) copy-start(bf16[256,1024]{1,0:T(8,128)(2,1)S(1)} %get-tuple-element.387) | copy-start | bytes 1572868
  317.1 63.3 %collective-permute-start.10 = (bf16[1,768,1024]{2,1,0:T(8,128)(2,1)}, bf16[1,768,1024]{2,1,0:T(8,128)(2,1)}, u32[]{:S(2)}, u32[]{:S(2)}) collective-permute-start(bf16[1,768,1024]{2,1,0:T(8,128)(2,1)} %fusion.12), channel_id=1, source_target_pairs={{0,4},{4,0},{8,12},{12,8},{16,20},{20,16},{24,28},{28,24},{1,5},{5... | collective-permute-start | bytes 4718600 | tf_op jit(solution)/shard_map/ppermute | solution.py:981
  321.0 59.4 %collective-permute-start.8 = (bf16[1,384,1024]{1,2,0:T(8,128)(2,1)}, bf16[1,384,1024]{1,2,0:T(8,128)(2,1)}, u32[]{:S(2)}, u32[]{:S(2)}) collective-permute-start(bf16[1,384,1024]{1,2,0:T(8,128)(2,1)} %slice.596), channel_id=1, source_target_pairs={{0,8},{4,12},{8,0},{12,4},{16,24},{20,28},{24,16},{28,20},{1,9},{5... | collective-permute-start | bytes 2359304 | tf_op jit(solution)/shard_map/ppermute | solution.py:981
  325.6 54.8 %collective-permute-start.7 = (bf16[4,192,512]{2,1,0:T(8,128)(2,1)}, bf16[4,192,512]{2,1,0:T(8,128)(2,1)}, u32[]{:S(2)}, u32[]{:S(2)}) collective-permute-start(bf16[4,192,512]{2,1,0:T(8,128)(2,1)} %fusion.9), channel_id=1, source_target_pairs={{0,16},{4,20},{8,24},{12,28},{16,0},{20,4},{24,8},{28,12},{1,17},{... | collective-permute-start | bytes 2359304 | tf_op jit(solution)/shard_map/ppermute | solution.py:981
  332.8 47.6 %collective-permute-start.6 = (bf16[4,192,256]{2,1,0:T(8,128)(2,1)}, bf16[4,192,256]{2,1,0:T(8,128)(2,1)}, u32[]{:S(2)}, u32[]{:S(2)}) collective-permute-start(bf16[4,192,256]{2,1,0:T(8,128)(2,1)} %fusion.76), channel_id=1, source_target_pairs={{0,16},{4,20},{8,24},{12,28},{16,0},{20,4},{24,8},{28,12},{1,17},{... | collective-permute-start | bytes 1179656 | tf_op jit(solution)/shard_map/ppermute | solution.py:981
  396.2 39.5 %collective-permute-start.13 = (bf16[1,192,1024]{1,2,0:T(8,128)(2,1)}, bf16[1,192,1024]{1,2,0:T(8,128)(2,1)}, u32[]{:S(2)}, u32[]{:S(2)}) collective-permute-start(bf16[1,192,1024]{1,2,0:T(8,128)(2,1)} %fusion.25), channel_id=1, source_target_pairs={{0,16},{4,20},{8,24},{12,28},{16,0},{20,4},{24,8},{28,12},{1,17},{... | collective-permute-start | bytes 1179656 | tf_op jit(solution)/shard_map/ppermute | solution.py:981
  400.6 35.2 %collective-permute-start.12 = (bf16[1,384,1024]{2,1,0:T(8,128)(2,1)}, bf16[1,384,1024]{2,1,0:T(8,128)(2,1)}, u32[]{:S(2)}, u32[]{:S(2)}) collective-permute-start(bf16[1,384,1024]{2,1,0:T(8,128)(2,1)} %slice.595), channel_id=1, source_target_pairs={{0,8},{4,12},{8,0},{12,4},{16,24},{20,28},{24,16},{28,20},{1,9},{5... | collective-permute-start | bytes 2359304 | tf_op jit(solution)/shard_map/ppermute | solution.py:981
  403.2 37.6 %collective-permute-start.11 = (bf16[1,768,1024]{2,1,0:T(8,128)(2,1)}, bf16[1,768,1024]{2,1,0:T(8,128)(2,1)}, u32[]{:S(2)}, u32[]{:S(2)}) collective-permute-start(bf16[1,768,1024]{2,1,0:T(8,128)(2,1)} %fusion.10), channel_id=1, source_target_pairs={{0,4},{4,0},{8,12},{12,8},{16,20},{20,16},{24,28},{28,24},{1,5},{5... | collective-permute-start | bytes 4718600 | tf_op jit(solution)/shard_map/ppermute | solution.py:981
  424.6 42.1 %collective-permute-start.14 = (bf16[1,768,768]{2,1,0:T(8,128)(2,1)}, bf16[1,768,768]{2,1,0:T(8,128)(2,1)}, u32[]{:S(2)}, u32[]{:S(2)}) collective-permute-start(bf16[1,768,768]{2,1,0:T(8,128)(2,1)} %fusion.13), channel_id=1, source_target_pairs={{0,8},{4,12},{8,0},{12,4},{16,24},{20,28},{24,16},{28,20},{1,9},{5... | collective-permute-start | bytes 3538952 | tf_op jit(solution)/shard_map/ppermute | solution.py:981
  424.9 56.4 %collective-permute-start.17 = (bf16[1,768,768]{2,1,0:T(8,128)(2,1)}, bf16[1,768,768]{2,1,0:T(8,128)(2,1)}, u32[]{:S(2)}, u32[]{:S(2)}) collective-permute-start(bf16[1,768,768]{2,1,0:T(8,128)(2,1)} %fusion.14), channel_id=1, source_target_pairs={{0,4},{4,0},{8,12},{12,8},{16,20},{20,16},{24,28},{28,24},{1,5},{5... | collective-permute-start | bytes 3538952 | tf_op jit(solution)/shard_map/ppermute | solution.py:981
  443.8 35.2 %collective-permute-start.15 = (bf16[1,384,1024]{2,1,0:T(8,128)(2,1)}, bf16[1,384,1024]{2,1,0:T(8,128)(2,1)}, u32[]{:S(2)}, u32[]{:S(2)}) collective-permute-start(bf16[1,384,1024]{2,1,0:T(8,128)(2,1)} %slice.594), channel_id=1, source_target_pairs={{0,4},{4,0},{8,12},{12,8},{16,20},{20,16},{24,28},{28,24},{1,5},{5... | collective-permute-start | bytes 2359304 | tf_op jit(solution)/shard_map/ppermute | solution.py:981
  447.3 33.9 %collective-permute-start.18 = (bf16[1,192,1024]{2,1,0:T(8,128)(2,1)}, bf16[1,192,1024]{2,1,0:T(8,128)(2,1)}, u32[]{:S(2)}, u32[]{:S(2)}) collective-permute-start(bf16[1,192,1024]{2,1,0:T(8,128)(2,1)} %fusion.75), channel_id=1, source_target_pairs={{0,16},{4,20},{8,24},{12,28},{16,0},{20,4},{24,8},{28,12},{1,17},{... | collective-permute-start | bytes 1179656 | tf_op jit(solution)/shard_map/ppermute | solution.py:981
  451.3 30.0 %collective-permute-start.16 = (bf16[1,384,1024]{2,1,0:T(8,128)(2,1)}, bf16[1,384,1024]{2,1,0:T(8,128)(2,1)}, u32[]{:S(2)}, u32[]{:S(2)}) collective-permute-start(bf16[1,384,1024]{2,1,0:T(8,128)(2,1)} %slice.593), channel_id=1, source_target_pairs={{0,8},{4,12},{8,0},{12,4},{16,24},{20,28},{24,16},{28,20},{1,9},{5... | collective-permute-start | bytes 2359304 | tf_op jit(solution)/shard_map/ppermute | solution.py:981
  484.5 25.8 %collective-permute-start.20 = (bf16[1,192,1024]{2,1,0:T(8,128)(2,1)S(1)}, bf16[1,192,1024]{2,1,0:T(8,128)(2,1)S(1)}, u32[]{:S(2)}, u32[]{:S(2)}) collective-permute-start(bf16[1,192,1024]{2,1,0:T(8,128)(2,1)S(1)} %fusion.74), channel_id=1, source_target_pairs={{0,16},{4,20},{8,24},{12,28},{16,0},{20,4},{24,8},{28,12},{1,17},{... | collective-permute-start | bytes 1179656 | tf_op jit(solution)/shard_map/ppermute | solution.py:981
  486.2 16.0 %collective-permute-start.19 = (f32[3,768]{1,0:T(4,128)S(1)}, f32[3,768]{1,0:T(4,128)S(1)}, u32[]{:S(2)}, u32[]{:S(2)}) collective-permute-start(f32[3,768]{1,0:T(4,128)S(1)} %slice.334), channel_id=1, source_target_pairs={{4,0},{8,4},{12,8},{16,12},{20,16},{24,20},{28,24},{5,1},{9,5},{13... | collective-permute-start | bytes 27656 | tf_op jit(solution)/shard_map/ppermute | solution.py:31
  488.8 29.7 %collective-permute-start.25 = (bf16[1,192,1024]{2,1,0:T(8,128)(2,1)S(1)}, bf16[1,192,1024]{2,1,0:T(8,128)(2,1)S(1)}, u32[]{:S(2)}, u32[]{:S(2)}) collective-permute-start(bf16[1,192,1024]{2,1,0:T(8,128)(2,1)S(1)} %fusion.62), channel_id=1, source_target_pairs={{0,16},{4,20},{8,24},{12,28},{16,0},{20,4},{24,8},{28,12},{1,17},{... | collective-permute-start | bytes 1179656 | tf_op jit(solution)/shard_map/ppermute | solution.py:981
  495.6 27.6 %collective-permute-start.22 = (bf16[1,384,768]{2,1,0:T(8,128)(2,1)}, bf16[1,384,768]{2,1,0:T(8,128)(2,1)}, u32[]{:S(2)}, u32[]{:S(2)}) collective-permute-start(bf16[1,384,768]{2,1,0:T(8,128)(2,1)} %slice.598), channel_id=1, source_target_pairs={{0,4},{4,0},{8,12},{12,8},{16,20},{20,16},{24,28},{28,24},{1,5},{5... | collective-permute-start | bytes 1769480 | tf_op jit(solution)/shard_map/ppermute | solution.py:981
  498.8 28.5 %collective-permute-start.21 = (bf16[1,384,768]{2,1,0:T(8,128)(2,1)}, bf16[1,384,768]{2,1,0:T(8,128)(2,1)}, u32[]{:S(2)}, u32[]{:S(2)}) collective-permute-start(bf16[1,384,768]{2,1,0:T(8,128)(2,1)} %slice.599), channel_id=1, source_target_pairs={{0,8},{4,12},{8,0},{12,4},{16,24},{20,28},{24,16},{28,20},{1,9},{5... | collective-permute-start | bytes 1769480 | tf_op jit(solution)/shard_map/ppermute | solution.py:981
  529.2 68.0 %collective-permute-start.24 = (bf16[1,192,768]{2,1,0:T(8,128)(2,1)}, bf16[1,192,768]{2,1,0:T(8,128)(2,1)S(1)}, u32[]{:S(2)}, u32[]{:S(2)}) collective-permute-start(bf16[1,192,768]{2,1,0:T(8,128)(2,1)} %fusion.81), channel_id=1, source_target_pairs={{0,16},{4,20},{8,24},{12,28},{16,0},{20,4},{24,8},{28,12},{1,17},{... | collective-permute-start | bytes 884744 | tf_op jit(solution)/shard_map/ppermute | solution.py:981
  531.2 68.1 %collective-permute-start.23 = (bf16[1,192,768]{2,1,0:T(8,128)(2,1)}, bf16[1,192,768]{2,1,0:T(8,128)(2,1)S(1)}, u32[]{:S(2)}, u32[]{:S(2)}) collective-permute-start(bf16[1,192,768]{2,1,0:T(8,128)(2,1)} %fusion.84), channel_id=1, source_target_pairs={{0,16},{4,20},{8,24},{12,28},{16,0},{20,4},{24,8},{28,12},{1,17},{... | collective-permute-start | bytes 884744 | tf_op jit(solution)/shard_map/ppermute | solution.py:981
  (232 other events, 1353.2 us)

commit v8 on v7

--- a/solution.py
+++ b/solution.py
@@ -192,108 +192,124 @@
     return [(seq + 1 - 2 * place, head)] + others
 
 
+def level_count():
+    return lax.axis_size("seq").bit_length() - 1
+
+
+def level_peers():
+    seq = lax.axis_index("seq")
+    head = lax.axis_index("head")
+    bits = [1 << level for level in range(level_count())]
+    return [(seq + bit * (1 - 2 * ((seq // bit) % 2)), head) for bit in bits]
+
+
 def scatter_shapes(arrays):
     seq_count = lax.axis_size("seq")
     return [(a.shape[0] // seq_count, a.shape[1]) for a in arrays]
 
 
 def scatter_blocks(arrays):
-    pairs = lax.axis_size("seq") // 2
+    half = lax.axis_size("seq") // 2
     return [
-        a.reshape(pairs, 2, shape[0], shape[1])
+        a.reshape(half, 2, shape[0], shape[1])
         for a, shape in zip(arrays, scatter_shapes(arrays), strict=True)
     ]
 
 
 def scatter_scratch(shapes):
-    pairs = lax.axis_size("seq") // 2
+    half = lax.axis_size("seq") // 2
+    levels = level_count()
     count = len(shapes)
+    spaces = []
+    for shape in shapes:
+        for level in range(levels):
+            spaces.append(pltpu.VMEM((half >> level,) + shape, jnp.bfloat16))
+        for level in range(levels - 1):
+            spaces.append(pltpu.VMEM((half >> level + 1, 2) + shape, jnp.bfloat16))
     return (
-        [pltpu.VMEM((pairs,) + shape, jnp.bfloat16) for shape in shapes] * 2
-        + [pltpu.VMEM((pairs - 1,) + shape, jnp.bfloat16) for shape in shapes]
-        + [pltpu.SemaphoreType.DMA((count,))] * 3
-        + [pltpu.SemaphoreType.DMA((count, pairs - 1))] * 2
+        spaces
+        + [pltpu.SemaphoreType.DMA((count, half))]
+        + [pltpu.SemaphoreType.DMA((count, levels))] * 2
     )
 
 
 def scatter_job(takes, gives, scratch, shapes):
     count = len(takes)
-    pairs = lax.axis_size("seq") // 2
-    own, near, far = scratch[:count], scratch[count : 2 * count], scratch[2 * count : 3 * count]
-    own_sem, near_send, near_recv, far_send, far_recv = scratch[3 * count :]
+    levels = level_count()
+    half = lax.axis_size("seq") // 2
+    own_sem, send, recv = scratch[-3:]
+    per_array = 2 * levels - 1
+    got = [scratch[i * per_array : i * per_array + levels] for i in range(count)]
+    kept = [scratch[i * per_array + levels : (i + 1) * per_array] for i in range(count)]
     seq = lax.axis_index("seq")
-    place = seq % 2
-    pair = seq // 2
-    partner, *others = pair_peers()
-    owners = [(pair + k) % pairs for k in range(1, pairs)]
+    bits = [(seq // (1 << level)) % 2 for level in range(levels)]
+    peers = level_peers()
+
+    def exchange(i, level):
+        source = takes[i] if level == 0 else kept[i][level - 1]
+        return send_to(
+            source.at[:, 1 - bits[level]],
+            got[i][level],
+            send.at[i, level],
+            recv.at[i, level],
+            peers[level],
+        )
+
     loads = [
-        pltpu.make_async_copy(takes[i].at[:, place], own[i], own_sem.at[i]) for i in range(count)
-    ]
-    halves = [
-        send_to(takes[i].at[:, 1 - place], near[i], near_send.at[i], near_recv.at[i], partner)
+        [
+            pltpu.make_async_copy(
+                takes[i].at[j, bits[0]], kept[i][0].at[j // 2, j % 2], own_sem.at[i, j]
+            )
+            for j in range(half)
+        ]
         for i in range(count)
     ]
-
-    def launch(i):
-        if i < count:
-            halves[i].start()
-            loads[i].start()
-
-    sums = []
-
-    def finish(i):
-        for copy in sums[i]:
-            copy.wait_recv()
-
-        @pl.loop(0, shapes[i][0] // 16)
-        def add(step):
-            part = pl.ds(pl.multiple_of(step * 16, 16), 16)
-            total = own[i][pair, part].astype(jnp.float32)
-            for k in range(pairs - 1):
-                total = total + far[i][k, part].astype(jnp.float32)
-            gives[i][part] = total
-
-    launch(0)
-    launch(1)
-    for i in range(count):
-        yield
-        halves[i].wait_recv()
-        loads[i].wait()
-        launch(i + 2)
-
-        @pl.loop(0, pairs)
-        def merge(block):
+    sent = []
+
+    def launch(i, level):
+        copy = exchange(i, level)
+        copy.start()
+        sent.append(copy)
+        if level == 0:
+            for load in loads[i]:
+                load.start()
+
+    def merge(i, level):
+        exchange(i, level).wait_recv()
+        if level == 0:
+            for load in loads[i]:
+                load.wait()
+
+        @pl.loop(0, half >> level)
+        def blocks(j):
             @pl.loop(0, shapes[i][0] // 16)
             def add(step):
                 part = pl.ds(pl.multiple_of(step * 16, 16), 16)
-                total = own[i][block, part].astype(jnp.float32) + near[i][block, part].astype(
-                    jnp.float32
-                )
-                own[i][block, part] = total.astype(jnp.bfloat16)
-
-        sums.append(
-            [
-                send_to(
-                    own[i].at[owners[k]],
-                    far[i].at[k],
-                    far_send.at[i, k],
-                    far_recv.at[i, k],
-                    others[k],
-                )
-                for k in range(pairs - 1)
-            ]
-        )
-        for copy in sums[i]:
-            copy.start()
-        if i > 0:
-            finish(i - 1)
-    yield
-    finish(count - 1)
-    for copy in halves:
+                if level == 0:
+                    mine = kept[i][0][j // 2, j % 2, part]
+                else:
+                    mine = kept[i][level - 1][j, bits[level], part]
+                total = mine.astype(jnp.float32) + got[i][level][j, part].astype(jnp.float32)
+                if level == levels - 1:
+                    gives[i][part] = total
+                else:
+                    kept[i][level][j // 2, j % 2, part] = total.astype(jnp.bfloat16)
+
+    launch(0, 0)
+    if count > 1:
+        launch(1, 0)
+    for turn in range(count + levels - 1):
+        for level in range(levels):
+            i = turn - level
+            if 0 <= i < count:
+                yield
+                merge(i, level)
+                if level == 0 and i + 2 < count:
+                    launch(i + 2, 0)
+                if level + 1 < levels:
+                    launch(i, level + 1)
+    for copy in sent:
         copy.wait_send()
-    for group in sums:
-        for copy in group:
-            copy.wait_send()
 
 
 def scatter_and_head_sum(arrays, values, number):
@@ -306,7 +322,7 @@
         takes, x_ref = refs[:count], refs[count]
         gives, o_ref = refs[count + 1 : 2 * count + 1], refs[2 * count + 1]
         scratch = refs[2 * count + 2 :]
-        meet(pair_peers() + head_peers())
+        meet(level_peers() + head_peers())
         together(
             scatter_job(takes, gives, scratch[: len(spaces)], shapes),
             head_job(x_ref, o_ref, scratch[len(spaces) :], jnp.bfloat16, 4),

time: 609 us -> 606 us (level)
  transfers between devices with their start and end apart: 26 -> 26, of which waited for: 6 -> 6; matrix products, arithmetic and copies ran while one was open for 25% -> 25% of each run, Pallas kernels for 27% -> 28%
where the time goes in v8:
time: 606 us; the launch traced here: 600 us
  Pallas kernels  266 us (44%)
  local copies, waits for them, and re-layouts  82 us (14%)
  other arithmetic  78.4 us (13%)
  matrix products  78 us (13%)
  waiting for transfers between devices  50.6 us (8%)
  starting transfers between devices  40.7 us (7%)
    pallas_call x8, Pallas kernels, head_sum(): pl.pallas_call(kernel, out_shape=jax.ShapeDtypeStruct((rows, width), jnp....  95.4 us
    dot_general x46, matrix products, product(): return jnp.dot(left, right, preferred_element_type=jnp.float32)  59.2 us
    pallas_call x1, Pallas kernels, last_sums(): pl.pallas_call(kernel, out_shape=[jax.ShapeDtypeStruct(shape, jnp.float32...  51.7 us
    ppermute x24, waiting for transfers between devices, send(): flow['got'].append(lax.ppermute(flow['out'], 'seq', route))  50.6 us
    pallas_call x1, Pallas kernels, scatter_and_head_sum(): pl.pallas_call(kernel, out_shape=[jax.ShapeDtypeStruct(shape, jnp.float32...  50.5 us
    unnamed x488, local copies, waits for them, and re-layouts  35.9 us
    ppermute x24, starting transfers between devices, send(): flow['got'].append(lax.ppermute(flow['out'], 'seq', route))  34.3 us
    convert_element_type x20, other arithmetic, to_low(): return values.astype(jnp.bfloat16)  31.7 us
  transfers between devices with their start and end apart: 26, of which 6 were waited for; matrix products, arithmetic and copies ran while one was open for 25% of the time, Pallas kernels for 28%

profile of v8, /device:TPU:0, one launch (start us, length us, event | category | flops | bytes accessed | tf_op | source)
XLA Modules:
  0.0 599.9 jit_solution(10060150019635609223)
XLA Ops:
  5.2 4.9 collective-permute-start
  20.7 6.5 %head_sum.8 = f32[256,128]{1,0:T(8,128)S(1)} custom-call(f32[256,128]{1,0:T(8,128)S(1)} %fusion.158.x_ref), custom_call_target="tpu_custom_call" | custom-call | flops 6000 | bytes 6000 | tf_op jit(solution)/shard_map/head_sum/pallas_call | solution.py:173
  29.6 13.3 %run_summary.2.init_ref = f32[16,768]{1,0:T(8,128)S(1)} custom-call(f32[256,768]{1,0:T(8,128)S(1)} %get-tuple-element.446.step_ref, f32[256,768]{1,0:T(8,128)S(1)} %get-tuple-element.445.drive_ref, f32[256,16,128]{2,1,0:T(8,128)S(1)} %broadcast_in_dim.85.coef_ref.inject_ref, f32[16,768]{1,0:T(8,128)S(1)} %bitcast_multiply_fusion.3.slope_ref), custom_call_target="tpu_custom_call" | custom-call | flops 16000 | bytes 16000 | tf_op jit(solution)/shard_map/run_summary/pallas_call | solution.py:504
  43.6 8.1 %state_sweep.1 = (f32[256,768]{1,0:T(8,128)S(1)}, f32[256,16,768]{2,1,0:T(8,128)}, f32[16,768]{1,0:T(8,128)S(1)}) custom-call(f32[16,768]{1,0:T(8,128)S(1)} %run_summary.2.init_ref, f32[256,768]{1,0:T(8,128)S(1)} %get-tuple-element.446.step_ref, f32[256,768]{1,0:T(8,128)S(1)} %get-tuple-element.445.drive_ref, ...), custom_call_target="tpu_custom_call" | custom-call | flops 11000 | bytes 11000 | tf_op jit(solution)/shard_map/state_sweep/pallas_call | solution.py:555
  54.7 13.8 %head_sum.9 = f32[256,1536]{1,0:T(8,128)S(1)} custom-call(f32[256,1536]{1,0:T(8,128)S(1)} %fusion.205.x_ref), custom_call_target="tpu_custom_call" | custom-call | flops 15000 | bytes 15000 | tf_op jit(solution)/shard_map/head_sum/pallas_call | solution.py:173
  80.6 14.0 %head_sum.10 = f32[256,1536]{1,0:T(8,128)S(1)} custom-call(f32[256,1536]{1,0:T(8,128)S(1)} %copy-done.14), custom_call_target="tpu_custom_call" | custom-call | flops 15000 | bytes 15000 | tf_op jit(solution)/shard_map/head_sum/pallas_call | solution.py:173
  98.4 21.5 %attend.1 = (bf16[256,384]{1,0:T(8,128)(2,1)S(1)}, f32[128,1536]{1,0:T(8,128)S(1)}, f32[1,1536]{1,0:T(1,128)S(1)}, bf16[8,256,256]{2,1,0:T(8,128)(2,1)S(1)}) custom-call(bf16[256,384]{1,0:T(8,128)(2,1)S(1)} %convolution_convert_fusion.17.q_ref, bf16[256,256]{1,0:T(8,128)(2,1)S(1)} %pad_maximum_fusion.9.x_ref, s32[2048,1]{1,0:T(8,128)S(1)} %copy-done.10, ...), custom_call_target="tpu_custom_call" | custom-call | flops 12000 | bytes 12000 | tf_op jit(solution)/shard_map/attend/pallas_call | solution.py:830
  120.7 13.1 %head_sum.11 = f32[256,1536]{1,0:T(8,128)S(1)} custom-call(f32[256,1536]{1,0:T(8,128)S(1)} %fusion.208.x_ref), custom_call_target="tpu_custom_call" | custom-call | flops 15000 | bytes 15000 | tf_op jit(solution)/shard_map/head_sum/pallas_call | solution.py:173
  159.9 3.3 convolution_convert_fusion.2
  170.8 14.7 %head_sum.12 = f32[256,1664]{1,0:T(8,128)S(1)} custom-call(f32[256,1664]{1,0:T(8,128)S(1)} %select_maximum_fusion.x_ref), custom_call_target="tpu_custom_call" | custom-call | flops 16000 | bytes 16000 | tf_op jit(solution)/shard_map/head_sum/pallas_call | solution.py:173
  209.6 50.5 %scatter_and_head_sum.1 = (f32[256,128]{1,0:T(8,128)S(1)}, f32[256,128]{1,0:T(8,128)S(1)}, f32[256,1536]{1,0:T(8,128)S(1)}) custom-call(bf16[4,2,256,128]{3,2,1,0:T(8,128)(2,1)S(1)} %bitcast.453, bf16[4,2,256,128]{3,2,1,0:T(8,128)(2,1)S(1)} %bitcast.454, f32[256,1536]{1,0:T(8,128)S(1)} %fusion.150.refs_2_), custom_call_target="tpu_custom_call" | custom-call | flops 20000 | bytes 20000 | tf_op jit(solution)/shard_map/scatter_and_head_sum/pallas_call | solution.py:331
  265.1 3.0 convert_add_fusion
  269.7 3.0 collective-permute-start.4
  279.5 13.9 %head_sum.13 = f32[256,1536]{1,0:T(8,128)S(1)} custom-call(f32[256,1536]{1,0:T(8,128)S(1)} %convolution_add_fusion.3.x_ref), custom_call_target="tpu_custom_call" | custom-call | flops 15000 | bytes 15000 | tf_op jit(solution)/shard_map/head_sum/pallas_call | solution.py:173
  294.9 3.7 fusion.196
  305.3 3.8 fusion.129
  310.1 6.2 %collective-permute-done.3 = bf16[4,384,256]{2,1,0:T(8,128)(2,1)} collective-permute-done((bf16[4,384,256]{2,1,0:T(8,128)(2,1)}, bf16[4,384,256]{2,1,0:T(8,128)(2,1)}, u32[]{:S(2)}, u32[]{:S(2)}) %collective-permute-start.3) | collective-permute-done | bytes 786464 | tf_op jit(solution)/shard_map/ppermute | solution.py:997
  325.5 4.1 collective-permute-start.8
  329.7 3.1 fusion.9
  335.9 3.0 collective-permute-start.6
  338.9 13.5 %head_sum.14 = f32[256,1536]{1,0:T(8,128)S(1)} custom-call(f32[256,1536]{1,0:T(8,128)S(1)} %convolution_add_fusion.x_ref), custom_call_target="tpu_custom_call" | custom-call | flops 15000 | bytes 15000 | tf_op jit(solution)/shard_map/head_sum/pallas_call | solution.py:173
  367.0 18.6 %collective-permute-done.6 = bf16[4,192,256]{2,1,0:T(8,128)(2,1)} collective-permute-done((bf16[4,192,256]{2,1,0:T(8,128)(2,1)}, bf16[4,192,256]{2,1,0:T(8,128)(2,1)}, u32[]{:S(2)}, u32[]{:S(2)}) %collective-permute-start.6) | collective-permute-done | bytes 393248 | tf_op jit(solution)/shard_map/ppermute | solution.py:997
  386.8 10.7 %run_summary.3.in_ref = f32[16,768]{1,0:T(8,128)S(1)} custom-call(f32[256,768]{1,0:T(8,128)S(1)} %copy-done.7, f32[256,768]{1,0:T(8,128)S(1)} %copy-done.16, f32[256,16,128]{2,1,0:T(8,128)S(1)} %copy-done.5, f32[16,768]{1,0:T(8,128)S(1)} %bitcast_multiply_fusion.3.slope_ref), custom_call_target="tpu_custom_call" | custom-call | flops 16000 | bytes 16000 | tf_op jit(solution)/shard_map/run_summary/pallas_call | solution.py:504
  407.8 12.8 %adjoint_sweep.1 = (f32[256,768]{1,0:T(8,128)S(1)}, f32[256,768]{1,0:T(8,128)S(1)}, f32[256,16,128]{2,1,0:T(8,128)S(1)}, f32[256,16,128]{2,1,0:T(8,128)S(1)}, f32[16,768]{1,0:T(8,128)S(1)}) custom-call(f32[16,768]{1,0:T(8,128)S(1)} %run_summary.3.in_ref, f32[16,768]{1,0:T(8,128)S(1)} %copy-done.33, f32[256,16,768]{2,1,0:T(8,128)} %get-tuple-element.131.before_ref, ...), custom_call_target="tpu_custom_call" | custom-call | flops 15000 | bytes 15000 | tf_op jit(solution)/shard_map/adjoint_sweep/pallas_call | solution.py:640
  423.7 3.0 reduce_sum.297
  429.4 3.4 fusion.8
  439.1 5.1 collective-permute-done.11
  459.5 6.0 %head_sum.15 = f32[256,128]{1,0:T(8,128)S(1)} custom-call(f32[256,128]{1,0:T(8,128)S(1)} %pad_maximum_fusion.10.x_ref), custom_call_target="tpu_custom_call" | custom-call | flops 6000 | bytes 6000 | tf_op jit(solution)/shard_map/head_sum/pallas_call | solution.py:173
  471.0 10.9 %collective-permute-done.15 = bf16[1,384,1024]{2,1,0:T(8,128)(2,1)} collective-permute-done((bf16[1,384,1024]{2,1,0:T(8,128)(2,1)}, bf16[1,384,1024]{2,1,0:T(8,128)(2,1)}, u32[]{:S(2)}, u32[]{:S(2)}) %collective-permute-start.15) | collective-permute-done | bytes 786464 | tf_op jit(solution)/shard_map/ppermute | solution.py:997
  491.1 4.0 collective-permute-start.25
  505.1 7.8 %collective-permute-done.20 = bf16[1,192,1024]{2,1,0:T(8,128)(2,1)S(1)} collective-permute-done((bf16[1,192,1024]{2,1,0:T(8,128)(2,1)S(1)}, bf16[1,192,1024]{2,1,0:T(8,128)(2,1)S(1)}, u32[]{:S(2)}, u32[]{:S(2)}) %collective-permute-start.20) | collective-permute-done | bytes 393248 | tf_op jit(solution)/shard_map/ppermute | solution.py:997
  534.6 51.7 %last_sums.1 = (f32[192,384]{1,0:T(8,128)S(1)}, f32[192,384]{1,0:T(8,128)S(1)}, f32[96,256]{1,0:T(8,128)S(1)}, f32[32,128]{1,0:T(8,128)S(1)}, f32[256,1536]{1,0:T(8,128)S(1)}, /*index=5*/f32[1,1536]{1,0:T(1,128)S(1)}) custom-call(bf16[4,2,192,384]{3,2,1,0:T(8,128)(2,1)S(1)} %bitcast.451, bf16[4,2,192,384]{3,2,1,0:T(8,128)(2,1)S(1)} %bitcast.450, ...), custom_call_target="tpu_custom_call" | custom-call | flops 20000 | bytes 20000 | tf_op jit(solution)/shard_map/last_sums/pallas_call | solution.py:399
  (739 shorter events, 240.9 us)
Async XLA Ops:
  0.7 148.6 %copy-start = (bf16[4,256,1536]{2,1,0:T(8,128)(2,1)S(1)}, bf16[4,256,1536]{2,1,0:T(8,128)(2,1)}, u32[]{:S(2)}) copy-start(bf16[4,256,1536]{2,1,0:T(8,128)(2,1)} %param.59) | copy-start | bytes 9437188
  5.2 13.5 %collective-permute-start = (bf16[3,768]{1,0:T(4,128)(2,1)S(1)}, bf16[3,768]{1,0:T(4,128)(2,1)S(1)}, u32[]{:S(2)}, u32[]{:S(2)}) collective-permute-start(bf16[3,768]{1,0:T(4,128)(2,1)S(1)} %slice.392), channel_id=1, source_target_pairs={{0,4},{4,8},{8,12},{12,16},{16,20},{20,24},{24,28},{1,5},{5,9},{9,... | collective-permute-start | bytes 13832 | tf_op jit(solution)/shard_map/ppermute | solution.py:31
  20.7 48.1 %copy-start.167 = (f32[1536]{0:T(1024)}, f32[1536]{0:T(1024)S(1)}, u32[]{:S(2)}) copy-start(f32[1536]{0:T(1024)S(1)} %convert_element_type.382) | copy-start | bytes 18436
  54.7 40.2 %copy-start.173 = (f32[1536]{0:T(1024)}, f32[1536]{0:T(1024)S(1)}, u32[]{:S(2)}) copy-start(f32[1536]{0:T(1024)S(1)} %convert_element_type.385) | copy-start | bytes 18436
  94.9 38.9 %copy-start.43 = (f32[256,1536]{1,0:T(8,128)}, f32[256,1536]{1,0:T(8,128)S(1)}, u32[]{:S(2)}) copy-start(f32[256,1536]{1,0:T(8,128)S(1)} %get-tuple-element.363) | copy-start | bytes 4718596
  163.2 99.0 %collective-permute-start.2 = (bf16[4,768,512]{2,1,0:T(8,128)(2,1)}, bf16[4,768,512]{2,1,0:T(8,128)(2,1)}, u32[]{:S(2)}, u32[]{:S(2)}) collective-permute-start(bf16[4,768,512]{2,1,0:T(8,128)(2,1)} %convolution_convert_fusion.2), channel_id=1, source_target_pairs={{0,4},{4,0},{8,12},{12,8},{16,20},{20,16},{24,28},{28,24},{1,5},{5... | collective-permute-start | bytes 9437192 | tf_op jit(solution)/shard_map/ppermute | solution.py:997
  170.2 39.4 %collective-permute-start.1 = (bf16[4,768,256]{2,1,0:T(8,128)(2,1)}, bf16[4,768,256]{2,1,0:T(8,128)(2,1)}, u32[]{:S(2)}, u32[]{:S(2)}) collective-permute-start(bf16[4,768,256]{2,1,0:T(8,128)(2,1)} %convolution_convert_fusion.7), channel_id=1, source_target_pairs={{0,8},{4,12},{8,0},{12,4},{16,24},{20,28},{24,16},{28,20},{1,9},{5... | collective-permute-start | bytes 4718600 | tf_op jit(solution)/shard_map/ppermute | solution.py:997
  203.7 197.6 %copy-start.121 = (bf16[1,192,256]{1,2,0:T(8,128)(2,1)}, bf16[1,192,256]{1,2,0:T(8,128)(2,1)S(1)}, u32[]{:S(2)}) copy-start(bf16[1,192,256]{1,2,0:T(8,128)(2,1)S(1)} %get-tuple-element.421) | copy-start | bytes 294916
  264.0 52.2 %collective-permute-start.5 = (bf16[1,768,1024]{1,2,0:T(8,128)(2,1)}, bf16[1,768,1024]{1,2,0:T(8,128)(2,1)}, u32[]{:S(2)}, u32[]{:S(2)}) collective-permute-start(bf16[1,768,1024]{1,2,0:T(8,128)(2,1)} %pad_maximum_fusion), channel_id=1, source_target_pairs={{0,4},{4,0},{8,12},{12,8},{16,20},{20,16},{24,28},{28,24},{1,5},{5... | collective-permute-start | bytes 4718600 | tf_op jit(solution)/shard_map/ppermute | solution.py:997
  269.7 46.6 %collective-permute-start.4 = (bf16[4,384,512]{2,1,0:T(8,128)(2,1)}, bf16[4,384,512]{2,1,0:T(8,128)(2,1)}, u32[]{:S(2)}, u32[]{:S(2)}) collective-permute-start(bf16[4,384,512]{2,1,0:T(8,128)(2,1)} %slice.592), channel_id=1, source_target_pairs={{0,8},{4,12},{8,0},{12,4},{16,24},{20,28},{24,16},{28,20},{1,9},{5... | collective-permute-start | bytes 4718600 | tf_op jit(solution)/shard_map/ppermute | solution.py:997
  278.5 37.7 %collective-permute-start.3 = (bf16[4,384,256]{2,1,0:T(8,128)(2,1)}, bf16[4,384,256]{2,1,0:T(8,128)(2,1)}, u32[]{:S(2)}, u32[]{:S(2)}) collective-permute-start(bf16[4,384,256]{2,1,0:T(8,128)(2,1)} %slice.597), channel_id=1, source_target_pairs={{0,4},{4,0},{8,12},{12,8},{16,20},{20,16},{24,28},{28,24},{1,5},{5... | collective-permute-start | bytes 2359304 | tf_op jit(solution)/shard_map/ppermute | solution.py:997
  301.9 65.1 %collective-permute-start.9 = (bf16[1,768,1024]{2,1,0:T(8,128)(2,1)}, bf16[1,768,1024]{2,1,0:T(8,128)(2,1)}, u32[]{:S(2)}, u32[]{:S(2)}) collective-permute-start(bf16[1,768,1024]{2,1,0:T(8,128)(2,1)} %fusion.11), channel_id=1, source_target_pairs={{0,8},{4,12},{8,0},{12,4},{16,24},{20,28},{24,16},{28,20},{1,9},{5... | collective-permute-start | bytes 4718600 | tf_op jit(solution)/shard_map/ppermute | solution.py:997
  317.0 46.7 %copy-start.64 = (bf16[256,1024]{1,0:T(8,128)(2,1)}, bf16[256,1024]{1,0:T(8,128)(2,1)S(1)}, u32[]{:S(2)}) copy-start(bf16[256,1024]{1,0:T(8,128)(2,1)S(1)} %get-tuple-element.387) | copy-start | bytes 1572868
  321.6 64.0 %collective-permute-start.10 = (bf16[1,768,1024]{2,1,0:T(8,128)(2,1)}, bf16[1,768,1024]{2,1,0:T(8,128)(2,1)}, u32[]{:S(2)}, u32[]{:S(2)}) collective-permute-start(bf16[1,768,1024]{2,1,0:T(8,128)(2,1)} %fusion.12), channel_id=1, source_target_pairs={{0,4},{4,0},{8,12},{12,8},{16,20},{20,16},{24,28},{28,24},{1,5},{5... | collective-permute-start | bytes 4718600 | tf_op jit(solution)/shard_map/ppermute | solution.py:997
  325.5 60.1 %collective-permute-start.8 = (bf16[1,384,1024]{1,2,0:T(8,128)(2,1)}, bf16[1,384,1024]{1,2,0:T(8,128)(2,1)}, u32[]{:S(2)}, u32[]{:S(2)}) collective-permute-start(bf16[1,384,1024]{1,2,0:T(8,128)(2,1)} %slice.596), channel_id=1, source_target_pairs={{0,8},{4,12},{8,0},{12,4},{16,24},{20,28},{24,16},{28,20},{1,9},{5... | collective-permute-start | bytes 2359304 | tf_op jit(solution)/shard_map/ppermute | solution.py:997
  332.8 52.8 %collective-permute-start.7 = (bf16[4,192,512]{2,1,0:T(8,128)(2,1)}, bf16[4,192,512]{2,1,0:T(8,128)(2,1)}, u32[]{:S(2)}, u32[]{:S(2)}) collective-permute-start(bf16[4,192,512]{2,1,0:T(8,128)(2,1)} %fusion.9), channel_id=1, source_target_pairs={{0,16},{4,20},{8,24},{12,28},{16,0},{20,4},{24,8},{28,12},{1,17},{... | collective-permute-start | bytes 2359304 | tf_op jit(solution)/shard_map/ppermute | solution.py:997
  335.9 49.7 %collective-permute-start.6 = (bf16[4,192,256]{2,1,0:T(8,128)(2,1)}, bf16[4,192,256]{2,1,0:T(8,128)(2,1)}, u32[]{:S(2)}, u32[]{:S(2)}) collective-permute-start(bf16[4,192,256]{2,1,0:T(8,128)(2,1)} %fusion.76), channel_id=1, source_target_pairs={{0,16},{4,20},{8,24},{12,28},{16,0},{20,4},{24,8},{28,12},{1,17},{... | collective-permute-start | bytes 1179656 | tf_op jit(solution)/shard_map/ppermute | solution.py:997
  400.5 38.6 %collective-permute-start.13 = (bf16[1,192,1024]{1,2,0:T(8,128)(2,1)}, bf16[1,192,1024]{1,2,0:T(8,128)(2,1)}, u32[]{:S(2)}, u32[]{:S(2)}) collective-permute-start(bf16[1,192,1024]{1,2,0:T(8,128)(2,1)} %fusion.25), channel_id=1, source_target_pairs={{0,16},{4,20},{8,24},{12,28},{16,0},{20,4},{24,8},{28,12},{1,17},{... | collective-permute-start | bytes 1179656 | tf_op jit(solution)/shard_map/ppermute | solution.py:997
  404.7 34.3 %collective-permute-start.12 = (bf16[1,384,1024]{2,1,0:T(8,128)(2,1)}, bf16[1,384,1024]{2,1,0:T(8,128)(2,1)}, u32[]{:S(2)}, u32[]{:S(2)}) collective-permute-start(bf16[1,384,1024]{2,1,0:T(8,128)(2,1)} %slice.595), channel_id=1, source_target_pairs={{0,8},{4,12},{8,0},{12,4},{16,24},{20,28},{24,16},{28,20},{1,9},{5... | collective-permute-start | bytes 2359304 | tf_op jit(solution)/shard_map/ppermute | solution.py:997
  406.5 37.6 %collective-permute-start.11 = (bf16[1,768,1024]{2,1,0:T(8,128)(2,1)}, bf16[1,768,1024]{2,1,0:T(8,128)(2,1)}, u32[]{:S(2)}, u32[]{:S(2)}) collective-permute-start(bf16[1,768,1024]{2,1,0:T(8,128)(2,1)} %fusion.10), channel_id=1, source_target_pairs={{0,4},{4,0},{8,12},{12,8},{16,20},{20,16},{24,28},{28,24},{1,5},{5... | collective-permute-start | bytes 4718600 | tf_op jit(solution)/shard_map/ppermute | solution.py:997
  428.0 43.0 %collective-permute-start.14 = (bf16[1,768,768]{2,1,0:T(8,128)(2,1)}, bf16[1,768,768]{2,1,0:T(8,128)(2,1)}, u32[]{:S(2)}, u32[]{:S(2)}) collective-permute-start(bf16[1,768,768]{2,1,0:T(8,128)(2,1)} %fusion.13), channel_id=1, source_target_pairs={{0,8},{4,12},{8,0},{12,4},{16,24},{20,28},{24,16},{28,20},{1,9},{5... | collective-permute-start | bytes 3538952 | tf_op jit(solution)/shard_map/ppermute | solution.py:997
  428.3 55.9 %collective-permute-start.17 = (bf16[1,768,768]{2,1,0:T(8,128)(2,1)}, bf16[1,768,768]{2,1,0:T(8,128)(2,1)}, u32[]{:S(2)}, u32[]{:S(2)}) collective-permute-start(bf16[1,768,768]{2,1,0:T(8,128)(2,1)} %fusion.14), channel_id=1, source_target_pairs={{0,4},{4,0},{8,12},{12,8},{16,20},{20,16},{24,28},{28,24},{1,5},{5... | collective-permute-start | bytes 3538952 | tf_op jit(solution)/shard_map/ppermute | solution.py:997
  447.1 34.8 %collective-permute-start.15 = (bf16[1,384,1024]{2,1,0:T(8,128)(2,1)}, bf16[1,384,1024]{2,1,0:T(8,128)(2,1)}, u32[]{:S(2)}, u32[]{:S(2)}) collective-permute-start(bf16[1,384,1024]{2,1,0:T(8,128)(2,1)} %slice.594), channel_id=1, source_target_pairs={{0,4},{4,0},{8,12},{12,8},{16,20},{20,16},{24,28},{28,24},{1,5},{5... | collective-permute-start | bytes 2359304 | tf_op jit(solution)/shard_map/ppermute | solution.py:997
  450.7 33.5 %collective-permute-start.18 = (bf16[1,192,1024]{2,1,0:T(8,128)(2,1)}, bf16[1,192,1024]{2,1,0:T(8,128)(2,1)}, u32[]{:S(2)}, u32[]{:S(2)}) collective-permute-start(bf16[1,192,1024]{2,1,0:T(8,128)(2,1)} %fusion.75), channel_id=1, source_target_pairs={{0,16},{4,20},{8,24},{12,28},{16,0},{20,4},{24,8},{28,12},{1,17},{... | collective-permute-start | bytes 1179656 | tf_op jit(solution)/shard_map/ppermute | solution.py:997
  455.5 28.7 %collective-permute-start.16 = (bf16[1,384,1024]{2,1,0:T(8,128)(2,1)}, bf16[1,384,1024]{2,1,0:T(8,128)(2,1)}, u32[]{:S(2)}, u32[]{:S(2)}) collective-permute-start(bf16[1,384,1024]{2,1,0:T(8,128)(2,1)} %slice.593), channel_id=1, source_target_pairs={{0,8},{4,12},{8,0},{12,4},{16,24},{20,28},{24,16},{28,20},{1,9},{5... | collective-permute-start | bytes 2359304 | tf_op jit(solution)/shard_map/ppermute | solution.py:997
  487.4 25.6 %collective-permute-start.20 = (bf16[1,192,1024]{2,1,0:T(8,128)(2,1)S(1)}, bf16[1,192,1024]{2,1,0:T(8,128)(2,1)S(1)}, u32[]{:S(2)}, u32[]{:S(2)}) collective-permute-start(bf16[1,192,1024]{2,1,0:T(8,128)(2,1)S(1)} %fusion.74), channel_id=1, source_target_pairs={{0,16},{4,20},{8,24},{12,28},{16,0},{20,4},{24,8},{28,12},{1,17},{... | collective-permute-start | bytes 1179656 | tf_op jit(solution)/shard_map/ppermute | solution.py:997
  488.5 16.6 %collective-permute-start.19 = (f32[3,768]{1,0:T(4,128)S(1)}, f32[3,768]{1,0:T(4,128)S(1)}, u32[]{:S(2)}, u32[]{:S(2)}) collective-permute-start(f32[3,768]{1,0:T(4,128)S(1)} %slice.334), channel_id=1, source_target_pairs={{4,0},{8,4},{12,8},{16,12},{20,16},{24,20},{28,24},{5,1},{9,5},{13... | collective-permute-start | bytes 27656 | tf_op jit(solution)/shard_map/ppermute | solution.py:31
  491.1 30.1 %collective-permute-start.25 = (bf16[1,192,1024]{2,1,0:T(8,128)(2,1)S(1)}, bf16[1,192,1024]{2,1,0:T(8,128)(2,1)S(1)}, u32[]{:S(2)}, u32[]{:S(2)}) collective-permute-start(bf16[1,192,1024]{2,1,0:T(8,128)(2,1)S(1)} %fusion.62), channel_id=1, source_target_pairs={{0,16},{4,20},{8,24},{12,28},{16,0},{20,4},{24,8},{28,12},{1,17},{... | collective-permute-start | bytes 1179656 | tf_op jit(solution)/shard_map/ppermute | solution.py:997
  498.1 27.7 %collective-permute-start.22 = (bf16[1,384,768]{2,1,0:T(8,128)(2,1)}, bf16[1,384,768]{2,1,0:T(8,128)(2,1)}, u32[]{:S(2)}, u32[]{:S(2)}) collective-permute-start(bf16[1,384,768]{2,1,0:T(8,128)(2,1)} %slice.598), channel_id=1, source_target_pairs={{0,4},{4,0},{8,12},{12,8},{16,20},{20,16},{24,28},{28,24},{1,5},{5... | collective-permute-start | bytes 1769480 | tf_op jit(solution)/shard_map/ppermute | solution.py:997
  501.7 26.2 %collective-permute-start.21 = (bf16[1,384,768]{2,1,0:T(8,128)(2,1)}, bf16[1,384,768]{2,1,0:T(8,128)(2,1)}, u32[]{:S(2)}, u32[]{:S(2)}) collective-permute-start(bf16[1,384,768]{2,1,0:T(8,128)(2,1)} %slice.599), channel_id=1, source_target_pairs={{0,8},{4,12},{8,0},{12,4},{16,24},{20,28},{24,16},{28,20},{1,9},{5... | collective-permute-start | bytes 1769480 | tf_op jit(solution)/shard_map/ppermute | solution.py:997
  529.8 64.4 %collective-permute-start.24 = (bf16[1,192,768]{2,1,0:T(8,128)(2,1)}, bf16[1,192,768]{2,1,0:T(8,128)(2,1)S(1)}, u32[]{:S(2)}, u32[]{:S(2)}) collective-permute-start(bf16[1,192,768]{2,1,0:T(8,128)(2,1)} %fusion.81), channel_id=1, source_target_pairs={{0,16},{4,20},{8,24},{12,28},{16,0},{20,4},{24,8},{28,12},{1,17},{... | collective-permute-start | bytes 884744 | tf_op jit(solution)/shard_map/ppermute | solution.py:997
  531.7 64.7 %collective-permute-start.23 = (bf16[1,192,768]{2,1,0:T(8,128)(2,1)}, bf16[1,192,768]{2,1,0:T(8,128)(2,1)S(1)}, u32[]{:S(2)}, u32[]{:S(2)}) collective-permute-start(bf16[1,192,768]{2,1,0:T(8,128)(2,1)} %fusion.84), channel_id=1, source_target_pairs={{0,16},{4,20},{8,24},{12,28},{16,0},{20,4},{24,8},{28,12},{1,17},{... | collective-permute-start | bytes 884744 | tf_op jit(solution)/shard_map/ppermute | solution.py:997
  (232 other events, 1351.4 us)
